TPU v7x, 32 devices: a whole 2x2x4 slice. The times are simulated.
32 devices in a mesh: dp: 16 (over z, x, core), mp: 2 (over y).
Axes of the slice: x: 2, y: 2, z: 4, core: 2. Of those that a mesh axis runs over, the one named last changes fastest.
Arguments:
- tokens: bfloat16 [64, 512, 512], P(('dp', 'mp')), may hold values from -6 to 6
- memory: bfloat16 [64, 512, 512], P('dp'), may hold values from -6 to 6
- neighbours: bfloat16 [64, 512, 4, 512], P(('dp', 'mp')), may hold values from -6 to 6
- neighbour_ids: int32 [64, 512, 4], P(('dp', 'mp')), may hold values from 0 to 267734
- doc_starts: int32 [64], P('dp'), may hold values 0 or 1
- bin_edges: int32 [129], replicated, may hold values from 0 to 267735, as said below
- w_query: bfloat16 [512, 512], P(None, 'mp'), may hold values from -0.25 to 0.25
- w_key: bfloat16 [512, 512], P(None, 'mp'), may hold values from -0.25 to 0.25
- w_value: bfloat16 [512, 512], P(None, 'mp'), may hold values from -0.25 to 0.25
- w_out: bfloat16 [512, 512], P('mp'), may hold values from -4 to 4
- w_up: bfloat16 [512, 2048], P(None, 'mp'), may hold values from -0.25 to 0.25
- w_down: bfloat16 [2048, 512], P('mp'), may hold values from -0.125 to 0.125
- gain_attn: float32 [512], replicated, may hold values from 0.5 to 1.5
- gain_ffn: float32 [512], replicated, may hold values from 0.5 to 1.5
- w_gate: float32 [512], replicated, may hold values from -0.25 to 0.25
- cotangent: bfloat16 [64, 512, 512], P(('dp', 'mp')), may hold values from -6 to 6
Outputs:
- result: bfloat16 [64, 512, 512], P(('dp', 'mp'))
- grad_input: bfloat16 [64, 512, 512], P(('dp', 'mp'))
- grad_w_query: float32 [512, 512], P(None, 'mp')
- grad_w_key: float32 [512, 512], P(None, 'mp')
- grad_w_value: float32 [512, 512], P(None, 'mp')
- grad_w_out: float32 [512, 512], P('mp')
- grad_w_up: float32 [512, 2048], P(None, 'mp')
- grad_w_down: float32 [2048, 512], P('mp')
- grad_gain_attn: float32 [512], replicated
- grad_gain_ffn: float32 [512], replicated
- grad_w_gate: float32 [512], replicated
- gate_mean: float32 [], replicated
- gate_hist: float32 [128], replicated
Inputs may be any that keep to these rules, and one draw needn't show every extreme that they name: bin_edges[0] is 0, bin_edges[128] is 267735, strictly increasing.
All inputs are finite; a program needn't handle non-finite values. No bound on the sum of `doc_starts` on one device may be relied on, other than what follows from the above.
Results may differ from a plain program's by a relative error of at most 0.015.
The roundings to bfloat16 on the way count: a program that leaves them out, or rounds other values in their place, can miss the bound.
Values may be sent and summed in bfloat16 or wider, within the bound.
No kernel may reach another device: no remote copies, remote signals or barrier semaphores. Data moves between devices by JAX's collectives and lax.ppermute only.
A program may use at most 192 MiB of HBM per device.

v0:
```python
import jax
import jax.numpy as jnp
from jax import lax
from jax.sharding import PartitionSpec as P

HEAD = 64
NEIGH = 4
BINS = 128


EPS = 1e-05
HIGH = lax.Precision.HIGHEST


def layer_norm(values, gain):
    centre = values - jnp.mean(values, -1, keepdims=True)
    spread = jnp.mean(centre * centre, -1, keepdims=True)
    return centre * lax.rsqrt(spread + EPS) * gain


def key_mask(length, starts):
    query_pos = lax.broadcasted_iota(jnp.int32, (length, 2 * length), 0)
    key_pos = lax.broadcasted_iota(jnp.int32, (length, 2 * length), 1)
    causal = (key_pos >= length) & (key_pos - length <= query_pos)
    return causal | (key_pos < length) & (starts == 0)


def neighbour_mix(hidden, neighbours, w_gate):
    affinity = jnp.einsum("rtkd,rtd->rtk", neighbours, hidden, precision=HIGH) * hidden.shape[
        -1
    ] ** (-0.5)
    weights = jax.nn.softmax(affinity, axis=-1)
    recalled = jnp.einsum("rtk,rtkd->rtd", weights, neighbours, precision=HIGH)
    gate = jax.nn.sigmoid(jnp.sum(hidden * w_gate, -1))
    return (hidden + gate[..., None] * recalled, gate)


def project(left, right):
    return jnp.einsum("rtd,dc->rtc", left, right, preferred_element_type=jnp.float32)


def project_back(left, right):
    return jnp.einsum("rtc,dc->rtd", left, right, preferred_element_type=jnp.float32)


def outer_sum(left, right):
    return jnp.einsum("rtd,rtc->dc", left, right, preferred_element_type=jnp.float32)


def shards(
    tokens,
    memory,
    neighbours,
    neighbour_ids,
    doc_starts,
    bin_edges,
    w_query,
    w_key,
    w_value,
    w_out,
    w_up,
    w_down,
    gain_attn,
    gain_ffn,
    w_gate,
    cotangent,
):
    length = tokens.shape[1]
    own_rows = tokens.shape[0]
    scale = HEAD ** (-0.5)
    tok_float = tokens.astype(jnp.float32)
    normed = layer_norm(tok_float, gain_attn).astype(jnp.bfloat16)
    query_full, key_full, value_full, out_full = (
        lax.all_gather(w_query, "mp", axis=1, tiled=True),
        lax.all_gather(w_key, "mp", axis=1, tiled=True),
        lax.all_gather(w_value, "mp", axis=1, tiled=True),
        lax.all_gather(w_out, "mp", axis=0, tiled=True),
    )
    offset = lax.axis_index("mp") * own_rows
    memory_rows = lax.dynamic_slice_in_dim(memory, offset, own_rows, 0)
    start_rows = lax.dynamic_slice_in_dim(doc_starts, offset, own_rows, 0)
    mem_float = memory_rows.astype(jnp.float32)
    mem_normed = layer_norm(mem_float, gain_attn).astype(jnp.bfloat16)
    kv_input = jnp.concatenate([mem_normed, normed], axis=1)
    query = project(normed, query_full).astype(jnp.bfloat16)
    keys = project(kv_input, key_full).astype(jnp.bfloat16)
    values = project(kv_input, value_full).astype(jnp.bfloat16)
    local_heads = query.shape[-1] // HEAD

    def head_view(block, span):
        return block.reshape(span, local_heads, HEAD)

    def row_scores(query_row, key_row, start_flag):
        raw = (
            jnp.einsum(
                "qhc,khc->hqk",
                head_view(query_row, length),
                head_view(key_row, 2 * length),
                preferred_element_type=jnp.float32,
            )
            * scale
        )
        return jnp.where(key_mask(length, start_flag)[None], raw, -1e30)

    def attend_row(blocks):
        query_row, key_row, value_row, start_flag = blocks
        scores = row_scores(query_row, key_row, start_flag)
        top = jnp.max(scores, -1, keepdims=True)
        log_total = top + jnp.log(jnp.sum(jnp.exp(scores - top), -1, keepdims=True))
        probs = jnp.exp(scores - log_total).astype(jnp.bfloat16)
        context_row = jnp.einsum(
            "hqk,khc->qhc",
            probs,
            head_view(value_row, 2 * length),
            preferred_element_type=jnp.float32,
        )
        return (context_row.reshape(length, -1).astype(jnp.bfloat16), log_total)

    context, log_totals = lax.map(attend_row, (query, keys, values, start_rows))
    attn_part = project(context, out_full)
    hidden = tok_float + attn_part
    neigh_float = neighbours.astype(jnp.float32)
    mixed, gate = neighbour_mix(hidden, neigh_float, w_gate)
    ffn_in = layer_norm(mixed, gain_ffn).astype(jnp.bfloat16)
    up_full, down_full = (w_up, w_down)
    ffn_rows = lax.all_gather(ffn_in, "mp", axis=0, tiled=True)
    pre_act = project(ffn_rows, up_full)
    activ = jax.nn.gelu(pre_act).astype(jnp.bfloat16)
    down_part = project(activ, down_full)
    ffn_out = lax.psum_scatter(
        down_part.astype(jnp.bfloat16), "mp", scatter_dimension=0, tiled=True
    ).astype(jnp.float32)
    result = (mixed + ffn_out).astype(jnp.bfloat16)
    grad_out = cotangent.astype(jnp.float32)
    grad_rows = lax.all_gather(cotangent, "mp", axis=0, tiled=True)
    grad_down = outer_sum(activ, grad_rows)
    grad_act = project_back(grad_rows, down_full)
    _, gelu_pull = jax.vjp(jax.nn.gelu, pre_act)
    grad_pre = gelu_pull(grad_act)[0].astype(jnp.bfloat16)
    grad_up = outer_sum(ffn_rows, grad_pre)
    grad_in_part = project_back(grad_pre, up_full)
    grad_ffn_in = lax.psum_scatter(
        grad_in_part.astype(jnp.bfloat16), "mp", scatter_dimension=0, tiled=True
    ).astype(jnp.float32)
    _, ffn_norm_pull = jax.vjp(layer_norm, mixed, gain_ffn)
    grad_mixed, grad_gain_ffn = ffn_norm_pull(grad_ffn_in)
    grad_mixed = grad_mixed + grad_out
    _, mix_pull = jax.vjp(
        lambda state, vector: neighbour_mix(state, neigh_float, vector)[0], hidden, w_gate
    )
    grad_hidden, grad_gate_vec = mix_pull(grad_mixed)
    grad_hidden_low = grad_hidden.astype(jnp.bfloat16)
    grad_wout = outer_sum(context, grad_hidden_low)
    grad_context = project_back(grad_hidden_low, out_full).astype(jnp.bfloat16)

    def back_row(blocks):
        query_row, key_row, value_row, start_flag, log_total, grad_row = blocks
        scores = row_scores(query_row, key_row, start_flag)
        probs = jnp.exp(scores - log_total)
        grad_view = head_view(grad_row, length)
        key_view = head_view(key_row, 2 * length)
        query_view = head_view(query_row, length)
        grad_probs = jnp.einsum(
            "qhc,khc->hqk",
            grad_view,
            head_view(value_row, 2 * length),
            preferred_element_type=jnp.float32,
        )
        inner = jnp.sum(probs * grad_probs, -1, keepdims=True)
        grad_scores = (probs * (grad_probs - inner)).astype(jnp.bfloat16)
        grad_q = (
            jnp.einsum("hqk,khc->qhc", grad_scores, key_view, preferred_element_type=jnp.float32)
            * scale
        )
        grad_k = (
            jnp.einsum("hqk,qhc->khc", grad_scores, query_view, preferred_element_type=jnp.float32)
            * scale
        )
        grad_v = jnp.einsum(
            "hqk,qhc->khc",
            probs.astype(jnp.bfloat16),
            grad_view,
            preferred_element_type=jnp.float32,
        )
        return (
            grad_q.reshape(length, -1).astype(jnp.bfloat16),
            grad_k.reshape(2 * length, -1).astype(jnp.bfloat16),
            grad_v.reshape(2 * length, -1).astype(jnp.bfloat16),
        )

    grad_query, grad_keys, grad_values = lax.map(
        back_row, (query, keys, values, start_rows, log_totals, grad_context)
    )
    grad_wq = outer_sum(normed, grad_query)
    grad_wk = outer_sum(kv_input, grad_keys)
    grad_wv = outer_sum(kv_input, grad_values)
    grad_seg = (
        project_back(grad_query, query_full)
        + project_back(grad_keys[:, length:], key_full)
        + project_back(grad_values[:, length:], value_full)
    )
    grad_mem = project_back(grad_keys[:, :length], key_full) + project_back(
        grad_values[:, :length], value_full
    )
    grad_wq, grad_wk, grad_wv, grad_wout = (
        lax.psum_scatter(
            grad_wq.astype(jnp.bfloat16), "mp", scatter_dimension=1, tiled=True
        ).astype(jnp.float32),
        lax.psum_scatter(
            grad_wk.astype(jnp.bfloat16), "mp", scatter_dimension=1, tiled=True
        ).astype(jnp.float32),
        lax.psum_scatter(
            grad_wv.astype(jnp.bfloat16), "mp", scatter_dimension=1, tiled=True
        ).astype(jnp.float32),
        lax.psum_scatter(
            grad_wout.astype(jnp.bfloat16), "mp", scatter_dimension=0, tiled=True
        ).astype(jnp.float32),
    )
    _, attn_norm_pull = jax.vjp(layer_norm, tok_float, gain_attn)
    grad_tok, grad_gain_tok = attn_norm_pull(grad_seg)
    _, mem_norm_pull = jax.vjp(lambda gain: layer_norm(mem_float, gain), gain_attn)
    grad_gain_mem = mem_norm_pull(grad_mem)[0]
    grad_input = (grad_hidden + grad_tok).astype(jnp.bfloat16)
    low_edge = bin_edges[:-1]
    high_edge = bin_edges[1:]
    inside = (
        (neighbour_ids[..., None] >= low_edge) & (neighbour_ids[..., None] < high_edge)
    ).astype(jnp.float32)
    bin_part = jnp.einsum("rt,rtkb->b", gate, inside, precision=HIGH)
    gate_total = jnp.sum(gate)
    summed = lax.psum((grad_wq, grad_wk, grad_wv, grad_wout, grad_up, grad_down), "dp")
    small_sums = lax.psum(
        (grad_gain_tok + grad_gain_mem, grad_gain_ffn, grad_gate_vec, gate_total, bin_part),
        ("dp", "mp"),
    )
    total_count = own_rows * length * lax.axis_size("dp") * lax.axis_size("mp")
    gate_mean = small_sums[3] / total_count
    gate_hist = small_sums[4] * (BINS / (total_count * NEIGH))
    return (
        result,
        grad_input,
        summed[0],
        summed[1],
        summed[2],
        summed[3],
        summed[4],
        summed[5],
        small_sums[0],
        small_sums[1],
        small_sums[2],
        gate_mean,
        gate_hist,
    )


def solution(mesh):
    in_specs = (
        P(("dp", "mp"), None, None),
        P("dp", None, None),
        P(("dp", "mp"), None, None, None),
        P(("dp", "mp"), None, None),
        P("dp"),
        P(),
        P(None, "mp"),
        P(None, "mp"),
        P(None, "mp"),
        P("mp", None),
        P(None, "mp"),
        P("mp", None),
        P(),
        P(),
        P(),
        P(("dp", "mp"), None, None),
    )
    out_specs = (
        P(("dp", "mp"), None, None),
        P(("dp", "mp"), None, None),
        P(None, "mp"),
        P(None, "mp"),
        P(None, "mp"),
        P("mp", None),
        P(None, "mp"),
        P("mp", None),
        P(),
        P(),
        P(),
        P(),
        P(),
    )
    return jax.shard_map(shards, mesh=mesh, in_specs=in_specs, out_specs=out_specs, check_vma=False)
```

profile of v0, /device:TPU:0, one launch (start us, length us, event | category | flops | bytes accessed | tf_op | source)
XLA Modules:
  0.0 610.7 jit_solution(12771567330247353223)
XLA Ops:
  9.7 1.7 fusion.43
  13.0 10.2 %all_gather.21 = bf16[512,512]{0,1:T(8,128)(2,1)} all-gather(bf16[256,512]{0,1:T(8,128)(2,1)S(1)} %copy.88), channel_id=1, replica_groups=mesh['dp'=16,'mp'=2] {'mp'}, dimensions={0}, use_global_device_ids=true | all-gather | bytes 786432 | tf_op jit(solution)/shard_map/all_gather | solution.py:77
  23.1 8.2 %all_gather.20 = bf16[512,512]{1,0:T(8,128)(2,1)S(1)} all-gather(bf16[512,256]{1,0:T(8,128)(2,1)S(1)} %copy-done.46), channel_id=1, replica_groups=mesh['dp'=16,'mp'=2] {'mp'}, dimensions={1}, use_global_device_ids=true | all-gather | bytes 786432 | tf_op jit(solution)/shard_map/all_gather | solution.py:75
  31.3 7.3 %all_gather.18 = bf16[512,512]{1,0:T(8,128)(2,1)} all-gather(bf16[512,256]{1,0:T(8,128)(2,1)S(1)} %copy-done.47), channel_id=1, replica_groups=mesh['dp'=16,'mp'=2] {'mp'}, dimensions={1}, use_global_device_ids=true | all-gather | bytes 786432 | tf_op jit(solution)/shard_map/all_gather | solution.py:76
  38.6 7.0 %all_gather.19 = bf16[512,512]{1,0:T(8,128)(2,1)S(1)} all-gather(bf16[512,256]{1,0:T(8,128)(2,1)S(1)} %copy-done.48), channel_id=1, replica_groups=mesh['dp'=16,'mp'=2] {'mp'}, dimensions={1}, use_global_device_ids=true | all-gather | bytes 786432 | tf_op jit(solution)/shard_map/all_gather | solution.py:74
  45.7 1.6 fusion.40
  50.4 4.1 convolution_convert_fusion.2
  54.5 3.0 copy.87
  57.5 4.3 convolution_convert_fusion.3
  61.7 3.9 copy.85
  66.7 34.6 %while.30 = (s32[]{:T(128)}, bf16[2,512,512]{1,2,0:T(8,128)(2,1)}, f32[2,8,512,1]{2,1,3,0:T(8,128)S(1)}, bf16[2,1024,512]{1,2,0:T(8,128)(2,1)}, s32[2]{0:T(128)S...) while((s32[]{:T(128)}, bf16[2,512,512]{1,2,0:T(8,128)(2,1)}, ...), condition=%wide.region_7.8_spmd, body=%wide.region_4.7_spmd.sunk | while | flops 1121714176 | bytes 70398152 | solution.py:119
  70.9 3.1 fusion.163
  74.0 4.2 exponential_reduce_fusion.2
  78.2 4.7 fusion.164
  88.2 3.1 fusion.163
  91.2 4.2 exponential_reduce_fusion.2
  95.5 4.7 fusion.164
  101.3 2.7 multiply_reduce_fusion.3
  105.3 15.6 %fusion.51 = f32[2,512,1,4]{3,2,1,0:T(1,128)} fusion(bf16[2,512,4,512]{3,2,1,0:T(4,128)(2,1)S(1)} %copy-done.74, f32[2,512,512,1]{2,1,0,3:T(8,128)S(1)} %bitcast.230), kind=kOutput, calls=%fused_computation.105 | convolution fusion | flops 25165824 | bytes 6307840 | tf_op jit(solution)/shard_map/rtkd,rtd->rtk/dot_general | solution.py:29
  123.2 9.9 %fusion.101 = f32[2,512,1,512]{3,2,1,0:T(1,128)S(1)} fusion(f32[2,512,4,1]{2,3,1,0:T(1,128)} %copy.116, bf16[2,512,4,512]{3,2,1,0:T(4,128)(2,1)} %param.22), kind=kOutput, calls=%fused_computation.186 | convolution fusion | flops 25165824 | bytes 6307840 | tf_op jit(solution)/shard_map/rtk,rtkd->rtd/dot_general | solution.py:33
  138.1 33.2 %all-gather.3.cloned.1.call-done = bf16[4,512,512]{2,1,0:T(8,128)(2,1)} async-done(((bf16[2,512,512]{2,1,0:T(8,128)(2,1)}), bf16[4,512,512]{2,1,0:T(8,128)(2,1)}) %all-gather.3.cloned.1.call-update) | async-done | bytes 2097168 | tf_op jit(solution)/shard_map/all_gather | solution.py:126
  171.4 7.2 %fusion.68 = f32[4,512,1024]{2,1,0:T(8,128)} fusion(bf16[4,512,512]{2,1,0:T(8,128)(2,1)} %all-gather.3.cloned.1.call-done, bf16[512,1024]{1,0:T(8,128)(2,1)S(1)} %copy-done), kind=kOutput, calls=%fused_computation.135 | convolution fusion | flops 2147483648 | bytes 11534336 | tf_op jit(solution)/shard_map/rtd,dc->rtc/dot_general | solution.py:39
  178.6 27.5 %all-gather.5.cloned.1.call-done = bf16[4,512,512]{2,1,0:T(8,128)(2,1)} async-done(((bf16[2,512,512]{2,1,0:T(8,128)(2,1)}), bf16[4,512,512]{2,1,0:T(8,128)(2,1)}) %all-gather.5.cloned.1.call-update) | async-done | bytes 2097168 | tf_op jit(solution)/shard_map/all_gather | solution.py:135
  206.1 9.5 %fusion.25 = bf16[4,512,1024]{2,1,0:T(8,128)(2,1)S(1)} fusion(f32[4,512,1024]{2,1,0:T(8,128)} %fusion.68, bf16[4,512,512]{2,1,0:T(8,128)(2,1)} %all-gather.5.cloned.1.call-done, bf16[1024,512]{1,0:T(8,128)(2,1)} %param.31), kind=kOutput, calls=%fused_computation.55 | convolution fusion | flops 2189426688 | bytes 15728640 | tf_op jit(solution)/shard_map/rtc,dc->rtd/dot_general | solution.py:43
  215.6 2.0 copy-done.32
  217.6 3.8 convolution_convert_fusion
  222.6 7.8 %convolution_convert_fusion.1 = bf16[4,512,512]{2,1,0:T(8,128)(2,1)} fusion(bf16[1024,512]{1,0:T(8,128)(2,1)S(1)} %copy-done.77, f32[4,512,1024]{2,1,0:T(8,128)} %fusion.68), kind=kOutput, calls=%fused_computation.108 | convolution fusion | flops 2167406592 | bytes 11534336 | tf_op jit(solution)/shard_map/rtd,dc->rtc/dot_general | solution.py:39
  230.5 22.9 %reduce-scatter.9.cloned.1.call-done = bf16[2,512,512]{2,1,0:T(8,128)(2,1)} async-done(((bf16[4,512,512]{2,1,0:T(8,128)(2,1)}), bf16[2,512,512]{2,1,0:T(8,128)(2,1)}) %reduce-scatter.9.cloned.1.call-update) | async-done | bytes 1048592 | tf_op jit(solution)/shard_map/reduce_scatter | solution.py:142
  253.4 2.6 fusion.42
  256.2 2.2 fusion.44
  258.4 29.1 %reduce-scatter.7.cloned.1.call-done = bf16[2,512,512]{2,1,0:T(8,128)(2,1)} async-done(((bf16[4,512,512]{2,1,0:T(8,128)(2,1)}), bf16[2,512,512]{2,1,0:T(8,128)(2,1)}) %reduce-scatter.7.cloned.1.call-update) | async-done | bytes 1048592 | tf_op jit(solution)/shard_map/reduce_scatter | solution.py:130
  287.4 4.4 fusion.48
  293.3 2.0 copy-done.75
  295.3 14.7 %fusion.49 = f32[2,512,1,4]{3,2,1,0:T(1,128)S(1)} fusion(bf16[2,512,4,512]{3,2,1,0:T(4,128)(2,1)S(1)} %copy-done.75, f32[2,512,512,1]{2,1,0,3:T(8,128)S(1)} %multiply_bitcast_fusion), kind=kOutput, calls=%fused_computation.103 | convolution fusion | flops 25165824 | bytes 6307840 | tf_op jit(solution)/shard_map/transpose(jvp(rtk,rtkd->rtd))/dot_general | solution.py:33
  310.8 9.0 %fusion.102 = f32[2,512,1,512]{3,2,1,0:T(1,128)S(1)} fusion(f32[2,512,4,1]{2,3,1,0:T(1,128)S(1)} %copy.120, bf16[2,512,4,512]{3,2,1,0:T(4,128)(2,1)} %param.22), kind=kOutput, calls=%fused_computation.187 | convolution fusion | flops 25165824 | bytes 6307840 | tf_op jit(solution)/shard_map/transpose(jvp(rtkd,rtd->rtk))/dot_general | solution.py:29
  323.6 3.0 convolution_convert_fusion.4
  327.7 90.0 %while.31 = (s32[]{:T(128)}, bf16[2,512,512]{1,2,0:T(8,128)(2,1)}, bf16[2,1024,512]{1,2,0:T(8,128)(2,1)}, bf16[2,1024,512]{1,2,0:T(8,128)(2,1)}, bf16[2,1024,512...) while((s32[]{:T(128)}, bf16[2,512,512]{1,2,0:T(8,128)(2,1)}, ...), condition=%wide.region_21.22_spmd, body=%wide.region_19.21_spmd.sunk | while | flops 2725773312 | bytes 212693552 | solution.py:191
  333.2 1.9 constant_dynamic-slice_fusion.18
  336.6 2.4 fusion.175
  338.9 11.4 %multiply_reduce_fusion.5 = (f32[8,512]{1,0:T(8,128)}, f32[8,512,1024]{2,1,0:T(8,128)}) fusion(f32[8,512,1024]{2,1,0:T(8,128)S(1)} %fusion.175, f32[8,512]{1,0:T(8,128)} %dynamic-slice_bitcast_fusion.2, bf16[512,8,64]{0,2,1:T(8,128)(2,1)} %bitcast.223, bf16[1024,8,64]{0,2,1:T(8,128)(2,1)S(1)} %bitcast.217, pred[512,1024]{1,0:T(8,128)(4,1)} %fusion.177), kind=kOutput, calls=%fused_computation.23.clone.1 | convolution fusion | flops 557838336 | bytes 35684352 | tf_op jit(solution)/shard_map/while/body/eval_jaxpr/qhc,khc->hqk/dot_general | solution.py:95
  350.4 6.9 %multiply_convert_fusion.8 = bf16[8,512,1024]{2,1,0:T(8,128)(2,1)S(1)} fusion(f32[8,512,1024]{2,1,0:T(8,128)} %get-tuple-element.490, f32[8,512,1024]{2,1,0:T(8,128)S(1)} %fusion.175, f32[8,512]{1,0:T(8,128)} %get-tuple-element.491), kind=kLoop, calls=%fused_computation.22.clone.1 | loop fusion | flops 12582912 | bytes 41959424 | tf_op jit(solution)/shard_map/while/body/eval_jaxpr/convert_element_type | solution.py:170
  357.3 7.3 %fusion.179 = bf16[8,64,1024]{2,1,0:T(8,128)(2,1)S(1)} fusion(bf16[512,8,64]{0,2,1:T(8,128)(2,1)S(1)} %bitcast.221, f32[8,512,1024]{2,1,0:T(8,128)} %get-tuple-element.490), kind=kOutput, calls=%fused_computation.31.clone.1 | convolution fusion | flops 541589504 | bytes 18350080 | tf_op jit(solution)/shard_map/while/body/eval_jaxpr/hqk,qhc->khc/dot_general | solution.py:179
  364.6 2.7 fusion.178
  367.3 1.6 multiply_convert_fusion.9
  378.1 1.9 constant_dynamic-slice_fusion.18
  381.5 2.4 fusion.175
  383.9 11.5 %multiply_reduce_fusion.5 = (f32[8,512]{1,0:T(8,128)}, f32[8,512,1024]{2,1,0:T(8,128)}) fusion(f32[8,512,1024]{2,1,0:T(8,128)S(1)} %fusion.175, f32[8,512]{1,0:T(8,128)} %dynamic-slice_bitcast_fusion.2, bf16[512,8,64]{0,2,1:T(8,128)(2,1)} %bitcast.223, bf16[1024,8,64]{0,2,1:T(8,128)(2,1)S(1)} %bitcast.217, pred[512,1024]{1,0:T(8,128)(4,1)} %fusion.177), kind=kOutput, calls=%fused_computation.23.clone.1 | convolution fusion | flops 557838336 | bytes 35684352 | tf_op jit(solution)/shard_map/while/body/eval_jaxpr/qhc,khc->hqk/dot_general | solution.py:95
  395.3 6.9 %multiply_convert_fusion.8 = bf16[8,512,1024]{2,1,0:T(8,128)(2,1)S(1)} fusion(f32[8,512,1024]{2,1,0:T(8,128)} %get-tuple-element.490, f32[8,512,1024]{2,1,0:T(8,128)S(1)} %fusion.175, f32[8,512]{1,0:T(8,128)} %get-tuple-element.491), kind=kLoop, calls=%fused_computation.22.clone.1 | loop fusion | flops 12582912 | bytes 41959424 | tf_op jit(solution)/shard_map/while/body/eval_jaxpr/convert_element_type | solution.py:170
  402.2 7.3 %fusion.179 = bf16[8,64,1024]{2,1,0:T(8,128)(2,1)S(1)} fusion(bf16[512,8,64]{0,2,1:T(8,128)(2,1)S(1)} %bitcast.221, f32[8,512,1024]{2,1,0:T(8,128)} %get-tuple-element.490), kind=kOutput, calls=%fused_computation.31.clone.1 | convolution fusion | flops 541589504 | bytes 18350080 | tf_op jit(solution)/shard_map/while/body/eval_jaxpr/hqk,qhc->khc/dot_general | solution.py:179
  409.6 2.7 fusion.178
  412.3 1.6 multiply_convert_fusion.9
  417.7 3.2 fusion.53
  422.1 3.6 fusion.54
  426.2 6.8 %convolution_bitcast_fusion.1 = f32[512,1024]{1,0:T(8,128)} fusion(bf16[4,512,512]{2,1,0:T(8,128)(2,1)} %all-gather.3.cloned.1.call-done, bf16[4,512,1024]{2,1,0:T(8,128)(2,1)} %copy-done.32), kind=kOutput, calls=%fused_computation.112 | convolution fusion | flops 2147483648 | bytes 8388608 | tf_op jit(solution)/shard_map/rtd,rtc->dc/dot_general | solution.py:47
  433.0 2.1 fusion.55
  435.2 7.9 %convolution_bitcast_fusion = f32[1024,512]{1,0:T(8,128)} fusion(bf16[4,512,512]{2,1,0:T(8,128)(2,1)S(1)} %copy-done.76, f32[4,512,1024]{2,1,0:T(8,128)} %fusion.68), kind=kOutput, calls=%fused_computation.111 | convolution fusion | flops 2166358016 | bytes 12582912 | tf_op jit(solution)/shard_map/rtd,rtc->dc/dot_general | solution.py:47
  443.1 3.1 copy.97
  446.3 4.0 copy.100
  450.3 1.9 fusion.78
  460.1 2.0 multiply_reduce_fusion.1
  462.1 40.4 %all-reduce = (f32[512]{0:T(512)}, f32[512]{0:T(512)}, f32[512]{0:T(512)}, f32[]{:T(128)}, f32[128]{0:T(128)S(1)}) all-reduce(f32[512]{0:T(512)S(1)} %add.172, f32[512]{0:T(512)S(1)} %copy-done.72, f32[512]{0:T(512)S(1)} %get-tuple-element.354, f32[]{:T(128)} %get-tuple-element.337, ...), channel_id=1, replica_groups=mesh['dp'=16,'mp'=2] {'dp','mp'}, use_global_device_ids=true, to_apply=%region_36.37 | all-reduce | flops 1665 | bytes 13320 | tf_op jit(solution)/shard_map/psum | solution.py:232
  503.7 82.6 %all-reduce.7 = (f32[512,256]{1,0:T(8,128)}, f32[512,256]{1,0:T(8,128)}, f32[512,256]{1,0:T(8,128)}, f32[256,512]{1,0:T(8,128)}) all-reduce(bf16[512,256]{1,0:T(8,128)(2,1)} %reduce-scatter.11.cloned.1.call-done, bf16[512,256]{1,0:T(8,128)(2,1)} %reduce-scatter.13.cloned.1.call-done, ...), channel_id=1, replica_groups=mesh['dp'=16,'mp'=2] {'dp'}, use_global_device_ids=true, to_apply=%region_25.26 | all-reduce | flops 524288 | bytes 3145728 | tf_op jit(solution)/shard_map/psum | solution.py:231
  586.3 11.6 %all-reduce.6.cloned.1.call-done = (f32[512,1024]{1,0:T(8,128)}, f32[1024,512]{1,0:T(8,128)}) async-done(((f32[512,1024]{1,0:T(8,128)}, f32[1024,512]{1,0:T(8,128)}), (f32[512,1024]{1,0:T(8,128)}, f32[1024,512]{1,0:T(8,128)})) %all-reduce.6.cloned.1.call-update) | async-done | bytes 4194320 | tf_op jit(solution)/shard_map/psum | solution.py:231
  597.9 3.3 copy.192
  (297 shorter events, 65.1 us)
Async XLA Ops:
  7.2 164.2 %copy-start = (bf16[512,1024]{1,0:T(8,128)(2,1)S(1)}, bf16[512,1024]{1,0:T(8,128)(2,1)}, u32[]{:S(2)}) copy-start(bf16[512,1024]{1,0:T(8,128)(2,1)} %param.30) | copy-start | bytes 3145732
  7.2 4.2 copy-start.9
  7.2 164.2 %all-gather.3.cloned.1.call-start = ((), (), s32[]{:S(2)}) async-start(), calls=%async_computation.6 | async-start | bytes 3145728 | tf_op jit(solution)/shard_map/all_gather | solution.py:126
  8.1 4.7 copy-start.49
  9.6 36.0 %copy-start.62 = (f32[2,512]{1,0:T(2,128)}, f32[2,512]{1,0:T(2,128)S(1)}, u32[]{:S(2)}) copy-start(f32[2,512]{1,0:T(2,128)S(1)} %broadcast_multiply_fusion.2) | copy-start | bytes 12292
  9.6 13.5 %copy-start.46 = (bf16[512,256]{1,0:T(8,128)(2,1)S(1)}, bf16[512,256]{1,0:T(8,128)(2,1)}, u32[]{:S(2)}) copy-start(bf16[512,256]{1,0:T(8,128)(2,1)} %param.27) | copy-start | bytes 786436
  11.4 34.3 %copy-start.70 = (f32[2,512]{1,0:T(2,128)}, f32[2,512]{1,0:T(2,128)S(1)}, u32[]{:S(2)}) copy-start(f32[2,512]{1,0:T(2,128)S(1)} %add_rsqrt_fusion) | copy-start | bytes 12292
  11.4 19.9 %copy-start.47 = (bf16[512,256]{1,0:T(8,128)(2,1)S(1)}, bf16[512,256]{1,0:T(8,128)(2,1)}, u32[]{:S(2)}) copy-start(bf16[512,256]{1,0:T(8,128)(2,1)} %param.28) | copy-start | bytes 786436
  11.6 27.0 %copy-start.48 = (bf16[512,256]{1,0:T(8,128)(2,1)S(1)}, bf16[512,256]{1,0:T(8,128)(2,1)}, u32[]{:S(2)}) copy-start(bf16[512,256]{1,0:T(8,128)(2,1)} %param.26) | copy-start | bytes 786436
  11.7 34.0 %copy-start.52 = (f32[2,512]{1,0:T(2,128)}, f32[2,512]{1,0:T(2,128)S(1)}, u32[]{:S(2)}) copy-start(f32[2,512]{1,0:T(2,128)S(1)} %broadcast_multiply_fusion.1) | copy-start | bytes 12292
  12.8 32.9 %copy-start.64 = (f32[512]{0:T(512)S(1)}, f32[512]{0:T(512)}, u32[]{:S(2)}) copy-start(f32[512]{0:T(512)} %param.32) | copy-start | bytes 6148
  12.8 34.6 %copy-start.56 = (f32[2,512]{1,0:T(2,128)}, f32[2,512]{1,0:T(2,128)S(1)}, u32[]{:S(2)}) copy-start(f32[2,512]{1,0:T(2,128)S(1)} %fusion.92) | copy-start | bytes 12292
  13.0 32.7 %copy-start.23 = (bf16[4,512,512]{2,1,0:T(8,128)(2,1)S(1)}, bf16[4,512,512]{2,1,0:T(8,128)(2,1)}, u32[]{:S(2)}) copy-start(bf16[4,512,512]{2,1,0:T(8,128)(2,1)} %param.21) | copy-start | bytes 6291460
  31.3 19.1 %copy-start.21 = (bf16[512,512]{1,0:T(8,128)(2,1)}, bf16[512,512]{1,0:T(8,128)(2,1)S(1)}, u32[]{:S(2)}) copy-start(bf16[512,512]{1,0:T(8,128)(2,1)S(1)} %all_gather.20) | copy-start | bytes 1572868
  66.7 34.6 %copy-start.67 = (f32[512]{0:T(512)S(1)}, f32[512]{0:T(512)}, u32[]{:S(2)}) copy-start(f32[512]{0:T(512)} %param.34) | copy-start | bytes 6148
  78.2 4.7 copy-start.29
  95.5 4.7 copy-start.29
  101.3 4.0 copy-start.74
  104.7 187.1 %copy-start.54 = (f32[2,512]{1,0:T(2,128)}, f32[2,512]{1,0:T(2,128)S(1)}, u32[]{:S(2)}) copy-start(f32[2,512]{1,0:T(2,128)S(1)} %get-tuple-element.338) | copy-start | bytes 12292
  123.2 10.0 %copy-start.15 = (f32[2,512,512]{2,1,0:T(8,128)S(1)}, f32[2,512,512]{2,1,0:T(8,128)}, u32[]{:S(2)}) copy-start(f32[2,512,512]{2,1,0:T(8,128)} %copy-done.14) | copy-start | bytes 6291460
  137.1 69.0 %all-gather.5.cloned.1.call-start = ((), (), s32[]{:S(2)}) async-start(), calls=%async_computation.8 | async-start | bytes 3145728 | tf_op jit(solution)/shard_map/all_gather | solution.py:135
  137.9 115.5 %reduce-scatter.9.cloned.1.call-start = ((), (), s32[]{:S(2)}) async-start(), calls=%async_computation.9 | async-start | bytes 3145728 | tf_op jit(solution)/shard_map/reduce_scatter | solution.py:142
  221.4 66.0 %reduce-scatter.7.cloned.1.call-start = ((), (), s32[]{:S(2)}) async-start(), calls=%async_computation.7 | async-start | bytes 3145728 | tf_op jit(solution)/shard_map/reduce_scatter | solution.py:130
  230.4 273.4 %reduce-scatter.17.cloned.1.call-start = ((), (), s32[]{:S(2)}) async-start(), calls=%async_computation.13 | async-start | bytes 786432 | tf_op jit(solution)/shard_map/reduce_scatter | solution.py:215
  253.4 2.7 copy-start.8
  253.4 2.8 copy-start.17
  291.8 27.9 %copy-start.58 = (f32[2,512]{1,0:T(2,128)}, f32[2,512]{1,0:T(2,128)S(1)}, u32[]{:S(2)}) copy-start(f32[2,512]{1,0:T(2,128)S(1)} %fusion.90) | copy-start | bytes 12292
  310.7 9.0 %copy-start.12 = (f32[2,512,512]{2,1,0:T(8,128)S(1)}, f32[2,512,512]{2,1,0:T(8,128)}, u32[]{:S(2)}) copy-start(f32[2,512,512]{2,1,0:T(8,128)} %copy-done.11) | copy-start | bytes 6291460
  319.8 2.2 copy-start.31
  326.6 177.1 %reduce-scatter.11.cloned.1.call-start = ((), (), s32[]{:S(2)}) async-start(), calls=%async_computation.10 | async-start | bytes 786432 | tf_op jit(solution)/shard_map/reduce_scatter | solution.py:206
  327.9 8.6 %copy-start.50 = (f32[2,8,512,1]{2,1,3,0:T(8,128)}, f32[2,8,512,1]{2,1,3,0:T(8,128)S(1)}, u32[]{:S(2)}) copy-start(f32[2,8,512,1]{2,1,3,0:T(8,128)S(1)} %get-tuple-element.552) | copy-start | bytes 98308 | tf_op jit(solution)/shard_map/while
  327.9 8.6 %copy-start.5 = (bf16[2,1024,512]{1,2,0:T(8,128)(2,1)}, bf16[2,1024,512]{1,2,0:T(8,128)(2,1)S(1)}, u32[]{:S(2)}) copy-start(bf16[2,1024,512]{1,2,0:T(8,128)(2,1)S(1)} %get-tuple-element.549) | copy-start | bytes 6291460 | tf_op jit(solution)/shard_map/while
  350.4 6.9 %copy-start.3 = (bf16[1,512,512]{1,2,0:T(8,128)(2,1)S(1)}, bf16[1,512,512]{1,2,0:T(8,128)(2,1)}, u32[]{:S(2)}) copy-start(bf16[1,512,512]{1,2,0:T(8,128)(2,1)} %copy.153) | copy-start | bytes 1572868 | tf_op jit(solution)/shard_map/while
  364.6 2.7 copy-start.4
  367.3 2.5 copy-start.39
  369.9 2.9 copy-start.6
  369.9 2.9 copy-start.51
  372.8 8.6 %copy-start.50 = (f32[2,8,512,1]{2,1,3,0:T(8,128)}, f32[2,8,512,1]{2,1,3,0:T(8,128)S(1)}, u32[]{:S(2)}) copy-start(f32[2,8,512,1]{2,1,3,0:T(8,128)S(1)} %get-tuple-element.552) | copy-start | bytes 98308 | tf_op jit(solution)/shard_map/while
  372.8 8.6 %copy-start.5 = (bf16[2,1024,512]{1,2,0:T(8,128)(2,1)}, bf16[2,1024,512]{1,2,0:T(8,128)(2,1)S(1)}, u32[]{:S(2)}) copy-start(bf16[2,1024,512]{1,2,0:T(8,128)(2,1)S(1)} %get-tuple-element.549) | copy-start | bytes 6291460 | tf_op jit(solution)/shard_map/while
  395.3 6.9 %copy-start.3 = (bf16[1,512,512]{1,2,0:T(8,128)(2,1)S(1)}, bf16[1,512,512]{1,2,0:T(8,128)(2,1)}, u32[]{:S(2)}) copy-start(bf16[1,512,512]{1,2,0:T(8,128)(2,1)} %copy.153) | copy-start | bytes 1572868 | tf_op jit(solution)/shard_map/while
  409.5 2.7 copy-start.4
  412.2 2.5 copy-start.39
  414.8 2.9 copy-start.6
  414.8 2.9 copy-start.51
  417.7 3.3 copy-start.73
  417.7 3.4 copy-start.69
  417.7 4.4 copy-start.41
  421.0 82.7 %reduce-scatter.13.cloned.1.call-start = ((), (), s32[]{:S(2)}) async-start(), calls=%async_computation.11 | async-start | bytes 786432 | tf_op jit(solution)/shard_map/reduce_scatter | solution.py:209
  422.1 3.7 copy-start.55
  425.8 78.0 %reduce-scatter.15.cloned.1.call-start = ((), (), s32[]{:S(2)}) async-start(), calls=%async_computation.12 | async-start | bytes 786432 | tf_op jit(solution)/shard_map/reduce_scatter | solution.py:212
  426.2 6.8 %copy-start.38 = (bf16[2,1024,512]{1,2,0:T(8,128)(2,1)S(1)}, bf16[2,1024,512]{1,2,0:T(8,128)(2,1)}, u32[]{:S(2)}) copy-start(bf16[2,1024,512]{1,2,0:T(8,128)(2,1)} %get-tuple-element.234) | copy-start | bytes 6291460
  426.2 6.8 %copy-start.42 = (bf16[2,512,512]{2,1,0:T(8,128)(2,1)S(1)}, bf16[2,512,512]{2,1,0:T(8,128)(2,1)}, u32[]{:S(2)}) copy-start(bf16[2,512,512]{2,1,0:T(8,128)(2,1)} %get-tuple-element.356) | copy-start | bytes 3145732
  426.2 6.8 %copy-start.44 = (bf16[2,512,512]{2,1,0:T(8,128)(2,1)S(1)}, bf16[2,512,512]{2,1,0:T(8,128)(2,1)}, u32[]{:S(2)}) copy-start(bf16[2,512,512]{2,1,0:T(8,128)(2,1)} %copy-done.43) | copy-start | bytes 3145732
  433.0 2.2 copy-start.76
  435.2 162.8 %all-reduce.6.cloned.1.call-start = ((), (), s32[]{:S(2)}) async-start(), calls=%async_computation.14 | async-start | bytes 8388608 | tf_op jit(solution)/shard_map/psum | solution.py:231
  446.3 4.0 copy-start.28
  450.3 2.7 copy-start.53
  450.3 2.7 copy-start.65
  456.2 2.5 copy-start.19
  457.7 2.4 copy-start.16
  457.7 2.4 copy-start.59
  457.7 2.4 copy-start.68
  597.9 3.3 copy-start.35
  597.9 4.6 copy-start.1
  (38 other events, 55.1 us)
Sparse Core Ops, SparseCore 0:
  137.2 34.0 all-gather.2
  172.9 33.1 all-gather.4
  221.5 31.8 reduce-scatter.8
  255.5 31.8 reduce-scatter.6
  326.8 14.5 reduce-scatter.16
  421.1 14.5 reduce-scatter.10
  438.6 14.5 reduce-scatter.12
  455.5 14.7 reduce-scatter.14
  474.0 123.8 all-reduce.5
where the time goes:
time: 621 us; the launch traced here: 611 us
  matrix products  190 us (31%)
  blocking collectives  156 us (25%)
  waiting for transfers between devices  125 us (20%)
  local copies, waits for them, and re-layouts  70.7 us (11%)
  other arithmetic  48.8 us (8%)
  between operations  16.9 us (3%)
    psum x1, blocking collectives, shards(): lax.psum((grad_wq, grad_wk, grad_wv, grad_wout, grad_up, grad_down), 'dp')  82.6 us
    psum x1, blocking collectives, shards(): lax.psum((grad_gain_tok + grad_gain_mem, grad_gain_ffn, grad_gate_vec, ga...  40.4 us
    all_gather x1, waiting for transfers between devices, shards(): ffn_rows = lax.all_gather(ffn_in, 'mp', axis=0, tiled=True)  33.2 us
    reduce_scatter x1, waiting for transfers between devices, shards(): lax.psum_scatter(down_part.astype(jnp.bfloat16), 'mp', scatter_dimension=...  29.1 us
    dot_general x4, matrix products, row_scores(): jnp.einsum('qhc,khc->hqk', head_view(query_row, length), head_view(key_ro...  29 us
    all_gather x1, waiting for transfers between devices, shards(): grad_rows = lax.all_gather(cotangent, 'mp', axis=0, tiled=True)  27.5 us
    dot_general x6, matrix products, project(): jnp.einsum('rtd,dc->rtc', left, right, preferred_element_type=jnp.float32)  26.7 us
    dot_general x6, matrix products, outer_sum(): jnp.einsum('rtd,rtc->dc', left, right, preferred_element_type=jnp.float32)  25.2 us
  transfers between devices with their start and end apart: 9, of which 5 were waited for; matrix products, arithmetic and copies ran while one was open for 23% of the time, Pallas kernels for 0%

commit v1 on v0

v1 whole, which is shorter than its diff:
```python
import jax
import jax.numpy as jnp
from jax import lax
from jax.experimental import pallas as pl
from jax.experimental.pallas import tpu as pltpu
from jax.sharding import PartitionSpec as P

HEAD = 64
NEIGH = 4
BINS = 128
PAIR = 2 * HEAD
QROWS = 256
TILE = 256

EPS = 1e-05
BF16 = jnp.bfloat16
F32 = jnp.float32
VMEM_LIMIT = 56 * 1024 * 1024


def dot(left, right, left_dim=1, right_dim=0):
    return lax.dot_general(
        left, right, (((left_dim,), (right_dim,)), ((), ())), preferred_element_type=F32
    )


def normalize(values):
    centre = values - jnp.mean(values, -1, keepdims=True)
    spread = jnp.mean(centre * centre, -1, keepdims=True)
    rstd = lax.rsqrt(spread + EPS)
    return centre * rstd, rstd


def core_index():
    return lax.rem(lax.axis_index("dp"), 2)


def head_lanes(rows, head):
    lane = lax.broadcasted_iota(jnp.int32, (rows, PAIR), 1)
    return (lane >= head * HEAD) & (lane < (head + 1) * HEAD)


def only_head(block, head):
    return jnp.where(head_lanes(block.shape[0], head), block, jnp.zeros_like(block))


def attend(qkv_ref, p_ref, ctx_ref, length, with_memory):
    mem_keys = pl.ds(length, length)
    values = [only_head(qkv_ref[0, 0, pl.ds(3 * length, 2 * length), :], head) for head in range(2)]
    for first in range(0, length, QROWS):
        rows = pl.ds(first, QROWS)
        seen = first + QROWS
        total = None
        for head in range(2):
            query = only_head(qkv_ref[0, 0, rows, :], head)
            seg = dot(query, qkv_ref[0, 0, pl.ds(2 * length, seen), :], 1, 1)
            at = lax.broadcasted_iota(jnp.int32, (QROWS, seen), 0) + first
            key = lax.broadcasted_iota(jnp.int32, (QROWS, seen), 1)
            seg = jnp.where(key <= at, seg, -1e30)
            top = jnp.max(seg, -1, keepdims=True)
            if with_memory:
                mem = dot(query, qkv_ref[0, 0, mem_keys, :], 1, 1)
                top = jnp.maximum(top, jnp.max(mem, -1, keepdims=True))
                mem = jnp.exp(mem - top)
            seg = jnp.exp(seg - top)
            mass = jnp.sum(seg, -1, keepdims=True)
            if with_memory:
                mass = mass + jnp.sum(mem, -1, keepdims=True)
            part = 1.0 / mass
            seg = (seg * part).astype(BF16)
            p_ref[0, 0, head, rows, pl.ds(length, seen)] = seg
            add = dot(seg, values[head][length : length + seen])
            if with_memory:
                mem = (mem * part).astype(BF16)
                p_ref[0, 0, head, rows, pl.ds(0, length)] = mem
                add = add + dot(mem, values[head][:length])
            total = add if total is None else total + add
        ctx_ref[0, rows, :] = total.astype(BF16)


def forward_body(starts_ref, kv_ref, pack_ref, qkv_ref, p_ref, ctx_ref):
    length = kv_ref.shape[1] // 2
    pair = pl.program_id(1)
    kv = kv_ref[0]
    here = pl.multiple_of(3 * pair * PAIR, PAIR)
    query = dot(kv[length:], pack_ref[:, pl.ds(here, PAIR)]).astype(BF16)
    qkv_ref[0, 0, pl.ds(0, length), :] = (query.astype(F32) * HEAD ** (-0.5)).astype(BF16)
    both = dot(kv, pack_ref[:, pl.ds(here + PAIR, 2 * PAIR)]).astype(BF16)
    qkv_ref[0, 0, pl.ds(length, 2 * length), :] = both[:, :PAIR]
    qkv_ref[0, 0, pl.ds(3 * length, 2 * length), :] = both[:, PAIR:]
    start = starts_ref[lax.axis_index("mp") * pl.num_programs(0) + pl.program_id(0)]

    @pl.when(start == 0)
    def _():
        attend(qkv_ref, p_ref, ctx_ref, length, True)

    @pl.when(start != 0)
    def _():
        attend(qkv_ref, p_ref, ctx_ref, length, False)


def first_forward(
    starts_ref, tok_ref, mem_ref, gain_ref, wq_ref, wk_ref, wv_ref, kv_ref, pack_ref, *outs
):
    length = tok_ref.shape[1]

    @pl.when((pl.program_id(0) == 0) & (pl.program_id(1) == 0))
    def _():
        for i, weight in enumerate((wq_ref, wk_ref, wv_ref)):
            for p in range(2):
                pack_ref[:, pl.ds((3 * p + i) * PAIR, PAIR)] = weight[:, pl.ds(p * PAIR, PAIR)]

    @pl.when(pl.program_id(1) == 0)
    def _():
        gain = gain_ref[...]
        kv_ref[0, pl.ds(0, length), :] = (normalize(mem_ref[0].astype(F32))[0] * gain).astype(BF16)
        kv_ref[0, pl.ds(length, length), :] = (
            normalize(tok_ref[0].astype(F32))[0] * gain
        ).astype(BF16)

    forward_body(starts_ref, kv_ref, pack_ref, *outs)


def second_forward(starts_ref, kv_ref, mine_ref, sibling_ref, pack_ref, *outs):
    rows = mine_ref.shape[0]
    core = core_index()

    @pl.when((pl.program_id(0) == 0) & (pl.program_id(1) == 0))
    def _():
        for block, which in ((mine_ref, core), (sibling_ref, 1 - core)):
            to = pl.ds(pl.multiple_of(which * rows, rows), rows)
            for i in range(3):
                for p in range(2):
                    pack_ref[to, pl.ds((3 * p + i) * PAIR, PAIR)] = block[
                        :, pl.ds((2 * i + p) * PAIR, PAIR)
                    ]

    forward_body(starts_ref, kv_ref, pack_ref, *outs)


def attention_forward(starts, tokens, memory, gain, kv, weights):
    rows, length, width = tokens.shape
    pairs = 2
    pack = (width, 3 * pairs * PAIR)
    outs = [
        jax.ShapeDtypeStruct(pack, BF16),
        jax.ShapeDtypeStruct((rows, pairs, 5 * length, PAIR), BF16),
        jax.ShapeDtypeStruct((rows, pairs, 2, length, 2 * length), BF16),
        jax.ShapeDtypeStruct((rows, length, pairs * PAIR), BF16),
    ]
    out_specs = [
        pl.BlockSpec(pack, lambda r, p: (0, 0)),
        pl.BlockSpec((1, 1, 5 * length, PAIR), lambda r, p: (r, p, 0, 0)),
        pl.BlockSpec((1, 1, 2, length, 2 * length), lambda r, p: (r, p, 0, 0, 0)),
        pl.BlockSpec((1, length, PAIR), lambda r, p: (r, 0, p)),
    ]
    kv_spec = pl.BlockSpec((1, 2 * length, width), lambda r, p: (r, 0, 0))
    in_specs = [pl.BlockSpec(memory_space=pltpu.SMEM)]
    if kv is None:
        body = first_forward
        ins = [tokens, memory, gain]
        in_specs += [
            pl.BlockSpec((1, length, width), lambda r, p: (r, 0, 0)),
            pl.BlockSpec((1, length, width), lambda r, p: (lax.axis_index("mp") * rows + r, 0, 0)),
            pl.BlockSpec((1, width), lambda r, p: (0, 0)),
        ]
        outs = [jax.ShapeDtypeStruct((rows, 2 * length, width), BF16)] + outs
        out_specs = [kv_spec] + out_specs
    else:
        body = second_forward
        ins = [kv]
        in_specs += [kv_spec]
    in_specs += [pl.BlockSpec(w.shape, lambda r, p: (0, 0)) for w in weights]
    return pl.pallas_call(
        body,
        grid=(rows, pairs),
        in_specs=in_specs,
        out_specs=out_specs,
        out_shape=outs,
        compiler_params=pltpu.CompilerParams(vmem_limit_bytes=VMEM_LIMIT),
        cost_estimate=pl.CostEstimate(flops=6 * 10**9, bytes_accessed=16 * 2**20, transcendentals=0),
    )(starts, *ins, *weights)


def gelu_parts(pre):
    c0 = 0.7978845608028654
    c1 = c0 * 0.044715
    square = pre * pre
    part = 0.5 * jnp.tanh(pre * (c1 * square + c0)) + 0.5
    act = pre * part
    return act, part + act * (1.0 - part) * ((6.0 * c1) * square + 2.0 * c0)


def weighted(weights, values):
    return sum(w * v for w, v in zip(weights[1:], values[1:])) + weights[0] * values[0]


def middle_body(
    tok_ref,
    ctx_own_ref,
    ctx_oth_ref,
    nb_ref,
    ids_ref,
    cot_ref,
    up_far,
    down_far,
    out_far,
    mine_far,
    sibling_far,
    edges_ref,
    gains_ref,
    result_ref,
    grad_hidden_ref,
    gctx_own_ref,
    gctx_oth_ref,
    sent_far,
    kept_far,
    sums_ref,
    e_ref,
    hist_ref,
    edge_ref,
    up_ref,
    down_ref,
    out_ref,
    oth_ref,
    stage_ref,
    ffn_in_ref,
    act_ref,
    gpre_ref,
    cots_ref,
    low_ref,
    ctx_ref,
    in_sems,
    out_sems,
):
    step = pl.program_id(0)
    here = pl.ds(pl.multiple_of(step * TILE, TILE), TILE)
    width = tok_ref.shape[-1]
    hidden_units = down_ref.shape[0]
    half = width // 2
    chunks = hidden_units // width
    scale = width ** (-0.5)
    core = core_index()
    copies = [
        pltpu.make_async_copy(far, near, in_sems.at[i])
        for i, (far, near) in enumerate(
            (
                (out_far, out_ref),
                (mine_far, oth_ref.at[core]),
                (sibling_far, oth_ref.at[1 - core]),
                (up_far, up_ref),
                (down_far, down_ref),
            )
        )
    ]

    @pl.when(step == 0)
    def _():
        for copy in copies:
            copy.start()
        sums_ref[...] = jnp.zeros_like(sums_ref)
        hist_ref[...] = jnp.zeros_like(hist_ref)
        edges = edges_ref[...].astype(F32)
        for i in range(2):
            edge_ref[i] = jnp.broadcast_to(edges[:, i : i + BINS], (BINS, BINS)).T
        for copy in copies[:3]:
            copy.wait()

    def other_out():
        at = pl.ds(2 * width, half // 2)
        return jnp.concatenate([oth_ref[0, at, :], oth_ref[1, at, :]], 0)

    wgate = gains_ref[pl.ds(1, 1), :]
    gain = gains_ref[pl.ds(0, 1), :]

    def front():
        ctx_ref[here, pl.ds(0, half)] = ctx_own_ref[0]
        ctx_ref[here, pl.ds(half, half)] = ctx_oth_ref[0]
        cots_ref[here, :] = cot_ref[0]
        hidden = (
            tok_ref[0].astype(F32)
            + dot(ctx_own_ref[0], out_ref[...])
            + dot(ctx_oth_ref[0], other_out())
        )
        affinity = []
        for k in range(NEIGH):
            e = nb_ref[0, :, k, :].astype(F32)
            e_ref[k] = e
            affinity.append(jnp.sum(e * hidden, -1, keepdims=True) * scale)
        top = jnp.maximum(
            jnp.maximum(affinity[0], affinity[1]), jnp.maximum(affinity[2], affinity[3])
        )
        raised = [jnp.exp(a - top) for a in affinity]
        inverse = 1.0 / (raised[0] + raised[1] + raised[2] + raised[3])
        weights = [a * inverse for a in raised]
        gate = jax.nn.sigmoid(jnp.sum(hidden * wgate, -1, keepdims=True))
        recalled = weighted(weights, [e_ref[k] for k in range(NEIGH)])
        mixed = hidden + gate * recalled
        normal, rstd = normalize(mixed)
        ffn_in_ref[here, :] = (normal * gain).astype(BF16)
        return hidden, weights, gate, mixed, normal, rstd

    def feed():
        ffn_in = ffn_in_ref[here, :]
        cot = cot_ref[0]
        down_sum = None
        grad_sum = None
        for side in range(2):
            for c in range(chunks):
                if side == 0:
                    up = up_ref[:, pl.ds(c * width, width)]
                    down = down_ref[pl.ds(c * width, width), :]
                else:
                    part = pl.ds(c * half, half)
                    up = jnp.concatenate([oth_ref[0, part, :], oth_ref[1, part, :]], 0)
                    down = oth_ref[c, pl.ds(width, width), :]
                at = pl.ds((side * chunks + c) * width, width)
                act, slope = gelu_parts(dot(ffn_in, up))
                act = act.astype(BF16)
                gpre = (dot(cot, down, 1, 1) * slope).astype(BF16)
                act_ref[here, at] = act
                gpre_ref[here, at] = gpre
                add = dot(act, down)
                down_sum = add if down_sum is None else down_sum + add
                add = dot(gpre, up, 1, 1)
                grad_sum = add if grad_sum is None else grad_sum + add
        return down_sum, grad_sum

    def back(kept, sums):
        hidden, weights, gate, mixed, normal, rstd = kept
        down_sum, grad_sum = sums
        result_ref[0] = (mixed + down_sum).astype(BF16)
        gain_part = jnp.sum(grad_sum * normal, 0, keepdims=True)
        grad_normal = grad_sum * gain
        grad_mixed = cot_ref[0].astype(F32) + rstd * (
            grad_normal
            - jnp.mean(grad_normal, -1, keepdims=True)
            - normal * jnp.mean(grad_normal * normal, -1, keepdims=True)
        )
        pulls = [
            jnp.sum(grad_mixed * e_ref[k], -1, keepdims=True) for k in range(NEIGH)
        ]
        pulled = weighted(weights, pulls)
        gate_grad = gate * (1.0 - gate) * pulled
        grad_hidden = grad_mixed + gate_grad * wgate
        for k in range(NEIGH):
            grad_hidden = (
                grad_hidden + (scale * gate * weights[k] * (pulls[k] - pulled)) * e_ref[k]
            )
        grad_hidden_ref[0] = grad_hidden
        low = grad_hidden.astype(BF16)
        low_ref[here, :] = low
        gctx_own_ref[0] = dot(low, out_ref[...], 1, 1).astype(BF16)
        gctx_oth_ref[0] = dot(low, other_out(), 1, 1).astype(BF16)
        gate_wide = jnp.broadcast_to(gate, (TILE, BINS)).T
        low_edge = jnp.concatenate([edge_ref[0]] * (TILE // BINS), 1)
        high_edge = jnp.concatenate([edge_ref[1]] * (TILE // BINS), 1)
        mass = jnp.zeros_like(gate_wide)
        for k in range(NEIGH):
            ids = ids_ref[0, pl.ds(k, 1), :].astype(F32)
            mass = mass + jnp.where((ids >= low_edge) & (ids < high_edge), gate_wide, 0.0)
        gate_sum = jnp.sum(jnp.broadcast_to(gate, (TILE, width)), 0, keepdims=True)
        sums_ref[pl.ds(0, 1), :] += gain_part
        sums_ref[pl.ds(1, 1), :] += gate_sum
        sums_ref[pl.ds(2, 1), :] += jnp.sum(gate_grad * hidden, 0, keepdims=True)
        hist_ref[...] += mass

    kept = front()

    @pl.when(step == 0)
    def _():
        for copy in copies[3:]:
            copy.wait()

    back(kept, feed())

    @pl.when(step == pl.num_programs(0) - 1)
    def _():
        sums_ref[pl.ds(3, 1), pl.ds(0, BINS)] = jnp.sum(hist_ref[...].T, 0, keepdims=True)
        moves = []
        for far, which in ((sent_far, 1 - core), (kept_far, core)):
            for side in range(2):
                at = pl.ds(pl.multiple_of((side * chunks + which) * width, width), width)
                here = pl.ds(pl.multiple_of((2 * side + which) * PAIR, PAIR), PAIR)
                for to, left, right in (
                    (pl.ds(0, width), ffn_in_ref[...], gpre_ref[:, at]),
                    (pl.ds(width, width), act_ref[:, at], cots_ref[...]),
                    (pl.ds(2 * width, PAIR), ctx_ref[:, here], low_ref[...]),
                ):
                    slot = len(moves)
                    stage = stage_ref.at[slot // 3, to, :]
                    stage[...] = dot(left, right, 0, 0).astype(BF16)
                    move = pltpu.make_async_copy(stage, far.at[side, to, :], out_sems.at[slot])
                    move.start()
                    moves.append(move)
        for move in moves:
            move.wait()


def middle_layer(tokens, ctx_own, ctx_oth, nb, ids, cot, weights, received, edges, gains):
    rows, length, width = tokens.shape
    hidden_units = weights[1].shape[0]
    steps = length // TILE
    tiles = rows * steps
    count = rows * length
    assert hidden_units == 2 * width

    def place_of(i):
        return i // steps, i % steps

    def tiled(last):
        return pl.BlockSpec((1, TILE, last), lambda i: (*place_of(i), 0))

    def whole(shape):
        return pl.BlockSpec(shape, lambda i: (0,) * len(shape))

    far = pl.BlockSpec(memory_space=pl.ANY)
    return pl.pallas_call(
        middle_body,
        grid=(tiles,),
            in_specs=[
                tiled(width),
                tiled(width // 2),
                tiled(width // 2),
                pl.BlockSpec((1, TILE, NEIGH, width), lambda i: (*place_of(i), 0, 0)),
                pl.BlockSpec(
                    (1, NEIGH, TILE), lambda i: (place_of(i)[0], 0, place_of(i)[1])
                ),
                tiled(width),
                *[far] * 5,
                whole((1, BINS + 1)),
                whole((2, width)),
            ],
            out_specs=[
                tiled(width),
                tiled(width),
                tiled(width // 2),
                tiled(width // 2),
                far,
                far,
                whole((8, width)),
            ],
            scratch_shapes=[
                pltpu.VMEM((NEIGH, TILE, width), F32),
                pltpu.VMEM((BINS, TILE), F32),
                pltpu.VMEM((2, BINS, BINS), F32),
                *[pltpu.VMEM(w.shape, BF16) for w in weights],
                pltpu.VMEM((2, *received[0].shape), BF16),
                pltpu.VMEM((4, 2 * width + PAIR, width), BF16),
                pltpu.VMEM((count, width), BF16),
                pltpu.VMEM((count, 2 * hidden_units), BF16),
                pltpu.VMEM((count, 2 * hidden_units), BF16),
                pltpu.VMEM((count, width), BF16),
                pltpu.VMEM((count, width), BF16),
                pltpu.VMEM((count, width), BF16),
                pltpu.SemaphoreType.DMA((5,)),
                pltpu.SemaphoreType.DMA((12,)),
            ],
        out_shape=[
            jax.ShapeDtypeStruct((rows, length, width), BF16),
            jax.ShapeDtypeStruct((rows, length, width), F32),
            jax.ShapeDtypeStruct((rows, length, width // 2), BF16),
            jax.ShapeDtypeStruct((rows, length, width // 2), BF16),
            jax.ShapeDtypeStruct((2, 2 * width + PAIR, width), BF16),
            jax.ShapeDtypeStruct((2, 2 * width + PAIR, width), BF16),
            jax.ShapeDtypeStruct((8, width), F32),
        ],
        compiler_params=pltpu.CompilerParams(vmem_limit_bytes=VMEM_LIMIT),
        cost_estimate=pl.CostEstimate(flops=15 * 10**9, bytes_accessed=30 * 2**20, transcendentals=0),
    )(tokens, ctx_own, ctx_oth, nb, ids, cot, *weights, *received, edges, gains)


def attend_back(
    head, qkv_ref, p_ref, gctx_ref, ctx_ref, ds_ref, dq_ref, t_ref, dk_ref, dv_ref, with_memory
):
    length = ctx_ref.shape[1]
    grad = only_head(gctx_ref[0], head)
    delta = jnp.sum(grad.astype(F32) * ctx_ref[0].astype(F32), -1, keepdims=True)
    keys = only_head(qkv_ref[0, 0, pl.ds(length, 2 * length), :], head)
    lanes = pl.ds(pl.multiple_of(head * HEAD, HEAD), HEAD)
    for first in range(0, length, QROWS):
        rows = pl.ds(first, QROWS)
        seen = first + QROWS
        spans = [(length, seen)] + ([(0, length)] if with_memory else [])
        total = dq_ref[rows, :]
        for at, span in spans:
            here = pl.ds(at, span)
            probs = p_ref[0, 0, 0, rows, here].astype(F32)
            values = qkv_ref[0, 0, pl.ds(3 * length + at, span), :]
            grad_probs = dot(grad[first : first + QROWS], values, 1, 1)
            ds = (probs * (grad_probs - delta[first : first + QROWS])).astype(BF16)
            ds_ref[rows, here] = ds
            total = total + dot(ds, keys[at : at + span])
        dq_ref[rows, :] = total
    for out_ref, left, right in (
        (dk_ref, t_ref[0, lanes, :], ds_ref),
        (dv_ref, t_ref[1, lanes, :], p_ref.at[0, 0, 0]),
    ):
        if with_memory:
            out_ref[lanes, :length] = dot(left, right[:, :length]).astype(BF16)
        else:
            out_ref[lanes, :length] = jnp.zeros((HEAD, length), BF16)
        for first in range(0, length, QROWS):
            here = pl.ds(length + first, QROWS)
            out_ref[lanes, here] = dot(
                left[:, first:], right[pl.ds(first, length - first), here]
            ).astype(BF16)


def backward_body(
    starts_ref,
    qkv_ref,
    p_ref,
    gctx_ref,
    ctx_ref,
    kv_far,
    pack_ref,
    grads_ref,
    dw_ref,
    gain_ref,
    ds_ref,
    dq_ref,
    t_ref,
    dk_ref,
    dv_ref,
    acc_ref,
    kv_ref,
    sem,
):
    length = ctx_ref.shape[1]
    row = pl.program_id(0)
    head = pl.program_id(1)
    start = starts_ref[lax.axis_index("mp") * pl.num_programs(0) + row]
    fetch = pltpu.make_async_copy(kv_far.at[row], kv_ref, sem)
    args = (qkv_ref, p_ref, gctx_ref, ctx_ref, ds_ref, dq_ref, t_ref, dk_ref, dv_ref)

    @pl.when(head == 0)
    def _():
        fetch.start()
        dq_ref[...] = jnp.zeros_like(dq_ref)
        t_ref[0] = qkv_ref[0, 0, pl.ds(0, length), :].T
        t_ref[1] = gctx_ref[0].T

    @pl.when(start == 0)
    def _():
        attend_back(head, *args, True)

    @pl.when(start != 0)
    def _():
        attend_back(head, *args, False)

    @pl.when(head == 1)
    def _():
        dq_t = (dq_ref[...] * HEAD ** (-0.5)).astype(BF16).T
        grads_ref[0, pl.ds(0, PAIR), :] = dq_t
        grads_ref[0, pl.ds(PAIR, PAIR), :] = dk_ref[:, length:]
        grads_ref[0, pl.ds(2 * PAIR, PAIR), :] = dv_ref[:, length:]
        fetch.wait()
        for i, add in enumerate(
            (
                dot(dq_t, kv_ref[pl.ds(length, length), :]),
                dot(dk_ref[...], kv_ref[...]),
                dot(dv_ref[...], kv_ref[...]),
            )
        ):
            acc_ref[i] = jnp.where(row == 0, add, acc_ref[i] + add)

    @pl.when((head == 1) & (row == pl.num_programs(0) - 1))
    def _():
        part = None
        for i in range(3):
            total = acc_ref[i]
            dw_ref[i] = total.astype(BF16)
            weight = pack_ref[:, pl.ds(i * PAIR, PAIR)].T.astype(F32)
            add = jnp.sum(total * weight, 0, keepdims=True)
            part = add if part is None else part + add
        gain_ref[...] = jnp.broadcast_to(part, gain_ref.shape)


def attention_backward(starts, saved, gctx, kv, sibling):
    pack, qkv, p, ctx = saved
    rows, _, _, length, _ = p.shape
    width = kv.shape[-1]

    def pair():
        return 1 - core_index() if sibling else core_index()

    return pl.pallas_call(
        backward_body,
        grid=(rows, 2),
        in_specs=[
            pl.BlockSpec(memory_space=pltpu.SMEM),
            pl.BlockSpec((1, 1, 5 * length, PAIR), lambda r, h: (r, pair(), 0, 0)),
            pl.BlockSpec((1, 1, 1, length, 2 * length), lambda r, h: (r, pair(), h, 0, 0)),
            pl.BlockSpec((1, length, PAIR), lambda r, h: (r, 0, pair())),
            pl.BlockSpec((1, length, PAIR), lambda r, h: (r, 0, pair())),
            pl.BlockSpec(memory_space=pl.ANY),
            pl.BlockSpec((width, 3 * PAIR), lambda r, h: (0, pair())),
        ],
        out_specs=[
            pl.BlockSpec((1, 3 * PAIR, length), lambda r, h: (r, 0, 0)),
            pl.BlockSpec((3, PAIR, width), lambda r, h: (0, 0, 0)),
            pl.BlockSpec((8, width), lambda r, h: (0, 0)),
        ],
        scratch_shapes=[
            pltpu.VMEM((length, 2 * length), BF16),
            pltpu.VMEM((length, PAIR), F32),
            pltpu.VMEM((2, PAIR, length), BF16),
            pltpu.VMEM((PAIR, 2 * length), BF16),
            pltpu.VMEM((PAIR, 2 * length), BF16),
            pltpu.VMEM((3, PAIR, width), F32),
            pltpu.VMEM((2 * length, width), BF16),
            pltpu.SemaphoreType.DMA,
        ],
        out_shape=[
            jax.ShapeDtypeStruct((rows, 3 * PAIR, length), BF16),
            jax.ShapeDtypeStruct((3, PAIR, width), BF16),
            jax.ShapeDtypeStruct((8, width), F32),
        ],
        compiler_params=pltpu.CompilerParams(vmem_limit_bytes=VMEM_LIMIT),
        cost_estimate=pl.CostEstimate(flops=4 * 10**9, bytes_accessed=8 * 2**20, transcendentals=0),
    )(starts, qkv, p, gctx, ctx, kv, pack)


def input_body(
    tok_ref,
    grad_hidden_ref,
    gain_ref,
    oth_first_ref,
    oth_last_ref,
    own_first_ref,
    own_last_ref,
    oth_pack_ref,
    own_pack_ref,
    out_ref,
):
    core = core_index()
    total = None
    for block, pack, which in (
        (oth_first_ref, oth_pack_ref, 1 - core),
        (oth_last_ref, oth_pack_ref, core),
        (own_first_ref, own_pack_ref, 1 - core),
        (own_last_ref, own_pack_ref, core),
    ):
        here = pl.ds(pl.multiple_of(which * 3 * PAIR, 3 * PAIR), 3 * PAIR)
        add = dot(block[0], pack[:, here], 0, 1)
        total = add if total is None else total + add
    normal, rstd = normalize(tok_ref[0].astype(F32))
    grad = total * gain_ref[...]
    out_ref[0] = (
        grad_hidden_ref[0]
        + rstd
        * (
            grad
            - jnp.mean(grad, -1, keepdims=True)
            - normal * jnp.mean(grad * normal, -1, keepdims=True)
        )
    ).astype(BF16)


def input_grad(tokens, grad_hidden, gain, grads, packs):
    rows, length, width = tokens.shape
    row = pl.BlockSpec((1, length, width), lambda r: (r, 0, 0))

    def whole(array):
        return pl.BlockSpec(array.shape, lambda r: (0, 0))

    return pl.pallas_call(
        input_body,
        grid=(rows,),
        in_specs=[
            row,
            row,
            whole(gain),
            *[pl.BlockSpec((1,) + g.shape[1:], lambda r: (r, 0, 0)) for g in grads],
            *[whole(p) for p in packs],
        ],
        out_specs=row,
        out_shape=jax.ShapeDtypeStruct(tokens.shape, BF16),
        compiler_params=pltpu.CompilerParams(vmem_limit_bytes=VMEM_LIMIT),
        cost_estimate=pl.CostEstimate(flops=2 * 10**9, bytes_accessed=8 * 2**20, transcendentals=0),
    )(tokens, grad_hidden, gain, *grads, *packs)


def finish_body(
    ffn_mine,
    ffn_sibling,
    attn_mine,
    attn_sibling,
    q_far,
    k_far,
    v_far,
    out_far,
    up_far,
    down_far,
    q_ref,
    k_ref,
    v_ref,
    out_ref,
    up_ref,
    down_ref,
    sems,
):
    core = core_index()
    width = up_far.shape[0]
    half = width // 2
    rows = attn_mine.shape[1]
    moves = []

    def pair(mine, sibling):
        return (
            jnp.where(core == 0, mine, sibling).astype(F32),
            jnp.where(core == 0, sibling, mine).astype(F32),
        )

    def move(near, far):
        moves.append(pltpu.make_async_copy(near, far, sems.at[len(moves)]))
        moves[-1].start()

    for x in range(2):
        to = pl.ds(x * half, half)
        for which, part in enumerate(
            pair(ffn_mine[x, pl.ds(0, half), :], ffn_sibling[x, pl.ds(0, half), :])
        ):
            up_ref[to, pl.ds(which * width, width)] = part
        move(up_ref.at[to, :], up_far.at[to, :])
    size = half + PAIR // 2
    for which, low in enumerate(
        zip(*(pair(ffn_mine[x, pl.ds(half, size), :], ffn_sibling[x, pl.ds(half, size), :]) for x in range(2)))
    ):
        first, last = low
        to = pl.ds(which * width, width)
        down_ref[pl.ds(which * width, size), :] = first
        down_ref[pl.ds(which * width + size, width - size), :] = last[: width - size]
        out_ref[pl.ds(which * PAIR, PAIR), :] = last[width - size :]
        move(down_ref.at[to, :], down_far.at[to, :])
    move(out_ref, out_far)
    for i, (near, far) in enumerate(((q_ref, q_far), (k_ref, k_far), (v_ref, v_far))):
        first, last = pair(attn_mine[i], attn_sibling[pl.ds(i * rows, rows), :])
        near[...] = jnp.concatenate([first, last], 0).T
        move(near, far)
    for one in moves:
        one.wait()


def finish(ffn, attn):
    width = ffn[0].shape[-1]
    quarter = attn[0].shape[1]
    shapes = [(width, 2 * quarter)] * 3
    shapes += [(2 * quarter, width), (width, 2 * width), (2 * width, width)]

    def whole(array):
        return pl.BlockSpec(array.shape, lambda i: (0,) * array.ndim)

    return pl.pallas_call(
        finish_body,
        grid=(1,),
        in_specs=[whole(a) for a in (*ffn, *attn)],
        out_specs=[pl.BlockSpec(memory_space=pl.ANY)] * 6,
        scratch_shapes=[pltpu.VMEM(s, F32) for s in shapes] + [pltpu.SemaphoreType.DMA((8,))],
        out_shape=[jax.ShapeDtypeStruct(s, F32) for s in shapes],
        compiler_params=pltpu.CompilerParams(vmem_limit_bytes=VMEM_LIMIT),
    )(*ffn, *attn)


def swap(array, axis, bit):
    size = lax.axis_size(axis)
    return lax.ppermute(array, axis, [(i, i ^ bit) for i in range(size)])


def bit_of(axis, bit):
    return (lax.axis_index(axis) // bit) % 2


def part_of(array, which, dim):
    half = array.shape[dim] // 2
    return lax.dynamic_slice_in_dim(array, which * half, half, dim)


def add_low(left, right):
    return (left.astype(F32) + right.astype(F32)).astype(BF16)


def join(mine, other, bit, dim):
    return jnp.where(
        bit_of("dp", bit) == 0,
        lax.concatenate([mine, other], dim),
        lax.concatenate([other, mine], dim),
    )


def after(value, *others):
    return lax.optimization_barrier((value, *others))[0]


class Chain:
    def __init__(self, array, dim):
        self.pieces = (array,)
        self.dim = dim

    def total(self, cut=lambda piece: piece):
        pieces = [cut(piece) for piece in self.pieces]
        if len(pieces) == 1:
            return pieces[0]
        return sum(piece.astype(F32) for piece in pieces).astype(BF16)

    def pass_on(self, sent, kept, bit, *others):
        self.sent = after(sent, *others)
        self.kept = kept
        self.come = swap(self.sent, "dp", bit)
        return self.sent

    def halve(self, bit, *others):
        mine = bit_of("dp", bit)
        self.sent = after(self.total(lambda p: part_of(p, 1 - mine, self.dim)), *others)
        self.kept = self.total(lambda p: part_of(p, mine, self.dim))
        self.come = swap(self.sent, "dp", bit)
        return self.sent

    def give(self, index, *others):
        self.sent = after(self.total(lambda p: p[index]), *others)
        self.kept = self.total(lambda p: p[1 - index])
        self.dim -= 1
        self.come = swap(self.sent, "mp", 1)
        return self.sent

    def send(self, bit, *others):
        self.sent = self.kept = after(self.total(), *others)
        self.come = swap(self.sent, "dp", bit)
        return self.sent

    def add(self, *others):
        self.come = after(self.come, *others)
        self.pieces = (self.kept, self.come)

    def join(self, bit, *others):
        self.pieces = (join(self.sent, after(self.come, *others), bit, self.dim),)


class Ride:
    def __init__(self, rows):
        self.rows = rows

    def below(self, array):
        left = self.rows
        parts = [array.reshape(-1, array.shape[-1])]
        for _ in range(3):
            part = lax.reduce_precision(left, 8, 7)
            parts.append(part.astype(BF16))
            left = left - part
        spare = -3 * left.shape[0] % 16
        parts.append(jnp.zeros((spare, left.shape[1]), BF16))
        return lax.concatenate(parts, 0)

    def add(self, block, like):
        size = like.size // like.shape[-1]
        count = self.rows.shape[0]
        for i in range(3):
            at = size + i * count
            self.rows = self.rows + block[at : at + count].astype(F32)
        return block[:size].reshape(like.shape)


def shards(
    tokens,
    memory,
    neighbours,
    neighbour_ids,
    doc_starts,
    bin_edges,
    w_query,
    w_key,
    w_value,
    w_out,
    w_up,
    w_down,
    gain_attn,
    gain_ffn,
    w_gate,
    cotangent,
):
    rows, length, width = tokens.shape
    count = rows * length
    dp = lax.axis_size("dp")
    core = bit_of("dp", 1)
    attn_gain = gain_attn.reshape(1, width)
    gains = jnp.stack([gain_ffn, w_gate])
    qkv = (w_query, w_key, w_value)
    far = []
    bit = 2
    while bit < dp:
        far.append(bit)
        bit *= 2

    qkv_sent = lax.concatenate([part_of(w, core, 0) for w in qkv], 1)
    up_part = part_of(w_up, core, 0)
    ffn_sent = lax.concatenate(
        [up_part[:, :width], up_part[:, width:], part_of(w_down, core, 0), part_of(w_out, core, 0)],
        0,
    )
    qkv_mine = swap(qkv_sent, "mp", 1)
    ffn_mine = swap(after(ffn_sent, qkv_sent), "mp", 1)
    kv, *own = attention_forward(
        doc_starts, after(tokens, qkv_sent, ffn_sent), memory, attn_gain, None, qkv
    )
    qkv_mine = after(qkv_mine, kv)
    qkv_got = (qkv_mine, swap(qkv_mine, "dp", 1))
    oth = attention_forward(doc_starts, tokens, memory, attn_gain, kv, qkv_got)
    ffn_mine = after(ffn_mine, oth[3])
    ffn_got = (ffn_mine, swap(ffn_mine, "dp", 1))
    ids = jnp.swapaxes(neighbour_ids, 1, 2)
    edges = bin_edges.reshape(1, BINS + 1)
    (
        result,
        grad_hidden,
        gctx_own,
        gctx_oth,
        ffn_first,
        ffn_last,
        sums,
    ) = middle_layer(
        tokens,
        own[3],
        oth[3],
        neighbours,
        ids,
        cotangent,
        (w_up, w_down, w_out),
        ffn_got,
        edges,
        gains,
    )
    ffn = Chain(None, 1)
    sent = ffn.pass_on(ffn_first, ffn_last, 1)
    g_oth_first, da_first, gain_1 = attention_backward(
        doc_starts, oth, after(gctx_oth, sent), kv, True
    )
    ffn.add(da_first)
    up = Chain(None, 1)
    up.pieces = tuple(p[:, :width] for p in ffn.pieces)
    down = Chain(None, 1)
    down.pieces = tuple(p[:, width:] for p in ffn.pieces)
    sent = up.give(1)
    sent = down.halve(far[0], sent)
    attn = Chain(None, 1)
    sent = attn.pass_on(da_first, None, 1, sent)
    g_oth_last, da_last, gain_2 = attention_backward(
        doc_starts, oth, after(gctx_oth, sent), kv, False
    )
    attn.come = after(attn.come, da_last)
    up.add(da_last)
    down.add(da_last)
    sent = up.halve(far[0])
    sent = down.give(1, sent)
    attn_sent = after(add_low(da_last, attn.come), sent)
    attn_come = swap(attn_sent, "mp", 1)
    g_own_first, da_first, gain_3 = attention_backward(
        doc_starts, own, after(gctx_own, attn_sent), kv, True
    )
    up.add(da_first)
    down.add(da_first)
    both = Chain(None, 0)
    both.pieces = tuple(lax.concatenate([u, d], 0) for u, d in zip(up.pieces, down.pieces))
    sent = both.halve(far[1])
    first_sent = after(da_first, sent)
    first_come = swap(first_sent, "dp", 1)
    g_own_last, da_last, gain_4 = attention_backward(
        doc_starts, own, after(gctx_own, first_sent), kv, False
    )
    attn_come, first_come = lax.optimization_barrier((attn_come, first_come, da_last))[:2]
    attn = Chain(None, 1)
    attn.pieces = (da_last, first_come, attn_come)
    both.add(da_last)
    gain_part = (gain_1[:1] + gain_2[:1] + gain_3[:1] + gain_4[:1]) / attn_gain
    small = lax.concatenate([sums[:4], gain_part], 0)
    sent = attn.halve(far[0])
    sent = both.send(far[2], sent)
    small_sent = after(small, sent)
    small_come = swap(small_sent, "mp", 1)
    grad_input = input_grad(
        tokens,
        after(grad_hidden, small_sent),
        attn_gain,
        (g_oth_first, g_oth_last, g_own_first, g_own_last),
        (oth[0], own[0]),
    )
    attn.come, small_come = lax.optimization_barrier((attn.come, small_come, grad_input))[:2]
    attn.pieces = (attn.kept, attn.come)
    ride = Ride(small_sent + small_come)

    mine = bit_of("dp", far[1])
    part = attn.total(lambda p: part_of(p, 1 - mine, 1))
    kept = attn.total(lambda p: part_of(p, mine, 1))
    come = swap(ride.below(part), "dp", far[1])
    come, both.come = lax.optimization_barrier((come, both.come))
    total = add_low(kept, ride.add(come, kept))
    ffn_total = add_low(both.sent, both.come)
    for bit in far[3:]:
        ffn_total = add_low(ffn_total, swap(ffn_total, "dp", bit))
    for bit in far[2:]:
        sent = ride.below(total)
        come = swap(sent, "dp", bit)
        if bit == far[2]:
            ffn_sent = after(ffn_total, sent)
            ffn_come = swap(ffn_sent, "dp", far[0])
            come, ffn_come = lax.optimization_barrier((come, ffn_come))
        total = add_low(total, ride.add(come, total))
    come = swap(total, "dp", far[1])
    ffn_halves = after(join(ffn_sent[None], ffn_come[None], far[0], 0), total)
    ffn_come = swap(ffn_halves[0], "dp", far[1])
    come, ffn_come = lax.optimization_barrier((come, ffn_come))
    ffn_first = join(ffn_halves[0], ffn_come, far[1], 0)
    total = join(total, come, far[1], 1)
    sent = ride.below(total)
    come = swap(sent, "dp", far[0])
    ffn_come = swap(after(ffn_halves[1], sent), "dp", far[1])
    come, ffn_come = lax.optimization_barrier((come, ffn_come))
    total = join(total, ride.add(come, total), far[0], 1)
    sent = ride.below(total)
    come = swap(sent, "dp", 1)
    ffn_last = join(ffn_halves[1], ffn_come, far[1], 0)
    ffn_total = after(lax.concatenate([ffn_first[None], ffn_last[None]], 0), sent)
    ffn_come = swap(ffn_total, "dp", 1)
    ride.add(come, total)
    small = ride.rows
    total_count = count * dp * lax.axis_size("mp")
    g_query, g_key, g_value, g_out, g_up, g_down = finish(
        (ffn_total, ffn_come), (total, come)
    )
    return (
        result,
        grad_input,
        g_query,
        g_key,
        g_value,
        g_out,
        g_up,
        g_down,
        small[4],
        small[0],
        small[2],
        small[1, 0] / total_count,
        small[3, :BINS] * (BINS / (total_count * NEIGH)),
    )


def solution(mesh):
    in_specs = (
        P(("dp", "mp"), None, None),
        P("dp", None, None),
        P(("dp", "mp"), None, None, None),
        P(("dp", "mp"), None, None),
        P("dp"),
        P(),
        P(None, "mp"),
        P(None, "mp"),
        P(None, "mp"),
        P("mp", None),
        P(None, "mp"),
        P("mp", None),
        P(),
        P(),
        P(),
        P(("dp", "mp"), None, None),
    )
    out_specs = (
        P(("dp", "mp"), None, None),
        P(("dp", "mp"), None, None),
        P(None, "mp"),
        P(None, "mp"),
        P(None, "mp"),
        P("mp", None),
        P(None, "mp"),
        P("mp", None),
        P(),
        P(),
        P(),
        P(),
        P(),
    )
    return jax.shard_map(shards, mesh=mesh, in_specs=in_specs, out_specs=out_specs, check_vma=False)
```

time: 621 us -> 200 us (0.32); the launches traced: 611 us -> 199 us
  matrix products: 190 us -> 0 us
  blocking collectives: 156 us -> 0 us
  Pallas kernels: 0 us -> 107 us
  waiting for transfers between devices: 125 us -> 40.3 us
  local copies, waits for them, and re-layouts: 70.7 us -> 10.6 us
  other arithmetic: 48.8 us -> 8.44 us
  starting transfers between devices: 0.58 us -> 29.9 us
  between operations: 16.9 us -> 3 us
    dot_general x39 -> x0, matrix products: 190 us -> none  [the longest x4 29 us: row_scores(): jnp.einsum('qhc,khc->hqk', head_view(query_row, length), head_view(key_ro...]
    psum x2 -> x0, blocking collectives: 123 us -> none  [the longest x1 82.6 us: shards(): lax.psum((grad_wq, grad_wk, grad_wv, grad_wout, grad_up, grad_down), 'dp')]
    pallas_call x0 -> x9, Pallas kernels: none -> 107 us  [the longest x4 34.3 us: attention_backward(): pl.pallas_call(backward_body, grid=(rows, 2), in_specs=[pl.BlockSpec(memo...]
    all_gather x2 -> x0, waiting for transfers between devices: 60.7 us -> none  [the longest x1 33.2 us: shards(): ffn_rows = lax.all_gather(ffn_in, 'mp', axis=0, tiled=True)]
    reduce_scatter x6 -> x0, waiting for transfers between devices: 52 us -> none  [the longest x1 29.1 us: shards(): lax.psum_scatter(down_part.astype(jnp.bfloat16), 'mp', scatter_dimension=...]
    ppermute x0 -> x25, waiting for transfers between devices: none -> 40.3 us  [swap(): return lax.ppermute(array, axis, [(i, i ^ bit) for i in range(size)])]
    all_gather x4 -> x0, blocking collectives: 32.7 us -> none  [the longest x1 10.2 us: shards(): lax.all_gather(w_out, 'mp', axis=0, tiled=True)]
    ppermute x0 -> x25, starting transfers between devices: none -> 29.9 us  [swap(): return lax.ppermute(array, axis, [(i, i ^ bit) for i in range(size)])]
  transfers between devices with their start and end apart: 9 -> 25, of which waited for: 5 -> 12; matrix products, arithmetic and copies ran while one was open for 23% -> 4% of each run, Pallas kernels for 0% -> 35%
where the time goes in v1:
time: 200 us; the launch traced here: 199 us
  Pallas kernels  107 us (54%)
  waiting for transfers between devices  40.3 us (20%)
  starting transfers between devices  29.9 us (15%)
  local copies, waits for them, and re-layouts  10.6 us (5%)
  other arithmetic  8.44 us (4%)
  between operations  3 us (2%)
    ppermute x25, waiting for transfers between devices, swap(): return lax.ppermute(array, axis, [(i, i ^ bit) for i in range(size)])  40.3 us
    pallas_call x4, Pallas kernels, attention_backward(): pl.pallas_call(backward_body, grid=(rows, 2), in_specs=[pl.BlockSpec(memo...  34.3 us
    pallas_call x1, Pallas kernels, middle_layer(): pl.pallas_call(middle_body, grid=(tiles,), in_specs=[tiled(width), tiled(...  32.5 us
    ppermute x25, starting transfers between devices, swap(): return lax.ppermute(array, axis, [(i, i ^ bit) for i in range(size)])  29.9 us
    pallas_call x2, Pallas kernels, attention_forward(): pl.pallas_call(body, grid=(rows, pairs), in_specs=in_specs, out_specs=out...  28.2 us
    pallas_call x1, Pallas kernels, input_grad(): pl.pallas_call(input_body, grid=(rows,), in_specs=[row, row, whole(gain),...  6.79 us
    pallas_call x1, Pallas kernels, finish(): pl.pallas_call(finish_body, grid=(1,), in_specs=[whole(a) for a in (*ffn,...  4.89 us
    convert_element_type x8, other arithmetic, total(): return sum((piece.astype(F32) for piece in pieces)).astype(BF16)  4.2 us
  transfers between devices with their start and end apart: 25, of which 12 were waited for; matrix products, arithmetic and copies ran while one was open for 4% of the time, Pallas kernels for 35%

profile of v1, /device:TPU:0, one launch (start us, length us, event | category | flops | bytes accessed | tf_op | source)
XLA Modules:
  0.0 199.0 jit_solution(15332341928512069541)
XLA Ops:
  0.7 1.1 constant_dynamic-slice_fusion.5
  1.7 1.0 constant_dynamic-slice_fusion.3
  2.8 3.0 %collective-permute-start = (bf16[256,768]{1,0:T(8,128)(2,1)S(1)}, bf16[256,768]{1,0:T(8,128)(2,1)}, u32[]{:S(2)}, u32[]{:S(2)}) collective-permute-start(bf16[256,768]{1,0:T(8,128)(2,1)S(1)} %pad_maximum_fusion.2), channel_id=1, source_target_pairs={{0,1},{1,0},{2,3},{3,2},{4,5},{5,4},{6,7},{7,6},{8,9},{9,8},{10,11... | collective-permute-start | bytes 1179656 | tf_op jit(solution)/shard_map/ppermute | solution.py:768
  5.9 0.9 constant_dynamic-slice_fusion.1
  7.0 15.0 %shard_map.255 = (bf16[2,1024,512]{2,1,0:T(8,128)(2,1)}, bf16[512,768]{1,0:T(8,128)(2,1)}, bf16[2,2,2560,128]{3,2,1,0:T(8,128)(2,1)}, bf16[2,2,2,512,1024]{4,3,2,1,0:T(8,128)(2,1)}, bf16[2,512,256]{2,1,0:T(8,128)(2,1)}) custom-call(s32[4]{0:T(128)} %starts_ref.11, bf16[2,512,512]{2,1,0:T(8,128)(2,1)} %tok_ref.4, bf16[4,512,512]{2,1,0:T(8,128)(2,1)} %mem_ref.1, ...), custom_call_target="tpu_custom_call" | custom-call | flops 6000000000 | bytes 16777216 | tf_op jit(solution)/shard_map/pallas_call | solution.py:174
  22.2 1.9 collective-permute-done.1.sibling_ref
  24.1 0.7 copy-done.13
  24.9 13.1 %shard_map.256 = (bf16[512,768]{1,0:T(8,128)(2,1)}, bf16[2,2,2560,128]{3,2,1,0:T(8,128)(2,1)}, bf16[2,2,2,512,1024]{4,3,2,1,0:T(8,128)(2,1)}, bf16[2,512,256]{2,1,0:T(8,128)(2,1)}) custom-call(s32[4]{0:T(128)} %starts_ref.11, bf16[2,1024,512]{2,1,0:T(8,128)(2,1)} %get-tuple-element.88.kv_ref.kv_far, bf16[256,768]{1,0:T(8,128)(2,1)} %collective-permute-done.mine_ref, ...), custom_call_target="tpu_custom_call" | custom-call | flops 6000000000 | bytes 16777216 | tf_op jit(solution)/shard_map/pallas_call | solution.py:174
  38.0 2.2 %collective-permute-done.2.mine_far = bf16[1152,512]{1,0:T(8,128)(2,1)S(1)} collective-permute-done((bf16[1152,512]{1,0:T(8,128)(2,1)S(1)}, bf16[1152,512]{1,0:T(8,128)(2,1)S(1)}, u32[]{:S(2)}, u32[]{:S(2)}) %collective-permute-start.2) | collective-permute-done | bytes 1179680 | tf_op jit(solution)/shard_map/ppermute | solution.py:768
  40.2 0.7 pad_maximum_fusion.4.gains_ref
  40.9 2.2 %collective-permute-done.3.sibling_far = bf16[1152,512]{1,0:T(8,128)(2,1)S(1)} collective-permute-done((bf16[1152,512]{1,0:T(8,128)(2,1)S(1)}, bf16[1152,512]{1,0:T(8,128)(2,1)S(1)}, u32[]{:S(2)}, u32[]{:S(2)}) %collective-permute-start.3) | collective-permute-done | bytes 1179680 | tf_op jit(solution)/shard_map/ppermute | solution.py:768
  43.1 1.1 copy-done.11
  44.1 32.5 %shard_map.257 = (bf16[2,512,512]{2,1,0:T(8,128)(2,1)}, f32[2,512,512]{2,1,0:T(8,128)}, bf16[2,512,256]{2,1,0:T(8,128)(2,1)}, bf16[2,512,256]{2,1,0:T(8,128)(2,1...) custom-call(bf16[2,512,512]{2,1,0:T(8,128)(2,1)} %tok_ref.4, ...), custom_call_target="tpu_custom_call" | custom-call | flops 15000000512 | bytes 31457280 | tf_op jit(solution)/shard_map/pallas_call | solution.py:418
  76.7 0.2 collective-permute-start.4
  76.9 1.4 slice.129
  78.3 8.6 %shard_map.258 = (bf16[2,384,512]{2,1,0:T(8,128)(2,1)}, bf16[3,128,512]{2,1,0:T(8,128)(2,1)}, f32[8,512]{1,0:T(8,128)}) custom-call(s32[4]{0:T(128)} %starts_ref.11, bf16[2,2,2560,128]{3,2,1,0:T(8,128)(2,1)} %get-tuple-element.96.qkv_ref, bf16[2,2,2,512,1024]{4,3,2,1,0:T(8,128)(2,1)} %get-tuple-element.97.p_ref, ...), custom_call_target="tpu_custom_call" | custom-call | flops 4000000000 | bytes 8388608 | tf_op jit(solution)/shard_map/pallas_call | solution.py:588
  86.9 1.5 add_convert_fusion.2
  88.5 0.4 add_convert_fusion
  88.9 0.4 collective-permute-start.5
  89.4 1.7 collective-permute-start.7
  91.1 5.2 %collective-permute-start.6 = (bf16[2,320,512]{2,1,0:T(8,128)(2,1)S(1)}, bf16[2,320,512]{2,1,0:T(8,128)(2,1)S(1)}, u32[]{:S(2)}, u32[]{:S(2)}) collective-permute-start(bf16[2,320,512]{2,1,0:T(8,128)(2,1)S(1)} %get-tuple-element.106), channel_id=1, source_target_pairs={{0,4},{2,6},{4,0},{6,2},{8,12},{10,14},{12,8},{14,10},{16,20},{18,... | collective-permute-start | bytes 1966088 | tf_op jit(solution)/shard_map/ppermute | solution.py:768
  96.3 8.6 %shard_map.259 = (bf16[2,384,512]{2,1,0:T(8,128)(2,1)}, bf16[3,128,512]{2,1,0:T(8,128)(2,1)}, f32[8,512]{1,0:T(8,128)}) custom-call(s32[4]{0:T(128)} %starts_ref.11, bf16[2,2,2560,128]{3,2,1,0:T(8,128)(2,1)} %get-tuple-element.96.qkv_ref, bf16[2,2,2,512,1024]{4,3,2,1,0:T(8,128)(2,1)} %get-tuple-element.97.p_ref, ...), custom_call_target="tpu_custom_call" | custom-call | flops 4000000000 | bytes 8388608 | tf_op jit(solution)/shard_map/pallas_call | solution.py:588
  104.9 1.1 add_convert_fusion.4
  106.2 2.9 %collective-permute-start.8 = (bf16[256,512]{1,0:T(8,128)(2,1)S(1)}, bf16[256,512]{1,0:T(8,128)(2,1)S(1)}, u32[]{:S(2)}, u32[]{:S(2)}) collective-permute-start(bf16[256,512]{1,0:T(8,128)(2,1)S(1)} %get-tuple-element.176), channel_id=1, source_target_pairs={{0,4},{2,6},{4,0},{6,2},{8,12},{10,14},{12,8},{14,10},{16,20},{18,... | collective-permute-start | bytes 786440 | tf_op jit(solution)/shard_map/ppermute | solution.py:768
  109.0 2.8 %collective-permute-done.6 = bf16[2,320,512]{2,1,0:T(8,128)(2,1)S(1)} collective-permute-done((bf16[2,320,512]{2,1,0:T(8,128)(2,1)S(1)}, bf16[2,320,512]{2,1,0:T(8,128)(2,1)S(1)}, u32[]{:S(2)}, u32[]{:S(2)}) %collective-permute-start.6) | collective-permute-done | bytes 655392 | tf_op jit(solution)/shard_map/ppermute | solution.py:768
  112.0 0.6 collective-permute-start.9
  112.6 1.5 collective-permute-start.11
  114.1 8.6 %shard_map.260 = (bf16[2,384,512]{2,1,0:T(8,128)(2,1)}, bf16[3,128,512]{2,1,0:T(8,128)(2,1)}, f32[8,512]{1,0:T(8,128)}) custom-call(s32[4]{0:T(128)} %starts_ref.11, bf16[2,2,2560,128]{3,2,1,0:T(8,128)(2,1)} %get-tuple-element.110.qkv_ref, bf16[2,2,2,512,1024]{4,3,2,1,0:T(8,128)(2,1)} %get-tuple-element.111.p_ref, ...), custom_call_target="tpu_custom_call" | custom-call | flops 4000000000 | bytes 8388608 | tf_op jit(solution)/shard_map/pallas_call | solution.py:588
  122.8 0.4 add_convert_fusion.10
  123.2 0.5 copy-done.12
  123.8 8.6 %shard_map.261 = (bf16[2,384,512]{2,1,0:T(8,128)(2,1)}, bf16[3,128,512]{2,1,0:T(8,128)(2,1)}, f32[8,512]{1,0:T(8,128)}) custom-call(s32[4]{0:T(128)} %starts_ref.11, bf16[2,2,2560,128]{3,2,1,0:T(8,128)(2,1)} %get-tuple-element.110.qkv_ref, bf16[2,2,2,512,1024]{4,3,2,1,0:T(8,128)(2,1)} %get-tuple-element.111.p_ref, ...), custom_call_target="tpu_custom_call" | custom-call | flops 4000000000 | bytes 8388608 | tf_op jit(solution)/shard_map/pallas_call | solution.py:588
  132.4 0.8 add_divide_fusion
  133.2 1.2 add_convert_fusion.11
  134.4 3.5 %collective-permute-start.13 = (bf16[3,64,512]{2,1,0:T(8,128)(2,1)S(1)}, bf16[3,64,512]{2,1,0:T(8,128)(2,1)S(1)}, u32[]{:S(2)}, u32[]{:S(2)}) collective-permute-start(bf16[3,64,512]{2,1,0:T(8,128)(2,1)S(1)} %get-tuple-element.174), channel_id=1, source_target_pairs={{0,4},{2,6},{4,0},{6,2},{8,12},{10,14},{12,8},{14,10},{16,20},{18,... | collective-permute-start | bytes 589832 | tf_op jit(solution)/shard_map/ppermute | solution.py:768
  137.9 0.4 add_convert_fusion.8
  138.4 2.7 %collective-permute-start.16 = (bf16[288,512]{1,0:T(8,128)(2,1)S(1)}, bf16[288,512]{1,0:T(8,128)(2,1)S(1)}, u32[]{:S(2)}, u32[]{:S(2)}) collective-permute-start(bf16[288,512]{1,0:T(8,128)(2,1)S(1)} %add_convert_fusion.8), channel_id=1, source_target_pairs={{0,16},{2,18},{4,20},{6,22},{8,24},{10,26},{12,28},{14,30},{16,0},... | collective-permute-start | bytes 884744 | tf_op jit(solution)/shard_map/ppermute | solution.py:768
  141.1 0.7 collective-permute-start.14
  141.8 6.8 %shard_map.262 = bf16[2,512,512]{2,1,0:T(8,128)(2,1)} custom-call(bf16[2,512,512]{2,1,0:T(8,128)(2,1)} %tok_ref.4, f32[2,512,512]{2,1,0:T(8,128)} %get-tuple-element.134.grad_hidden_ref, f32[1,512]{1,0:T(1,128)} %bitcast.52, bf16[2,384,512]{2,1,0:T(8,128)(2,1)} %get-tuple-element.135.oth_first_ref, bf16[2,384,512]{2,1,0:T(8,128)(2,1)} %get-tuple-element.136.oth_last_ref, ...), custom_call_target="tpu_custom_call" | custom-call | flops 2000000000 | bytes 8388608 | tf_op jit(solution)/shard_map/pallas_call | solution.py:668
  148.7 0.4 concatenate.97
  149.1 1.0 collective-permute-start.15
  150.1 4.7 %collective-permute-done.16 = bf16[288,512]{1,0:T(8,128)(2,1)S(1)} collective-permute-done((bf16[288,512]{1,0:T(8,128)(2,1)S(1)}, bf16[288,512]{1,0:T(8,128)(2,1)S(1)}, u32[]{:S(2)}, u32[]{:S(2)}) %collective-permute-start.16) | collective-permute-done | bytes 294944 | tf_op jit(solution)/shard_map/ppermute | solution.py:768
  154.8 2.4 %collective-permute-done.15 = bf16[112,512]{1,0:T(8,128)(2,1)S(1)} collective-permute-done((bf16[112,512]{1,0:T(8,128)(2,1)S(1)}, bf16[112,512]{1,0:T(8,128)(2,1)S(1)}, u32[]{:S(2)}, u32[]{:S(2)}) %collective-permute-start.15) | collective-permute-done | bytes 114720 | tf_op jit(solution)/shard_map/ppermute | solution.py:768
  157.5 0.4 collective-permute-start.18
  157.9 0.9 collective-permute-start.17
  158.8 7.3 %collective-permute-done.17 = bf16[112,512]{1,0:T(8,128)(2,1)S(1)} collective-permute-done((bf16[112,512]{1,0:T(8,128)(2,1)S(1)}, bf16[112,512]{1,0:T(8,128)(2,1)S(1)}, u32[]{:S(2)}, u32[]{:S(2)}) %collective-permute-start.17) | collective-permute-done | bytes 114720 | tf_op jit(solution)/shard_map/ppermute | solution.py:768
  166.1 0.4 collective-permute-done.18
  166.8 2.1 %collective-permute-start.19 = (bf16[3,32,512]{2,1,0:T(8,128)(2,1)S(1)}, bf16[3,32,512]{2,1,0:T(8,128)(2,1)S(1)}, u32[]{:S(2)}, u32[]{:S(2)}) collective-permute-start(bf16[3,32,512]{2,1,0:T(8,128)(2,1)S(1)} %fusion.7), channel_id=1, source_target_pairs={{0,8},{2,10},{4,12},{6,14},{8,0},{10,2},{12,4},{14,6},{16,24},{18,... | collective-permute-start | bytes 294920 | tf_op jit(solution)/shard_map/ppermute | solution.py:768
  168.9 8.3 %collective-permute-done.19 = bf16[3,32,512]{2,1,0:T(8,128)(2,1)S(1)} collective-permute-done((bf16[3,32,512]{2,1,0:T(8,128)(2,1)S(1)}, bf16[3,32,512]{2,1,0:T(8,128)(2,1)S(1)}, u32[]{:S(2)}, u32[]{:S(2)}) %collective-permute-start.19) | collective-permute-done | bytes 98336 | tf_op jit(solution)/shard_map/ppermute | solution.py:768
  177.3 0.2 concatenate.106
  177.5 0.3 collective-permute-start.22
  177.8 1.7 collective-permute-start.21
  179.5 0.2 maximum_select_fusion.1
  179.7 4.1 %collective-permute-done.21 = bf16[208,512]{1,0:T(8,128)(2,1)S(1)} collective-permute-done((bf16[208,512]{1,0:T(8,128)(2,1)S(1)}, bf16[208,512]{1,0:T(8,128)(2,1)S(1)}, u32[]{:S(2)}, u32[]{:S(2)}) %collective-permute-start.21) | collective-permute-done | bytes 213024 | tf_op jit(solution)/shard_map/ppermute | solution.py:768
  183.9 1.0 collective-permute-done.22
  185.1 0.2 maximum_select_fusion.2
  185.5 0.4 copy-done.1
  185.9 0.2 concatenate.113
  186.2 0.5 collective-permute-start.24
  186.7 2.9 %collective-permute-done.24.attn_sibling = bf16[400,512]{1,0:T(8,128)(2,1)S(1)} collective-permute-done((bf16[400,512]{1,0:T(8,128)(2,1)S(1)}, bf16[400,512]{1,0:T(8,128)(2,1)S(1)}, u32[]{:S(2)}, u32[]{:S(2)}) %collective-permute-start.24) | collective-permute-done | bytes 409632 | tf_op jit(solution)/shard_map/ppermute | solution.py:768
  189.6 0.6 slice.172
  190.8 0.5 fusion.17
  191.3 0.6 fusion.19
  192.0 1.0 copy-done.2
  193.0 4.9 %shard_map.263 = (f32[512,256]{1,0:T(8,128)}, f32[512,256]{1,0:T(8,128)}, f32[512,256]{1,0:T(8,128)}, f32[256,512]{1,0:T(8,128)}, f32[512,1024]{1,0:T(8,128)}, /*index=5*/f32[1024,512]{1,0:T(8,128)}) custom-call(bf16[2,576,512]{2,1,0:T(8,128)(2,1)} %copy-done, bf16[2,576,512]{2,1,0:T(8,128)(2,1)} %copy-done.2, bf16[3,128,512]{2,1,0:T(8,128)(2,1)} %copy-done.1, ...), custom_call_target="tpu_custom_call" | custom-call | tf_op jit(solution)/shard_map/pallas_call | solution.py:755
  (77 shorter events, 2.1 us)
Async XLA Ops:
  0.6 5.2 %copy-start.5 = (bf16[1024,512]{1,0:T(8,128)(2,1)S(1)}, bf16[1024,512]{1,0:T(8,128)(2,1)}, u32[]{:S(2)}) copy-start(bf16[1024,512]{1,0:T(8,128)(2,1)} %down_far.1) | copy-start | bytes 3145732
  0.7 5.2 %copy-start.4 = (bf16[512,1024]{1,0:T(8,128)(2,1)S(1)}, bf16[512,1024]{1,0:T(8,128)(2,1)}, u32[]{:S(2)}) copy-start(bf16[512,1024]{1,0:T(8,128)(2,1)} %up_far.1) | copy-start | bytes 3145732
  2.8 19.3 %collective-permute-start = (bf16[256,768]{1,0:T(8,128)(2,1)S(1)}, bf16[256,768]{1,0:T(8,128)(2,1)}, u32[]{:S(2)}, u32[]{:S(2)}) collective-permute-start(bf16[256,768]{1,0:T(8,128)(2,1)S(1)} %pad_maximum_fusion.2), channel_id=1, source_target_pairs={{0,1},{1,0},{2,3},{3,2},{4,5},{5,4},{6,7},{7,6},{8,9},{9,8},{10,11... | collective-permute-start | bytes 1179656 | tf_op jit(solution)/shard_map/ppermute | solution.py:768
  6.9 33.3 %collective-permute-start.2 = (bf16[1152,512]{1,0:T(8,128)(2,1)S(1)}, bf16[1152,512]{1,0:T(8,128)(2,1)S(1)}, u32[]{:S(2)}, u32[]{:S(2)}) collective-permute-start(bf16[1152,512]{1,0:T(8,128)(2,1)S(1)} %pad_maximum_fusion), channel_id=1, source_target_pairs={{0,1},{1,0},{2,3},{3,2},{4,5},{5,4},{6,7},{7,6},{8,9},{9,8},{10,11... | collective-permute-start | bytes 3538952 | tf_op jit(solution)/shard_map/ppermute | solution.py:768
  22.1 18.1 %copy-start.8 = (f32[512]{0:T(512)S(1)}, f32[512]{0:T(512)}, u32[]{:S(2)}) copy-start(f32[512]{0:T(512)} %param.30) | copy-start | bytes 6148
  22.1 18.1 %copy-start.9 = (f32[512]{0:T(512)S(1)}, f32[512]{0:T(512)}, u32[]{:S(2)}) copy-start(f32[512]{0:T(512)} %param.29) | copy-start | bytes 6148
  22.1 2.0 %collective-permute-start.1 = (bf16[256,768]{1,0:T(8,128)(2,1)}, bf16[256,768]{1,0:T(8,128)(2,1)S(1)}, u32[]{:S(2)}, u32[]{:S(2)}) collective-permute-start(bf16[256,768]{1,0:T(8,128)(2,1)} %collective-permute-done.mine_ref), channel_id=1, source_target_pairs={{0,2},{2,0},{4,6},{6,4},{8,10},{10,8},{12,14},{14,12},{16,18},{18,... | collective-permute-start | bytes 1179656 | tf_op jit(solution)/shard_map/ppermute | solution.py:768
  24.1 0.7 copy-start.13
  40.2 2.9 %copy-start.10 = (bf16[1152,512]{1,0:T(8,128)(2,1)}, bf16[1152,512]{1,0:T(8,128)(2,1)S(1)}, u32[]{:S(2)}) copy-start(bf16[1152,512]{1,0:T(8,128)(2,1)S(1)} %collective-permute-done.2.mine_far) | copy-start | bytes 3538948
  40.2 2.8 %collective-permute-start.3 = (bf16[1152,512]{1,0:T(8,128)(2,1)S(1)}, bf16[1152,512]{1,0:T(8,128)(2,1)S(1)}, u32[]{:S(2)}, u32[]{:S(2)}) collective-permute-start(bf16[1152,512]{1,0:T(8,128)(2,1)S(1)} %collective-permute-done.2.mine_far), channel_id=1, source_target_pairs={{0,2},{2,0},{4,6},{6,4},{8,10},{10,8},{12,14},{14,12},{16,18},{18,... | collective-permute-start | bytes 3538952 | tf_op jit(solution)/shard_map/ppermute | solution.py:768
  43.1 1.1 copy-start.11
  76.7 10.3 %collective-permute-start.4 = (bf16[2,1152,512]{2,1,0:T(8,128)(2,1)}, bf16[2,1152,512]{2,1,0:T(8,128)(2,1)S(1)}, u32[]{:S(2)}, u32[]{:S(2)}) collective-permute-start(bf16[2,1152,512]{2,1,0:T(8,128)(2,1)} %get-tuple-element.99), channel_id=1, source_target_pairs={{0,2},{2,0},{4,6},{6,4},{8,10},{10,8},{12,14},{14,12},{16,18},{18,... | collective-permute-start | bytes 7077896 | tf_op jit(solution)/shard_map/ppermute | solution.py:768
  88.5 0.9 copy-start.7
  88.9 16.0 %collective-permute-start.5 = (bf16[3,128,512]{2,1,0:T(8,128)(2,1)}, bf16[3,128,512]{2,1,0:T(8,128)(2,1)S(1)}, u32[]{:S(2)}, u32[]{:S(2)}) collective-permute-start(bf16[3,128,512]{2,1,0:T(8,128)(2,1)} %get-tuple-element.107), channel_id=1, source_target_pairs={{0,2},{2,0},{4,6},{6,4},{8,10},{10,8},{12,14},{14,12},{16,18},{18,... | collective-permute-start | bytes 1179656 | tf_op jit(solution)/shard_map/ppermute | solution.py:768
  89.4 16.6 %collective-permute-start.7 = (bf16[512,512]{1,0:T(8,128)(2,1)S(1)}, bf16[512,512]{1,0:T(8,128)(2,1)S(1)}, u32[]{:S(2)}, u32[]{:S(2)}) collective-permute-start(bf16[512,512]{1,0:T(8,128)(2,1)S(1)} %get-tuple-element.168), channel_id=1, source_target_pairs={{0,1},{1,0},{2,3},{3,2},{4,5},{5,4},{6,7},{7,6},{8,9},{9,8},{10,11... | collective-permute-start | bytes 1572872 | tf_op jit(solution)/shard_map/ppermute | solution.py:768
  91.1 20.7 %collective-permute-start.6 = (bf16[2,320,512]{2,1,0:T(8,128)(2,1)S(1)}, bf16[2,320,512]{2,1,0:T(8,128)(2,1)S(1)}, u32[]{:S(2)}, u32[]{:S(2)}) collective-permute-start(bf16[2,320,512]{2,1,0:T(8,128)(2,1)S(1)} %get-tuple-element.106), channel_id=1, source_target_pairs={{0,4},{2,6},{4,0},{6,2},{8,12},{10,14},{12,8},{14,10},{16,20},{18,... | collective-permute-start | bytes 1966088 | tf_op jit(solution)/shard_map/ppermute | solution.py:768
  106.2 16.5 %collective-permute-start.8 = (bf16[256,512]{1,0:T(8,128)(2,1)S(1)}, bf16[256,512]{1,0:T(8,128)(2,1)S(1)}, u32[]{:S(2)}, u32[]{:S(2)}) collective-permute-start(bf16[256,512]{1,0:T(8,128)(2,1)S(1)} %get-tuple-element.176), channel_id=1, source_target_pairs={{0,4},{2,6},{4,0},{6,2},{8,12},{10,14},{12,8},{14,10},{16,20},{18,... | collective-permute-start | bytes 786440 | tf_op jit(solution)/shard_map/ppermute | solution.py:768
  112.0 10.7 %collective-permute-start.9 = (bf16[320,512]{1,0:T(8,128)(2,1)S(1)}, bf16[320,512]{1,0:T(8,128)(2,1)S(1)}, u32[]{:S(2)}, u32[]{:S(2)}) collective-permute-start(bf16[320,512]{1,0:T(8,128)(2,1)S(1)} %get-tuple-element.117), channel_id=1, source_target_pairs={{0,1},{1,0},{2,3},{3,2},{4,5},{5,4},{6,7},{7,6},{8,9},{9,8},{10,11... | collective-permute-start | bytes 983048 | tf_op jit(solution)/shard_map/ppermute | solution.py:768
  112.6 20.6 %collective-permute-start.11 = (bf16[3,128,512]{2,1,0:T(8,128)(2,1)S(1)}, bf16[3,128,512]{2,1,0:T(8,128)(2,1)S(1)}, u32[]{:S(2)}, u32[]{:S(2)}) collective-permute-start(bf16[3,128,512]{2,1,0:T(8,128)(2,1)S(1)} %add_convert_fusion.4), channel_id=1, source_target_pairs={{0,1},{1,0},{2,3},{3,2},{4,5},{5,4},{6,7},{7,6},{8,9},{9,8},{10,11... | collective-permute-start | bytes 1179656 | tf_op jit(solution)/shard_map/ppermute | solution.py:768
  122.7 1.0 copy-start.12
  123.7 8.7 %copy-start.6 = (f32[512]{0:T(512)S(1)}, f32[512]{0:T(512)}, u32[]{:S(2)}) copy-start(f32[512]{0:T(512)} %param.28) | copy-start | bytes 6148
  123.7 9.5 %collective-permute-start.12 = (bf16[3,128,512]{2,1,0:T(8,128)(2,1)S(1)}, bf16[3,128,512]{2,1,0:T(8,128)(2,1)S(1)}, u32[]{:S(2)}, u32[]{:S(2)}) collective-permute-start(bf16[3,128,512]{2,1,0:T(8,128)(2,1)S(1)} %copy-done.12), channel_id=1, source_target_pairs={{0,2},{2,0},{4,6},{6,4},{8,10},{10,8},{12,14},{14,12},{16,18},{18,... | collective-permute-start | bytes 1179656 | tf_op jit(solution)/shard_map/ppermute | solution.py:768
  123.7 9.5 %collective-permute-start.10 = (bf16[288,512]{1,0:T(8,128)(2,1)S(1)}, bf16[288,512]{1,0:T(8,128)(2,1)S(1)}, u32[]{:S(2)}, u32[]{:S(2)}) collective-permute-start(bf16[288,512]{1,0:T(8,128)(2,1)S(1)} %add_convert_fusion.10), channel_id=1, source_target_pairs={{0,8},{2,10},{4,12},{6,14},{8,0},{10,2},{12,4},{14,6},{16,24},{18,... | collective-permute-start | bytes 884744 | tf_op jit(solution)/shard_map/ppermute | solution.py:768
  134.4 14.2 %collective-permute-start.13 = (bf16[3,64,512]{2,1,0:T(8,128)(2,1)S(1)}, bf16[3,64,512]{2,1,0:T(8,128)(2,1)S(1)}, u32[]{:S(2)}, u32[]{:S(2)}) collective-permute-start(bf16[3,64,512]{2,1,0:T(8,128)(2,1)S(1)} %get-tuple-element.174), channel_id=1, source_target_pairs={{0,4},{2,6},{4,0},{6,2},{8,12},{10,14},{12,8},{14,10},{16,20},{18,... | collective-permute-start | bytes 589832 | tf_op jit(solution)/shard_map/ppermute | solution.py:768
  138.4 16.5 %collective-permute-start.16 = (bf16[288,512]{1,0:T(8,128)(2,1)S(1)}, bf16[288,512]{1,0:T(8,128)(2,1)S(1)}, u32[]{:S(2)}, u32[]{:S(2)}) collective-permute-start(bf16[288,512]{1,0:T(8,128)(2,1)S(1)} %add_convert_fusion.8), channel_id=1, source_target_pairs={{0,16},{2,18},{4,20},{6,22},{8,24},{10,26},{12,28},{14,30},{16,0},... | collective-permute-start | bytes 884744 | tf_op jit(solution)/shard_map/ppermute | solution.py:768
  141.1 7.5 %collective-permute-start.14 = (f32[5,512]{1,0:T(8,128)S(1)}, f32[5,512]{1,0:T(8,128)S(1)}, u32[]{:S(2)}, u32[]{:S(2)}) collective-permute-start(f32[5,512]{1,0:T(8,128)S(1)} %pad_maximum_fusion.3), channel_id=1, source_target_pairs={{0,1},{1,0},{2,3},{3,2},{4,5},{5,4},{6,7},{7,6},{8,9},{9,8},{10,11... | collective-permute-start | bytes 30728 | tf_op jit(solution)/shard_map/ppermute | solution.py:768
  149.1 8.1 %collective-permute-start.15 = (bf16[112,512]{1,0:T(8,128)(2,1)S(1)}, bf16[112,512]{1,0:T(8,128)(2,1)S(1)}, u32[]{:S(2)}, u32[]{:S(2)}) collective-permute-start(bf16[112,512]{1,0:T(8,128)(2,1)S(1)} %concatenate.97), channel_id=1, source_target_pairs={{0,8},{2,10},{4,12},{6,14},{8,0},{10,2},{12,4},{14,6},{16,24},{18,... | collective-permute-start | bytes 344072 | tf_op jit(solution)/shard_map/ppermute | solution.py:768
  157.5 9.0 %collective-permute-start.18 = (bf16[288,512]{1,0:T(8,128)(2,1)S(1)}, bf16[288,512]{1,0:T(8,128)(2,1)S(1)}, u32[]{:S(2)}, u32[]{:S(2)}) collective-permute-start(bf16[288,512]{1,0:T(8,128)(2,1)S(1)} %add_convert_fusion.7), channel_id=1, source_target_pairs={{0,4},{2,6},{4,0},{6,2},{8,12},{10,14},{12,8},{14,10},{16,20},{18,... | collective-permute-start | bytes 884744 | tf_op jit(solution)/shard_map/ppermute | solution.py:768
  157.9 8.2 %collective-permute-start.17 = (bf16[112,512]{1,0:T(8,128)(2,1)S(1)}, bf16[112,512]{1,0:T(8,128)(2,1)S(1)}, u32[]{:S(2)}, u32[]{:S(2)}) collective-permute-start(bf16[112,512]{1,0:T(8,128)(2,1)S(1)} %concatenate.98), channel_id=1, source_target_pairs={{0,16},{2,18},{4,20},{6,22},{8,24},{10,26},{12,28},{14,30},{16,0},... | collective-permute-start | bytes 344072 | tf_op jit(solution)/shard_map/ppermute | solution.py:768
  166.7 10.5 %collective-permute-start.20 = (bf16[288,512]{1,0:T(8,128)(2,1)S(1)}, bf16[288,512]{1,0:T(8,128)(2,1)S(1)}, u32[]{:S(2)}, u32[]{:S(2)}) collective-permute-start(bf16[288,512]{1,0:T(8,128)(2,1)S(1)} %get-tuple-element.180), channel_id=1, source_target_pairs={{0,8},{2,10},{4,12},{6,14},{8,0},{10,2},{12,4},{14,6},{16,24},{18,... | collective-permute-start | bytes 884744 | tf_op jit(solution)/shard_map/ppermute | solution.py:768
  166.8 10.4 %collective-permute-start.19 = (bf16[3,32,512]{2,1,0:T(8,128)(2,1)S(1)}, bf16[3,32,512]{2,1,0:T(8,128)(2,1)S(1)}, u32[]{:S(2)}, u32[]{:S(2)}) collective-permute-start(bf16[3,32,512]{2,1,0:T(8,128)(2,1)S(1)} %fusion.7), channel_id=1, source_target_pairs={{0,8},{2,10},{4,12},{6,14},{8,0},{10,2},{12,4},{14,6},{16,24},{18,... | collective-permute-start | bytes 294920 | tf_op jit(solution)/shard_map/ppermute | solution.py:768
  177.5 7.4 %collective-permute-start.22 = (bf16[288,512]{1,0:T(8,128)(2,1)S(1)}, bf16[288,512]{1,0:T(8,128)(2,1)S(1)}, u32[]{:S(2)}, u32[]{:S(2)}) collective-permute-start(bf16[288,512]{1,0:T(8,128)(2,1)S(1)} %get-tuple-element.149), channel_id=1, source_target_pairs={{0,8},{2,10},{4,12},{6,14},{8,0},{10,2},{12,4},{14,6},{16,24},{18,... | collective-permute-start | bytes 884744 | tf_op jit(solution)/shard_map/ppermute | solution.py:768
  177.8 6.1 %collective-permute-start.21 = (bf16[208,512]{1,0:T(8,128)(2,1)S(1)}, bf16[208,512]{1,0:T(8,128)(2,1)S(1)}, u32[]{:S(2)}, u32[]{:S(2)}) collective-permute-start(bf16[208,512]{1,0:T(8,128)(2,1)S(1)} %concatenate.106), channel_id=1, source_target_pairs={{0,4},{2,6},{4,0},{6,2},{8,12},{10,14},{12,8},{14,10},{16,20},{18,... | collective-permute-start | bytes 638984 | tf_op jit(solution)/shard_map/ppermute | solution.py:768
  185.1 0.8 copy-start.1
  185.5 6.5 %copy-start = (bf16[2,576,512]{2,1,0:T(8,128)(2,1)}, bf16[2,576,512]{2,1,0:T(8,128)(2,1)S(1)}, u32[]{:S(2)}) copy-start(bf16[2,576,512]{2,1,0:T(8,128)(2,1)S(1)} %pad_maximum_fusion.1.ffn_mine) | copy-start | bytes 3538948
  186.1 5.8 %collective-permute-start.23 = (bf16[2,576,512]{2,1,0:T(8,128)(2,1)S(1)}, bf16[2,576,512]{2,1,0:T(8,128)(2,1)S(1)}, u32[]{:S(2)}, u32[]{:S(2)}) collective-permute-start(bf16[2,576,512]{2,1,0:T(8,128)(2,1)S(1)} %pad_maximum_fusion.1.ffn_mine), channel_id=1, source_target_pairs={{0,2},{2,0},{4,6},{6,4},{8,10},{10,8},{12,14},{14,12},{16,18},{18,... | collective-permute-start | bytes 3538952 | tf_op jit(solution)/shard_map/ppermute | solution.py:768
  186.2 3.4 %collective-permute-start.24 = (bf16[400,512]{1,0:T(8,128)(2,1)S(1)}, bf16[400,512]{1,0:T(8,128)(2,1)S(1)}, u32[]{:S(2)}, u32[]{:S(2)}) collective-permute-start(bf16[400,512]{1,0:T(8,128)(2,1)S(1)} %concatenate.113), channel_id=1, source_target_pairs={{0,2},{2,0},{4,6},{6,4},{8,10},{10,8},{12,14},{14,12},{16,18},{18,... | collective-permute-start | bytes 1228808 | tf_op jit(solution)/shard_map/ppermute | solution.py:768
  189.6 2.3 %copy-start.3 = (bf16[400,512]{1,0:T(8,128)(2,1)}, bf16[400,512]{1,0:T(8,128)(2,1)S(1)}, u32[]{:S(2)}) copy-start(bf16[400,512]{1,0:T(8,128)(2,1)S(1)} %collective-permute-done.24.attn_sibling) | copy-start | bytes 1228804
  191.9 1.0 copy-start.2

commit v2 on v1

--- a/solution.py
+++ b/solution.py
@@ -11,11 +11,14 @@
 PAIR = 2 * HEAD
 QROWS = 256
 TILE = 256
+GROUP = 64
 
 EPS = 1e-05
 BF16 = jnp.bfloat16
 F32 = jnp.float32
 VMEM_LIMIT = 56 * 1024 * 1024
+MIDDLE_VMEM = 56 * 1024 * 1024
+FINISH_VMEM = 24 * 1024 * 1024
 
 
 def dot(left, right, left_dim=1, right_dim=0):
@@ -45,35 +48,34 @@
 
 
 def attend(qkv_ref, p_ref, ctx_ref, length, with_memory):
-    mem_keys = pl.ds(length, length)
     values = [only_head(qkv_ref[0, 0, pl.ds(3 * length, 2 * length), :], head) for head in range(2)]
+    low = 0 if with_memory else length
     for first in range(0, length, QROWS):
         rows = pl.ds(first, QROWS)
-        seen = first + QROWS
+        high = length + first + QROWS
         total = None
         for head in range(2):
             query = only_head(qkv_ref[0, 0, rows, :], head)
-            seg = dot(query, qkv_ref[0, 0, pl.ds(2 * length, seen), :], 1, 1)
-            at = lax.broadcasted_iota(jnp.int32, (QROWS, seen), 0) + first
-            key = lax.broadcasted_iota(jnp.int32, (QROWS, seen), 1)
+            scores = dot(query, qkv_ref[0, 0, pl.ds(length + low, high - low), :], 1, 1)
+            seg = scores[:, length - low :]
+            at = lax.broadcasted_iota(jnp.int32, seg.shape, 0) + first
+            key = lax.broadcasted_iota(jnp.int32, seg.shape, 1)
             seg = jnp.where(key <= at, seg, -1e30)
             top = jnp.max(seg, -1, keepdims=True)
             if with_memory:
-                mem = dot(query, qkv_ref[0, 0, mem_keys, :], 1, 1)
+                mem = scores[:, :length]
                 top = jnp.maximum(top, jnp.max(mem, -1, keepdims=True))
                 mem = jnp.exp(mem - top)
-            seg = jnp.exp(seg - top)
-            mass = jnp.sum(seg, -1, keepdims=True)
+            probs = jnp.exp(seg - top)
+            mass = jnp.sum(probs, -1, keepdims=True)
             if with_memory:
                 mass = mass + jnp.sum(mem, -1, keepdims=True)
             part = 1.0 / mass
-            seg = (seg * part).astype(BF16)
-            p_ref[0, 0, head, rows, pl.ds(length, seen)] = seg
-            add = dot(seg, values[head][length : length + seen])
+            probs = (probs * part).astype(BF16)
             if with_memory:
-                mem = (mem * part).astype(BF16)
-                p_ref[0, 0, head, rows, pl.ds(0, length)] = mem
-                add = add + dot(mem, values[head][:length])
+                probs = jnp.concatenate([(mem * part).astype(BF16), probs], 1)
+            p_ref[0, 0, head, rows, pl.ds(low, high - low)] = probs
+            add = dot(probs, values[head][low:high])
             total = add if total is None else total + add
         ctx_ref[0, rows, :] = total.astype(BF16)
 
@@ -213,12 +215,15 @@
     grad_hidden_ref,
     gctx_own_ref,
     gctx_oth_ref,
-    sent_far,
-    kept_far,
+    sent_up_far,
+    sent_down_far,
+    kept_up_far,
+    kept_down_far,
     sums_ref,
     e_ref,
     hist_ref,
     edge_ref,
+    pick_ref,
     up_ref,
     down_ref,
     out_ref,
@@ -260,6 +265,10 @@
             copy.start()
         sums_ref[...] = jnp.zeros_like(sums_ref)
         hist_ref[...] = jnp.zeros_like(hist_ref)
+        row = lax.broadcasted_iota(jnp.int32, pick_ref.shape, 0)
+        column = lax.broadcasted_iota(jnp.int32, pick_ref.shape, 1)
+        from_row = NEIGH * (row % GROUP) + row // GROUP
+        pick_ref[...] = (column == from_row).astype(F32).astype(BF16)
         edges = edges_ref[...].astype(F32)
         for i in range(2):
             edge_ref[i] = jnp.broadcast_to(edges[:, i : i + BINS], (BINS, BINS)).T
@@ -282,11 +291,14 @@
             + dot(ctx_own_ref[0], out_ref[...])
             + dot(ctx_oth_ref[0], other_out())
         )
-        affinity = []
-        for k in range(NEIGH):
-            e = nb_ref[0, :, k, :].astype(F32)
-            e_ref[k] = e
-            affinity.append(jnp.sum(e * hidden, -1, keepdims=True) * scale)
+        for first in range(0, TILE, GROUP):
+            mixed_rows = nb_ref[0, pl.ds(first, GROUP)].reshape(NEIGH * GROUP, width)
+            planes = dot(pick_ref[...], mixed_rows)
+            for k in range(NEIGH):
+                e_ref[k, pl.ds(first, GROUP), :] = planes[k * GROUP : (k + 1) * GROUP]
+        affinity = [
+            jnp.sum(e_ref[k] * hidden, -1, keepdims=True) * scale for k in range(NEIGH)
+        ]
         top = jnp.maximum(
             jnp.maximum(affinity[0], affinity[1]), jnp.maximum(affinity[2], affinity[3])
         )
@@ -377,20 +389,31 @@
     @pl.when(step == pl.num_programs(0) - 1)
     def _():
         sums_ref[pl.ds(3, 1), pl.ds(0, BINS)] = jnp.sum(hist_ref[...].T, 0, keepdims=True)
+        cut = sent_up_far.shape[1]
         moves = []
-        for far, which in ((sent_far, 1 - core), (kept_far, core)):
+        for fars, which in (
+            ((sent_up_far, sent_down_far), 1 - core),
+            ((kept_up_far, kept_down_far), core),
+        ):
             for side in range(2):
                 at = pl.ds(pl.multiple_of((side * chunks + which) * width, width), width)
                 here = pl.ds(pl.multiple_of((2 * side + which) * PAIR, PAIR), PAIR)
-                for to, left, right in (
-                    (pl.ds(0, width), ffn_in_ref[...], gpre_ref[:, at]),
-                    (pl.ds(width, width), act_ref[:, at], cots_ref[...]),
-                    (pl.ds(2 * width, PAIR), ctx_ref[:, here], low_ref[...]),
+                slot = len(moves) // 2
+                first = 0
+                for left, right in (
+                    (ffn_in_ref[...], gpre_ref[:, at]),
+                    (act_ref[:, at], cots_ref[...]),
+                    (ctx_ref[:, here], low_ref[...]),
                 ):
-                    slot = len(moves)
-                    stage = stage_ref.at[slot // 3, to, :]
-                    stage[...] = dot(left, right, 0, 0).astype(BF16)
-                    move = pltpu.make_async_copy(stage, far.at[side, to, :], out_sems.at[slot])
+                    piece = dot(left, right, 0, 0).astype(BF16)
+                    stage_ref[slot, pl.ds(first, piece.shape[0]), :] = piece
+                    first += piece.shape[0]
+                for i, far in enumerate(fars):
+                    move = pltpu.make_async_copy(
+                        stage_ref.at[slot, pl.ds(i * cut, cut), :],
+                        far.at[side],
+                        out_sems.at[len(moves)],
+                    )
                     move.start()
                     moves.append(move)
         for move in moves:
@@ -438,12 +461,15 @@
                 tiled(width // 2),
                 far,
                 far,
+                far,
+                far,
                 whole((8, width)),
             ],
             scratch_shapes=[
                 pltpu.VMEM((NEIGH, TILE, width), F32),
                 pltpu.VMEM((BINS, TILE), F32),
                 pltpu.VMEM((2, BINS, BINS), F32),
+                pltpu.VMEM((NEIGH * GROUP, NEIGH * GROUP), BF16),
                 *[pltpu.VMEM(w.shape, BF16) for w in weights],
                 pltpu.VMEM((2, *received[0].shape), BF16),
                 pltpu.VMEM((4, 2 * width + PAIR, width), BF16),
@@ -454,18 +480,17 @@
                 pltpu.VMEM((count, width), BF16),
                 pltpu.VMEM((count, width), BF16),
                 pltpu.SemaphoreType.DMA((5,)),
-                pltpu.SemaphoreType.DMA((12,)),
+                pltpu.SemaphoreType.DMA((8,)),
             ],
         out_shape=[
             jax.ShapeDtypeStruct((rows, length, width), BF16),
             jax.ShapeDtypeStruct((rows, length, width), F32),
             jax.ShapeDtypeStruct((rows, length, width // 2), BF16),
             jax.ShapeDtypeStruct((rows, length, width // 2), BF16),
-            jax.ShapeDtypeStruct((2, 2 * width + PAIR, width), BF16),
-            jax.ShapeDtypeStruct((2, 2 * width + PAIR, width), BF16),
+            *[jax.ShapeDtypeStruct((2, width + PAIR // 2, width), BF16)] * 4,
             jax.ShapeDtypeStruct((8, width), F32),
         ],
-        compiler_params=pltpu.CompilerParams(vmem_limit_bytes=VMEM_LIMIT),
+        compiler_params=pltpu.CompilerParams(vmem_limit_bytes=MIDDLE_VMEM),
         cost_estimate=pl.CostEstimate(flops=15 * 10**9, bytes_accessed=30 * 2**20, transcendentals=0),
     )(tokens, ctx_own, ctx_oth, nb, ids, cot, *weights, *received, edges, gains)
 
@@ -478,30 +503,26 @@
     delta = jnp.sum(grad.astype(F32) * ctx_ref[0].astype(F32), -1, keepdims=True)
     keys = only_head(qkv_ref[0, 0, pl.ds(length, 2 * length), :], head)
     lanes = pl.ds(pl.multiple_of(head * HEAD, HEAD), HEAD)
+    low = 0 if with_memory else length
     for first in range(0, length, QROWS):
         rows = pl.ds(first, QROWS)
-        seen = first + QROWS
-        spans = [(length, seen)] + ([(0, length)] if with_memory else [])
-        total = dq_ref[rows, :]
-        for at, span in spans:
-            here = pl.ds(at, span)
-            probs = p_ref[0, 0, 0, rows, here].astype(F32)
-            values = qkv_ref[0, 0, pl.ds(3 * length + at, span), :]
-            grad_probs = dot(grad[first : first + QROWS], values, 1, 1)
-            ds = (probs * (grad_probs - delta[first : first + QROWS])).astype(BF16)
-            ds_ref[rows, here] = ds
-            total = total + dot(ds, keys[at : at + span])
-        dq_ref[rows, :] = total
+        high = length + first + QROWS
+        here = pl.ds(low, high - low)
+        probs = p_ref[0, 0, 0, rows, here].astype(F32)
+        values = qkv_ref[0, 0, pl.ds(3 * length + low, high - low), :]
+        grad_probs = dot(grad[first : first + QROWS], values, 1, 1)
+        ds = (probs * (grad_probs - delta[first : first + QROWS])).astype(BF16)
+        ds_ref[rows, here] = ds
+        dq_ref[rows, :] += dot(ds, keys[low:high])
     for out_ref, left, right in (
         (dk_ref, t_ref[0, lanes, :], ds_ref),
         (dv_ref, t_ref[1, lanes, :], p_ref.at[0, 0, 0]),
     ):
-        if with_memory:
-            out_ref[lanes, :length] = dot(left, right[:, :length]).astype(BF16)
-        else:
+        if not with_memory:
             out_ref[lanes, :length] = jnp.zeros((HEAD, length), BF16)
         for first in range(0, length, QROWS):
-            here = pl.ds(length + first, QROWS)
+            start = low if first == 0 else length + first
+            here = pl.ds(start, length + first + QROWS - start)
             out_ref[lanes, here] = dot(
                 left[:, first:], right[pl.ds(first, length - first), here]
             ).astype(BF16)
@@ -528,9 +549,9 @@
     sem,
 ):
     length = ctx_ref.shape[1]
-    row = pl.program_id(0)
-    head = pl.program_id(1)
-    start = starts_ref[lax.axis_index("mp") * pl.num_programs(0) + row]
+    row = pl.program_id(1)
+    head = pl.program_id(2)
+    start = starts_ref[lax.axis_index("mp") * pl.num_programs(1) + row]
     fetch = pltpu.make_async_copy(kv_far.at[row], kv_ref, sem)
     args = (qkv_ref, p_ref, gctx_ref, ctx_ref, ds_ref, dq_ref, t_ref, dk_ref, dv_ref)
 
@@ -552,9 +573,9 @@
     @pl.when(head == 1)
     def _():
         dq_t = (dq_ref[...] * HEAD ** (-0.5)).astype(BF16).T
-        grads_ref[0, pl.ds(0, PAIR), :] = dq_t
-        grads_ref[0, pl.ds(PAIR, PAIR), :] = dk_ref[:, length:]
-        grads_ref[0, pl.ds(2 * PAIR, PAIR), :] = dv_ref[:, length:]
+        grads_ref[0, 0, pl.ds(0, PAIR), :] = dq_t
+        grads_ref[0, 0, pl.ds(PAIR, PAIR), :] = dk_ref[:, length:]
+        grads_ref[0, 0, pl.ds(2 * PAIR, PAIR), :] = dv_ref[:, length:]
         fetch.wait()
         for i, add in enumerate(
             (
@@ -565,42 +586,42 @@
         ):
             acc_ref[i] = jnp.where(row == 0, add, acc_ref[i] + add)
 
-    @pl.when((head == 1) & (row == pl.num_programs(0) - 1))
+    @pl.when((head == 1) & (row == pl.num_programs(1) - 1))
     def _():
         part = None
         for i in range(3):
             total = acc_ref[i]
-            dw_ref[i] = total.astype(BF16)
+            dw_ref[0, i] = total.astype(BF16)
             weight = pack_ref[:, pl.ds(i * PAIR, PAIR)].T.astype(F32)
             add = jnp.sum(total * weight, 0, keepdims=True)
             part = add if part is None else part + add
-        gain_ref[...] = jnp.broadcast_to(part, gain_ref.shape)
-
-
-def attention_backward(starts, saved, gctx, kv, sibling):
+        gain_ref[0] = jnp.broadcast_to(part, gain_ref.shape[1:])
+
+
+def attention_backward(starts, saved, gctx, kv, shift, many):
     pack, qkv, p, ctx = saved
     rows, _, _, length, _ = p.shape
     width = kv.shape[-1]
 
-    def pair():
-        return 1 - core_index() if sibling else core_index()
+    def pair(n):
+        return lax.rem(core_index() + shift + n, 2)
 
     return pl.pallas_call(
         backward_body,
-        grid=(rows, 2),
+        grid=(many, rows, 2),
         in_specs=[
             pl.BlockSpec(memory_space=pltpu.SMEM),
-            pl.BlockSpec((1, 1, 5 * length, PAIR), lambda r, h: (r, pair(), 0, 0)),
-            pl.BlockSpec((1, 1, 1, length, 2 * length), lambda r, h: (r, pair(), h, 0, 0)),
-            pl.BlockSpec((1, length, PAIR), lambda r, h: (r, 0, pair())),
-            pl.BlockSpec((1, length, PAIR), lambda r, h: (r, 0, pair())),
+            pl.BlockSpec((1, 1, 5 * length, PAIR), lambda n, r, h: (r, pair(n), 0, 0)),
+            pl.BlockSpec((1, 1, 1, length, 2 * length), lambda n, r, h: (r, pair(n), h, 0, 0)),
+            pl.BlockSpec((1, length, PAIR), lambda n, r, h: (r, 0, pair(n))),
+            pl.BlockSpec((1, length, PAIR), lambda n, r, h: (r, 0, pair(n))),
             pl.BlockSpec(memory_space=pl.ANY),
-            pl.BlockSpec((width, 3 * PAIR), lambda r, h: (0, pair())),
+            pl.BlockSpec((width, 3 * PAIR), lambda n, r, h: (0, pair(n))),
         ],
         out_specs=[
-            pl.BlockSpec((1, 3 * PAIR, length), lambda r, h: (r, 0, 0)),
-            pl.BlockSpec((3, PAIR, width), lambda r, h: (0, 0, 0)),
-            pl.BlockSpec((8, width), lambda r, h: (0, 0)),
+            pl.BlockSpec((1, 1, 3 * PAIR, length), lambda n, r, h: (n, r, 0, 0)),
+            pl.BlockSpec((1, 3, PAIR, width), lambda n, r, h: (n, 0, 0, 0)),
+            pl.BlockSpec((1, 8, width), lambda n, r, h: (n, 0, 0)),
         ],
         scratch_shapes=[
             pltpu.VMEM((length, 2 * length), BF16),
@@ -613,12 +634,14 @@
             pltpu.SemaphoreType.DMA,
         ],
         out_shape=[
-            jax.ShapeDtypeStruct((rows, 3 * PAIR, length), BF16),
-            jax.ShapeDtypeStruct((3, PAIR, width), BF16),
-            jax.ShapeDtypeStruct((8, width), F32),
+            jax.ShapeDtypeStruct((many, rows, 3 * PAIR, length), BF16),
+            jax.ShapeDtypeStruct((many, 3, PAIR, width), BF16),
+            jax.ShapeDtypeStruct((many, 8, width), F32),
         ],
         compiler_params=pltpu.CompilerParams(vmem_limit_bytes=VMEM_LIMIT),
-        cost_estimate=pl.CostEstimate(flops=4 * 10**9, bytes_accessed=8 * 2**20, transcendentals=0),
+        cost_estimate=pl.CostEstimate(
+            flops=4 * 10**9 * many, bytes_accessed=8 * 2**20 * many, transcendentals=0
+        ),
     )(starts, qkv, p, gctx, ctx, kv, pack)
 
 
@@ -626,8 +649,7 @@
     tok_ref,
     grad_hidden_ref,
     gain_ref,
-    oth_first_ref,
-    oth_last_ref,
+    oth_ref,
     own_first_ref,
     own_last_ref,
     oth_pack_ref,
@@ -637,13 +659,13 @@
     core = core_index()
     total = None
     for block, pack, which in (
-        (oth_first_ref, oth_pack_ref, 1 - core),
-        (oth_last_ref, oth_pack_ref, core),
-        (own_first_ref, own_pack_ref, 1 - core),
-        (own_last_ref, own_pack_ref, core),
+        (oth_ref[0, 0], oth_pack_ref, 1 - core),
+        (oth_ref[1, 0], oth_pack_ref, core),
+        (own_first_ref[0, 0], own_pack_ref, 1 - core),
+        (own_last_ref[0, 0], own_pack_ref, core),
     ):
         here = pl.ds(pl.multiple_of(which * 3 * PAIR, 3 * PAIR), 3 * PAIR)
-        add = dot(block[0], pack[:, here], 0, 1)
+        add = dot(block, pack[:, here], 0, 1)
         total = add if total is None else total + add
     normal, rstd = normalize(tok_ref[0].astype(F32))
     grad = total * gain_ref[...]
@@ -672,7 +694,7 @@
             row,
             row,
             whole(gain),
-            *[pl.BlockSpec((1,) + g.shape[1:], lambda r: (r, 0, 0)) for g in grads],
+            *[pl.BlockSpec((g.shape[0], 1) + g.shape[2:], lambda r: (0, r, 0, 0)) for g in grads],
             *[whole(p) for p in packs],
         ],
         out_specs=row,
@@ -703,7 +725,6 @@
 ):
     core = core_index()
     width = up_far.shape[0]
-    half = width // 2
     rows = attn_mine.shape[1]
     moves = []
 
@@ -717,23 +738,17 @@
         moves.append(pltpu.make_async_copy(near, far, sems.at[len(moves)]))
         moves[-1].start()
 
-    for x in range(2):
-        to = pl.ds(x * half, half)
-        for which, part in enumerate(
-            pair(ffn_mine[x, pl.ds(0, half), :], ffn_sibling[x, pl.ds(0, half), :])
-        ):
-            up_ref[to, pl.ds(which * width, width)] = part
-        move(up_ref.at[to, :], up_far.at[to, :])
-    size = half + PAIR // 2
-    for which, low in enumerate(
-        zip(*(pair(ffn_mine[x, pl.ds(half, size), :], ffn_sibling[x, pl.ds(half, size), :]) for x in range(2)))
-    ):
-        first, last = low
+    size = ffn_mine.shape[1] // 2
+    pieces = [(x, pl.ds(y * size, size)) for y in range(2) for x in range(2)]
+    halves = zip(*(pair(ffn_mine[x, y, :], ffn_sibling[x, y, :]) for x, y in pieces))
+    for which, parts in enumerate(halves):
+        rows_of = jnp.concatenate(parts, 0)
         to = pl.ds(which * width, width)
-        down_ref[pl.ds(which * width, size), :] = first
-        down_ref[pl.ds(which * width + size, width - size), :] = last[: width - size]
-        out_ref[pl.ds(which * PAIR, PAIR), :] = last[width - size :]
+        up_ref[:, to] = rows_of[:width]
+        down_ref[to, :] = rows_of[width : 2 * width]
+        out_ref[pl.ds(which * PAIR, PAIR), :] = rows_of[2 * width :]
         move(down_ref.at[to, :], down_far.at[to, :])
+    move(up_ref, up_far)
     move(out_ref, out_far)
     for i, (near, far) in enumerate(((q_ref, q_far), (k_ref, k_far), (v_ref, v_far))):
         first, last = pair(attn_mine[i], attn_sibling[pl.ds(i * rows, rows), :])
@@ -759,7 +774,7 @@
         out_specs=[pl.BlockSpec(memory_space=pl.ANY)] * 6,
         scratch_shapes=[pltpu.VMEM(s, F32) for s in shapes] + [pltpu.SemaphoreType.DMA((8,))],
         out_shape=[jax.ShapeDtypeStruct(s, F32) for s in shapes],
-        compiler_params=pltpu.CompilerParams(vmem_limit_bytes=VMEM_LIMIT),
+        compiler_params=pltpu.CompilerParams(vmem_limit_bytes=FINISH_VMEM),
     )(*ffn, *attn)
 
 
@@ -786,6 +801,17 @@
         bit_of("dp", bit) == 0,
         lax.concatenate([mine, other], dim),
         lax.concatenate([other, mine], dim),
+    )
+
+
+def swap_diagonal(array, first, last):
+    size = lax.axis_size("dp")
+    return lax.ppermute(array, "dp", [(i, i ^ first ^ last) for i in range(size)])
+
+
+def join_four(mine, by_first, by_last, by_both, first, last):
+    return join(
+        join(mine, by_last, last, 0)[None], join(by_first, by_both, last, 0)[None], first, 0
     )
 
 
@@ -915,8 +941,10 @@
         grad_hidden,
         gctx_own,
         gctx_oth,
-        ffn_first,
-        ffn_last,
+        sent_up,
+        sent_down,
+        kept_up,
+        kept_down,
         sums,
     ) = middle_layer(
         tokens,
@@ -930,58 +958,56 @@
         edges,
         gains,
     )
-    ffn = Chain(None, 1)
-    sent = ffn.pass_on(ffn_first, ffn_last, 1)
-    g_oth_first, da_first, gain_1 = attention_backward(
-        doc_starts, oth, after(gctx_oth, sent), kv, True
-    )
-    ffn.add(da_first)
     up = Chain(None, 1)
-    up.pieces = tuple(p[:, :width] for p in ffn.pieces)
     down = Chain(None, 1)
-    down.pieces = tuple(p[:, width:] for p in ffn.pieces)
+    up.pass_on(sent_up, kept_up, 1)
+    down.pass_on(sent_down, kept_down, 1)
+    up.add()
+    down.add()
     sent = up.give(1)
     sent = down.halve(far[0], sent)
-    attn = Chain(None, 1)
-    sent = attn.pass_on(da_first, None, 1, sent)
-    g_oth_last, da_last, gain_2 = attention_backward(
-        doc_starts, oth, after(gctx_oth, sent), kv, False
-    )
-    attn.come = after(attn.come, da_last)
-    up.add(da_last)
-    down.add(da_last)
+    g_oth, da, gain_oth = attention_backward(
+        doc_starts, oth, after(gctx_oth, sent), kv, 1, 2
+    )
+    up.add(da)
+    down.add(da)
     sent = up.halve(far[0])
     sent = down.give(1, sent)
-    attn_sent = after(add_low(da_last, attn.come), sent)
-    attn_come = swap(attn_sent, "mp", 1)
-    g_own_first, da_first, gain_3 = attention_backward(
-        doc_starts, own, after(gctx_own, attn_sent), kv, True
-    )
+    attn = Chain(None, 1)
+    sent = attn.pass_on(da[0], da[1], 1, sent)
+    g_own_first, da_first, gain_first = attention_backward(
+        doc_starts, own, after(gctx_own, sent), kv, 1, 1
+    )
+    da_first = da_first[0]
+    attn.add(da_first)
     up.add(da_first)
     down.add(da_first)
     both = Chain(None, 0)
     both.pieces = tuple(lax.concatenate([u, d], 0) for u, d in zip(up.pieces, down.pieces))
     sent = both.halve(far[1])
-    first_sent = after(da_first, sent)
+    attn_sent = after(attn.total(), sent)
+    attn_come = swap(attn_sent, "mp", 1)
+    first_sent = after(da_first, attn_sent)
     first_come = swap(first_sent, "dp", 1)
-    g_own_last, da_last, gain_4 = attention_backward(
-        doc_starts, own, after(gctx_own, first_sent), kv, False
-    )
+    g_own_last, da_last, gain_last = attention_backward(
+        doc_starts, own, after(gctx_own, first_sent), kv, 0, 1
+    )
+    da_last = da_last[0]
     attn_come, first_come = lax.optimization_barrier((attn_come, first_come, da_last))[:2]
     attn = Chain(None, 1)
     attn.pieces = (da_last, first_come, attn_come)
     both.add(da_last)
-    gain_part = (gain_1[:1] + gain_2[:1] + gain_3[:1] + gain_4[:1]) / attn_gain
+    gain_part = sum(g[:, 0].sum(0) for g in (gain_oth, gain_first, gain_last))[None] / attn_gain
     small = lax.concatenate([sums[:4], gain_part], 0)
-    sent = attn.halve(far[0])
-    sent = both.send(far[2], sent)
+    sent = both.send(far[2])
+    sent = attn.halve(far[0], sent)
     small_sent = after(small, sent)
     small_come = swap(small_sent, "mp", 1)
     grad_input = input_grad(
         tokens,
         after(grad_hidden, small_sent),
         attn_gain,
-        (g_oth_first, g_oth_last, g_own_first, g_own_last),
+        (g_oth, g_own_first, g_own_last),
         (oth[0], own[0]),
     )
     attn.come, small_come = lax.optimization_barrier((attn.come, small_come, grad_input))[:2]
@@ -991,35 +1017,41 @@
     mine = bit_of("dp", far[1])
     part = attn.total(lambda p: part_of(p, 1 - mine, 1))
     kept = attn.total(lambda p: part_of(p, mine, 1))
-    come = swap(ride.below(part), "dp", far[1])
+    come = swap(part, "dp", far[1])
     come, both.come = lax.optimization_barrier((come, both.come))
-    total = add_low(kept, ride.add(come, kept))
+    total = add_low(kept, come)
     ffn_total = add_low(both.sent, both.come)
     for bit in far[3:]:
         ffn_total = add_low(ffn_total, swap(ffn_total, "dp", bit))
+    ffn_sent = ffn_total
     for bit in far[2:]:
         sent = ride.below(total)
         come = swap(sent, "dp", bit)
         if bit == far[2]:
             ffn_sent = after(ffn_total, sent)
-            ffn_come = swap(ffn_sent, "dp", far[0])
-            come, ffn_come = lax.optimization_barrier((come, ffn_come))
+            ffn_x = swap(ffn_sent, "dp", far[0])
+            ffn_z = swap(ffn_sent, "dp", far[1])
+            come, ffn_x, ffn_z = lax.optimization_barrier((come, ffn_x, ffn_z))
         total = add_low(total, ride.add(come, total))
-    come = swap(total, "dp", far[1])
-    ffn_halves = after(join(ffn_sent[None], ffn_come[None], far[0], 0), total)
-    ffn_come = swap(ffn_halves[0], "dp", far[1])
-    come, ffn_come = lax.optimization_barrier((come, ffn_come))
-    ffn_first = join(ffn_halves[0], ffn_come, far[1], 0)
-    total = join(total, come, far[1], 1)
     sent = ride.below(total)
-    come = swap(sent, "dp", far[0])
-    ffn_come = swap(after(ffn_halves[1], sent), "dp", far[1])
-    come, ffn_come = lax.optimization_barrier((come, ffn_come))
-    total = join(total, ride.add(come, total), far[0], 1)
+    come_x = swap(sent, "dp", far[0])
+    come_z = swap(sent, "dp", far[1])
+    come_d = swap_diagonal(sent, far[0], far[1])
+    ffn_d = swap_diagonal(after(ffn_sent, sent), far[0], far[1])
+    come_x, come_z, come_d, ffn_d = lax.optimization_barrier((come_x, come_z, come_d, ffn_d))
+    flat = total.reshape(-1, width)
+    parts = [ride.add(come, flat) for come in (come_x, come_z, come_d)]
+    shape = total.shape
+    total = join_four(
+        flat.reshape(shape).swapaxes(0, 1),
+        *[part.reshape(shape).swapaxes(0, 1) for part in parts],
+        far[0],
+        far[1],
+    )
+    total = total.reshape(-1, *shape[:1], width).swapaxes(0, 1)
     sent = ride.below(total)
     come = swap(sent, "dp", 1)
-    ffn_last = join(ffn_halves[1], ffn_come, far[1], 0)
-    ffn_total = after(lax.concatenate([ffn_first[None], ffn_last[None]], 0), sent)
+    ffn_total = after(join_four(ffn_sent, ffn_x, ffn_z, ffn_d, far[0], far[1]), sent)
     ffn_come = swap(ffn_total, "dp", 1)
     ride.add(come, total)
     small = ride.rows

time: 200 us -> 181 us (0.905)
  Pallas kernels: 107 us -> 95.6 us
  waiting for transfers between devices: 40.3 us -> 36.8 us
    ppermute x25, starting transfers between devices: 29.9 us -> 24.2 us  [swap(): return lax.ppermute(array, axis, [(i, i ^ bit) for i in range(size)])]
    ppermute x0 -> x2, starting transfers between devices: none -> 5.15 us  [swap_diagonal(): lax.ppermute(array, 'dp', [(i, i ^ first ^ last) for i in range(size)])]
    pallas_call x4 -> x3, Pallas kernels: 34.3 us -> 29.5 us  [attention_backward(): pl.pallas_call(backward_body, grid=(many, rows, 2), in_specs=[pl.BlockSpe...]
    ppermute x25, waiting for transfers between devices: 40.3 us -> 35.5 us  [swap(): return lax.ppermute(array, axis, [(i, i ^ bit) for i in range(size)])]
    pallas_call x1, Pallas kernels: 32.5 us -> 29.9 us  [middle_layer(): pl.pallas_call(middle_body, grid=(tiles,), in_specs=[tiled(width), tiled(...]
    convert_element_type x8 -> x9, other arithmetic: 4.2 us -> 3.51 us  [total(): return sum((piece.astype(F32) for piece in pieces)).astype(BF16)]
  transfers between devices with their start and end apart: 25 -> 27, of which waited for: 12 -> 12; matrix products, arithmetic and copies ran while one was open for 4% -> 6% of each run, Pallas kernels for 35% -> 35%
where the time goes in v2:
time: 181 us; the launch traced here: 180 us
  Pallas kernels  95.6 us (53%)
  waiting for transfers between devices  36.8 us (20%)
  starting transfers between devices  29.3 us (16%)
  local copies, waits for them, and re-layouts  9 us (5%)
  other arithmetic  6.59 us (4%)
  between operations  2.96 us (2%)
    ppermute x25, waiting for transfers between devices, swap(): return lax.ppermute(array, axis, [(i, i ^ bit) for i in range(size)])  35.5 us
    pallas_call x1, Pallas kernels, middle_layer(): pl.pallas_call(middle_body, grid=(tiles,), in_specs=[tiled(width), tiled(...  29.9 us
    pallas_call x3, Pallas kernels, attention_backward(): pl.pallas_call(backward_body, grid=(many, rows, 2), in_specs=[pl.BlockSpe...  29.5 us
    pallas_call x2, Pallas kernels, attention_forward(): pl.pallas_call(body, grid=(rows, pairs), in_specs=in_specs, out_specs=out...  26.7 us
    ppermute x25, starting transfers between devices, swap(): return lax.ppermute(array, axis, [(i, i ^ bit) for i in range(size)])  24.2 us
    pallas_call x1, Pallas kernels, input_grad(): pl.pallas_call(input_body, grid=(rows,), in_specs=[row, row, whole(gain),...  6.35 us
    ppermute x2, starting transfers between devices, swap_diagonal(): lax.ppermute(array, 'dp', [(i, i ^ first ^ last) for i in range(size)])  5.15 us
  transfers between devices with their start and end apart: 27, of which 12 were waited for; matrix products, arithmetic and copies ran while one was open for 6% of the time, Pallas kernels for 35%

profile of v2, /device:TPU:0, one launch (start us, length us, event | category | flops | bytes accessed | tf_op | source)
XLA Modules:
  0.0 180.3 jit_solution(14900751413109327308)
XLA Ops:
  0.7 1.0 constant_dynamic-slice_fusion.5
  1.7 1.1 constant_dynamic-slice_fusion.3
  2.8 3.0 %collective-permute-start = (bf16[256,768]{1,0:T(8,128)(2,1)S(1)}, bf16[256,768]{1,0:T(8,128)(2,1)}, u32[]{:S(2)}, u32[]{:S(2)}) collective-permute-start(bf16[256,768]{1,0:T(8,128)(2,1)S(1)} %pad_maximum_fusion.1), channel_id=1, source_target_pairs={{0,1},{1,0},{2,3},{3,2},{4,5},{5,4},{6,7},{7,6},{8,9},{9,8},{10,11... | collective-permute-start | bytes 1179656 | tf_op jit(solution)/shard_map/ppermute | solution.py:783
  6.1 0.9 collective-permute-start.2
  7.0 14.3 %shard_map.255 = (bf16[2,1024,512]{2,1,0:T(8,128)(2,1)}, bf16[512,768]{1,0:T(8,128)(2,1)}, bf16[2,2,2560,128]{3,2,1,0:T(8,128)(2,1)}, bf16[2,2,2,512,1024]{4,3,2,1,0:T(8,128)(2,1)}, bf16[2,512,256]{2,1,0:T(8,128)(2,1)}) custom-call(s32[4]{0:T(128)} %starts_ref.9, bf16[2,512,512]{2,1,0:T(8,128)(2,1)} %tok_ref.4, bf16[4,512,512]{2,1,0:T(8,128)(2,1)} %mem_ref.1, ...), custom_call_target="tpu_custom_call" | custom-call | flops 6000000000 | bytes 16777216 | tf_op jit(solution)/shard_map/pallas_call | solution.py:176
  21.3 1.9 %collective-permute-done.1.sibling_ref = bf16[256,768]{1,0:T(8,128)(2,1)S(1)} collective-permute-done((bf16[256,768]{1,0:T(8,128)(2,1)}, bf16[256,768]{1,0:T(8,128)(2,1)S(1)}, u32[]{:S(2)}, u32[]{:S(2)}) %collective-permute-start.1) | collective-permute-done | bytes 393248 | tf_op jit(solution)/shard_map/ppermute | solution.py:783
  23.3 0.7 copy-done.12
  24.0 12.4 %shard_map.256 = (bf16[512,768]{1,0:T(8,128)(2,1)}, bf16[2,2,2560,128]{3,2,1,0:T(8,128)(2,1)}, bf16[2,2,2,512,1024]{4,3,2,1,0:T(8,128)(2,1)}, bf16[2,512,256]{2,1,0:T(8,128)(2,1)}) custom-call(s32[4]{0:T(128)} %starts_ref.9, bf16[2,1024,512]{2,1,0:T(8,128)(2,1)} %get-tuple-element.85.kv_ref.kv_far, bf16[256,768]{1,0:T(8,128)(2,1)} %collective-permute-done.mine_ref, ...), custom_call_target="tpu_custom_call" | custom-call | flops 6000000000 | bytes 16777216 | tf_op jit(solution)/shard_map/pallas_call | solution.py:176
  36.5 3.8 %collective-permute-done.2.mine_far = bf16[1152,512]{1,0:T(8,128)(2,1)S(1)} collective-permute-done((bf16[1152,512]{1,0:T(8,128)(2,1)S(1)}, bf16[1152,512]{1,0:T(8,128)(2,1)S(1)}, u32[]{:S(2)}, u32[]{:S(2)}) %collective-permute-start.2) | collective-permute-done | bytes 1179680 | tf_op jit(solution)/shard_map/ppermute | solution.py:783
  40.3 0.7 pad_maximum_fusion.3.gains_ref
  40.9 2.2 %collective-permute-done.3.sibling_far = bf16[1152,512]{1,0:T(8,128)(2,1)S(1)} collective-permute-done((bf16[1152,512]{1,0:T(8,128)(2,1)S(1)}, bf16[1152,512]{1,0:T(8,128)(2,1)S(1)}, u32[]{:S(2)}, u32[]{:S(2)}) %collective-permute-start.3) | collective-permute-done | bytes 1179680 | tf_op jit(solution)/shard_map/ppermute | solution.py:783
  43.1 1.1 copy-done.10
  44.2 29.9 %shard_map.257 = (bf16[2,512,512]{2,1,0:T(8,128)(2,1)}, f32[2,512,512]{2,1,0:T(8,128)}, bf16[2,512,256]{2,1,0:T(8,128)(2,1)}, bf16[2,512,256]{2,1,0:T(8,128)(2,1...) custom-call(bf16[2,512,512]{2,1,0:T(8,128)(2,1)} %tok_ref.4, ...), custom_call_target="tpu_custom_call" | custom-call | flops 15000000512 | bytes 31457280 | tf_op jit(solution)/shard_map/pallas_call | solution.py:441
  74.1 0.2 collective-permute-start.5
  74.3 0.4 collective-permute-start.4
  74.7 0.7 slice.122
  75.4 1.8 %collective-permute-done.5 = bf16[2,576,512]{2,1,0:T(8,128)(2,1)S(1)} collective-permute-done((bf16[2,576,512]{2,1,0:T(8,128)(2,1)}, bf16[2,576,512]{2,1,0:T(8,128)(2,1)S(1)}, u32[]{:S(2)}, u32[]{:S(2)}) %collective-permute-start.5) | collective-permute-done | bytes 1179680 | tf_op jit(solution)/shard_map/ppermute | solution.py:783
  77.2 1.7 add_convert_fusion
  78.9 1.8 %collective-permute-start.7 = (bf16[576,512]{1,0:T(8,128)(2,1)S(1)}, bf16[576,512]{1,0:T(8,128)(2,1)S(1)}, u32[]{:S(2)}, u32[]{:S(2)}) collective-permute-start(bf16[576,512]{1,0:T(8,128)(2,1)S(1)} %get-tuple-element.160), channel_id=1, source_target_pairs={{0,1},{1,0},{2,3},{3,2},{4,5},{5,4},{6,7},{7,6},{8,9},{9,8},{10,11... | collective-permute-start | bytes 1769480 | tf_op jit(solution)/shard_map/ppermute | solution.py:783
  80.7 0.3 add_convert_fusion.1
  81.0 1.5 collective-permute-start.6
  82.6 13.8 %shard_map.258 = (bf16[2,2,384,512]{3,2,1,0:T(8,128)(2,1)}, bf16[2,3,128,512]{3,2,1,0:T(8,128)(2,1)}, f32[2,8,512]{2,1,0:T(8,128)}) custom-call(s32[4]{0:T(128)} %starts_ref.9, bf16[2,2,2560,128]{3,2,1,0:T(8,128)(2,1)} %get-tuple-element.93.qkv_ref, bf16[2,2,2,512,1024]{4,3,2,1,0:T(8,128)(2,1)} %get-tuple-element.94.p_ref, ...), custom_call_target="tpu_custom_call" | custom-call | flops 8000000000 | bytes 16777216 | tf_op jit(solution)/shard_map/pallas_call | solution.py:609
  96.4 0.8 slice_reduce_fusion
  97.2 1.0 slice_bitcast_fusion
  98.3 0.2 fusion.2
  98.4 1.5 collective-permute-start.9
  100.0 0.2 fusion.9
  100.3 7.9 %shard_map.259 = (bf16[1,2,384,512]{3,2,1,0:T(8,128)(2,1)}, bf16[1,3,128,512]{3,2,1,0:T(8,128)(2,1)}, f32[1,8,512]{2,1,0:T(8,128)}) custom-call(s32[4]{0:T(128)} %starts_ref.9, bf16[2,2,2560,128]{3,2,1,0:T(8,128)(2,1)} %get-tuple-element.104.qkv_ref, bf16[2,2,2,512,1024]{4,3,2,1,0:T(8,128)(2,1)} %get-tuple-element.105.p_ref, ...), custom_call_target="tpu_custom_call" | custom-call | flops 4000000000 | bytes 8388608 | tf_op jit(solution)/shard_map/pallas_call | solution.py:609
  108.2 0.7 slice.131
  109.0 0.4 add_convert_fusion.7
  109.4 2.6 %collective-permute-start.13 = (bf16[288,512]{1,0:T(8,128)(2,1)S(1)}, bf16[288,512]{1,0:T(8,128)(2,1)S(1)}, u32[]{:S(2)}, u32[]{:S(2)}) collective-permute-start(bf16[288,512]{1,0:T(8,128)(2,1)S(1)} %add_convert_fusion.7), channel_id=1, source_target_pairs={{0,8},{2,10},{4,12},{6,14},{8,0},{10,2},{12,4},{14,6},{16,24},{18,... | collective-permute-start | bytes 884744 | tf_op jit(solution)/shard_map/ppermute | solution.py:783
  112.3 0.6 collective-permute-start.11
  112.8 7.8 %shard_map.260 = (bf16[1,2,384,512]{3,2,1,0:T(8,128)(2,1)}, bf16[1,3,128,512]{3,2,1,0:T(8,128)(2,1)}, f32[1,8,512]{2,1,0:T(8,128)}) custom-call(s32[4]{0:T(128)} %starts_ref.9, bf16[2,2,2560,128]{3,2,1,0:T(8,128)(2,1)} %get-tuple-element.104.qkv_ref, bf16[2,2,2,512,1024]{4,3,2,1,0:T(8,128)(2,1)} %get-tuple-element.105.p_ref, ...), custom_call_target="tpu_custom_call" | custom-call | flops 4000000000 | bytes 8388608 | tf_op jit(solution)/shard_map/pallas_call | solution.py:609
  120.7 0.8 slice.135
  121.5 0.5 add_convert_fusion.5
  121.9 1.9 %collective-permute-done.11 = bf16[3,128,512]{2,1,0:T(8,128)(2,1)S(1)} collective-permute-done((bf16[3,128,512]{2,1,0:T(8,128)(2,1)S(1)}, bf16[3,128,512]{2,1,0:T(8,128)(2,1)S(1)}, u32[]{:S(2)}, u32[]{:S(2)}) %collective-permute-start.11) | collective-permute-done | bytes 393248 | tf_op jit(solution)/shard_map/ppermute | solution.py:783
  123.8 0.2 fusion.5
  124.0 1.3 collective-permute-start.14
  125.3 2.6 %collective-permute-start.17 = (bf16[288,512]{1,0:T(8,128)(2,1)S(1)}, bf16[288,512]{1,0:T(8,128)(2,1)S(1)}, u32[]{:S(2)}, u32[]{:S(2)}) collective-permute-start(bf16[288,512]{1,0:T(8,128)(2,1)S(1)} %add_convert_fusion.5), channel_id=1, source_target_pairs={{0,16},{2,18},{4,20},{6,22},{8,24},{10,26},{12,28},{14,30},{16,0},... | collective-permute-start | bytes 884744 | tf_op jit(solution)/shard_map/ppermute | solution.py:783
  127.9 0.8 collective-permute-start.15
  128.7 6.4 %shard_map.261 = bf16[2,512,512]{2,1,0:T(8,128)(2,1)} custom-call(bf16[2,512,512]{2,1,0:T(8,128)(2,1)} %tok_ref.4, f32[2,512,512]{2,1,0:T(8,128)} %get-tuple-element.129.grad_hidden_ref, f32[1,512]{1,0:T(1,128)} %bitcast.84, bf16[2,2,384,512]{3,2,1,0:T(8,128)(2,1)} %get-tuple-element.130.oth_ref, bf16[1,2,384,512]{3,2,1,0:T(8,128)(2,1)} %get-tuple-element.131.own_first_ref, ...), custom_call_target="tpu_custom_call" | custom-call | flops 2000000000 | bytes 8388608 | tf_op jit(solution)/shard_map/pallas_call | solution.py:690
  135.1 1.6 collective-permute-start.16
  136.7 4.7 %collective-permute-done.17 = bf16[288,512]{1,0:T(8,128)(2,1)S(1)} collective-permute-done((bf16[288,512]{1,0:T(8,128)(2,1)S(1)}, bf16[288,512]{1,0:T(8,128)(2,1)S(1)}, u32[]{:S(2)}, u32[]{:S(2)}) %collective-permute-start.17) | collective-permute-done | bytes 294944 | tf_op jit(solution)/shard_map/ppermute | solution.py:783
  141.3 2.0 %collective-permute-done.16 = bf16[3,32,512]{2,1,0:T(8,128)(2,1)S(1)} collective-permute-done((bf16[3,32,512]{2,1,0:T(8,128)(2,1)S(1)}, bf16[3,32,512]{2,1,0:T(8,128)(2,1)S(1)}, u32[]{:S(2)}, u32[]{:S(2)}) %collective-permute-start.16) | collective-permute-done | bytes 98336 | tf_op jit(solution)/shard_map/ppermute | solution.py:783
  143.6 0.4 collective-permute-start.19
  144.1 3.1 %collective-permute-start.18 = (bf16[112,512]{1,0:T(8,128)(2,1)S(1)}, bf16[112,512]{1,0:T(8,128)(2,1)S(1)}, u32[]{:S(2)}, u32[]{:S(2)}) collective-permute-start(bf16[112,512]{1,0:T(8,128)(2,1)S(1)} %concatenate.137), channel_id=1, source_target_pairs={{0,16},{2,18},{4,20},{6,22},{8,24},{10,26},{12,28},{14,30},{16,0},... | collective-permute-start | bytes 344072 | tf_op jit(solution)/shard_map/ppermute | solution.py:783
  147.2 5.8 %collective-permute-done.18 = bf16[112,512]{1,0:T(8,128)(2,1)S(1)} collective-permute-done((bf16[112,512]{1,0:T(8,128)(2,1)S(1)}, bf16[112,512]{1,0:T(8,128)(2,1)S(1)}, u32[]{:S(2)}, u32[]{:S(2)}) %collective-permute-start.18) | collective-permute-done | bytes 114720 | tf_op jit(solution)/shard_map/ppermute | solution.py:783
  153.0 2.2 %collective-permute-done.20 = bf16[288,512]{1,0:T(8,128)(2,1)S(1)} collective-permute-done((bf16[288,512]{1,0:T(8,128)(2,1)S(1)}, bf16[288,512]{1,0:T(8,128)(2,1)S(1)}, u32[]{:S(2)}, u32[]{:S(2)}) %collective-permute-start.20) | collective-permute-done | bytes 294944 | tf_op jit(solution)/shard_map/ppermute | solution.py:783
  155.4 2.6 %collective-permute-start.24 = (bf16[288,512]{1,0:T(8,128)(2,1)S(1)}, bf16[288,512]{1,0:T(8,128)(2,1)S(1)}, u32[]{:S(2)}, u32[]{:S(2)}) collective-permute-start(bf16[288,512]{1,0:T(8,128)(2,1)S(1)} %add_convert_fusion.4), channel_id=1, source_target_pairs={{0,12},{2,14},{4,8},{6,10},{8,4},{10,6},{12,0},{14,2},{16,28},{18,... | collective-permute-start | bytes 884744 | tf_op jit(solution)/shard_map/ppermute | solution.py:809
  158.0 0.4 collective-permute-start.21
  158.4 0.6 collective-permute-start.22
  159.0 2.5 %collective-permute-start.23 = (bf16[112,512]{1,0:T(8,128)(2,1)S(1)}, bf16[112,512]{1,0:T(8,128)(2,1)S(1)}, u32[]{:S(2)}, u32[]{:S(2)}) collective-permute-start(bf16[112,512]{1,0:T(8,128)(2,1)S(1)} %concatenate.143), channel_id=1, source_target_pairs={{0,12},{2,14},{4,8},{6,10},{8,4},{10,6},{12,0},{14,2},{16,28},{18,... | collective-permute-start | bytes 344072 | tf_op jit(solution)/shard_map/ppermute | solution.py:809
  161.5 0.2 maximum_select_fusion.1
  161.7 6.3 %collective-permute-done.21 = bf16[112,512]{1,0:T(8,128)(2,1)S(1)} collective-permute-done((bf16[112,512]{1,0:T(8,128)(2,1)S(1)}, bf16[112,512]{1,0:T(8,128)(2,1)S(1)}, u32[]{:S(2)}, u32[]{:S(2)}) %collective-permute-start.21) | collective-permute-done | bytes 114720 | tf_op jit(solution)/shard_map/ppermute | solution.py:783
  168.1 1.3 collective-permute-done.23
  169.6 0.2 maximum_select_fusion.2
  169.8 0.2 maximum_select_fusion.ffn_mine
  170.0 0.3 concatenate.159
  170.4 0.5 collective-permute-start.26
  170.9 2.9 %collective-permute-done.26.attn_sibling = bf16[400,512]{1,0:T(8,128)(2,1)S(1)} collective-permute-done((bf16[400,512]{1,0:T(8,128)(2,1)S(1)}, bf16[400,512]{1,0:T(8,128)(2,1)S(1)}, u32[]{:S(2)}, u32[]{:S(2)}) %collective-permute-start.26) | collective-permute-done | bytes 409632 | tf_op jit(solution)/shard_map/ppermute | solution.py:783
  173.8 0.5 slice.170
  175.0 0.5 fusion.19
  175.5 0.6 fusion.20
  176.1 3.1 %shard_map.262 = (f32[512,256]{1,0:T(8,128)}, f32[512,256]{1,0:T(8,128)}, f32[512,256]{1,0:T(8,128)}, f32[256,512]{1,0:T(8,128)}, f32[512,1024]{1,0:T(8,128)}, /*index=5*/f32[1024,512]{1,0:T(8,128)}) custom-call(bf16[2,576,512]{2,1,0:T(8,128)(2,1)S(1)} %maximum_select_fusion.ffn_mine, bf16[2,576,512]{2,1,0:T(8,128)(2,1)S(1)} %collective-permute-done.25.ffn_sibling, ...), custom_call_target="tpu_custom_call" | custom-call | tf_op jit(solution)/shard_map/pallas_call | solution.py:770
  (78 shorter events, 1.6 us)
Async XLA Ops:
  0.6 5.2 %copy-start.4 = (bf16[1024,512]{1,0:T(8,128)(2,1)S(1)}, bf16[1024,512]{1,0:T(8,128)(2,1)}, u32[]{:S(2)}) copy-start(bf16[1024,512]{1,0:T(8,128)(2,1)} %down_far.1) | copy-start | bytes 3145732
  1.7 4.2 %copy-start.3 = (bf16[512,1024]{1,0:T(8,128)(2,1)S(1)}, bf16[512,1024]{1,0:T(8,128)(2,1)}, u32[]{:S(2)}) copy-start(bf16[512,1024]{1,0:T(8,128)(2,1)} %up_far.1) | copy-start | bytes 3145732
  2.8 3.2 %copy-start.5 = (bf16[256,512]{1,0:T(8,128)(2,1)S(1)}, bf16[256,512]{1,0:T(8,128)(2,1)}, u32[]{:S(2)}) copy-start(bf16[256,512]{1,0:T(8,128)(2,1)} %out_far.1) | copy-start | bytes 786436
  2.8 18.4 %collective-permute-start = (bf16[256,768]{1,0:T(8,128)(2,1)S(1)}, bf16[256,768]{1,0:T(8,128)(2,1)}, u32[]{:S(2)}, u32[]{:S(2)}) collective-permute-start(bf16[256,768]{1,0:T(8,128)(2,1)S(1)} %pad_maximum_fusion.1), channel_id=1, source_target_pairs={{0,1},{1,0},{2,3},{3,2},{4,5},{5,4},{6,7},{7,6},{8,9},{9,8},{10,11... | collective-permute-start | bytes 1179656 | tf_op jit(solution)/shard_map/ppermute | solution.py:783
  6.1 34.2 %collective-permute-start.2 = (bf16[1152,512]{1,0:T(8,128)(2,1)S(1)}, bf16[1152,512]{1,0:T(8,128)(2,1)S(1)}, u32[]{:S(2)}, u32[]{:S(2)}) collective-permute-start(bf16[1152,512]{1,0:T(8,128)(2,1)S(1)} %pad_maximum_fusion), channel_id=1, source_target_pairs={{0,1},{1,0},{2,3},{3,2},{4,5},{5,4},{6,7},{7,6},{8,9},{9,8},{10,11... | collective-permute-start | bytes 3538952 | tf_op jit(solution)/shard_map/ppermute | solution.py:783
  21.2 19.0 %copy-start.7 = (f32[512]{0:T(512)S(1)}, f32[512]{0:T(512)}, u32[]{:S(2)}) copy-start(f32[512]{0:T(512)} %param.30) | copy-start | bytes 6148
  21.3 19.0 %copy-start.8 = (f32[512]{0:T(512)S(1)}, f32[512]{0:T(512)}, u32[]{:S(2)}) copy-start(f32[512]{0:T(512)} %param.29) | copy-start | bytes 6148
  21.3 2.0 %collective-permute-start.1 = (bf16[256,768]{1,0:T(8,128)(2,1)}, bf16[256,768]{1,0:T(8,128)(2,1)S(1)}, u32[]{:S(2)}, u32[]{:S(2)}) collective-permute-start(bf16[256,768]{1,0:T(8,128)(2,1)} %collective-permute-done.mine_ref), channel_id=1, source_target_pairs={{0,2},{2,0},{4,6},{6,4},{8,10},{10,8},{12,14},{14,12},{16,18},{18,... | collective-permute-start | bytes 1179656 | tf_op jit(solution)/shard_map/ppermute | solution.py:783
  23.3 0.7 copy-start.12
  40.2 2.9 %copy-start.9 = (bf16[1152,512]{1,0:T(8,128)(2,1)}, bf16[1152,512]{1,0:T(8,128)(2,1)S(1)}, u32[]{:S(2)}) copy-start(bf16[1152,512]{1,0:T(8,128)(2,1)S(1)} %collective-permute-done.2.mine_far) | copy-start | bytes 3538948
  40.3 2.8 %collective-permute-start.3 = (bf16[1152,512]{1,0:T(8,128)(2,1)S(1)}, bf16[1152,512]{1,0:T(8,128)(2,1)S(1)}, u32[]{:S(2)}, u32[]{:S(2)}) collective-permute-start(bf16[1152,512]{1,0:T(8,128)(2,1)S(1)} %collective-permute-done.2.mine_far), channel_id=1, source_target_pairs={{0,2},{2,0},{4,6},{6,4},{8,10},{10,8},{12,14},{14,12},{16,18},{18,... | collective-permute-start | bytes 3538952 | tf_op jit(solution)/shard_map/ppermute | solution.py:783
  43.1 1.1 copy-start.10
  74.1 3.1 %collective-permute-start.5 = (bf16[2,576,512]{2,1,0:T(8,128)(2,1)}, bf16[2,576,512]{2,1,0:T(8,128)(2,1)S(1)}, u32[]{:S(2)}, u32[]{:S(2)}) collective-permute-start(bf16[2,576,512]{2,1,0:T(8,128)(2,1)} %get-tuple-element.99), channel_id=1, source_target_pairs={{0,2},{2,0},{4,6},{6,4},{8,10},{10,8},{12,14},{14,12},{16,18},{18,... | collective-permute-start | bytes 3538952 | tf_op jit(solution)/shard_map/ppermute | solution.py:783
  74.3 6.4 %collective-permute-start.4 = (bf16[2,576,512]{2,1,0:T(8,128)(2,1)}, bf16[2,576,512]{2,1,0:T(8,128)(2,1)S(1)}, u32[]{:S(2)}, u32[]{:S(2)}) collective-permute-start(bf16[2,576,512]{2,1,0:T(8,128)(2,1)} %get-tuple-element.97), channel_id=1, source_target_pairs={{0,2},{2,0},{4,6},{6,4},{8,10},{10,8},{12,14},{14,12},{16,18},{18,... | collective-permute-start | bytes 3538952 | tf_op jit(solution)/shard_map/ppermute | solution.py:783
  77.2 3.5 %copy-start = (bf16[2,576,512]{2,1,0:T(8,128)(2,1)S(1)}, bf16[2,576,512]{2,1,0:T(8,128)(2,1)}, u32[]{:S(2)}) copy-start(bf16[2,576,512]{2,1,0:T(8,128)(2,1)} %get-tuple-element.96) | copy-start | bytes 3538948
  78.9 19.4 %collective-permute-start.7 = (bf16[576,512]{1,0:T(8,128)(2,1)S(1)}, bf16[576,512]{1,0:T(8,128)(2,1)S(1)}, u32[]{:S(2)}, u32[]{:S(2)}) collective-permute-start(bf16[576,512]{1,0:T(8,128)(2,1)S(1)} %get-tuple-element.160), channel_id=1, source_target_pairs={{0,1},{1,0},{2,3},{3,2},{4,5},{5,4},{6,7},{7,6},{8,9},{9,8},{10,11... | collective-permute-start | bytes 1769480 | tf_op jit(solution)/shard_map/ppermute | solution.py:783
  81.0 17.4 %collective-permute-start.6 = (bf16[2,288,512]{2,1,0:T(8,128)(2,1)S(1)}, bf16[2,288,512]{2,1,0:T(8,128)(2,1)S(1)}, u32[]{:S(2)}, u32[]{:S(2)}) collective-permute-start(bf16[2,288,512]{2,1,0:T(8,128)(2,1)S(1)} %get-tuple-element.100), channel_id=1, source_target_pairs={{0,4},{2,6},{4,0},{6,2},{8,12},{10,14},{12,8},{14,10},{16,20},{18,... | collective-permute-start | bytes 1769480 | tf_op jit(solution)/shard_map/ppermute | solution.py:783
  98.4 10.5 %collective-permute-start.9 = (bf16[288,512]{1,0:T(8,128)(2,1)S(1)}, bf16[288,512]{1,0:T(8,128)(2,1)S(1)}, u32[]{:S(2)}, u32[]{:S(2)}) collective-permute-start(bf16[288,512]{1,0:T(8,128)(2,1)S(1)} %get-tuple-element.168), channel_id=1, source_target_pairs={{0,4},{2,6},{4,0},{6,2},{8,12},{10,14},{12,8},{14,10},{16,20},{18,... | collective-permute-start | bytes 884744 | tf_op jit(solution)/shard_map/ppermute | solution.py:783
  100.1 8.8 %collective-permute-start.10 = (bf16[288,512]{1,0:T(8,128)(2,1)S(1)}, bf16[288,512]{1,0:T(8,128)(2,1)S(1)}, u32[]{:S(2)}, u32[]{:S(2)}) collective-permute-start(bf16[288,512]{1,0:T(8,128)(2,1)S(1)} %get-tuple-element.110), channel_id=1, source_target_pairs={{0,1},{1,0},{2,3},{3,2},{4,5},{5,4},{6,7},{7,6},{8,9},{9,8},{10,11... | collective-permute-start | bytes 884744 | tf_op jit(solution)/shard_map/ppermute | solution.py:783
  100.2 11.9 %collective-permute-start.8 = (bf16[3,128,512]{2,1,0:T(8,128)(2,1)S(1)}, bf16[3,128,512]{2,1,0:T(8,128)(2,1)S(1)}, u32[]{:S(2)}, u32[]{:S(2)}) collective-permute-start(bf16[3,128,512]{2,1,0:T(8,128)(2,1)S(1)} %slice_bitcast_fusion), channel_id=1, source_target_pairs={{0,2},{2,0},{4,6},{6,4},{8,10},{10,8},{12,14},{14,12},{16,18},{18,... | collective-permute-start | bytes 1179656 | tf_op jit(solution)/shard_map/ppermute | solution.py:783
  108.9 3.2 %copy-start.1 = (bf16[2,3,128,512]{3,2,1,0:T(8,128)(2,1)S(1)}, bf16[2,3,128,512]{3,2,1,0:T(8,128)(2,1)}, u32[]{:S(2)}) copy-start(bf16[2,3,128,512]{3,2,1,0:T(8,128)(2,1)} %get-tuple-element.107) | copy-start | bytes 2359300
  109.0 3.2 %copy-start.11 = (bf16[1,3,128,512]{3,2,1,0:T(8,128)(2,1)S(1)}, bf16[1,3,128,512]{3,2,1,0:T(8,128)(2,1)}, u32[]{:S(2)}) copy-start(bf16[1,3,128,512]{3,2,1,0:T(8,128)(2,1)} %get-tuple-element.115) | copy-start | bytes 1179652
  109.4 12.0 %collective-permute-start.13 = (bf16[288,512]{1,0:T(8,128)(2,1)S(1)}, bf16[288,512]{1,0:T(8,128)(2,1)S(1)}, u32[]{:S(2)}, u32[]{:S(2)}) collective-permute-start(bf16[288,512]{1,0:T(8,128)(2,1)S(1)} %add_convert_fusion.7), channel_id=1, source_target_pairs={{0,8},{2,10},{4,12},{6,14},{8,0},{10,2},{12,4},{14,6},{16,24},{18,... | collective-permute-start | bytes 884744 | tf_op jit(solution)/shard_map/ppermute | solution.py:783
  112.2 9.2 %copy-start.6 = (f32[512]{0:T(512)S(1)}, f32[512]{0:T(512)}, u32[]{:S(2)}) copy-start(f32[512]{0:T(512)} %param.28) | copy-start | bytes 6148
  112.2 9.7 %collective-permute-start.12 = (bf16[3,128,512]{2,1,0:T(8,128)(2,1)S(1)}, bf16[3,128,512]{2,1,0:T(8,128)(2,1)S(1)}, u32[]{:S(2)}, u32[]{:S(2)}) collective-permute-start(bf16[3,128,512]{2,1,0:T(8,128)(2,1)S(1)} %bitcast.93), channel_id=1, source_target_pairs={{0,2},{2,0},{4,6},{6,4},{8,10},{10,8},{12,14},{14,12},{16,18},{18,... | collective-permute-start | bytes 1179656 | tf_op jit(solution)/shard_map/ppermute | solution.py:783
  112.3 11.5 %collective-permute-start.11 = (bf16[3,128,512]{2,1,0:T(8,128)(2,1)S(1)}, bf16[3,128,512]{2,1,0:T(8,128)(2,1)S(1)}, u32[]{:S(2)}, u32[]{:S(2)}) collective-permute-start(bf16[3,128,512]{2,1,0:T(8,128)(2,1)S(1)} %fusion), channel_id=1, source_target_pairs={{0,1},{1,0},{2,3},{3,2},{4,5},{5,4},{6,7},{7,6},{8,9},{9,8},{10,11... | collective-permute-start | bytes 1179656 | tf_op jit(solution)/shard_map/ppermute | solution.py:783
  120.6 3.2 %copy-start.2 = (bf16[1,3,128,512]{3,2,1,0:T(8,128)(2,1)S(1)}, bf16[1,3,128,512]{3,2,1,0:T(8,128)(2,1)}, u32[]{:S(2)}) copy-start(bf16[1,3,128,512]{3,2,1,0:T(8,128)(2,1)} %get-tuple-element.123) | copy-start | bytes 1179652
  124.0 11.0 %collective-permute-start.14 = (bf16[3,64,512]{2,1,0:T(8,128)(2,1)S(1)}, bf16[3,64,512]{2,1,0:T(8,128)(2,1)S(1)}, u32[]{:S(2)}, u32[]{:S(2)}) collective-permute-start(bf16[3,64,512]{2,1,0:T(8,128)(2,1)S(1)} %get-tuple-element.127), channel_id=1, source_target_pairs={{0,4},{2,6},{4,0},{6,2},{8,12},{10,14},{12,8},{14,10},{16,20},{18,... | collective-permute-start | bytes 589832 | tf_op jit(solution)/shard_map/ppermute | solution.py:783
  125.3 16.0 %collective-permute-start.17 = (bf16[288,512]{1,0:T(8,128)(2,1)S(1)}, bf16[288,512]{1,0:T(8,128)(2,1)S(1)}, u32[]{:S(2)}, u32[]{:S(2)}) collective-permute-start(bf16[288,512]{1,0:T(8,128)(2,1)S(1)} %add_convert_fusion.5), channel_id=1, source_target_pairs={{0,16},{2,18},{4,20},{6,22},{8,24},{10,26},{12,28},{14,30},{16,0},... | collective-permute-start | bytes 884744 | tf_op jit(solution)/shard_map/ppermute | solution.py:783
  127.9 7.1 %collective-permute-start.15 = (f32[5,512]{1,0:T(8,128)S(1)}, f32[5,512]{1,0:T(8,128)S(1)}, u32[]{:S(2)}, u32[]{:S(2)}) collective-permute-start(f32[5,512]{1,0:T(8,128)S(1)} %pad_maximum_fusion.2), channel_id=1, source_target_pairs={{0,1},{1,0},{2,3},{3,2},{4,5},{5,4},{6,7},{7,6},{8,9},{9,8},{10,11... | collective-permute-start | bytes 30728 | tf_op jit(solution)/shard_map/ppermute | solution.py:783
  135.1 8.3 %collective-permute-start.16 = (bf16[3,32,512]{2,1,0:T(8,128)(2,1)S(1)}, bf16[3,32,512]{2,1,0:T(8,128)(2,1)S(1)}, u32[]{:S(2)}, u32[]{:S(2)}) collective-permute-start(bf16[3,32,512]{2,1,0:T(8,128)(2,1)S(1)} %add_convert_fusion.12), channel_id=1, source_target_pairs={{0,8},{2,10},{4,12},{6,14},{8,0},{10,2},{12,4},{14,6},{16,24},{18,... | collective-permute-start | bytes 294920 | tf_op jit(solution)/shard_map/ppermute | solution.py:783
  143.6 9.4 %collective-permute-start.19 = (bf16[288,512]{1,0:T(8,128)(2,1)S(1)}, bf16[288,512]{1,0:T(8,128)(2,1)S(1)}, u32[]{:S(2)}, u32[]{:S(2)}) collective-permute-start(bf16[288,512]{1,0:T(8,128)(2,1)S(1)} %add_convert_fusion.4), channel_id=1, source_target_pairs={{0,4},{2,6},{4,0},{6,2},{8,12},{10,14},{12,8},{14,10},{16,20},{18,... | collective-permute-start | bytes 884744 | tf_op jit(solution)/shard_map/ppermute | solution.py:783
  144.1 11.1 %collective-permute-start.20 = (bf16[288,512]{1,0:T(8,128)(2,1)S(1)}, bf16[288,512]{1,0:T(8,128)(2,1)S(1)}, u32[]{:S(2)}, u32[]{:S(2)}) collective-permute-start(bf16[288,512]{1,0:T(8,128)(2,1)S(1)} %add_convert_fusion.4), channel_id=1, source_target_pairs={{0,8},{2,10},{4,12},{6,14},{8,0},{10,2},{12,4},{14,6},{16,24},{18,... | collective-permute-start | bytes 884744 | tf_op jit(solution)/shard_map/ppermute | solution.py:783
  144.1 8.9 %collective-permute-start.18 = (bf16[112,512]{1,0:T(8,128)(2,1)S(1)}, bf16[112,512]{1,0:T(8,128)(2,1)S(1)}, u32[]{:S(2)}, u32[]{:S(2)}) collective-permute-start(bf16[112,512]{1,0:T(8,128)(2,1)S(1)} %concatenate.137), channel_id=1, source_target_pairs={{0,16},{2,18},{4,20},{6,22},{8,24},{10,26},{12,28},{14,30},{16,0},... | collective-permute-start | bytes 344072 | tf_op jit(solution)/shard_map/ppermute | solution.py:783
  155.4 13.9 %collective-permute-start.24 = (bf16[288,512]{1,0:T(8,128)(2,1)S(1)}, bf16[288,512]{1,0:T(8,128)(2,1)S(1)}, u32[]{:S(2)}, u32[]{:S(2)}) collective-permute-start(bf16[288,512]{1,0:T(8,128)(2,1)S(1)} %add_convert_fusion.4), channel_id=1, source_target_pairs={{0,12},{2,14},{4,8},{6,10},{8,4},{10,6},{12,0},{14,2},{16,28},{18,... | collective-permute-start | bytes 884744 | tf_op jit(solution)/shard_map/ppermute | solution.py:809
  158.0 10.0 %collective-permute-start.21 = (bf16[112,512]{1,0:T(8,128)(2,1)S(1)}, bf16[112,512]{1,0:T(8,128)(2,1)S(1)}, u32[]{:S(2)}, u32[]{:S(2)}) collective-permute-start(bf16[112,512]{1,0:T(8,128)(2,1)S(1)} %concatenate.143), channel_id=1, source_target_pairs={{0,4},{2,6},{4,0},{6,2},{8,12},{10,14},{12,8},{14,10},{16,20},{18,... | collective-permute-start | bytes 344072 | tf_op jit(solution)/shard_map/ppermute | solution.py:783
  158.4 9.7 %collective-permute-start.22 = (bf16[112,512]{1,0:T(8,128)(2,1)S(1)}, bf16[112,512]{1,0:T(8,128)(2,1)S(1)}, u32[]{:S(2)}, u32[]{:S(2)}) collective-permute-start(bf16[112,512]{1,0:T(8,128)(2,1)S(1)} %concatenate.143), channel_id=1, source_target_pairs={{0,8},{2,10},{4,12},{6,14},{8,0},{10,2},{12,4},{14,6},{16,24},{18,... | collective-permute-start | bytes 344072 | tf_op jit(solution)/shard_map/ppermute | solution.py:783
  159.0 10.4 %collective-permute-start.23 = (bf16[112,512]{1,0:T(8,128)(2,1)S(1)}, bf16[112,512]{1,0:T(8,128)(2,1)S(1)}, u32[]{:S(2)}, u32[]{:S(2)}) collective-permute-start(bf16[112,512]{1,0:T(8,128)(2,1)S(1)} %concatenate.143), channel_id=1, source_target_pairs={{0,12},{2,14},{4,8},{6,10},{8,4},{10,6},{12,0},{14,2},{16,28},{18,... | collective-permute-start | bytes 344072 | tf_op jit(solution)/shard_map/ppermute | solution.py:809
  170.3 5.8 %collective-permute-start.25 = (bf16[2,576,512]{2,1,0:T(8,128)(2,1)S(1)}, bf16[2,576,512]{2,1,0:T(8,128)(2,1)S(1)}, u32[]{:S(2)}, u32[]{:S(2)}) collective-permute-start(bf16[2,576,512]{2,1,0:T(8,128)(2,1)S(1)} %maximum_select_fusion.ffn_mine), channel_id=1, source_target_pairs={{0,2},{2,0},{4,6},{6,4},{8,10},{10,8},{12,14},{14,12},{16,18},{18,... | collective-permute-start | bytes 3538952 | tf_op jit(solution)/shard_map/ppermute | solution.py:783
  170.4 3.4 %collective-permute-start.26 = (bf16[400,512]{1,0:T(8,128)(2,1)S(1)}, bf16[400,512]{1,0:T(8,128)(2,1)S(1)}, u32[]{:S(2)}, u32[]{:S(2)}) collective-permute-start(bf16[400,512]{1,0:T(8,128)(2,1)S(1)} %concatenate.159), channel_id=1, source_target_pairs={{0,2},{2,0},{4,6},{6,4},{8,10},{10,8},{12,14},{14,12},{16,18},{18,... | collective-permute-start | bytes 1228808 | tf_op jit(solution)/shard_map/ppermute | solution.py:783

commit v3 on v2

--- a/solution.py
+++ b/solution.py
@@ -1,3 +1,5 @@
+import functools
+
 import jax
 import jax.numpy as jnp
 from jax import lax
@@ -17,7 +19,8 @@
 BF16 = jnp.bfloat16
 F32 = jnp.float32
 VMEM_LIMIT = 56 * 1024 * 1024
-MIDDLE_VMEM = 56 * 1024 * 1024
+FORWARD_VMEM = 52 * 1024 * 1024
+BACKWARD_VMEM = 48 * 1024 * 1024
 FINISH_VMEM = 24 * 1024 * 1024
 
 
@@ -179,7 +182,7 @@
         in_specs=in_specs,
         out_specs=out_specs,
         out_shape=outs,
-        compiler_params=pltpu.CompilerParams(vmem_limit_bytes=VMEM_LIMIT),
+        compiler_params=pltpu.CompilerParams(vmem_limit_bytes=FORWARD_VMEM),
         cost_estimate=pl.CostEstimate(flops=6 * 10**9, bytes_accessed=16 * 2**20, transcendentals=0),
     )(starts, *ins, *weights)
 
@@ -490,7 +493,7 @@
             *[jax.ShapeDtypeStruct((2, width + PAIR // 2, width), BF16)] * 4,
             jax.ShapeDtypeStruct((8, width), F32),
         ],
-        compiler_params=pltpu.CompilerParams(vmem_limit_bytes=MIDDLE_VMEM),
+        compiler_params=pltpu.CompilerParams(vmem_limit_bytes=VMEM_LIMIT),
         cost_estimate=pl.CostEstimate(flops=15 * 10**9, bytes_accessed=30 * 2**20, transcendentals=0),
     )(tokens, ctx_own, ctx_oth, nb, ids, cot, *weights, *received, edges, gains)
 
@@ -638,7 +641,7 @@
             jax.ShapeDtypeStruct((many, 3, PAIR, width), BF16),
             jax.ShapeDtypeStruct((many, 8, width), F32),
         ],
-        compiler_params=pltpu.CompilerParams(vmem_limit_bytes=VMEM_LIMIT),
+        compiler_params=pltpu.CompilerParams(vmem_limit_bytes=BACKWARD_VMEM),
         cost_estimate=pl.CostEstimate(
             flops=4 * 10**9 * many, bytes_accessed=8 * 2**20 * many, transcendentals=0
         ),
@@ -709,12 +712,18 @@
     ffn_sibling,
     attn_mine,
     attn_sibling,
+    small_ref,
     q_far,
     k_far,
     v_far,
     out_far,
     up_far,
     down_far,
+    gain_attn_ref,
+    gain_ffn_ref,
+    gate_ref,
+    mean_ref,
+    hist_ref,
     q_ref,
     k_ref,
     v_ref,
@@ -722,6 +731,7 @@
     up_ref,
     down_ref,
     sems,
+    tokens,
 ):
     core = core_index()
     width = up_far.shape[0]
@@ -754,28 +764,40 @@
         first, last = pair(attn_mine[i], attn_sibling[pl.ds(i * rows, rows), :])
         near[...] = jnp.concatenate([first, last], 0).T
         move(near, far)
+    count = small_ref.shape[0]
+    below = attn_sibling[pl.ds(3 * rows, -(-3 * count // 16) * 16), :].astype(F32)
+    small = small_ref[...]
+    for i in range(3):
+        small = small + below[i * count : (i + 1) * count]
+    gain_ffn_ref[...] = small[0:1]
+    mean_ref[...] = small[1:2, 0:1] / tokens
+    gate_ref[...] = small[2:3]
+    hist_ref[...] = small[3:4, :BINS] * (BINS / (tokens * NEIGH))
+    gain_attn_ref[...] = small[4:5]
     for one in moves:
         one.wait()
 
 
-def finish(ffn, attn):
+def finish(ffn, attn, small, tokens):
     width = ffn[0].shape[-1]
     quarter = attn[0].shape[1]
     shapes = [(width, 2 * quarter)] * 3
     shapes += [(2 * quarter, width), (width, 2 * width), (2 * width, width)]
+    rows = [(1, width)] * 3 + [(1, 1), (1, BINS)]
 
     def whole(array):
         return pl.BlockSpec(array.shape, lambda i: (0,) * array.ndim)
 
     return pl.pallas_call(
-        finish_body,
+        functools.partial(finish_body, tokens=tokens),
         grid=(1,),
-        in_specs=[whole(a) for a in (*ffn, *attn)],
-        out_specs=[pl.BlockSpec(memory_space=pl.ANY)] * 6,
+        in_specs=[whole(a) for a in (*ffn, *attn, small)],
+        out_specs=[pl.BlockSpec(memory_space=pl.ANY)] * 6
+        + [pl.BlockSpec(s, lambda i: (0, 0)) for s in rows],
         scratch_shapes=[pltpu.VMEM(s, F32) for s in shapes] + [pltpu.SemaphoreType.DMA((8,))],
-        out_shape=[jax.ShapeDtypeStruct(s, F32) for s in shapes],
+        out_shape=[jax.ShapeDtypeStruct(s, F32) for s in shapes + rows],
         compiler_params=pltpu.CompilerParams(vmem_limit_bytes=FINISH_VMEM),
-    )(*ffn, *attn)
+    )(*ffn, *attn, small)
 
 
 def swap(array, axis, bit):
@@ -999,8 +1021,21 @@
     both.add(da_last)
     gain_part = sum(g[:, 0].sum(0) for g in (gain_oth, gain_first, gain_last))[None] / attn_gain
     small = lax.concatenate([sums[:4], gain_part], 0)
-    sent = both.send(far[2])
-    sent = attn.halve(far[0], sent)
+    first_bit, last_bit = far[:2]
+
+    def quarter(piece, by_first, by_last):
+        at = 2 * (bit_of("dp", first_bit) ^ by_first) + (bit_of("dp", last_bit) ^ by_last)
+        size = piece.shape[1] // 4
+        return lax.dynamic_slice_in_dim(piece, at * size, size, 1)
+
+    sent_x = attn.total(lambda p: quarter(p, 1, 0))
+    sent_z = attn.total(lambda p: quarter(p, 0, 1))
+    sent_d = attn.total(lambda p: quarter(p, 1, 1))
+    kept = attn.total(lambda p: quarter(p, 0, 0))
+    come_x = swap(sent_x, "dp", first_bit)
+    come_z = swap(sent_z, "dp", last_bit)
+    come_d = swap_diagonal(sent_d, first_bit, last_bit)
+    sent = both.send(far[2], sent_x, sent_z, sent_d)
     small_sent = after(small, sent)
     small_come = swap(small_sent, "mp", 1)
     grad_input = input_grad(
@@ -1010,35 +1045,31 @@
         (g_oth, g_own_first, g_own_last),
         (oth[0], own[0]),
     )
-    attn.come, small_come = lax.optimization_barrier((attn.come, small_come, grad_input))[:2]
-    attn.pieces = (attn.kept, attn.come)
+    come_x, come_z, come_d, small_come = lax.optimization_barrier(
+        (come_x, come_z, come_d, small_come, grad_input)
+    )[:4]
     ride = Ride(small_sent + small_come)
-
-    mine = bit_of("dp", far[1])
-    part = attn.total(lambda p: part_of(p, 1 - mine, 1))
-    kept = attn.total(lambda p: part_of(p, mine, 1))
-    come = swap(part, "dp", far[1])
-    come, both.come = lax.optimization_barrier((come, both.come))
-    total = add_low(kept, come)
-    ffn_total = add_low(both.sent, both.come)
-    for bit in far[3:]:
-        ffn_total = add_low(ffn_total, swap(ffn_total, "dp", bit))
-    ffn_sent = ffn_total
+    total = sum(part.astype(F32) for part in (kept, come_x, come_z, come_d)).astype(BF16)
     for bit in far[2:]:
         sent = ride.below(total)
         come = swap(sent, "dp", bit)
         if bit == far[2]:
-            ffn_sent = after(ffn_total, sent)
-            ffn_x = swap(ffn_sent, "dp", far[0])
-            ffn_z = swap(ffn_sent, "dp", far[1])
-            come, ffn_x, ffn_z = lax.optimization_barrier((come, ffn_x, ffn_z))
+            come, both.come = lax.optimization_barrier((come, both.come))
         total = add_low(total, ride.add(come, total))
+    ffn_sent = add_low(both.sent, both.come)
+    for bit in far[3:]:
+        ffn_sent = add_low(ffn_sent, swap(ffn_sent, "dp", bit))
     sent = ride.below(total)
-    come_x = swap(sent, "dp", far[0])
-    come_z = swap(sent, "dp", far[1])
-    come_d = swap_diagonal(sent, far[0], far[1])
-    ffn_d = swap_diagonal(after(ffn_sent, sent), far[0], far[1])
-    come_x, come_z, come_d, ffn_d = lax.optimization_barrier((come_x, come_z, come_d, ffn_d))
+    come_x = swap(sent, "dp", first_bit)
+    come_z = swap(sent, "dp", last_bit)
+    come_d = swap_diagonal(sent, first_bit, last_bit)
+    ffn_sent = after(ffn_sent, sent)
+    ffn_x = swap(ffn_sent, "dp", first_bit)
+    ffn_z = swap(ffn_sent, "dp", last_bit)
+    ffn_d = swap_diagonal(ffn_sent, first_bit, last_bit)
+    come_x, come_z, come_d, ffn_x, ffn_z, ffn_d = lax.optimization_barrier(
+        (come_x, come_z, come_d, ffn_x, ffn_z, ffn_d)
+    )
     flat = total.reshape(-1, width)
     parts = [ride.add(come, flat) for come in (come_x, come_z, come_d)]
     shape = total.shape
@@ -1053,26 +1084,22 @@
     come = swap(sent, "dp", 1)
     ffn_total = after(join_four(ffn_sent, ffn_x, ffn_z, ffn_d, far[0], far[1]), sent)
     ffn_come = swap(ffn_total, "dp", 1)
-    ride.add(come, total)
-    small = ride.rows
-    total_count = count * dp * lax.axis_size("mp")
-    g_query, g_key, g_value, g_out, g_up, g_down = finish(
-        (ffn_total, ffn_come), (total, come)
-    )
+    grads = finish(
+        (ffn_total, ffn_come),
+        (total, come),
+        ride.rows,
+        count * dp * lax.axis_size("mp"),
+    )
+    gain_attn_sum, gain_ffn_sum, gate_sum, mean, histogram = grads[6:]
     return (
         result,
         grad_input,
-        g_query,
-        g_key,
-        g_value,
-        g_out,
-        g_up,
-        g_down,
-        small[4],
-        small[0],
-        small[2],
-        small[1, 0] / total_count,
-        small[3, :BINS] * (BINS / (total_count * NEIGH)),
+        *grads[:6],
+        gain_attn_sum.reshape(width),
+        gain_ffn_sum.reshape(width),
+        gate_sum.reshape(width),
+        mean.reshape(()),
+        histogram.reshape(BINS),
     )
 
 

time: 181 us -> 174 us (0.961)
  starting transfers between devices: 29.3 us -> 23.8 us
  Pallas kernels: 95.6 us -> 97.9 us
    ppermute x25, starting transfers between devices: 24.2 us -> 19 us  [swap(): return lax.ppermute(array, axis, [(i, i ^ bit) for i in range(size)])]
    unnamed x27 -> x49, local copies, waits for them, and re-layouts: 1.88 us -> 5.12 us
    pallas_call x2, Pallas kernels: 26.7 us -> 29.3 us  [attention_forward(): pl.pallas_call(body, grid=(rows, pairs), in_specs=in_specs, out_specs=out...]
    ppermute x25, waiting for transfers between devices: 35.5 us -> 33.6 us  [swap(): return lax.ppermute(array, axis, [(i, i ^ bit) for i in range(size)])]
    ppermute x2 -> x3, starting transfers between devices: 5.15 us -> 4.79 us  [swap_diagonal(): lax.ppermute(array, 'dp', [(i, i ^ first ^ last) for i in range(size)])]
  transfers between devices with their start and end apart: 27 -> 28, of which waited for: 12 -> 10; matrix products, arithmetic and copies ran while one was open for 6% -> 4% of each run, Pallas kernels for 35% -> 37%
where the time goes in v3:
time: 174 us
  Pallas kernels  97.9 us (56%)
  waiting for transfers between devices  35.9 us (21%)
  starting transfers between devices  23.8 us (14%)
  local copies, waits for them, and re-layouts  9.57 us (6%)
  other arithmetic  5.3 us (3%)
    ppermute x25, waiting for transfers between devices, swap(): return lax.ppermute(array, axis, [(i, i ^ bit) for i in range(size)])  33.6 us
    pallas_call x1, Pallas kernels, middle_layer(): pl.pallas_call(middle_body, grid=(tiles,), in_specs=[tiled(width), tiled(...  30 us
    pallas_call x2, Pallas kernels, attention_forward(): pl.pallas_call(body, grid=(rows, pairs), in_specs=in_specs, out_specs=out...  29.3 us
    pallas_call x3, Pallas kernels, attention_backward(): pl.pallas_call(backward_body, grid=(many, rows, 2), in_specs=[pl.BlockSpe...  28.6 us
    ppermute x25, starting transfers between devices, swap(): return lax.ppermute(array, axis, [(i, i ^ bit) for i in range(size)])  19 us
    pallas_call x1, Pallas kernels, input_grad(): pl.pallas_call(input_body, grid=(rows,), in_specs=[row, row, whole(gain),...  6.36 us
    unnamed x49, local copies, waits for them, and re-layouts  5.12 us
    ppermute x3, starting transfers between devices, swap_diagonal(): lax.ppermute(array, 'dp', [(i, i ^ first ^ last) for i in range(size)])  4.79 us
  transfers between devices with their start and end apart: 28, of which 10 were waited for; matrix products, arithmetic and copies ran while one was open for 4% of the time, Pallas kernels for 37%

profile of v3, /device:TPU:0, one launch (start us, length us, event | category | flops | bytes accessed | tf_op | source)
XLA Modules:
  0.0 173.9 jit_solution(9081866060872145706)
XLA Ops:
  0.7 1.0 constant_dynamic-slice_fusion.5
  1.7 1.1 constant_dynamic-slice_fusion.3
  2.8 3.0 %collective-permute-start = (bf16[256,768]{1,0:T(8,128)(2,1)S(1)}, bf16[256,768]{1,0:T(8,128)(2,1)S(1)}, u32[]{:S(2)}, u32[]{:S(2)}) collective-permute-start(bf16[256,768]{1,0:T(8,128)(2,1)S(1)} %pad_maximum_fusion.1), channel_id=1, source_target_pairs={{0,1},{1,0},{2,3},{3,2},{4,5},{5,4},{6,7},{7,6},{8,9},{9,8},{10,11... | collective-permute-start | bytes 1179656 | tf_op jit(solution)/shard_map/ppermute | solution.py:805
  6.0 0.9 constant_dynamic-slice_fusion.1
  7.0 0.2 collective-permute-start.2
  7.2 0.6 copy-done.9
  8.0 15.6 %shard_map.255 = (bf16[2,1024,512]{2,1,0:T(8,128)(2,1)}, bf16[512,768]{1,0:T(8,128)(2,1)}, bf16[2,2,2560,128]{3,2,1,0:T(8,128)(2,1)}, bf16[2,2,2,512,1024]{4,3,2,1,0:T(8,128)(2,1)}, bf16[2,512,256]{2,1,0:T(8,128)(2,1)S(1)}) custom-call(s32[4]{0:T(128)S(1)} %copy-done.13, bf16[2,512,512]{2,1,0:T(8,128)(2,1)} %tok_ref.4, bf16[4,512,512]{2,1,0:T(8,128)(2,1)} %mem_ref.1, ...), custom_call_target="tpu_custom_call" | custom-call | flops 6000000000 | bytes 16777216 | tf_op jit(solution)/shard_map/pallas_call | solution.py:179
  23.6 0.8 copy-done.2
  24.4 1.7 collective-permute-done.1.sibling_ref
  26.1 13.7 %shard_map.256 = (bf16[512,768]{1,0:T(8,128)(2,1)}, bf16[2,2,2560,128]{3,2,1,0:T(8,128)(2,1)}, bf16[2,2,2,512,1024]{4,3,2,1,0:T(8,128)(2,1)}, bf16[2,512,256]{2,1,0:T(8,128)(2,1)S(1)}) custom-call(s32[4]{0:T(128)S(1)} %copy-done.13, bf16[2,1024,512]{2,1,0:T(8,128)(2,1)} %get-tuple-element.90.kv_ref.kv_far, ...), custom_call_target="tpu_custom_call" | custom-call | flops 6000000000 | bytes 16777216 | tf_op jit(solution)/shard_map/pallas_call | solution.py:179
  39.8 0.8 copy-done.14
  40.6 0.7 pad_maximum_fusion.3.gains_ref
  41.3 2.2 %collective-permute-done.3.sibling_far = bf16[1152,512]{1,0:T(8,128)(2,1)S(1)} collective-permute-done((bf16[1152,512]{1,0:T(8,128)(2,1)S(1)}, bf16[1152,512]{1,0:T(8,128)(2,1)S(1)}, u32[]{:S(2)}, u32[]{:S(2)}) %collective-permute-start.3) | collective-permute-done | bytes 1179680 | tf_op jit(solution)/shard_map/ppermute | solution.py:805
  43.5 1.1 copy-done.23
  44.5 30.0 %shard_map.257 = (bf16[2,512,512]{2,1,0:T(8,128)(2,1)}, f32[2,512,512]{2,1,0:T(8,128)}, bf16[2,512,256]{2,1,0:T(8,128)(2,1)}, bf16[2,512,256]{2,1,0:T(8,128)(2,1...) custom-call(bf16[2,512,512]{2,1,0:T(8,128)(2,1)} %tok_ref.4, ...), custom_call_target="tpu_custom_call" | custom-call | flops 15000000512 | bytes 31457280 | tf_op jit(solution)/shard_map/pallas_call | solution.py:444
  74.5 0.2 collective-permute-start.5
  74.7 0.4 collective-permute-start.4
  75.1 0.7 slice.98
  75.8 1.8 %collective-permute-done.5 = bf16[2,576,512]{2,1,0:T(8,128)(2,1)S(1)} collective-permute-done((bf16[2,576,512]{2,1,0:T(8,128)(2,1)}, bf16[2,576,512]{2,1,0:T(8,128)(2,1)S(1)}, u32[]{:S(2)}, u32[]{:S(2)}) %collective-permute-start.5) | collective-permute-done | bytes 1179680 | tf_op jit(solution)/shard_map/ppermute | solution.py:805
  77.7 1.7 add_convert_fusion
  79.3 1.4 collective-permute-start.7
  80.8 0.3 add_convert_fusion.1
  81.1 1.6 collective-permute-start.6
  82.7 13.8 %shard_map.258 = (bf16[2,2,384,512]{3,2,1,0:T(8,128)(2,1)S(1)}, bf16[2,3,128,512]{3,2,1,0:T(8,128)(2,1)S(1)}, f32[2,8,512]{2,1,0:T(8,128)S(1)}) custom-call(s32[4]{0:T(128)S(1)} %copy-done.13, bf16[2,2,2560,128]{3,2,1,0:T(8,128)(2,1)} %get-tuple-element.98.qkv_ref, bf16[2,2,2,512,1024]{4,3,2,1,0:T(8,128)(2,1)} %get-tuple-element.99.p_ref, ...), custom_call_target="tpu_custom_call" | custom-call | flops 8000000000 | bytes 16777216 | tf_op jit(solution)/shard_map/pallas_call | solution.py:612
  96.6 0.2 fusion.2
  96.7 0.9 copy-done.5
  97.6 0.1 collective-permute-start.9
  97.8 0.2 fusion.5
  97.9 0.6 collective-permute-start.10
  98.5 0.3 copy-done
  98.8 0.3 copy-done.1
  99.1 0.1 copy-done.3
  99.2 7.4 %shard_map.259 = (bf16[1,2,384,512]{3,2,1,0:T(8,128)(2,1)S(1)}, bf16[1,3,128,512]{3,2,1,0:T(8,128)(2,1)S(1)}, f32[1,8,512]{2,1,0:T(8,128)S(1)}) custom-call(s32[4]{0:T(128)S(1)} %copy-done.13, bf16[2,2,2560,128]{3,2,1,0:T(8,128)(2,1)} %get-tuple-element.109.qkv_ref, bf16[2,2,2,512,1024]{4,3,2,1,0:T(8,128)(2,1)} %get-tuple-element.110.p_ref, ...), custom_call_target="tpu_custom_call" | custom-call | flops 4000000000 | bytes 8388608 | tf_op jit(solution)/shard_map/pallas_call | solution.py:612
  106.7 0.6 collective-permute-done.10
  107.3 0.4 add_convert_fusion.7
  107.8 1.6 collective-permute-start.11
  109.4 0.1 fusion
  109.6 1.4 collective-permute-start.12
  111.0 7.4 %shard_map.260 = (bf16[1,2,384,512]{3,2,1,0:T(8,128)(2,1)S(1)}, bf16[1,3,128,512]{3,2,1,0:T(8,128)(2,1)S(1)}, f32[1,8,512]{2,1,0:T(8,128)S(1)}) custom-call(s32[4]{0:T(128)S(1)} %copy-done.13, bf16[2,2,2560,128]{3,2,1,0:T(8,128)(2,1)} %get-tuple-element.109.qkv_ref, bf16[2,2,2,512,1024]{4,3,2,1,0:T(8,128)(2,1)} %get-tuple-element.110.p_ref, ...), custom_call_target="tpu_custom_call" | custom-call | flops 4000000000 | bytes 8388608 | tf_op jit(solution)/shard_map/pallas_call | solution.py:612
  118.5 0.5 add_convert_fusion.5
  119.0 2.1 %collective-permute-done.12 = bf16[3,128,512]{2,1,0:T(8,128)(2,1)S(1)} collective-permute-done((bf16[3,128,512]{2,1,0:T(8,128)(2,1)S(1)}, bf16[3,128,512]{2,1,0:T(8,128)(2,1)S(1)}, u32[]{:S(2)}, u32[]{:S(2)}) %collective-permute-start.12) | collective-permute-done | bytes 393248 | tf_op jit(solution)/shard_map/ppermute | solution.py:805
  121.1 0.1 fusion.12
  121.2 1.2 collective-permute-start.14
  122.4 2.4 %collective-permute-start.16 = (bf16[3,32,512]{2,1,0:T(8,128)(2,1)S(1)}, bf16[3,32,512]{2,1,0:T(8,128)(2,1)S(1)}, u32[]{:S(2)}, u32[]{:S(2)}) collective-permute-start(bf16[3,32,512]{2,1,0:T(8,128)(2,1)S(1)} %get-tuple-element.173), channel_id=1, source_target_pairs={{0,12},{2,14},{4,8},{6,10},{8,4},{10,6},{12,0},{14,2},{16,28},{18,... | collective-permute-start | bytes 294920 | tf_op jit(solution)/shard_map/ppermute | solution.py:831
  124.8 2.6 %collective-permute-start.19 = (bf16[288,512]{1,0:T(8,128)(2,1)S(1)}, bf16[288,512]{1,0:T(8,128)(2,1)S(1)}, u32[]{:S(2)}, u32[]{:S(2)}) collective-permute-start(bf16[288,512]{1,0:T(8,128)(2,1)S(1)} %add_convert_fusion.5), channel_id=1, source_target_pairs={{0,16},{2,18},{4,20},{6,22},{8,24},{10,26},{12,28},{14,30},{16,0},... | collective-permute-start | bytes 884744 | tf_op jit(solution)/shard_map/ppermute | solution.py:805
  127.4 1.3 collective-permute-start.17
  128.7 6.4 %shard_map.261 = bf16[2,512,512]{2,1,0:T(8,128)(2,1)} custom-call(bf16[2,512,512]{2,1,0:T(8,128)(2,1)} %tok_ref.4, f32[2,512,512]{2,1,0:T(8,128)} %get-tuple-element.134.grad_hidden_ref, f32[1,512]{1,0:T(1,128)} %bitcast.77, bf16[2,2,384,512]{3,2,1,0:T(8,128)(2,1)} %copy-done.5, bf16[1,2,384,512]{3,2,1,0:T(8,128)(2,1)} %copy-done.7, ...), custom_call_target="tpu_custom_call" | custom-call | flops 2000000000 | bytes 8388608 | tf_op jit(solution)/shard_map/pallas_call | solution.py:693
  135.3 0.1 concatenate.137
  135.4 0.4 collective-permute-start.18
  135.8 8.9 %collective-permute-done.18 = bf16[112,512]{1,0:T(8,128)(2,1)S(1)} collective-permute-done((bf16[112,512]{1,0:T(8,128)(2,1)S(1)}, bf16[112,512]{1,0:T(8,128)(2,1)S(1)}, u32[]{:S(2)}, u32[]{:S(2)}) %collective-permute-start.18) | collective-permute-done | bytes 114720 | tf_op jit(solution)/shard_map/ppermute | solution.py:805
  144.9 0.1 concatenate.138
  145.0 1.2 collective-permute-start.23
  146.2 2.4 %collective-permute-start.25 = (bf16[288,512]{1,0:T(8,128)(2,1)S(1)}, bf16[288,512]{1,0:T(8,128)(2,1)S(1)}, u32[]{:S(2)}, u32[]{:S(2)}) collective-permute-start(bf16[288,512]{1,0:T(8,128)(2,1)S(1)} %add_convert_fusion.4), channel_id=1, source_target_pairs={{0,12},{2,14},{4,8},{6,10},{8,4},{10,6},{12,0},{14,2},{16,28},{18,... | collective-permute-start | bytes 884744 | tf_op jit(solution)/shard_map/ppermute | solution.py:831
  148.6 1.1 collective-permute-start.20
  149.7 9.9 %collective-permute-done.20 = bf16[112,512]{1,0:T(8,128)(2,1)S(1)} collective-permute-done((bf16[112,512]{1,0:T(8,128)(2,1)S(1)}, bf16[112,512]{1,0:T(8,128)(2,1)S(1)}, u32[]{:S(2)}, u32[]{:S(2)}) %collective-permute-start.20) | collective-permute-done | bytes 114720 | tf_op jit(solution)/shard_map/ppermute | solution.py:805
  159.6 3.3 %collective-permute-done.21 = bf16[112,512]{1,0:T(8,128)(2,1)S(1)} collective-permute-done((bf16[112,512]{1,0:T(8,128)(2,1)S(1)}, bf16[112,512]{1,0:T(8,128)(2,1)S(1)}, u32[]{:S(2)}, u32[]{:S(2)}) %collective-permute-start.21) | collective-permute-done | bytes 114720 | tf_op jit(solution)/shard_map/ppermute | solution.py:805
  163.0 2.3 %collective-permute-done.22 = bf16[112,512]{1,0:T(8,128)(2,1)S(1)} collective-permute-done((bf16[112,512]{1,0:T(8,128)(2,1)S(1)}, bf16[112,512]{1,0:T(8,128)(2,1)S(1)}, u32[]{:S(2)}, u32[]{:S(2)}) %collective-permute-start.22) | collective-permute-done | bytes 114720 | tf_op jit(solution)/shard_map/ppermute | solution.py:831
  165.6 0.2 maximum_select_fusion.1
  165.8 0.2 maximum_select_fusion.2
  166.1 0.2 maximum_select_fusion.ffn_mine
  166.3 0.3 concatenate.159
  166.6 0.5 collective-permute-start.27
  167.1 2.9 %collective-permute-done.27.attn_sibling = bf16[400,512]{1,0:T(8,128)(2,1)S(1)} collective-permute-done((bf16[400,512]{1,0:T(8,128)(2,1)S(1)}, bf16[400,512]{1,0:T(8,128)(2,1)S(1)}, u32[]{:S(2)}, u32[]{:S(2)}) %collective-permute-start.27) | collective-permute-done | bytes 409632 | tf_op jit(solution)/shard_map/ppermute | solution.py:805
  170.0 3.7 %shard_map.262 = (f32[512,256]{1,0:T(8,128)}, f32[512,256]{1,0:T(8,128)}, f32[512,256]{1,0:T(8,128)}, f32[256,512]{1,0:T(8,128)}, f32[512,1024]{1,0:T(8,128)}, /...) custom-call(bf16[2,576,512]{2,1,0:T(8,128)(2,1)S(1)} %maximum_select, ...), custom_call_target="tpu_custom_call" | custom-call | tf_op jit(solution)/shard_map/pallas_call | solution.py:791
  (97 shorter events, 1.2 us)
Async XLA Ops:
  0.6 5.2 %copy-start.19 = (bf16[1024,512]{1,0:T(8,128)(2,1)S(1)}, bf16[1024,512]{1,0:T(8,128)(2,1)}, u32[]{:S(2)}) copy-start(bf16[1024,512]{1,0:T(8,128)(2,1)} %down_far.1) | copy-start | bytes 3145732
  1.7 4.2 %copy-start.18 = (bf16[512,1024]{1,0:T(8,128)(2,1)S(1)}, bf16[512,1024]{1,0:T(8,128)(2,1)}, u32[]{:S(2)}) copy-start(bf16[512,1024]{1,0:T(8,128)(2,1)} %up_far.1) | copy-start | bytes 3145732
  2.8 21.6 %collective-permute-start = (bf16[256,768]{1,0:T(8,128)(2,1)S(1)}, bf16[256,768]{1,0:T(8,128)(2,1)S(1)}, u32[]{:S(2)}, u32[]{:S(2)}) collective-permute-start(bf16[256,768]{1,0:T(8,128)(2,1)S(1)} %pad_maximum_fusion.1), channel_id=1, source_target_pairs={{0,1},{1,0},{2,3},{3,2},{4,5},{5,4},{6,7},{7,6},{8,9},{9,8},{10,11... | collective-permute-start | bytes 1179656 | tf_op jit(solution)/shard_map/ppermute | solution.py:805
  6.9 1.0 copy-start.9
  6.9 1.0 copy-start.10
  6.9 1.1 copy-start.11
  6.9 1.1 copy-start.12
  6.9 1.1 copy-start.13
  7.0 33.6 %collective-permute-start.2 = (bf16[1152,512]{1,0:T(8,128)(2,1)S(1)}, bf16[1152,512]{1,0:T(8,128)(2,1)S(1)}, u32[]{:S(2)}, u32[]{:S(2)}) collective-permute-start(bf16[1152,512]{1,0:T(8,128)(2,1)S(1)} %pad_maximum_fusion), channel_id=1, source_target_pairs={{0,1},{1,0},{2,3},{3,2},{4,5},{5,4},{6,7},{7,6},{8,9},{9,8},{10,11... | collective-permute-start | bytes 3538952 | tf_op jit(solution)/shard_map/ppermute | solution.py:805
  23.6 0.8 copy-start.2
  24.4 16.2 %copy-start.20 = (f32[512]{0:T(512)S(1)}, f32[512]{0:T(512)}, u32[]{:S(2)}) copy-start(f32[512]{0:T(512)} %param.30) | copy-start | bytes 6148
  24.4 16.2 %copy-start.21 = (f32[512]{0:T(512)S(1)}, f32[512]{0:T(512)}, u32[]{:S(2)}) copy-start(f32[512]{0:T(512)} %param.29) | copy-start | bytes 6148
  24.4 1.7 collective-permute-start.1
  39.8 0.8 copy-start.14
  40.6 2.9 %copy-start.22 = (bf16[1152,512]{1,0:T(8,128)(2,1)}, bf16[1152,512]{1,0:T(8,128)(2,1)S(1)}, u32[]{:S(2)}) copy-start(bf16[1152,512]{1,0:T(8,128)(2,1)S(1)} %collective-permute-done.2.mine_far) | copy-start | bytes 3538948
  40.6 2.8 %collective-permute-start.3 = (bf16[1152,512]{1,0:T(8,128)(2,1)S(1)}, bf16[1152,512]{1,0:T(8,128)(2,1)S(1)}, u32[]{:S(2)}, u32[]{:S(2)}) collective-permute-start(bf16[1152,512]{1,0:T(8,128)(2,1)S(1)} %collective-permute-done.2.mine_far), channel_id=1, source_target_pairs={{0,2},{2,0},{4,6},{6,4},{8,10},{10,8},{12,14},{14,12},{16,18},{18,... | collective-permute-start | bytes 3538952 | tf_op jit(solution)/shard_map/ppermute | solution.py:805
  43.5 1.1 copy-start.23
  74.5 3.1 %collective-permute-start.5 = (bf16[2,576,512]{2,1,0:T(8,128)(2,1)}, bf16[2,576,512]{2,1,0:T(8,128)(2,1)S(1)}, u32[]{:S(2)}, u32[]{:S(2)}) collective-permute-start(bf16[2,576,512]{2,1,0:T(8,128)(2,1)} %get-tuple-element.104), channel_id=1, source_target_pairs={{0,2},{2,0},{4,6},{6,4},{8,10},{10,8},{12,14},{14,12},{16,18},{18,... | collective-permute-start | bytes 3538952 | tf_op jit(solution)/shard_map/ppermute | solution.py:805
  74.7 6.0 %collective-permute-start.4 = (bf16[2,576,512]{2,1,0:T(8,128)(2,1)}, bf16[2,576,512]{2,1,0:T(8,128)(2,1)S(1)}, u32[]{:S(2)}, u32[]{:S(2)}) collective-permute-start(bf16[2,576,512]{2,1,0:T(8,128)(2,1)} %get-tuple-element.102), channel_id=1, source_target_pairs={{0,2},{2,0},{4,6},{6,4},{8,10},{10,8},{12,14},{14,12},{16,18},{18,... | collective-permute-start | bytes 3538952 | tf_op jit(solution)/shard_map/ppermute | solution.py:805
  77.6 3.1 %copy-start.17 = (bf16[2,576,512]{2,1,0:T(8,128)(2,1)S(1)}, bf16[2,576,512]{2,1,0:T(8,128)(2,1)}, u32[]{:S(2)}) copy-start(bf16[2,576,512]{2,1,0:T(8,128)(2,1)} %get-tuple-element.101) | copy-start | bytes 3538948
  79.3 17.2 %collective-permute-start.7 = (bf16[576,512]{1,0:T(8,128)(2,1)S(1)}, bf16[576,512]{1,0:T(8,128)(2,1)S(1)}, u32[]{:S(2)}, u32[]{:S(2)}) collective-permute-start(bf16[576,512]{1,0:T(8,128)(2,1)S(1)} %get-tuple-element.170), channel_id=1, source_target_pairs={{0,1},{1,0},{2,3},{3,2},{4,5},{5,4},{6,7},{7,6},{8,9},{9,8},{10,11... | collective-permute-start | bytes 1769480 | tf_op jit(solution)/shard_map/ppermute | solution.py:805
  80.8 1.9 %copy-start.6 = (bf16[512,768]{1,0:T(8,128)(2,1)S(1)}, bf16[512,768]{1,0:T(8,128)(2,1)}, u32[]{:S(2)}) copy-start(bf16[512,768]{1,0:T(8,128)(2,1)} %get-tuple-element.107.pack_ref.oth_pack_ref) | copy-start | bytes 2359300
  80.8 1.9 %copy-start.15 = (bf16[2,512,256]{2,1,0:T(8,128)(2,1)S(1)}, bf16[2,512,256]{2,1,0:T(8,128)(2,1)}, u32[]{:S(2)}) copy-start(bf16[2,512,256]{2,1,0:T(8,128)(2,1)} %copy-done.14) | copy-start | bytes 1572868
  80.8 1.9 %copy-start.16 = (bf16[2,512,256]{2,1,0:T(8,128)(2,1)S(1)}, bf16[2,512,256]{2,1,0:T(8,128)(2,1)}, u32[]{:S(2)}) copy-start(bf16[2,512,256]{2,1,0:T(8,128)(2,1)} %get-tuple-element.106.gctx_ref) | copy-start | bytes 1572868
  81.1 16.5 %collective-permute-start.6 = (bf16[2,288,512]{2,1,0:T(8,128)(2,1)S(1)}, bf16[2,288,512]{2,1,0:T(8,128)(2,1)S(1)}, u32[]{:S(2)}, u32[]{:S(2)}) collective-permute-start(bf16[2,288,512]{2,1,0:T(8,128)(2,1)S(1)} %get-tuple-element.105), channel_id=1, source_target_pairs={{0,4},{2,6},{4,0},{6,2},{8,12},{10,14},{12,8},{14,10},{16,20},{18,... | collective-permute-start | bytes 1769480 | tf_op jit(solution)/shard_map/ppermute | solution.py:805
  96.5 1.2 copy-start.5
  96.5 2.0 %copy-start.4 = (bf16[2,512,256]{2,1,0:T(8,128)(2,1)S(1)}, bf16[2,512,256]{2,1,0:T(8,128)(2,1)}, u32[]{:S(2)}) copy-start(bf16[2,512,256]{2,1,0:T(8,128)(2,1)} %get-tuple-element.126.gctx_ref) | copy-start | bytes 1572868
  96.6 2.2 %copy-start = (bf16[2,1024,512]{2,1,0:T(8,128)(2,1)S(1)}, bf16[2,1024,512]{2,1,0:T(8,128)(2,1)}, u32[]{:S(2)}) copy-start(bf16[2,1024,512]{2,1,0:T(8,128)(2,1)} %get-tuple-element.90.kv_ref.kv_far) | copy-start | bytes 6291460
  97.6 1.5 copy-start.1
  97.6 1.6 copy-start.3
  97.6 9.7 %collective-permute-start.9 = (bf16[288,512]{1,0:T(8,128)(2,1)S(1)}, bf16[288,512]{1,0:T(8,128)(2,1)S(1)}, u32[]{:S(2)}, u32[]{:S(2)}) collective-permute-start(bf16[288,512]{1,0:T(8,128)(2,1)S(1)} %get-tuple-element.179), channel_id=1, source_target_pairs={{0,4},{2,6},{4,0},{6,2},{8,12},{10,14},{12,8},{14,10},{16,20},{18,... | collective-permute-start | bytes 884744 | tf_op jit(solution)/shard_map/ppermute | solution.py:805
  97.9 9.3 %collective-permute-start.10 = (bf16[288,512]{1,0:T(8,128)(2,1)S(1)}, bf16[288,512]{1,0:T(8,128)(2,1)S(1)}, u32[]{:S(2)}, u32[]{:S(2)}) collective-permute-start(bf16[288,512]{1,0:T(8,128)(2,1)S(1)} %get-tuple-element.115), channel_id=1, source_target_pairs={{0,1},{1,0},{2,3},{3,2},{4,5},{5,4},{6,7},{7,6},{8,9},{9,8},{10,11... | collective-permute-start | bytes 884744 | tf_op jit(solution)/shard_map/ppermute | solution.py:805
  98.5 10.9 %collective-permute-start.8 = (bf16[3,128,512]{2,1,0:T(8,128)(2,1)S(1)}, bf16[3,128,512]{2,1,0:T(8,128)(2,1)S(1)}, u32[]{:S(2)}, u32[]{:S(2)}) collective-permute-start(bf16[3,128,512]{2,1,0:T(8,128)(2,1)S(1)} %slice_bitcast_fusion), channel_id=1, source_target_pairs={{0,2},{2,0},{4,6},{6,4},{8,10},{10,8},{12,14},{14,12},{16,18},{18,... | collective-permute-start | bytes 1179656 | tf_op jit(solution)/shard_map/ppermute | solution.py:805
  106.6 1.1 copy-start.7
  107.8 10.7 %collective-permute-start.11 = (bf16[288,512]{1,0:T(8,128)(2,1)S(1)}, bf16[288,512]{1,0:T(8,128)(2,1)S(1)}, u32[]{:S(2)}, u32[]{:S(2)}) collective-permute-start(bf16[288,512]{1,0:T(8,128)(2,1)S(1)} %add_convert_fusion.7), channel_id=1, source_target_pairs={{0,8},{2,10},{4,12},{6,14},{8,0},{10,2},{12,4},{14,6},{16,24},{18,... | collective-permute-start | bytes 884744 | tf_op jit(solution)/shard_map/ppermute | solution.py:805
  109.5 9.5 %collective-permute-start.13 = (bf16[3,128,512]{2,1,0:T(8,128)(2,1)S(1)}, bf16[3,128,512]{2,1,0:T(8,128)(2,1)S(1)}, u32[]{:S(2)}, u32[]{:S(2)}) collective-permute-start(bf16[3,128,512]{2,1,0:T(8,128)(2,1)S(1)} %bitcast.79), channel_id=1, source_target_pairs={{0,2},{2,0},{4,6},{6,4},{8,10},{10,8},{12,14},{14,12},{16,18},{18,... | collective-permute-start | bytes 1179656 | tf_op jit(solution)/shard_map/ppermute | solution.py:805
  109.6 11.5 %collective-permute-start.12 = (bf16[3,128,512]{2,1,0:T(8,128)(2,1)S(1)}, bf16[3,128,512]{2,1,0:T(8,128)(2,1)S(1)}, u32[]{:S(2)}, u32[]{:S(2)}) collective-permute-start(bf16[3,128,512]{2,1,0:T(8,128)(2,1)S(1)} %fusion), channel_id=1, source_target_pairs={{0,1},{1,0},{2,3},{3,2},{4,5},{5,4},{6,7},{7,6},{8,9},{9,8},{10,11... | collective-permute-start | bytes 1179656 | tf_op jit(solution)/shard_map/ppermute | solution.py:805
  118.4 2.8 %copy-start.8 = (bf16[1,2,384,512]{3,2,1,0:T(8,128)(2,1)}, bf16[1,2,384,512]{3,2,1,0:T(8,128)(2,1)S(1)}, u32[]{:S(2)}) copy-start(bf16[1,2,384,512]{3,2,1,0:T(8,128)(2,1)S(1)} %get-tuple-element.137.own_last_ref) | copy-start | bytes 2359300
  121.2 13.9 %collective-permute-start.14 = (bf16[3,32,512]{2,1,0:T(8,128)(2,1)S(1)}, bf16[3,32,512]{2,1,0:T(8,128)(2,1)S(1)}, u32[]{:S(2)}, u32[]{:S(2)}) collective-permute-start(bf16[3,32,512]{2,1,0:T(8,128)(2,1)S(1)} %get-tuple-element.175), channel_id=1, source_target_pairs={{0,4},{2,6},{4,0},{6,2},{8,12},{10,14},{12,8},{14,10},{16,20},{18,... | collective-permute-start | bytes 294920 | tf_op jit(solution)/shard_map/ppermute | solution.py:805
  122.4 12.7 %collective-permute-start.15 = (bf16[3,32,512]{2,1,0:T(8,128)(2,1)S(1)}, bf16[3,32,512]{2,1,0:T(8,128)(2,1)S(1)}, u32[]{:S(2)}, u32[]{:S(2)}) collective-permute-start(bf16[3,32,512]{2,1,0:T(8,128)(2,1)S(1)} %get-tuple-element.174), channel_id=1, source_target_pairs={{0,8},{2,10},{4,12},{6,14},{8,0},{10,2},{12,4},{14,6},{16,24},{18,... | collective-permute-start | bytes 294920 | tf_op jit(solution)/shard_map/ppermute | solution.py:805
  122.4 12.7 %collective-permute-start.16 = (bf16[3,32,512]{2,1,0:T(8,128)(2,1)S(1)}, bf16[3,32,512]{2,1,0:T(8,128)(2,1)S(1)}, u32[]{:S(2)}, u32[]{:S(2)}) collective-permute-start(bf16[3,32,512]{2,1,0:T(8,128)(2,1)S(1)} %get-tuple-element.173), channel_id=1, source_target_pairs={{0,12},{2,14},{4,8},{6,10},{8,4},{10,6},{12,0},{14,2},{16,28},{18,... | collective-permute-start | bytes 294920 | tf_op jit(solution)/shard_map/ppermute | solution.py:831
  124.8 19.9 %collective-permute-start.19 = (bf16[288,512]{1,0:T(8,128)(2,1)S(1)}, bf16[288,512]{1,0:T(8,128)(2,1)S(1)}, u32[]{:S(2)}, u32[]{:S(2)}) collective-permute-start(bf16[288,512]{1,0:T(8,128)(2,1)S(1)} %add_convert_fusion.5), channel_id=1, source_target_pairs={{0,16},{2,18},{4,20},{6,22},{8,24},{10,26},{12,28},{14,30},{16,0},... | collective-permute-start | bytes 884744 | tf_op jit(solution)/shard_map/ppermute | solution.py:805
  127.4 7.7 %collective-permute-start.17 = (f32[5,512]{1,0:T(8,128)S(1)}, f32[5,512]{1,0:T(8,128)S(1)}, u32[]{:S(2)}, u32[]{:S(2)}) collective-permute-start(f32[5,512]{1,0:T(8,128)S(1)} %pad_maximum_fusion.2), channel_id=1, source_target_pairs={{0,1},{1,0},{2,3},{3,2},{4,5},{5,4},{6,7},{7,6},{8,9},{9,8},{10,11... | collective-permute-start | bytes 30728 | tf_op jit(solution)/shard_map/ppermute | solution.py:805
  135.4 9.3 %collective-permute-start.18 = (bf16[112,512]{1,0:T(8,128)(2,1)S(1)}, bf16[112,512]{1,0:T(8,128)(2,1)S(1)}, u32[]{:S(2)}, u32[]{:S(2)}) collective-permute-start(bf16[112,512]{1,0:T(8,128)(2,1)S(1)} %concatenate.137), channel_id=1, source_target_pairs={{0,16},{2,18},{4,20},{6,22},{8,24},{10,26},{12,28},{14,30},{16,0},... | collective-permute-start | bytes 344072 | tf_op jit(solution)/shard_map/ppermute | solution.py:805
  145.0 20.3 %collective-permute-start.23 = (bf16[288,512]{1,0:T(8,128)(2,1)S(1)}, bf16[288,512]{1,0:T(8,128)(2,1)S(1)}, u32[]{:S(2)}, u32[]{:S(2)}) collective-permute-start(bf16[288,512]{1,0:T(8,128)(2,1)S(1)} %add_convert_fusion.4), channel_id=1, source_target_pairs={{0,4},{2,6},{4,0},{6,2},{8,12},{10,14},{12,8},{14,10},{16,20},{18,... | collective-permute-start | bytes 884744 | tf_op jit(solution)/shard_map/ppermute | solution.py:805
  146.2 19.1 %collective-permute-start.24 = (bf16[288,512]{1,0:T(8,128)(2,1)S(1)}, bf16[288,512]{1,0:T(8,128)(2,1)S(1)}, u32[]{:S(2)}, u32[]{:S(2)}) collective-permute-start(bf16[288,512]{1,0:T(8,128)(2,1)S(1)} %add_convert_fusion.4), channel_id=1, source_target_pairs={{0,8},{2,10},{4,12},{6,14},{8,0},{10,2},{12,4},{14,6},{16,24},{18,... | collective-permute-start | bytes 884744 | tf_op jit(solution)/shard_map/ppermute | solution.py:805
  146.2 19.1 %collective-permute-start.25 = (bf16[288,512]{1,0:T(8,128)(2,1)S(1)}, bf16[288,512]{1,0:T(8,128)(2,1)S(1)}, u32[]{:S(2)}, u32[]{:S(2)}) collective-permute-start(bf16[288,512]{1,0:T(8,128)(2,1)S(1)} %add_convert_fusion.4), channel_id=1, source_target_pairs={{0,12},{2,14},{4,8},{6,10},{8,4},{10,6},{12,0},{14,2},{16,28},{18,... | collective-permute-start | bytes 884744 | tf_op jit(solution)/shard_map/ppermute | solution.py:831
  148.6 11.0 %collective-permute-start.20 = (bf16[112,512]{1,0:T(8,128)(2,1)S(1)}, bf16[112,512]{1,0:T(8,128)(2,1)S(1)}, u32[]{:S(2)}, u32[]{:S(2)}) collective-permute-start(bf16[112,512]{1,0:T(8,128)(2,1)S(1)} %concatenate.138), channel_id=1, source_target_pairs={{0,4},{2,6},{4,0},{6,2},{8,12},{10,14},{12,8},{14,10},{16,20},{18,... | collective-permute-start | bytes 344072 | tf_op jit(solution)/shard_map/ppermute | solution.py:805
  149.7 13.3 %collective-permute-start.21 = (bf16[112,512]{1,0:T(8,128)(2,1)S(1)}, bf16[112,512]{1,0:T(8,128)(2,1)S(1)}, u32[]{:S(2)}, u32[]{:S(2)}) collective-permute-start(bf16[112,512]{1,0:T(8,128)(2,1)S(1)} %concatenate.138), channel_id=1, source_target_pairs={{0,8},{2,10},{4,12},{6,14},{8,0},{10,2},{12,4},{14,6},{16,24},{18,... | collective-permute-start | bytes 344072 | tf_op jit(solution)/shard_map/ppermute | solution.py:805
  159.6 5.7 %collective-permute-start.22 = (bf16[112,512]{1,0:T(8,128)(2,1)S(1)}, bf16[112,512]{1,0:T(8,128)(2,1)S(1)}, u32[]{:S(2)}, u32[]{:S(2)}) collective-permute-start(bf16[112,512]{1,0:T(8,128)(2,1)S(1)} %concatenate.138), channel_id=1, source_target_pairs={{0,12},{2,14},{4,8},{6,10},{8,4},{10,6},{12,0},{14,2},{16,28},{18,... | collective-permute-start | bytes 344072 | tf_op jit(solution)/shard_map/ppermute | solution.py:831
  166.5 3.5 %collective-permute-start.26 = (bf16[2,576,512]{2,1,0:T(8,128)(2,1)S(1)}, bf16[2,576,512]{2,1,0:T(8,128)(2,1)S(1)}, u32[]{:S(2)}, u32[]{:S(2)}) collective-permute-start(bf16[2,576,512]{2,1,0:T(8,128)(2,1)S(1)} %maximum_select_fusion.ffn_mine), channel_id=1, source_target_pairs={{0,2},{2,0},{4,6},{6,4},{8,10},{10,8},{12,14},{14,12},{16,18},{18,... | collective-permute-start | bytes 3538952 | tf_op jit(solution)/shard_map/ppermute | solution.py:805
  166.6 3.4 %collective-permute-start.27 = (bf16[400,512]{1,0:T(8,128)(2,1)S(1)}, bf16[400,512]{1,0:T(8,128)(2,1)S(1)}, u32[]{:S(2)}, u32[]{:S(2)}) collective-permute-start(bf16[400,512]{1,0:T(8,128)(2,1)S(1)} %concatenate.159), channel_id=1, source_target_pairs={{0,2},{2,0},{4,6},{6,4},{8,10},{10,8},{12,14},{14,12},{16,18},{18,... | collective-permute-start | bytes 1228808 | tf_op jit(solution)/shard_map/ppermute | solution.py:805

commit v4 on v3

--- a/solution.py
+++ b/solution.py
@@ -1006,10 +1006,10 @@
     down.add(da_first)
     both = Chain(None, 0)
     both.pieces = tuple(lax.concatenate([u, d], 0) for u, d in zip(up.pieces, down.pieces))
-    sent = both.halve(far[1])
-    attn_sent = after(attn.total(), sent)
+    attn_sent = attn.total()
     attn_come = swap(attn_sent, "mp", 1)
-    first_sent = after(da_first, attn_sent)
+    sent = both.halve(far[1], attn_sent)
+    first_sent = after(da_first, sent)
     first_come = swap(first_sent, "dp", 1)
     g_own_last, da_last, gain_last = attention_backward(
         doc_starts, own, after(gctx_own, first_sent), kv, 0, 1
@@ -1028,15 +1028,15 @@
         size = piece.shape[1] // 4
         return lax.dynamic_slice_in_dim(piece, at * size, size, 1)
 
-    sent_x = attn.total(lambda p: quarter(p, 1, 0))
+    sent = both.send(far[2])
+    sent_x = after(attn.total(lambda p: quarter(p, 1, 0)), sent)
     sent_z = attn.total(lambda p: quarter(p, 0, 1))
     sent_d = attn.total(lambda p: quarter(p, 1, 1))
     kept = attn.total(lambda p: quarter(p, 0, 0))
     come_x = swap(sent_x, "dp", first_bit)
     come_z = swap(sent_z, "dp", last_bit)
     come_d = swap_diagonal(sent_d, first_bit, last_bit)
-    sent = both.send(far[2], sent_x, sent_z, sent_d)
-    small_sent = after(small, sent)
+    small_sent = after(small, sent_x, sent_z, sent_d)
     small_come = swap(small_sent, "mp", 1)
     grad_input = input_grad(
         tokens,
@@ -1050,23 +1050,23 @@
     )[:4]
     ride = Ride(small_sent + small_come)
     total = sum(part.astype(F32) for part in (kept, come_x, come_z, come_d)).astype(BF16)
+    ffn_x = ffn_z = None
     for bit in far[2:]:
         sent = ride.below(total)
         come = swap(sent, "dp", bit)
         if bit == far[2]:
-            come, both.come = lax.optimization_barrier((come, both.come))
+            ffn_sent = add_low(both.sent, after(both.come, sent))
+            for far_bit in far[3:]:
+                ffn_sent = add_low(ffn_sent, swap(ffn_sent, "dp", far_bit))
+            ffn_x = swap(ffn_sent, "dp", first_bit)
+            ffn_z = swap(ffn_sent, "dp", last_bit)
+            ffn_d = swap_diagonal(ffn_sent, first_bit, last_bit)
+            come = after(come, ffn_sent)
         total = add_low(total, ride.add(come, total))
-    ffn_sent = add_low(both.sent, both.come)
-    for bit in far[3:]:
-        ffn_sent = add_low(ffn_sent, swap(ffn_sent, "dp", bit))
     sent = ride.below(total)
     come_x = swap(sent, "dp", first_bit)
     come_z = swap(sent, "dp", last_bit)
     come_d = swap_diagonal(sent, first_bit, last_bit)
-    ffn_sent = after(ffn_sent, sent)
-    ffn_x = swap(ffn_sent, "dp", first_bit)
-    ffn_z = swap(ffn_sent, "dp", last_bit)
-    ffn_d = swap_diagonal(ffn_sent, first_bit, last_bit)
     come_x, come_z, come_d, ffn_x, ffn_z, ffn_d = lax.optimization_barrier(
         (come_x, come_z, come_d, ffn_x, ffn_z, ffn_d)
     )

time: 174 us -> 167 us (0.960)
  waiting for transfers between devices: 35.9 us -> 25.2 us
  starting transfers between devices: 23.8 us -> 32.9 us
  Pallas kernels: 97.9 us -> 92.7 us
    ppermute x25, waiting for transfers between devices: 33.6 us -> 22.5 us  [swap(): return lax.ppermute(array, axis, [(i, i ^ bit) for i in range(size)])]
    ppermute x25, starting transfers between devices: 19 us -> 29.8 us  [swap(): return lax.ppermute(array, axis, [(i, i ^ bit) for i in range(size)])]
    pallas_call x2, Pallas kernels: 29.3 us -> 26.3 us  [attention_forward(): pl.pallas_call(body, grid=(rows, pairs), in_specs=in_specs, out_specs=out...]
    pallas_call x3, Pallas kernels: 28.6 us -> 26.4 us  [attention_backward(): pl.pallas_call(backward_body, grid=(many, rows, 2), in_specs=[pl.BlockSpe...]
  transfers between devices with their start and end apart: 28 -> 28, of which waited for: 10 -> 11; matrix products, arithmetic and copies ran while one was open for 4% -> 4% of each run, Pallas kernels for 37% -> 35%
where the time goes in v4:
time: 167 us; the launch traced here: 166 us
  Pallas kernels  92.7 us (56%)
  starting transfers between devices  32.9 us (20%)
  waiting for transfers between devices  25.2 us (15%)
  local copies, waits for them, and re-layouts  8.87 us (5%)
  other arithmetic  5.29 us (3%)
    pallas_call x1, Pallas kernels, middle_layer(): pl.pallas_call(middle_body, grid=(tiles,), in_specs=[tiled(width), tiled(...  30 us
    ppermute x25, starting transfers between devices, swap(): return lax.ppermute(array, axis, [(i, i ^ bit) for i in range(size)])  29.8 us
    pallas_call x3, Pallas kernels, attention_backward(): pl.pallas_call(backward_body, grid=(many, rows, 2), in_specs=[pl.BlockSpe...  26.4 us
    pallas_call x2, Pallas kernels, attention_forward(): pl.pallas_call(body, grid=(rows, pairs), in_specs=in_specs, out_specs=out...  26.3 us
    ppermute x25, waiting for transfers between devices, swap(): return lax.ppermute(array, axis, [(i, i ^ bit) for i in range(size)])  22.5 us
    pallas_call x1, Pallas kernels, input_grad(): pl.pallas_call(input_body, grid=(rows,), in_specs=[row, row, whole(gain),...  6.36 us
    unnamed x49, local copies, waits for them, and re-layouts  4.43 us
    pallas_call x1, Pallas kernels, finish(): pl.pallas_call(functools.partial(finish_body, tokens=tokens), grid=(1,),...  3.68 us
  transfers between devices with their start and end apart: 28, of which 11 were waited for; matrix products, arithmetic and copies ran while one was open for 4% of the time, Pallas kernels for 35%

profile of v4, /device:TPU:0, one launch (start us, length us, event | category | flops | bytes accessed | tf_op | source)
XLA Modules:
  0.0 166.3 jit_solution(16543929803293777292)
XLA Ops:
  0.7 1.0 constant_dynamic-slice_fusion.5
  1.7 1.1 constant_dynamic-slice_fusion.3
  2.8 3.0 %collective-permute-start = (bf16[256,768]{1,0:T(8,128)(2,1)S(1)}, bf16[256,768]{1,0:T(8,128)(2,1)S(1)}, u32[]{:S(2)}, u32[]{:S(2)}) collective-permute-start(bf16[256,768]{1,0:T(8,128)(2,1)S(1)} %pad_maximum_fusion.1), channel_id=1, source_target_pairs={{0,1},{1,0},{2,3},{3,2},{4,5},{5,4},{6,7},{7,6},{8,9},{9,8},{10,11... | collective-permute-start | bytes 1179656 | tf_op jit(solution)/shard_map/ppermute | solution.py:805
  6.0 0.9 constant_dynamic-slice_fusion.1
  7.0 0.2 collective-permute-start.2
  7.2 0.6 copy-done.9
  8.0 14.1 %shard_map.255 = (bf16[2,1024,512]{2,1,0:T(8,128)(2,1)}, bf16[512,768]{1,0:T(8,128)(2,1)}, bf16[2,2,2560,128]{3,2,1,0:T(8,128)(2,1)}, bf16[2,2,2,512,1024]{4,3,2,1,0:T(8,128)(2,1)}, bf16[2,512,256]{2,1,0:T(8,128)(2,1)S(1)}) custom-call(s32[4]{0:T(128)S(1)} %copy-done.13, bf16[2,512,512]{2,1,0:T(8,128)(2,1)} %tok_ref.4, bf16[4,512,512]{2,1,0:T(8,128)(2,1)} %mem_ref.1, ...), custom_call_target="tpu_custom_call" | custom-call | flops 6000000000 | bytes 16777216 | tf_op jit(solution)/shard_map/pallas_call | solution.py:179
  22.1 0.8 copy-done.2
  22.9 1.1 collective-permute-start.1
  24.0 1.3 collective-permute-done.1.sibling_ref
  25.3 12.2 %shard_map.256 = (bf16[512,768]{1,0:T(8,128)(2,1)}, bf16[2,2,2560,128]{3,2,1,0:T(8,128)(2,1)}, bf16[2,2,2,512,1024]{4,3,2,1,0:T(8,128)(2,1)}, bf16[2,512,256]{2,1,0:T(8,128)(2,1)S(1)}) custom-call(s32[4]{0:T(128)S(1)} %copy-done.13, bf16[2,1024,512]{2,1,0:T(8,128)(2,1)} %get-tuple-element.89.kv_ref.kv_far, ...), custom_call_target="tpu_custom_call" | custom-call | flops 6000000000 | bytes 16777216 | tf_op jit(solution)/shard_map/pallas_call | solution.py:179
  37.6 0.8 copy-done.14
  38.4 1.9 %collective-permute-done.2.mine_far = bf16[1152,512]{1,0:T(8,128)(2,1)S(1)} collective-permute-done((bf16[1152,512]{1,0:T(8,128)(2,1)S(1)}, bf16[1152,512]{1,0:T(8,128)(2,1)S(1)}, u32[]{:S(2)}, u32[]{:S(2)}) %collective-permute-start.2) | collective-permute-done | bytes 1179680 | tf_op jit(solution)/shard_map/ppermute | solution.py:805
  40.3 0.6 pad_maximum_fusion.3.gains_ref
  40.9 2.2 %collective-permute-done.3.sibling_far = bf16[1152,512]{1,0:T(8,128)(2,1)S(1)} collective-permute-done((bf16[1152,512]{1,0:T(8,128)(2,1)S(1)}, bf16[1152,512]{1,0:T(8,128)(2,1)S(1)}, u32[]{:S(2)}, u32[]{:S(2)}) %collective-permute-start.3) | collective-permute-done | bytes 1179680 | tf_op jit(solution)/shard_map/ppermute | solution.py:805
  43.1 1.1 copy-done.23
  44.2 30.0 %shard_map.257 = (bf16[2,512,512]{2,1,0:T(8,128)(2,1)}, f32[2,512,512]{2,1,0:T(8,128)}, bf16[2,512,256]{2,1,0:T(8,128)(2,1)}, bf16[2,512,256]{2,1,0:T(8,128)(2,1...) custom-call(bf16[2,512,512]{2,1,0:T(8,128)(2,1)} %tok_ref.4, ...), custom_call_target="tpu_custom_call" | custom-call | flops 15000000512 | bytes 31457280 | tf_op jit(solution)/shard_map/pallas_call | solution.py:444
  74.2 0.2 collective-permute-start.5
  74.4 0.4 collective-permute-start.4
  74.7 0.7 slice.98
  75.5 1.8 %collective-permute-done.5 = bf16[2,576,512]{2,1,0:T(8,128)(2,1)S(1)} collective-permute-done((bf16[2,576,512]{2,1,0:T(8,128)(2,1)}, bf16[2,576,512]{2,1,0:T(8,128)(2,1)S(1)}, u32[]{:S(2)}, u32[]{:S(2)}) %collective-permute-start.5) | collective-permute-done | bytes 1179680 | tf_op jit(solution)/shard_map/ppermute | solution.py:805
  77.3 1.7 add_convert_fusion
  79.0 1.8 %collective-permute-start.7 = (bf16[576,512]{1,0:T(8,128)(2,1)S(1)}, bf16[576,512]{1,0:T(8,128)(2,1)S(1)}, u32[]{:S(2)}, u32[]{:S(2)}) collective-permute-start(bf16[576,512]{1,0:T(8,128)(2,1)S(1)} %get-tuple-element.168), channel_id=1, source_target_pairs={{0,1},{1,0},{2,3},{3,2},{4,5},{5,4},{6,7},{7,6},{8,9},{9,8},{10,11... | collective-permute-start | bytes 1769480 | tf_op jit(solution)/shard_map/ppermute | solution.py:805
  80.8 0.3 add_convert_fusion.1
  81.1 1.6 collective-permute-start.6
  82.7 12.8 %shard_map.258 = (bf16[2,2,384,512]{3,2,1,0:T(8,128)(2,1)S(1)}, bf16[2,3,128,512]{3,2,1,0:T(8,128)(2,1)S(1)}, f32[2,8,512]{2,1,0:T(8,128)S(1)}) custom-call(s32[4]{0:T(128)S(1)} %copy-done.13, bf16[2,2,2560,128]{3,2,1,0:T(8,128)(2,1)} %get-tuple-element.97.qkv_ref, bf16[2,2,2,512,1024]{4,3,2,1,0:T(8,128)(2,1)} %get-tuple-element.98.p_ref, ...), custom_call_target="tpu_custom_call" | custom-call | flops 8000000000 | bytes 16777216 | tf_op jit(solution)/shard_map/pallas_call | solution.py:612
  95.6 0.2 fusion.2
  95.7 0.9 copy-done.5
  96.6 1.1 collective-permute-start.8
  97.8 0.2 fusion.5
  97.9 1.4 collective-permute-start.9
  99.3 6.8 %shard_map.259 = (bf16[1,2,384,512]{3,2,1,0:T(8,128)(2,1)S(1)}, bf16[1,3,128,512]{3,2,1,0:T(8,128)(2,1)S(1)}, f32[1,8,512]{2,1,0:T(8,128)S(1)}) custom-call(s32[4]{0:T(128)S(1)} %copy-done.13, bf16[2,2,2560,128]{3,2,1,0:T(8,128)(2,1)} %get-tuple-element.108.qkv_ref, bf16[2,2,2,512,1024]{4,3,2,1,0:T(8,128)(2,1)} %get-tuple-element.109.p_ref, ...), custom_call_target="tpu_custom_call" | custom-call | flops 4000000000 | bytes 8388608 | tf_op jit(solution)/shard_map/pallas_call | solution.py:612
  106.2 1.1 collective-permute-done.9
  107.3 0.4 add_convert_fusion.7
  107.8 0.1 fusion
  107.9 1.6 collective-permute-start.13
  109.6 1.6 collective-permute-start.11
  111.1 6.8 %shard_map.260 = (bf16[1,2,384,512]{3,2,1,0:T(8,128)(2,1)S(1)}, bf16[1,3,128,512]{3,2,1,0:T(8,128)(2,1)S(1)}, f32[1,8,512]{2,1,0:T(8,128)S(1)}) custom-call(s32[4]{0:T(128)S(1)} %copy-done.13, bf16[2,2,2560,128]{3,2,1,0:T(8,128)(2,1)} %get-tuple-element.108.qkv_ref, bf16[2,2,2,512,1024]{4,3,2,1,0:T(8,128)(2,1)} %get-tuple-element.109.p_ref, ...), custom_call_target="tpu_custom_call" | custom-call | flops 4000000000 | bytes 8388608 | tf_op jit(solution)/shard_map/pallas_call | solution.py:612
  118.0 0.5 add_convert_fusion.5
  118.5 2.5 %collective-permute-start.14 = (bf16[288,512]{1,0:T(8,128)(2,1)S(1)}, bf16[288,512]{1,0:T(8,128)(2,1)S(1)}, u32[]{:S(2)}, u32[]{:S(2)}) collective-permute-start(bf16[288,512]{1,0:T(8,128)(2,1)S(1)} %add_convert_fusion.5), channel_id=1, source_target_pairs={{0,16},{2,18},{4,20},{6,22},{8,24},{10,26},{12,28},{14,30},{16,0},... | collective-permute-start | bytes 884744 | tf_op jit(solution)/shard_map/ppermute | solution.py:805
  121.1 0.1 fusion.12
  121.2 1.2 collective-permute-start.15
  122.4 0.8 collective-permute-start.16
  123.2 1.6 collective-permute-start.17
  124.8 1.4 collective-permute-start.18
  126.2 6.4 %shard_map.261 = bf16[2,512,512]{2,1,0:T(8,128)(2,1)} custom-call(bf16[2,512,512]{2,1,0:T(8,128)(2,1)} %tok_ref.4, f32[2,512,512]{2,1,0:T(8,128)} %get-tuple-element.133.grad_hidden_ref, f32[1,512]{1,0:T(1,128)} %bitcast.77, bf16[2,2,384,512]{3,2,1,0:T(8,128)(2,1)} %copy-done.5, bf16[1,2,384,512]{3,2,1,0:T(8,128)(2,1)} %copy-done.7, ...), custom_call_target="tpu_custom_call" | custom-call | flops 2000000000 | bytes 8388608 | tf_op jit(solution)/shard_map/pallas_call | solution.py:693
  132.6 0.1 add_convert_fusion.10
  132.7 0.1 concatenate.137
  132.8 1.8 %collective-permute-start.19 = (bf16[112,512]{1,0:T(8,128)(2,1)S(1)}, bf16[112,512]{1,0:T(8,128)(2,1)S(1)}, u32[]{:S(2)}, u32[]{:S(2)}) collective-permute-start(bf16[112,512]{1,0:T(8,128)(2,1)S(1)} %concatenate.137), channel_id=1, source_target_pairs={{0,16},{2,18},{4,20},{6,22},{8,24},{10,26},{12,28},{14,30},{16,0},... | collective-permute-start | bytes 344072 | tf_op jit(solution)/shard_map/ppermute | solution.py:805
  134.6 0.4 collective-permute-done.14
  135.1 3.3 %collective-permute-start.23 = (bf16[288,512]{1,0:T(8,128)(2,1)S(1)}, bf16[288,512]{1,0:T(8,128)(2,1)S(1)}, u32[]{:S(2)}, u32[]{:S(2)}) collective-permute-start(bf16[288,512]{1,0:T(8,128)(2,1)S(1)} %add_convert_fusion.4), channel_id=1, source_target_pairs={{0,4},{2,6},{4,0},{6,2},{8,12},{10,14},{12,8},{14,10},{16,20},{18,... | collective-permute-start | bytes 884744 | tf_op jit(solution)/shard_map/ppermute | solution.py:805
  138.4 1.5 collective-permute-start.25
  140.1 0.1 concatenate.139
  140.2 4.1 %collective-permute-start.20 = (bf16[112,512]{1,0:T(8,128)(2,1)S(1)}, bf16[112,512]{1,0:T(8,128)(2,1)S(1)}, u32[]{:S(2)}, u32[]{:S(2)}) collective-permute-start(bf16[112,512]{1,0:T(8,128)(2,1)S(1)} %concatenate.139), channel_id=1, source_target_pairs={{0,4},{2,6},{4,0},{6,2},{8,12},{10,14},{12,8},{14,10},{16,20},{18,... | collective-permute-start | bytes 344072 | tf_op jit(solution)/shard_map/ppermute | solution.py:805
  144.3 4.8 %collective-permute-done.20 = bf16[112,512]{1,0:T(8,128)(2,1)S(1)} collective-permute-done((bf16[112,512]{1,0:T(8,128)(2,1)S(1)}, bf16[112,512]{1,0:T(8,128)(2,1)S(1)}, u32[]{:S(2)}, u32[]{:S(2)}) %collective-permute-start.20) | collective-permute-done | bytes 114720 | tf_op jit(solution)/shard_map/ppermute | solution.py:805
  149.2 5.9 %collective-permute-done.21 = bf16[112,512]{1,0:T(8,128)(2,1)S(1)} collective-permute-done((bf16[112,512]{1,0:T(8,128)(2,1)S(1)}, bf16[112,512]{1,0:T(8,128)(2,1)S(1)}, u32[]{:S(2)}, u32[]{:S(2)}) %collective-permute-start.21) | collective-permute-done | bytes 114720 | tf_op jit(solution)/shard_map/ppermute | solution.py:805
  155.1 2.7 %collective-permute-done.22 = bf16[112,512]{1,0:T(8,128)(2,1)S(1)} collective-permute-done((bf16[112,512]{1,0:T(8,128)(2,1)S(1)}, bf16[112,512]{1,0:T(8,128)(2,1)S(1)}, u32[]{:S(2)}, u32[]{:S(2)}) %collective-permute-start.22) | collective-permute-done | bytes 114720 | tf_op jit(solution)/shard_map/ppermute | solution.py:831
  158.1 0.2 maximum_select_fusion.1
  158.3 0.2 maximum_select_fusion.2
  158.5 0.2 maximum_select_fusion.ffn_mine
  158.7 0.3 concatenate.159
  159.1 0.5 collective-permute-start.27
  159.6 2.9 %collective-permute-done.27.attn_sibling = bf16[400,512]{1,0:T(8,128)(2,1)S(1)} collective-permute-done((bf16[400,512]{1,0:T(8,128)(2,1)S(1)}, bf16[400,512]{1,0:T(8,128)(2,1)S(1)}, u32[]{:S(2)}, u32[]{:S(2)}) %collective-permute-start.27) | collective-permute-done | bytes 409632 | tf_op jit(solution)/shard_map/ppermute | solution.py:805
  162.5 3.7 %shard_map.262 = (f32[512,256]{1,0:T(8,128)}, f32[512,256]{1,0:T(8,128)}, f32[512,256]{1,0:T(8,128)}, f32[256,512]{1,0:T(8,128)}, f32[512,1024]{1,0:T(8,128)}, /...) custom-call(bf16[2,576,512]{2,1,0:T(8,128)(2,1)S(1)} %maximum_select, ...), custom_call_target="tpu_custom_call" | custom-call | tf_op jit(solution)/shard_map/pallas_call | solution.py:791
  (97 shorter events, 1.1 us)
Async XLA Ops:
  0.6 5.2 %copy-start.19 = (bf16[1024,512]{1,0:T(8,128)(2,1)S(1)}, bf16[1024,512]{1,0:T(8,128)(2,1)}, u32[]{:S(2)}) copy-start(bf16[1024,512]{1,0:T(8,128)(2,1)} %down_far.1) | copy-start | bytes 3145732
  1.7 4.2 %copy-start.18 = (bf16[512,1024]{1,0:T(8,128)(2,1)S(1)}, bf16[512,1024]{1,0:T(8,128)(2,1)}, u32[]{:S(2)}) copy-start(bf16[512,1024]{1,0:T(8,128)(2,1)} %up_far.1) | copy-start | bytes 3145732
  2.8 20.1 %collective-permute-start = (bf16[256,768]{1,0:T(8,128)(2,1)S(1)}, bf16[256,768]{1,0:T(8,128)(2,1)S(1)}, u32[]{:S(2)}, u32[]{:S(2)}) collective-permute-start(bf16[256,768]{1,0:T(8,128)(2,1)S(1)} %pad_maximum_fusion.1), channel_id=1, source_target_pairs={{0,1},{1,0},{2,3},{3,2},{4,5},{5,4},{6,7},{7,6},{8,9},{9,8},{10,11... | collective-permute-start | bytes 1179656 | tf_op jit(solution)/shard_map/ppermute | solution.py:805
  6.9 1.0 copy-start.9
  6.9 1.0 copy-start.10
  6.9 1.1 copy-start.11
  6.9 1.1 copy-start.12
  6.9 1.1 copy-start.13
  7.0 33.2 %collective-permute-start.2 = (bf16[1152,512]{1,0:T(8,128)(2,1)S(1)}, bf16[1152,512]{1,0:T(8,128)(2,1)S(1)}, u32[]{:S(2)}, u32[]{:S(2)}) collective-permute-start(bf16[1152,512]{1,0:T(8,128)(2,1)S(1)} %pad_maximum_fusion), channel_id=1, source_target_pairs={{0,1},{1,0},{2,3},{3,2},{4,5},{5,4},{6,7},{7,6},{8,9},{9,8},{10,11... | collective-permute-start | bytes 3538952 | tf_op jit(solution)/shard_map/ppermute | solution.py:805
  22.1 0.8 copy-start.2
  22.9 17.4 %copy-start.20 = (f32[512]{0:T(512)S(1)}, f32[512]{0:T(512)}, u32[]{:S(2)}) copy-start(f32[512]{0:T(512)} %param.30) | copy-start | bytes 6148
  22.9 17.4 %copy-start.21 = (f32[512]{0:T(512)S(1)}, f32[512]{0:T(512)}, u32[]{:S(2)}) copy-start(f32[512]{0:T(512)} %param.29) | copy-start | bytes 6148
  22.9 2.4 %collective-permute-start.1 = (bf16[256,768]{1,0:T(8,128)(2,1)S(1)}, bf16[256,768]{1,0:T(8,128)(2,1)S(1)}, u32[]{:S(2)}, u32[]{:S(2)}) collective-permute-start(bf16[256,768]{1,0:T(8,128)(2,1)S(1)} %collective-permute-done.mine_ref), channel_id=1, source_target_pairs={{0,2},{2,0},{4,6},{6,4},{8,10},{10,8},{12,14},{14,12},{16,18},{18,... | collective-permute-start | bytes 1179656 | tf_op jit(solution)/shard_map/ppermute | solution.py:805
  37.6 0.8 copy-start.14
  40.2 2.9 %copy-start.22 = (bf16[1152,512]{1,0:T(8,128)(2,1)}, bf16[1152,512]{1,0:T(8,128)(2,1)S(1)}, u32[]{:S(2)}) copy-start(bf16[1152,512]{1,0:T(8,128)(2,1)S(1)} %collective-permute-done.2.mine_far) | copy-start | bytes 3538948
  40.2 2.8 %collective-permute-start.3 = (bf16[1152,512]{1,0:T(8,128)(2,1)S(1)}, bf16[1152,512]{1,0:T(8,128)(2,1)S(1)}, u32[]{:S(2)}, u32[]{:S(2)}) collective-permute-start(bf16[1152,512]{1,0:T(8,128)(2,1)S(1)} %collective-permute-done.2.mine_far), channel_id=1, source_target_pairs={{0,2},{2,0},{4,6},{6,4},{8,10},{10,8},{12,14},{14,12},{16,18},{18,... | collective-permute-start | bytes 3538952 | tf_op jit(solution)/shard_map/ppermute | solution.py:805
  43.1 1.1 copy-start.23
  74.2 3.1 %collective-permute-start.5 = (bf16[2,576,512]{2,1,0:T(8,128)(2,1)}, bf16[2,576,512]{2,1,0:T(8,128)(2,1)S(1)}, u32[]{:S(2)}, u32[]{:S(2)}) collective-permute-start(bf16[2,576,512]{2,1,0:T(8,128)(2,1)} %get-tuple-element.103), channel_id=1, source_target_pairs={{0,2},{2,0},{4,6},{6,4},{8,10},{10,8},{12,14},{14,12},{16,18},{18,... | collective-permute-start | bytes 3538952 | tf_op jit(solution)/shard_map/ppermute | solution.py:805
  74.4 6.4 %collective-permute-start.4 = (bf16[2,576,512]{2,1,0:T(8,128)(2,1)}, bf16[2,576,512]{2,1,0:T(8,128)(2,1)S(1)}, u32[]{:S(2)}, u32[]{:S(2)}) collective-permute-start(bf16[2,576,512]{2,1,0:T(8,128)(2,1)} %get-tuple-element.101), channel_id=1, source_target_pairs={{0,2},{2,0},{4,6},{6,4},{8,10},{10,8},{12,14},{14,12},{16,18},{18,... | collective-permute-start | bytes 3538952 | tf_op jit(solution)/shard_map/ppermute | solution.py:805
  77.3 3.5 %copy-start.17 = (bf16[2,576,512]{2,1,0:T(8,128)(2,1)S(1)}, bf16[2,576,512]{2,1,0:T(8,128)(2,1)}, u32[]{:S(2)}) copy-start(bf16[2,576,512]{2,1,0:T(8,128)(2,1)} %get-tuple-element.100) | copy-start | bytes 3538948
  79.0 16.6 %collective-permute-start.7 = (bf16[576,512]{1,0:T(8,128)(2,1)S(1)}, bf16[576,512]{1,0:T(8,128)(2,1)S(1)}, u32[]{:S(2)}, u32[]{:S(2)}) collective-permute-start(bf16[576,512]{1,0:T(8,128)(2,1)S(1)} %get-tuple-element.168), channel_id=1, source_target_pairs={{0,1},{1,0},{2,3},{3,2},{4,5},{5,4},{6,7},{7,6},{8,9},{9,8},{10,11... | collective-permute-start | bytes 1769480 | tf_op jit(solution)/shard_map/ppermute | solution.py:805
  80.8 1.9 %copy-start.6 = (bf16[512,768]{1,0:T(8,128)(2,1)S(1)}, bf16[512,768]{1,0:T(8,128)(2,1)}, u32[]{:S(2)}) copy-start(bf16[512,768]{1,0:T(8,128)(2,1)} %get-tuple-element.106.pack_ref.oth_pack_ref) | copy-start | bytes 2359300
  80.8 1.9 %copy-start.15 = (bf16[2,512,256]{2,1,0:T(8,128)(2,1)S(1)}, bf16[2,512,256]{2,1,0:T(8,128)(2,1)}, u32[]{:S(2)}) copy-start(bf16[2,512,256]{2,1,0:T(8,128)(2,1)} %copy-done.14) | copy-start | bytes 1572868
  80.8 1.9 %copy-start.16 = (bf16[2,512,256]{2,1,0:T(8,128)(2,1)S(1)}, bf16[2,512,256]{2,1,0:T(8,128)(2,1)}, u32[]{:S(2)}) copy-start(bf16[2,512,256]{2,1,0:T(8,128)(2,1)} %get-tuple-element.105.gctx_ref) | copy-start | bytes 1572868
  81.1 15.5 %collective-permute-start.6 = (bf16[2,288,512]{2,1,0:T(8,128)(2,1)S(1)}, bf16[2,288,512]{2,1,0:T(8,128)(2,1)S(1)}, u32[]{:S(2)}, u32[]{:S(2)}) collective-permute-start(bf16[2,288,512]{2,1,0:T(8,128)(2,1)S(1)} %get-tuple-element.104), channel_id=1, source_target_pairs={{0,4},{2,6},{4,0},{6,2},{8,12},{10,14},{12,8},{14,10},{16,20},{18,... | collective-permute-start | bytes 1769480 | tf_op jit(solution)/shard_map/ppermute | solution.py:805
  95.5 1.2 copy-start.5
  95.5 3.8 %copy-start.4 = (bf16[2,512,256]{2,1,0:T(8,128)(2,1)S(1)}, bf16[2,512,256]{2,1,0:T(8,128)(2,1)}, u32[]{:S(2)}) copy-start(bf16[2,512,256]{2,1,0:T(8,128)(2,1)} %get-tuple-element.125.gctx_ref) | copy-start | bytes 1572868
  95.5 3.8 %copy-start = (bf16[2,1024,512]{2,1,0:T(8,128)(2,1)S(1)}, bf16[2,1024,512]{2,1,0:T(8,128)(2,1)}, u32[]{:S(2)}) copy-start(bf16[2,1024,512]{2,1,0:T(8,128)(2,1)} %get-tuple-element.89.kv_ref.kv_far) | copy-start | bytes 6291460
  96.6 2.7 %copy-start.1 = (bf16[512,768]{1,0:T(8,128)(2,1)S(1)}, bf16[512,768]{1,0:T(8,128)(2,1)}, u32[]{:S(2)}) copy-start(bf16[512,768]{1,0:T(8,128)(2,1)} %get-tuple-element.117.pack_ref.own_pack_ref) | copy-start | bytes 2359300
  96.6 2.7 %copy-start.3 = (bf16[2,512,256]{2,1,0:T(8,128)(2,1)S(1)}, bf16[2,512,256]{2,1,0:T(8,128)(2,1)}, u32[]{:S(2)}) copy-start(bf16[2,512,256]{2,1,0:T(8,128)(2,1)} %copy-done.2) | copy-start | bytes 1572868
  96.6 10.7 %collective-permute-start.8 = (bf16[288,512]{1,0:T(8,128)(2,1)S(1)}, bf16[288,512]{1,0:T(8,128)(2,1)S(1)}, u32[]{:S(2)}, u32[]{:S(2)}) collective-permute-start(bf16[288,512]{1,0:T(8,128)(2,1)S(1)} %get-tuple-element.177), channel_id=1, source_target_pairs={{0,4},{2,6},{4,0},{6,2},{8,12},{10,14},{12,8},{14,10},{16,20},{18,... | collective-permute-start | bytes 884744 | tf_op jit(solution)/shard_map/ppermute | solution.py:805
  97.9 9.3 %collective-permute-start.9 = (bf16[288,512]{1,0:T(8,128)(2,1)S(1)}, bf16[288,512]{1,0:T(8,128)(2,1)S(1)}, u32[]{:S(2)}, u32[]{:S(2)}) collective-permute-start(bf16[288,512]{1,0:T(8,128)(2,1)S(1)} %get-tuple-element.114), channel_id=1, source_target_pairs={{0,1},{1,0},{2,3},{3,2},{4,5},{5,4},{6,7},{7,6},{8,9},{9,8},{10,11... | collective-permute-start | bytes 884744 | tf_op jit(solution)/shard_map/ppermute | solution.py:805
  99.3 8.5 %collective-permute-start.10 = (bf16[3,128,512]{2,1,0:T(8,128)(2,1)S(1)}, bf16[3,128,512]{2,1,0:T(8,128)(2,1)S(1)}, u32[]{:S(2)}, u32[]{:S(2)}) collective-permute-start(bf16[3,128,512]{2,1,0:T(8,128)(2,1)S(1)} %slice_bitcast_fusion), channel_id=1, source_target_pairs={{0,2},{2,0},{4,6},{6,4},{8,10},{10,8},{12,14},{14,12},{16,18},{18,... | collective-permute-start | bytes 1179656 | tf_op jit(solution)/shard_map/ppermute | solution.py:805
  106.2 1.6 copy-start.7
  107.9 10.1 %collective-permute-start.13 = (bf16[288,512]{1,0:T(8,128)(2,1)S(1)}, bf16[288,512]{1,0:T(8,128)(2,1)S(1)}, u32[]{:S(2)}, u32[]{:S(2)}) collective-permute-start(bf16[288,512]{1,0:T(8,128)(2,1)S(1)} %add_convert_fusion.7), channel_id=1, source_target_pairs={{0,8},{2,10},{4,12},{6,14},{8,0},{10,2},{12,4},{14,6},{16,24},{18,... | collective-permute-start | bytes 884744 | tf_op jit(solution)/shard_map/ppermute | solution.py:805
  109.5 11.5 %collective-permute-start.12 = (bf16[3,128,512]{2,1,0:T(8,128)(2,1)S(1)}, bf16[3,128,512]{2,1,0:T(8,128)(2,1)S(1)}, u32[]{:S(2)}, u32[]{:S(2)}) collective-permute-start(bf16[3,128,512]{2,1,0:T(8,128)(2,1)S(1)} %bitcast.79), channel_id=1, source_target_pairs={{0,2},{2,0},{4,6},{6,4},{8,10},{10,8},{12,14},{14,12},{16,18},{18,... | collective-permute-start | bytes 1179656 | tf_op jit(solution)/shard_map/ppermute | solution.py:805
  109.6 11.5 %collective-permute-start.11 = (bf16[3,128,512]{2,1,0:T(8,128)(2,1)S(1)}, bf16[3,128,512]{2,1,0:T(8,128)(2,1)S(1)}, u32[]{:S(2)}, u32[]{:S(2)}) collective-permute-start(bf16[3,128,512]{2,1,0:T(8,128)(2,1)S(1)} %fusion), channel_id=1, source_target_pairs={{0,1},{1,0},{2,3},{3,2},{4,5},{5,4},{6,7},{7,6},{8,9},{9,8},{10,11... | collective-permute-start | bytes 1179656 | tf_op jit(solution)/shard_map/ppermute | solution.py:805
  117.9 3.3 %copy-start.8 = (bf16[1,2,384,512]{3,2,1,0:T(8,128)(2,1)}, bf16[1,2,384,512]{3,2,1,0:T(8,128)(2,1)S(1)}, u32[]{:S(2)}) copy-start(bf16[1,2,384,512]{3,2,1,0:T(8,128)(2,1)S(1)} %get-tuple-element.136.own_last_ref) | copy-start | bytes 2359300
  118.5 16.6 %collective-permute-start.14 = (bf16[288,512]{1,0:T(8,128)(2,1)S(1)}, bf16[288,512]{1,0:T(8,128)(2,1)S(1)}, u32[]{:S(2)}, u32[]{:S(2)}) collective-permute-start(bf16[288,512]{1,0:T(8,128)(2,1)S(1)} %add_convert_fusion.5), channel_id=1, source_target_pairs={{0,16},{2,18},{4,20},{6,22},{8,24},{10,26},{12,28},{14,30},{16,0},... | collective-permute-start | bytes 884744 | tf_op jit(solution)/shard_map/ppermute | solution.py:805
  121.2 11.3 %collective-permute-start.15 = (bf16[3,32,512]{2,1,0:T(8,128)(2,1)S(1)}, bf16[3,32,512]{2,1,0:T(8,128)(2,1)S(1)}, u32[]{:S(2)}, u32[]{:S(2)}) collective-permute-start(bf16[3,32,512]{2,1,0:T(8,128)(2,1)S(1)} %get-tuple-element.131), channel_id=1, source_target_pairs={{0,4},{2,6},{4,0},{6,2},{8,12},{10,14},{12,8},{14,10},{16,20},{18,... | collective-permute-start | bytes 294920 | tf_op jit(solution)/shard_map/ppermute | solution.py:805
  122.4 10.1 %collective-permute-start.16 = (bf16[3,32,512]{2,1,0:T(8,128)(2,1)S(1)}, bf16[3,32,512]{2,1,0:T(8,128)(2,1)S(1)}, u32[]{:S(2)}, u32[]{:S(2)}) collective-permute-start(bf16[3,32,512]{2,1,0:T(8,128)(2,1)S(1)} %get-tuple-element.172), channel_id=1, source_target_pairs={{0,8},{2,10},{4,12},{6,14},{8,0},{10,2},{12,4},{14,6},{16,24},{18,... | collective-permute-start | bytes 294920 | tf_op jit(solution)/shard_map/ppermute | solution.py:805
  123.2 9.4 %collective-permute-start.17 = (bf16[3,32,512]{2,1,0:T(8,128)(2,1)S(1)}, bf16[3,32,512]{2,1,0:T(8,128)(2,1)S(1)}, u32[]{:S(2)}, u32[]{:S(2)}) collective-permute-start(bf16[3,32,512]{2,1,0:T(8,128)(2,1)S(1)} %get-tuple-element.171), channel_id=1, source_target_pairs={{0,12},{2,14},{4,8},{6,10},{8,4},{10,6},{12,0},{14,2},{16,28},{18,... | collective-permute-start | bytes 294920 | tf_op jit(solution)/shard_map/ppermute | solution.py:831
  124.8 7.8 %collective-permute-start.18 = (f32[5,512]{1,0:T(8,128)S(1)}, f32[5,512]{1,0:T(8,128)S(1)}, u32[]{:S(2)}, u32[]{:S(2)}) collective-permute-start(f32[5,512]{1,0:T(8,128)S(1)} %pad_maximum_fusion.2), channel_id=1, source_target_pairs={{0,1},{1,0},{2,3},{3,2},{4,5},{5,4},{6,7},{7,6},{8,9},{9,8},{10,11... | collective-permute-start | bytes 30728 | tf_op jit(solution)/shard_map/ppermute | solution.py:805
  132.8 7.1 %collective-permute-start.19 = (bf16[112,512]{1,0:T(8,128)(2,1)S(1)}, bf16[112,512]{1,0:T(8,128)(2,1)S(1)}, u32[]{:S(2)}, u32[]{:S(2)}) collective-permute-start(bf16[112,512]{1,0:T(8,128)(2,1)S(1)} %concatenate.137), channel_id=1, source_target_pairs={{0,16},{2,18},{4,20},{6,22},{8,24},{10,26},{12,28},{14,30},{16,0},... | collective-permute-start | bytes 344072 | tf_op jit(solution)/shard_map/ppermute | solution.py:805
  135.1 22.7 %collective-permute-start.23 = (bf16[288,512]{1,0:T(8,128)(2,1)S(1)}, bf16[288,512]{1,0:T(8,128)(2,1)S(1)}, u32[]{:S(2)}, u32[]{:S(2)}) collective-permute-start(bf16[288,512]{1,0:T(8,128)(2,1)S(1)} %add_convert_fusion.4), channel_id=1, source_target_pairs={{0,4},{2,6},{4,0},{6,2},{8,12},{10,14},{12,8},{14,10},{16,20},{18,... | collective-permute-start | bytes 884744 | tf_op jit(solution)/shard_map/ppermute | solution.py:805
  138.4 19.3 %collective-permute-start.24 = (bf16[288,512]{1,0:T(8,128)(2,1)S(1)}, bf16[288,512]{1,0:T(8,128)(2,1)S(1)}, u32[]{:S(2)}, u32[]{:S(2)}) collective-permute-start(bf16[288,512]{1,0:T(8,128)(2,1)S(1)} %add_convert_fusion.4), channel_id=1, source_target_pairs={{0,8},{2,10},{4,12},{6,14},{8,0},{10,2},{12,4},{14,6},{16,24},{18,... | collective-permute-start | bytes 884744 | tf_op jit(solution)/shard_map/ppermute | solution.py:805
  138.4 19.3 %collective-permute-start.25 = (bf16[288,512]{1,0:T(8,128)(2,1)S(1)}, bf16[288,512]{1,0:T(8,128)(2,1)S(1)}, u32[]{:S(2)}, u32[]{:S(2)}) collective-permute-start(bf16[288,512]{1,0:T(8,128)(2,1)S(1)} %add_convert_fusion.4), channel_id=1, source_target_pairs={{0,12},{2,14},{4,8},{6,10},{8,4},{10,6},{12,0},{14,2},{16,28},{18,... | collective-permute-start | bytes 884744 | tf_op jit(solution)/shard_map/ppermute | solution.py:831
  140.2 9.0 %collective-permute-start.20 = (bf16[112,512]{1,0:T(8,128)(2,1)S(1)}, bf16[112,512]{1,0:T(8,128)(2,1)S(1)}, u32[]{:S(2)}, u32[]{:S(2)}) collective-permute-start(bf16[112,512]{1,0:T(8,128)(2,1)S(1)} %concatenate.139), channel_id=1, source_target_pairs={{0,4},{2,6},{4,0},{6,2},{8,12},{10,14},{12,8},{14,10},{16,20},{18,... | collective-permute-start | bytes 344072 | tf_op jit(solution)/shard_map/ppermute | solution.py:805
  144.3 10.7 %collective-permute-start.21 = (bf16[112,512]{1,0:T(8,128)(2,1)S(1)}, bf16[112,512]{1,0:T(8,128)(2,1)S(1)}, u32[]{:S(2)}, u32[]{:S(2)}) collective-permute-start(bf16[112,512]{1,0:T(8,128)(2,1)S(1)} %concatenate.139), channel_id=1, source_target_pairs={{0,8},{2,10},{4,12},{6,14},{8,0},{10,2},{12,4},{14,6},{16,24},{18,... | collective-permute-start | bytes 344072 | tf_op jit(solution)/shard_map/ppermute | solution.py:805
  149.2 8.6 %collective-permute-start.22 = (bf16[112,512]{1,0:T(8,128)(2,1)S(1)}, bf16[112,512]{1,0:T(8,128)(2,1)S(1)}, u32[]{:S(2)}, u32[]{:S(2)}) collective-permute-start(bf16[112,512]{1,0:T(8,128)(2,1)S(1)} %concatenate.139), channel_id=1, source_target_pairs={{0,12},{2,14},{4,8},{6,10},{8,4},{10,6},{12,0},{14,2},{16,28},{18,... | collective-permute-start | bytes 344072 | tf_op jit(solution)/shard_map/ppermute | solution.py:831
  159.0 3.5 %collective-permute-start.26 = (bf16[2,576,512]{2,1,0:T(8,128)(2,1)S(1)}, bf16[2,576,512]{2,1,0:T(8,128)(2,1)S(1)}, u32[]{:S(2)}, u32[]{:S(2)}) collective-permute-start(bf16[2,576,512]{2,1,0:T(8,128)(2,1)S(1)} %maximum_select_fusion.ffn_mine), channel_id=1, source_target_pairs={{0,2},{2,0},{4,6},{6,4},{8,10},{10,8},{12,14},{14,12},{16,18},{18,... | collective-permute-start | bytes 3538952 | tf_op jit(solution)/shard_map/ppermute | solution.py:805
  159.1 3.4 %collective-permute-start.27 = (bf16[400,512]{1,0:T(8,128)(2,1)S(1)}, bf16[400,512]{1,0:T(8,128)(2,1)S(1)}, u32[]{:S(2)}, u32[]{:S(2)}) collective-permute-start(bf16[400,512]{1,0:T(8,128)(2,1)S(1)} %concatenate.159), channel_id=1, source_target_pairs={{0,2},{2,0},{4,6},{6,4},{8,10},{10,8},{12,14},{14,12},{16,18},{18,... | collective-permute-start | bytes 1228808 | tf_op jit(solution)/shard_map/ppermute | solution.py:805

commit v5 on v4

--- a/solution.py
+++ b/solution.py
@@ -213,7 +213,8 @@
     mine_far,
     sibling_far,
     edges_ref,
-    gains_ref,
+    gain_ref,
+    wgate_ref,
     result_ref,
     grad_hidden_ref,
     gctx_own_ref,
@@ -282,8 +283,8 @@
         at = pl.ds(2 * width, half // 2)
         return jnp.concatenate([oth_ref[0, at, :], oth_ref[1, at, :]], 0)
 
-    wgate = gains_ref[pl.ds(1, 1), :]
-    gain = gains_ref[pl.ds(0, 1), :]
+    wgate = wgate_ref[...]
+    gain = gain_ref[...]
 
     def front():
         ctx_ref[here, pl.ds(0, half)] = ctx_own_ref[0]
@@ -315,11 +316,19 @@
         ffn_in_ref[here, :] = (normal * gain).astype(BF16)
         return hidden, weights, gate, mixed, normal, rstd
 
+    def other_up():
+        rows = [
+            jnp.concatenate([oth_ref[h, pl.ds(c * half, half), :] for c in range(chunks)], 1)
+            for h in range(2)
+        ]
+        return jnp.concatenate(rows, 0)
+
+    def other_down():
+        return jnp.concatenate([oth_ref[c, pl.ds(width, width), :] for c in range(chunks)], 0)
+
     def feed():
         ffn_in = ffn_in_ref[here, :]
         cot = cot_ref[0]
-        down_sum = None
-        grad_sum = None
         for side in range(2):
             for c in range(chunks):
                 if side == 0:
@@ -331,14 +340,14 @@
                     down = oth_ref[c, pl.ds(width, width), :]
                 at = pl.ds((side * chunks + c) * width, width)
                 act, slope = gelu_parts(dot(ffn_in, up))
-                act = act.astype(BF16)
-                gpre = (dot(cot, down, 1, 1) * slope).astype(BF16)
-                act_ref[here, at] = act
-                gpre_ref[here, at] = gpre
-                add = dot(act, down)
-                down_sum = add if down_sum is None else down_sum + add
-                add = dot(gpre, up, 1, 1)
-                grad_sum = add if grad_sum is None else grad_sum + add
+                act_ref[here, at] = act.astype(BF16)
+                gpre_ref[here, at] = (dot(cot, down, 1, 1) * slope).astype(BF16)
+        own = pl.ds(0, hidden_units)
+        oth = pl.ds(hidden_units, hidden_units)
+        down_sum = dot(act_ref[here, own], down_ref[...]) + dot(act_ref[here, oth], other_down())
+        grad_sum = dot(gpre_ref[here, own], up_ref[...], 1, 1) + dot(
+            gpre_ref[here, oth], other_up(), 1, 1
+        )
         return down_sum, grad_sum
 
     def back(kept, sums):
@@ -401,7 +410,7 @@
             for side in range(2):
                 at = pl.ds(pl.multiple_of((side * chunks + which) * width, width), width)
                 here = pl.ds(pl.multiple_of((2 * side + which) * PAIR, PAIR), PAIR)
-                slot = len(moves) // 2
+                slot = len(moves) // 3
                 first = 0
                 for left, right in (
                     (ffn_in_ref[...], gpre_ref[:, at]),
@@ -411,10 +420,16 @@
                     piece = dot(left, right, 0, 0).astype(BF16)
                     stage_ref[slot, pl.ds(first, piece.shape[0]), :] = piece
                     first += piece.shape[0]
-                for i, far in enumerate(fars):
+                part = cut // 2
+                own = lax.rem(lax.div(lax.axis_index("dp"), 2), 2) * part
+                for start, size, far, to in (
+                    (0, cut, fars[0], 0),
+                    (cut, part, fars[1], part - own),
+                    (cut + part, part, fars[1], own),
+                ):
                     move = pltpu.make_async_copy(
-                        stage_ref.at[slot, pl.ds(i * cut, cut), :],
-                        far.at[side],
+                        stage_ref.at[slot, pl.ds(start, size), :],
+                        far.at[side, pl.ds(pl.multiple_of(to, part), size), :],
                         out_sems.at[len(moves)],
                     )
                     move.start()
@@ -423,7 +438,7 @@
             move.wait()
 
 
-def middle_layer(tokens, ctx_own, ctx_oth, nb, ids, cot, weights, received, edges, gains):
+def middle_layer(tokens, ctx_own, ctx_oth, nb, ids, cot, weights, received, edges, gain, wgate):
     rows, length, width = tokens.shape
     hidden_units = weights[1].shape[0]
     steps = length // TILE
@@ -455,7 +470,8 @@
                 tiled(width),
                 *[far] * 5,
                 whole((1, BINS + 1)),
-                whole((2, width)),
+                whole((1, width)),
+                whole((1, width)),
             ],
             out_specs=[
                 tiled(width),
@@ -483,7 +499,7 @@
                 pltpu.VMEM((count, width), BF16),
                 pltpu.VMEM((count, width), BF16),
                 pltpu.SemaphoreType.DMA((5,)),
-                pltpu.SemaphoreType.DMA((8,)),
+                pltpu.SemaphoreType.DMA((12,)),
             ],
         out_shape=[
             jax.ShapeDtypeStruct((rows, length, width), BF16),
@@ -495,7 +511,7 @@
         ],
         compiler_params=pltpu.CompilerParams(vmem_limit_bytes=VMEM_LIMIT),
         cost_estimate=pl.CostEstimate(flops=15 * 10**9, bytes_accessed=30 * 2**20, transcendentals=0),
-    )(tokens, ctx_own, ctx_oth, nb, ids, cot, *weights, *received, edges, gains)
+    )(tokens, ctx_own, ctx_oth, nb, ids, cot, *weights, *received, edges, gain, wgate)
 
 
 def attend_back(
@@ -865,6 +881,15 @@
         self.come = swap(self.sent, "dp", bit)
         return self.sent
 
+    def first_half(self, bit, *others):
+        half = self.pieces[0].shape[self.dim] // 2
+        self.sent = after(
+            self.total(lambda p: lax.slice_in_dim(p, 0, half, axis=self.dim)), *others
+        )
+        self.kept = self.total(lambda p: lax.slice_in_dim(p, half, 2 * half, axis=self.dim))
+        self.come = swap(self.sent, "dp", bit)
+        return self.sent
+
     def give(self, index, *others):
         self.sent = after(self.total(lambda p: p[index]), *others)
         self.kept = self.total(lambda p: p[1 - index])
@@ -932,7 +957,6 @@
     dp = lax.axis_size("dp")
     core = bit_of("dp", 1)
     attn_gain = gain_attn.reshape(1, width)
-    gains = jnp.stack([gain_ffn, w_gate])
     qkv = (w_query, w_key, w_value)
     far = []
     bit = 2
@@ -978,7 +1002,8 @@
         (w_up, w_down, w_out),
         ffn_got,
         edges,
-        gains,
+        gain_ffn.reshape(1, width),
+        w_gate.reshape(1, width),
     )
     up = Chain(None, 1)
     down = Chain(None, 1)
@@ -987,7 +1012,7 @@
     up.add()
     down.add()
     sent = up.give(1)
-    sent = down.halve(far[0], sent)
+    sent = down.first_half(far[0], sent)
     g_oth, da, gain_oth = attention_backward(
         doc_starts, oth, after(gctx_oth, sent), kv, 1, 2
     )

time: 167 us -> 166 us (level)
  Pallas kernels: 92.7 us -> 97.6 us
  starting transfers between devices: 32.9 us -> 29.8 us
  waiting for transfers between devices: 25.2 us -> 22.2 us
    pallas_call x2, Pallas kernels: 26.3 us -> 29.3 us  [attention_forward(): pl.pallas_call(body, grid=(rows, pairs), in_specs=in_specs, out_specs=out...]
    pallas_call x3, Pallas kernels: 26.4 us -> 28.6 us  [attention_backward(): pl.pallas_call(backward_body, grid=(many, rows, 2), in_specs=[pl.BlockSpe...]
    ppermute x25, waiting for transfers between devices: 22.5 us -> 20.5 us  [swap(): return lax.ppermute(array, axis, [(i, i ^ bit) for i in range(size)])]
    ppermute x25, starting transfers between devices: 29.8 us -> 28 us  [swap(): return lax.ppermute(array, axis, [(i, i ^ bit) for i in range(size)])]
    unnamed x49 -> x45, local copies, waits for them, and re-layouts: 4.43 us -> 5.08 us
  transfers between devices with their start and end apart: 28 -> 28, of which waited for: 11 -> 9; matrix products, arithmetic and copies ran while one was open for 4% -> 3% of each run, Pallas kernels for 35% -> 39%
where the time goes in v5:
time: 166 us; the launch traced here: 165 us
  Pallas kernels  97.6 us (59%)
  starting transfers between devices  29.8 us (18%)
  waiting for transfers between devices  22.2 us (13%)
  local copies, waits for them, and re-layouts  9.52 us (6%)
  other arithmetic  4.63 us (3%)
    pallas_call x1, Pallas kernels, middle_layer(): pl.pallas_call(middle_body, grid=(tiles,), in_specs=[tiled(width), tiled(...  29.8 us
    pallas_call x2, Pallas kernels, attention_forward(): pl.pallas_call(body, grid=(rows, pairs), in_specs=in_specs, out_specs=out...  29.3 us
    pallas_call x3, Pallas kernels, attention_backward(): pl.pallas_call(backward_body, grid=(many, rows, 2), in_specs=[pl.BlockSpe...  28.6 us
    ppermute x25, starting transfers between devices, swap(): return lax.ppermute(array, axis, [(i, i ^ bit) for i in range(size)])  28 us
    ppermute x25, waiting for transfers between devices, swap(): return lax.ppermute(array, axis, [(i, i ^ bit) for i in range(size)])  20.5 us
    pallas_call x1, Pallas kernels, input_grad(): pl.pallas_call(input_body, grid=(rows,), in_specs=[row, row, whole(gain),...  6.36 us
    unnamed x45, local copies, waits for them, and re-layouts  5.08 us
    pallas_call x1, Pallas kernels, finish(): pl.pallas_call(functools.partial(finish_body, tokens=tokens), grid=(1,),...  3.68 us
  transfers between devices with their start and end apart: 28, of which 9 were waited for; matrix products, arithmetic and copies ran while one was open for 3% of the time, Pallas kernels for 39%

profile of v5, /device:TPU:0, one launch (start us, length us, event | category | flops | bytes accessed | tf_op | source)
XLA Modules:
  0.0 165.1 jit_solution(3103482189967240309)
XLA Ops:
  0.7 1.0 constant_dynamic-slice_fusion.5
  1.7 1.1 constant_dynamic-slice_fusion.3
  2.8 3.0 %collective-permute-start = (bf16[256,768]{1,0:T(8,128)(2,1)S(1)}, bf16[256,768]{1,0:T(8,128)(2,1)S(1)}, u32[]{:S(2)}, u32[]{:S(2)}) collective-permute-start(bf16[256,768]{1,0:T(8,128)(2,1)S(1)} %pad_maximum_fusion.1), channel_id=1, source_target_pairs={{0,1},{1,0},{2,3},{3,2},{4,5},{5,4},{6,7},{7,6},{8,9},{9,8},{10,11... | collective-permute-start | bytes 1179656 | tf_op jit(solution)/shard_map/ppermute | solution.py:821
  6.0 0.9 constant_dynamic-slice_fusion.1
  7.0 0.2 collective-permute-start.2
  7.2 0.6 copy-done.9
  8.0 15.6 %shard_map.255 = (bf16[2,1024,512]{2,1,0:T(8,128)(2,1)}, bf16[512,768]{1,0:T(8,128)(2,1)}, bf16[2,2,2560,128]{3,2,1,0:T(8,128)(2,1)}, bf16[2,2,2,512,1024]{4,3,2,1,0:T(8,128)(2,1)}, bf16[2,512,256]{2,1,0:T(8,128)(2,1)S(1)}) custom-call(s32[4]{0:T(128)S(1)} %copy-done.13, bf16[2,512,512]{2,1,0:T(8,128)(2,1)} %tok_ref.4, bf16[4,512,512]{2,1,0:T(8,128)(2,1)} %mem_ref.1, ...), custom_call_target="tpu_custom_call" | custom-call | flops 6000000000 | bytes 16777216 | tf_op jit(solution)/shard_map/pallas_call | solution.py:179
  23.6 0.8 copy-done.2
  24.4 1.7 %collective-permute-done.1.sibling_ref = bf16[256,768]{1,0:T(8,128)(2,1)S(1)} collective-permute-done((bf16[256,768]{1,0:T(8,128)(2,1)S(1)}, bf16[256,768]{1,0:T(8,128)(2,1)S(1)}, u32[]{:S(2)}, u32[]{:S(2)}) %collective-permute-start.1) | collective-permute-done | bytes 393248 | tf_op jit(solution)/shard_map/ppermute | solution.py:821
  26.1 13.6 %shard_map.256 = (bf16[512,768]{1,0:T(8,128)(2,1)}, bf16[2,2,2560,128]{3,2,1,0:T(8,128)(2,1)}, bf16[2,2,2,512,1024]{4,3,2,1,0:T(8,128)(2,1)}, bf16[2,512,256]{2,1,0:T(8,128)(2,1)S(1)}) custom-call(s32[4]{0:T(128)S(1)} %copy-done.13, bf16[2,1024,512]{2,1,0:T(8,128)(2,1)} %get-tuple-element.89.kv_ref.kv_far, ...), custom_call_target="tpu_custom_call" | custom-call | flops 6000000000 | bytes 16777216 | tf_op jit(solution)/shard_map/pallas_call | solution.py:179
  39.8 0.8 copy-done.14
  40.6 0.1 collective-permute-start.3
  40.7 2.7 %collective-permute-done.3.sibling_far = bf16[1152,512]{1,0:T(8,128)(2,1)S(1)} collective-permute-done((bf16[1152,512]{1,0:T(8,128)(2,1)S(1)}, bf16[1152,512]{1,0:T(8,128)(2,1)S(1)}, u32[]{:S(2)}, u32[]{:S(2)}) %collective-permute-start.3) | collective-permute-done | bytes 1179680 | tf_op jit(solution)/shard_map/ppermute | solution.py:821
  43.4 1.1 copy-done.21
  44.5 29.8 %shard_map.257 = (bf16[2,512,512]{2,1,0:T(8,128)(2,1)}, f32[2,512,512]{2,1,0:T(8,128)}, bf16[2,512,256]{2,1,0:T(8,128)(2,1)}, bf16[2,512,256]{2,1,0:T(8,128)(2,1...) custom-call(bf16[2,512,512]{2,1,0:T(8,128)(2,1)} %tok_ref.4, ...), custom_call_target="tpu_custom_call" | custom-call | flops 15000000512 | bytes 31457280 | tf_op jit(solution)/shard_map/pallas_call | solution.py:459
  74.3 0.2 collective-permute-start.5
  74.5 0.4 collective-permute-start.4
  74.9 0.7 slice.110
  75.6 1.8 %collective-permute-done.5 = bf16[2,576,512]{2,1,0:T(8,128)(2,1)S(1)} collective-permute-done((bf16[2,576,512]{2,1,0:T(8,128)(2,1)}, bf16[2,576,512]{2,1,0:T(8,128)(2,1)S(1)}, u32[]{:S(2)}, u32[]{:S(2)}) %collective-permute-start.5) | collective-permute-done | bytes 1179680 | tf_op jit(solution)/shard_map/ppermute | solution.py:821
  77.4 1.7 %add_convert_fusion = (bf16[1,576,512]{2,1,0:T(8,128)(2,1)S(1)}, bf16[576,512]{1,0:T(8,128)(2,1)S(1)}) fusion(bf16[2,576,512]{2,1,0:T(8,128)(2,1)S(1)} %collective-permute-done.5, bf16[2,576,512]{2,1,0:T(8,128)(2,1)} %get-tuple-element.102), kind=kLoop, calls=%fused_computation.2 | loop fusion | flops 2359296 | bytes 3538944 | tf_op jit(solution)/shard_map/convert_element_type | solution.py:869
  79.1 1.5 collective-permute-start.7
  80.6 0.3 add_convert_fusion.1
  80.9 1.5 collective-permute-start.6
  82.4 13.8 %shard_map.258 = (bf16[2,2,384,512]{3,2,1,0:T(8,128)(2,1)S(1)}, bf16[2,3,128,512]{3,2,1,0:T(8,128)(2,1)S(1)}, f32[2,8,512]{2,1,0:T(8,128)S(1)}) custom-call(s32[4]{0:T(128)S(1)} %copy-done.13, bf16[2,2,2560,128]{3,2,1,0:T(8,128)(2,1)} %get-tuple-element.97.qkv_ref, bf16[2,2,2,512,1024]{4,3,2,1,0:T(8,128)(2,1)} %get-tuple-element.98.p_ref, ...), custom_call_target="tpu_custom_call" | custom-call | flops 8000000000 | bytes 16777216 | tf_op jit(solution)/shard_map/pallas_call | solution.py:628
  96.3 0.2 fusion.2
  96.5 0.9 copy-done.5
  97.4 0.9 collective-permute-start.8
  98.3 0.2 fusion.5
  98.7 0.2 copy-done.1
  98.9 0.1 copy-done.3
  99.0 7.4 %shard_map.259 = (bf16[1,2,384,512]{3,2,1,0:T(8,128)(2,1)S(1)}, bf16[1,3,128,512]{3,2,1,0:T(8,128)(2,1)S(1)}, f32[1,8,512]{2,1,0:T(8,128)S(1)}) custom-call(s32[4]{0:T(128)S(1)} %copy-done.13, bf16[2,2,2560,128]{3,2,1,0:T(8,128)(2,1)} %get-tuple-element.108.qkv_ref, bf16[2,2,2,512,1024]{4,3,2,1,0:T(8,128)(2,1)} %get-tuple-element.109.p_ref, ...), custom_call_target="tpu_custom_call" | custom-call | flops 4000000000 | bytes 8388608 | tf_op jit(solution)/shard_map/pallas_call | solution.py:628
  106.5 0.4 add_convert_fusion.7
  107.0 0.3 copy-done.7
  107.4 1.7 %collective-permute-start.13 = (bf16[288,512]{1,0:T(8,128)(2,1)S(1)}, bf16[288,512]{1,0:T(8,128)(2,1)S(1)}, u32[]{:S(2)}, u32[]{:S(2)}) collective-permute-start(bf16[288,512]{1,0:T(8,128)(2,1)S(1)} %add_convert_fusion.7), channel_id=1, source_target_pairs={{0,8},{2,10},{4,12},{6,14},{8,0},{10,2},{12,4},{14,6},{16,24},{18,... | collective-permute-start | bytes 884744 | tf_op jit(solution)/shard_map/ppermute | solution.py:821
  109.1 1.9 %collective-permute-start.11 = (bf16[3,128,512]{2,1,0:T(8,128)(2,1)S(1)}, bf16[3,128,512]{2,1,0:T(8,128)(2,1)S(1)}, u32[]{:S(2)}, u32[]{:S(2)}) collective-permute-start(bf16[3,128,512]{2,1,0:T(8,128)(2,1)S(1)} %fusion), channel_id=1, source_target_pairs={{0,1},{1,0},{2,3},{3,2},{4,5},{5,4},{6,7},{7,6},{8,9},{9,8},{10,11... | collective-permute-start | bytes 1179656 | tf_op jit(solution)/shard_map/ppermute | solution.py:821
  110.9 7.4 %shard_map.260 = (bf16[1,2,384,512]{3,2,1,0:T(8,128)(2,1)S(1)}, bf16[1,3,128,512]{3,2,1,0:T(8,128)(2,1)S(1)}, f32[1,8,512]{2,1,0:T(8,128)S(1)}) custom-call(s32[4]{0:T(128)S(1)} %copy-done.13, bf16[2,2,2560,128]{3,2,1,0:T(8,128)(2,1)} %get-tuple-element.108.qkv_ref, bf16[2,2,2,512,1024]{4,3,2,1,0:T(8,128)(2,1)} %get-tuple-element.109.p_ref, ...), custom_call_target="tpu_custom_call" | custom-call | flops 4000000000 | bytes 8388608 | tf_op jit(solution)/shard_map/pallas_call | solution.py:628
  118.4 0.5 add_convert_fusion.5
  118.9 1.6 collective-permute-start.14
  120.5 0.1 collective-permute-done.11
  120.6 0.1 fusion.12
  120.7 1.2 collective-permute-start.15
  121.9 1.1 collective-permute-start.16
  123.0 1.3 collective-permute-start.17
  124.3 1.4 collective-permute-start.18
  125.7 6.4 %shard_map.261 = bf16[2,512,512]{2,1,0:T(8,128)(2,1)} custom-call(bf16[2,512,512]{2,1,0:T(8,128)(2,1)} %tok_ref.4, f32[2,512,512]{2,1,0:T(8,128)} %get-tuple-element.133.grad_hidden_ref, f32[1,512]{1,0:T(1,128)} %bitcast.77, bf16[2,2,384,512]{3,2,1,0:T(8,128)(2,1)} %copy-done.5, bf16[1,2,384,512]{3,2,1,0:T(8,128)(2,1)} %copy-done.7, ...), custom_call_target="tpu_custom_call" | custom-call | flops 2000000000 | bytes 8388608 | tf_op jit(solution)/shard_map/pallas_call | solution.py:709
  132.2 0.1 concatenate.137
  132.3 3.4 %collective-permute-start.19 = (bf16[112,512]{1,0:T(8,128)(2,1)S(1)}, bf16[112,512]{1,0:T(8,128)(2,1)S(1)}, u32[]{:S(2)}, u32[]{:S(2)}) collective-permute-start(bf16[112,512]{1,0:T(8,128)(2,1)S(1)} %concatenate.137), channel_id=1, source_target_pairs={{0,16},{2,18},{4,20},{6,22},{8,24},{10,26},{12,28},{14,30},{16,0},... | collective-permute-start | bytes 344072 | tf_op jit(solution)/shard_map/ppermute | solution.py:821
  135.8 0.2 collective-permute-done.14
  136.1 0.8 collective-permute-start.23
  136.9 2.9 %collective-permute-start.24 = (bf16[288,512]{1,0:T(8,128)(2,1)S(1)}, bf16[288,512]{1,0:T(8,128)(2,1)S(1)}, u32[]{:S(2)}, u32[]{:S(2)}) collective-permute-start(bf16[288,512]{1,0:T(8,128)(2,1)S(1)} %add_convert_fusion.4), channel_id=1, source_target_pairs={{0,8},{2,10},{4,12},{6,14},{8,0},{10,2},{12,4},{14,6},{16,24},{18,... | collective-permute-start | bytes 884744 | tf_op jit(solution)/shard_map/ppermute | solution.py:821
  139.8 0.5 collective-permute-start.25
  140.4 0.1 concatenate.139
  140.5 1.1 collective-permute-start.20
  141.6 2.4 %collective-permute-start.21 = (bf16[112,512]{1,0:T(8,128)(2,1)S(1)}, bf16[112,512]{1,0:T(8,128)(2,1)S(1)}, u32[]{:S(2)}, u32[]{:S(2)}) collective-permute-start(bf16[112,512]{1,0:T(8,128)(2,1)S(1)} %concatenate.139), channel_id=1, source_target_pairs={{0,8},{2,10},{4,12},{6,14},{8,0},{10,2},{12,4},{14,6},{16,24},{18,... | collective-permute-start | bytes 344072 | tf_op jit(solution)/shard_map/ppermute | solution.py:821
  144.0 6.6 %collective-permute-done.20 = bf16[112,512]{1,0:T(8,128)(2,1)S(1)} collective-permute-done((bf16[112,512]{1,0:T(8,128)(2,1)S(1)}, bf16[112,512]{1,0:T(8,128)(2,1)S(1)}, u32[]{:S(2)}, u32[]{:S(2)}) %collective-permute-start.20) | collective-permute-done | bytes 114720 | tf_op jit(solution)/shard_map/ppermute | solution.py:821
  150.6 4.3 %collective-permute-done.21 = bf16[112,512]{1,0:T(8,128)(2,1)S(1)} collective-permute-done((bf16[112,512]{1,0:T(8,128)(2,1)S(1)}, bf16[112,512]{1,0:T(8,128)(2,1)S(1)}, u32[]{:S(2)}, u32[]{:S(2)}) %collective-permute-start.21) | collective-permute-done | bytes 114720 | tf_op jit(solution)/shard_map/ppermute | solution.py:821
  154.9 1.7 %collective-permute-done.22 = bf16[112,512]{1,0:T(8,128)(2,1)S(1)} collective-permute-done((bf16[112,512]{1,0:T(8,128)(2,1)S(1)}, bf16[112,512]{1,0:T(8,128)(2,1)S(1)}, u32[]{:S(2)}, u32[]{:S(2)}) %collective-permute-start.22) | collective-permute-done | bytes 114720 | tf_op jit(solution)/shard_map/ppermute | solution.py:847
  156.8 0.2 maximum_select_fusion.1
  157.1 0.2 maximum_select_fusion.2
  157.3 0.2 maximum_select_fusion.ffn_mine
  157.5 0.3 concatenate.159
  157.8 0.5 collective-permute-start.27
  158.3 2.9 %collective-permute-done.27.attn_sibling = bf16[400,512]{1,0:T(8,128)(2,1)S(1)} collective-permute-done((bf16[400,512]{1,0:T(8,128)(2,1)S(1)}, bf16[400,512]{1,0:T(8,128)(2,1)S(1)}, u32[]{:S(2)}, u32[]{:S(2)}) %collective-permute-start.27) | collective-permute-done | bytes 409632 | tf_op jit(solution)/shard_map/ppermute | solution.py:821
  161.3 3.7 %shard_map.262 = (f32[512,256]{1,0:T(8,128)}, f32[512,256]{1,0:T(8,128)}, f32[512,256]{1,0:T(8,128)}, f32[256,512]{1,0:T(8,128)}, f32[512,1024]{1,0:T(8,128)}, /...) custom-call(bf16[2,576,512]{2,1,0:T(8,128)(2,1)S(1)} %maximum_select, ...), custom_call_target="tpu_custom_call" | custom-call | tf_op jit(solution)/shard_map/pallas_call | solution.py:807
  (92 shorter events, 1.4 us)
Async XLA Ops:
  0.6 5.2 %copy-start.19 = (bf16[1024,512]{1,0:T(8,128)(2,1)S(1)}, bf16[1024,512]{1,0:T(8,128)(2,1)}, u32[]{:S(2)}) copy-start(bf16[1024,512]{1,0:T(8,128)(2,1)} %down_far.1) | copy-start | bytes 3145732
  1.7 4.2 %copy-start.18 = (bf16[512,1024]{1,0:T(8,128)(2,1)S(1)}, bf16[512,1024]{1,0:T(8,128)(2,1)}, u32[]{:S(2)}) copy-start(bf16[512,1024]{1,0:T(8,128)(2,1)} %up_far.1) | copy-start | bytes 3145732
  2.8 21.6 %collective-permute-start = (bf16[256,768]{1,0:T(8,128)(2,1)S(1)}, bf16[256,768]{1,0:T(8,128)(2,1)S(1)}, u32[]{:S(2)}, u32[]{:S(2)}) collective-permute-start(bf16[256,768]{1,0:T(8,128)(2,1)S(1)} %pad_maximum_fusion.1), channel_id=1, source_target_pairs={{0,1},{1,0},{2,3},{3,2},{4,5},{5,4},{6,7},{7,6},{8,9},{9,8},{10,11... | collective-permute-start | bytes 1179656 | tf_op jit(solution)/shard_map/ppermute | solution.py:821
  6.9 1.0 copy-start.9
  6.9 1.0 copy-start.10
  6.9 1.1 copy-start.11
  6.9 1.1 copy-start.12
  6.9 1.1 copy-start.13
  7.0 33.6 %collective-permute-start.2 = (bf16[1152,512]{1,0:T(8,128)(2,1)S(1)}, bf16[1152,512]{1,0:T(8,128)(2,1)S(1)}, u32[]{:S(2)}, u32[]{:S(2)}) collective-permute-start(bf16[1152,512]{1,0:T(8,128)(2,1)S(1)} %pad_maximum_fusion), channel_id=1, source_target_pairs={{0,1},{1,0},{2,3},{3,2},{4,5},{5,4},{6,7},{7,6},{8,9},{9,8},{10,11... | collective-permute-start | bytes 3538952 | tf_op jit(solution)/shard_map/ppermute | solution.py:821
  23.6 0.8 copy-start.2
  24.4 1.7 %collective-permute-start.1 = (bf16[256,768]{1,0:T(8,128)(2,1)S(1)}, bf16[256,768]{1,0:T(8,128)(2,1)S(1)}, u32[]{:S(2)}, u32[]{:S(2)}) collective-permute-start(bf16[256,768]{1,0:T(8,128)(2,1)S(1)} %collective-permute-done.mine_ref), channel_id=1, source_target_pairs={{0,2},{2,0},{4,6},{6,4},{8,10},{10,8},{12,14},{14,12},{16,18},{18,... | collective-permute-start | bytes 1179656 | tf_op jit(solution)/shard_map/ppermute | solution.py:821
  39.8 0.8 copy-start.14
  40.6 2.9 %copy-start.20 = (bf16[1152,512]{1,0:T(8,128)(2,1)}, bf16[1152,512]{1,0:T(8,128)(2,1)S(1)}, u32[]{:S(2)}) copy-start(bf16[1152,512]{1,0:T(8,128)(2,1)S(1)} %collective-permute-done.2.mine_far) | copy-start | bytes 3538948
  40.6 2.8 %collective-permute-start.3 = (bf16[1152,512]{1,0:T(8,128)(2,1)S(1)}, bf16[1152,512]{1,0:T(8,128)(2,1)S(1)}, u32[]{:S(2)}, u32[]{:S(2)}) collective-permute-start(bf16[1152,512]{1,0:T(8,128)(2,1)S(1)} %collective-permute-done.2.mine_far), channel_id=1, source_target_pairs={{0,2},{2,0},{4,6},{6,4},{8,10},{10,8},{12,14},{14,12},{16,18},{18,... | collective-permute-start | bytes 3538952 | tf_op jit(solution)/shard_map/ppermute | solution.py:821
  43.4 1.1 copy-start.21
  74.3 3.1 %collective-permute-start.5 = (bf16[2,576,512]{2,1,0:T(8,128)(2,1)}, bf16[2,576,512]{2,1,0:T(8,128)(2,1)S(1)}, u32[]{:S(2)}, u32[]{:S(2)}) collective-permute-start(bf16[2,576,512]{2,1,0:T(8,128)(2,1)} %get-tuple-element.103), channel_id=1, source_target_pairs={{0,2},{2,0},{4,6},{6,4},{8,10},{10,8},{12,14},{14,12},{16,18},{18,... | collective-permute-start | bytes 3538952 | tf_op jit(solution)/shard_map/ppermute | solution.py:821
  74.5 6.1 %collective-permute-start.4 = (bf16[2,576,512]{2,1,0:T(8,128)(2,1)}, bf16[2,576,512]{2,1,0:T(8,128)(2,1)S(1)}, u32[]{:S(2)}, u32[]{:S(2)}) collective-permute-start(bf16[2,576,512]{2,1,0:T(8,128)(2,1)} %get-tuple-element.101), channel_id=1, source_target_pairs={{0,2},{2,0},{4,6},{6,4},{8,10},{10,8},{12,14},{14,12},{16,18},{18,... | collective-permute-start | bytes 3538952 | tf_op jit(solution)/shard_map/ppermute | solution.py:821
  77.4 3.1 %copy-start.17 = (bf16[2,576,512]{2,1,0:T(8,128)(2,1)S(1)}, bf16[2,576,512]{2,1,0:T(8,128)(2,1)}, u32[]{:S(2)}) copy-start(bf16[2,576,512]{2,1,0:T(8,128)(2,1)} %get-tuple-element.100) | copy-start | bytes 3538948
  79.1 17.2 %collective-permute-start.7 = (bf16[576,512]{1,0:T(8,128)(2,1)S(1)}, bf16[576,512]{1,0:T(8,128)(2,1)S(1)}, u32[]{:S(2)}, u32[]{:S(2)}) collective-permute-start(bf16[576,512]{1,0:T(8,128)(2,1)S(1)} %get-tuple-element.168), channel_id=1, source_target_pairs={{0,1},{1,0},{2,3},{3,2},{4,5},{5,4},{6,7},{7,6},{8,9},{9,8},{10,11... | collective-permute-start | bytes 1769480 | tf_op jit(solution)/shard_map/ppermute | solution.py:821
  80.5 1.9 %copy-start.6 = (bf16[512,768]{1,0:T(8,128)(2,1)S(1)}, bf16[512,768]{1,0:T(8,128)(2,1)}, u32[]{:S(2)}) copy-start(bf16[512,768]{1,0:T(8,128)(2,1)} %get-tuple-element.106.pack_ref.oth_pack_ref) | copy-start | bytes 2359300
  80.5 1.9 %copy-start.15 = (bf16[2,512,256]{2,1,0:T(8,128)(2,1)S(1)}, bf16[2,512,256]{2,1,0:T(8,128)(2,1)}, u32[]{:S(2)}) copy-start(bf16[2,512,256]{2,1,0:T(8,128)(2,1)} %copy-done.14) | copy-start | bytes 1572868
  80.6 1.9 %copy-start.16 = (bf16[2,512,256]{2,1,0:T(8,128)(2,1)S(1)}, bf16[2,512,256]{2,1,0:T(8,128)(2,1)}, u32[]{:S(2)}) copy-start(bf16[2,512,256]{2,1,0:T(8,128)(2,1)} %get-tuple-element.105.gctx_ref) | copy-start | bytes 1572868
  80.9 16.5 %collective-permute-start.6 = (bf16[2,288,512]{2,1,0:T(8,128)(2,1)S(1)}, bf16[2,288,512]{2,1,0:T(8,128)(2,1)S(1)}, u32[]{:S(2)}, u32[]{:S(2)}) collective-permute-start(bf16[2,288,512]{2,1,0:T(8,128)(2,1)S(1)} %get-tuple-element.104), channel_id=1, source_target_pairs={{0,4},{2,6},{4,0},{6,2},{8,12},{10,14},{12,8},{14,10},{16,20},{18,... | collective-permute-start | bytes 1769480 | tf_op jit(solution)/shard_map/ppermute | solution.py:821
  96.2 1.2 copy-start.5
  96.3 2.4 %copy-start.4 = (bf16[2,512,256]{2,1,0:T(8,128)(2,1)S(1)}, bf16[2,512,256]{2,1,0:T(8,128)(2,1)}, u32[]{:S(2)}) copy-start(bf16[2,512,256]{2,1,0:T(8,128)(2,1)} %get-tuple-element.125.gctx_ref) | copy-start | bytes 1572868
  96.3 2.4 %copy-start = (bf16[2,1024,512]{2,1,0:T(8,128)(2,1)S(1)}, bf16[2,1024,512]{2,1,0:T(8,128)(2,1)}, u32[]{:S(2)}) copy-start(bf16[2,1024,512]{2,1,0:T(8,128)(2,1)} %get-tuple-element.89.kv_ref.kv_far) | copy-start | bytes 6291460
  97.4 1.5 copy-start.1
  97.4 1.6 copy-start.3
  97.4 9.0 %collective-permute-start.8 = (bf16[288,512]{1,0:T(8,128)(2,1)S(1)}, bf16[288,512]{1,0:T(8,128)(2,1)S(1)}, u32[]{:S(2)}, u32[]{:S(2)}) collective-permute-start(bf16[288,512]{1,0:T(8,128)(2,1)S(1)} %get-tuple-element.177), channel_id=1, source_target_pairs={{0,4},{2,6},{4,0},{6,2},{8,12},{10,14},{12,8},{14,10},{16,20},{18,... | collective-permute-start | bytes 884744 | tf_op jit(solution)/shard_map/ppermute | solution.py:821
  98.5 7.9 %collective-permute-start.9 = (bf16[288,512]{1,0:T(8,128)(2,1)S(1)}, bf16[288,512]{1,0:T(8,128)(2,1)S(1)}, u32[]{:S(2)}, u32[]{:S(2)}) collective-permute-start(bf16[288,512]{1,0:T(8,128)(2,1)S(1)} %get-tuple-element.114), channel_id=1, source_target_pairs={{0,1},{1,0},{2,3},{3,2},{4,5},{5,4},{6,7},{7,6},{8,9},{9,8},{10,11... | collective-permute-start | bytes 884744 | tf_op jit(solution)/shard_map/ppermute | solution.py:821
  98.6 8.7 %collective-permute-start.10 = (bf16[3,128,512]{2,1,0:T(8,128)(2,1)S(1)}, bf16[3,128,512]{2,1,0:T(8,128)(2,1)S(1)}, u32[]{:S(2)}, u32[]{:S(2)}) collective-permute-start(bf16[3,128,512]{2,1,0:T(8,128)(2,1)S(1)} %slice_bitcast_fusion), channel_id=1, source_target_pairs={{0,2},{2,0},{4,6},{6,4},{8,10},{10,8},{12,14},{14,12},{16,18},{18,... | collective-permute-start | bytes 1179656 | tf_op jit(solution)/shard_map/ppermute | solution.py:821
  106.4 0.9 copy-start.7
  107.4 11.0 %collective-permute-start.13 = (bf16[288,512]{1,0:T(8,128)(2,1)S(1)}, bf16[288,512]{1,0:T(8,128)(2,1)S(1)}, u32[]{:S(2)}, u32[]{:S(2)}) collective-permute-start(bf16[288,512]{1,0:T(8,128)(2,1)S(1)} %add_convert_fusion.7), channel_id=1, source_target_pairs={{0,8},{2,10},{4,12},{6,14},{8,0},{10,2},{12,4},{14,6},{16,24},{18,... | collective-permute-start | bytes 884744 | tf_op jit(solution)/shard_map/ppermute | solution.py:821
  109.1 11.4 %collective-permute-start.12 = (bf16[3,128,512]{2,1,0:T(8,128)(2,1)S(1)}, bf16[3,128,512]{2,1,0:T(8,128)(2,1)S(1)}, u32[]{:S(2)}, u32[]{:S(2)}) collective-permute-start(bf16[3,128,512]{2,1,0:T(8,128)(2,1)S(1)} %bitcast.79), channel_id=1, source_target_pairs={{0,2},{2,0},{4,6},{6,4},{8,10},{10,8},{12,14},{14,12},{16,18},{18,... | collective-permute-start | bytes 1179656 | tf_op jit(solution)/shard_map/ppermute | solution.py:821
  109.1 11.5 %collective-permute-start.11 = (bf16[3,128,512]{2,1,0:T(8,128)(2,1)S(1)}, bf16[3,128,512]{2,1,0:T(8,128)(2,1)S(1)}, u32[]{:S(2)}, u32[]{:S(2)}) collective-permute-start(bf16[3,128,512]{2,1,0:T(8,128)(2,1)S(1)} %fusion), channel_id=1, source_target_pairs={{0,1},{1,0},{2,3},{3,2},{4,5},{5,4},{6,7},{7,6},{8,9},{9,8},{10,11... | collective-permute-start | bytes 1179656 | tf_op jit(solution)/shard_map/ppermute | solution.py:821
  118.4 2.4 %copy-start.8 = (bf16[1,2,384,512]{3,2,1,0:T(8,128)(2,1)}, bf16[1,2,384,512]{3,2,1,0:T(8,128)(2,1)S(1)}, u32[]{:S(2)}) copy-start(bf16[1,2,384,512]{3,2,1,0:T(8,128)(2,1)S(1)} %get-tuple-element.136.own_last_ref) | copy-start | bytes 2359300
  118.9 17.1 %collective-permute-start.14 = (bf16[288,512]{1,0:T(8,128)(2,1)S(1)}, bf16[288,512]{1,0:T(8,128)(2,1)S(1)}, u32[]{:S(2)}, u32[]{:S(2)}) collective-permute-start(bf16[288,512]{1,0:T(8,128)(2,1)S(1)} %add_convert_fusion.5), channel_id=1, source_target_pairs={{0,16},{2,18},{4,20},{6,22},{8,24},{10,26},{12,28},{14,30},{16,0},... | collective-permute-start | bytes 884744 | tf_op jit(solution)/shard_map/ppermute | solution.py:821
  120.7 11.3 %collective-permute-start.15 = (bf16[3,32,512]{2,1,0:T(8,128)(2,1)S(1)}, bf16[3,32,512]{2,1,0:T(8,128)(2,1)S(1)}, u32[]{:S(2)}, u32[]{:S(2)}) collective-permute-start(bf16[3,32,512]{2,1,0:T(8,128)(2,1)S(1)} %get-tuple-element.131), channel_id=1, source_target_pairs={{0,4},{2,6},{4,0},{6,2},{8,12},{10,14},{12,8},{14,10},{16,20},{18,... | collective-permute-start | bytes 294920 | tf_op jit(solution)/shard_map/ppermute | solution.py:821
  121.9 10.2 %collective-permute-start.16 = (bf16[3,32,512]{2,1,0:T(8,128)(2,1)S(1)}, bf16[3,32,512]{2,1,0:T(8,128)(2,1)S(1)}, u32[]{:S(2)}, u32[]{:S(2)}) collective-permute-start(bf16[3,32,512]{2,1,0:T(8,128)(2,1)S(1)} %get-tuple-element.172), channel_id=1, source_target_pairs={{0,8},{2,10},{4,12},{6,14},{8,0},{10,2},{12,4},{14,6},{16,24},{18,... | collective-permute-start | bytes 294920 | tf_op jit(solution)/shard_map/ppermute | solution.py:821
  123.0 9.1 %collective-permute-start.17 = (bf16[3,32,512]{2,1,0:T(8,128)(2,1)S(1)}, bf16[3,32,512]{2,1,0:T(8,128)(2,1)S(1)}, u32[]{:S(2)}, u32[]{:S(2)}) collective-permute-start(bf16[3,32,512]{2,1,0:T(8,128)(2,1)S(1)} %get-tuple-element.171), channel_id=1, source_target_pairs={{0,12},{2,14},{4,8},{6,10},{8,4},{10,6},{12,0},{14,2},{16,28},{18,... | collective-permute-start | bytes 294920 | tf_op jit(solution)/shard_map/ppermute | solution.py:847
  124.3 7.8 %collective-permute-start.18 = (f32[5,512]{1,0:T(8,128)S(1)}, f32[5,512]{1,0:T(8,128)S(1)}, u32[]{:S(2)}, u32[]{:S(2)}) collective-permute-start(f32[5,512]{1,0:T(8,128)S(1)} %pad_maximum_fusion.2), channel_id=1, source_target_pairs={{0,1},{1,0},{2,3},{3,2},{4,5},{5,4},{6,7},{7,6},{8,9},{9,8},{10,11... | collective-permute-start | bytes 30728 | tf_op jit(solution)/shard_map/ppermute | solution.py:821
  132.3 7.9 %collective-permute-start.19 = (bf16[112,512]{1,0:T(8,128)(2,1)S(1)}, bf16[112,512]{1,0:T(8,128)(2,1)S(1)}, u32[]{:S(2)}, u32[]{:S(2)}) collective-permute-start(bf16[112,512]{1,0:T(8,128)(2,1)S(1)} %concatenate.137), channel_id=1, source_target_pairs={{0,16},{2,18},{4,20},{6,22},{8,24},{10,26},{12,28},{14,30},{16,0},... | collective-permute-start | bytes 344072 | tf_op jit(solution)/shard_map/ppermute | solution.py:821
  136.1 20.5 %collective-permute-start.23 = (bf16[288,512]{1,0:T(8,128)(2,1)S(1)}, bf16[288,512]{1,0:T(8,128)(2,1)S(1)}, u32[]{:S(2)}, u32[]{:S(2)}) collective-permute-start(bf16[288,512]{1,0:T(8,128)(2,1)S(1)} %add_convert_fusion.4), channel_id=1, source_target_pairs={{0,4},{2,6},{4,0},{6,2},{8,12},{10,14},{12,8},{14,10},{16,20},{18,... | collective-permute-start | bytes 884744 | tf_op jit(solution)/shard_map/ppermute | solution.py:821
  136.9 19.6 %collective-permute-start.24 = (bf16[288,512]{1,0:T(8,128)(2,1)S(1)}, bf16[288,512]{1,0:T(8,128)(2,1)S(1)}, u32[]{:S(2)}, u32[]{:S(2)}) collective-permute-start(bf16[288,512]{1,0:T(8,128)(2,1)S(1)} %add_convert_fusion.4), channel_id=1, source_target_pairs={{0,8},{2,10},{4,12},{6,14},{8,0},{10,2},{12,4},{14,6},{16,24},{18,... | collective-permute-start | bytes 884744 | tf_op jit(solution)/shard_map/ppermute | solution.py:821
  139.8 16.7 %collective-permute-start.25 = (bf16[288,512]{1,0:T(8,128)(2,1)S(1)}, bf16[288,512]{1,0:T(8,128)(2,1)S(1)}, u32[]{:S(2)}, u32[]{:S(2)}) collective-permute-start(bf16[288,512]{1,0:T(8,128)(2,1)S(1)} %add_convert_fusion.4), channel_id=1, source_target_pairs={{0,12},{2,14},{4,8},{6,10},{8,4},{10,6},{12,0},{14,2},{16,28},{18,... | collective-permute-start | bytes 884744 | tf_op jit(solution)/shard_map/ppermute | solution.py:847
  140.5 10.0 %collective-permute-start.20 = (bf16[112,512]{1,0:T(8,128)(2,1)S(1)}, bf16[112,512]{1,0:T(8,128)(2,1)S(1)}, u32[]{:S(2)}, u32[]{:S(2)}) collective-permute-start(bf16[112,512]{1,0:T(8,128)(2,1)S(1)} %concatenate.139), channel_id=1, source_target_pairs={{0,4},{2,6},{4,0},{6,2},{8,12},{10,14},{12,8},{14,10},{16,20},{18,... | collective-permute-start | bytes 344072 | tf_op jit(solution)/shard_map/ppermute | solution.py:821
  141.6 13.3 %collective-permute-start.21 = (bf16[112,512]{1,0:T(8,128)(2,1)S(1)}, bf16[112,512]{1,0:T(8,128)(2,1)S(1)}, u32[]{:S(2)}, u32[]{:S(2)}) collective-permute-start(bf16[112,512]{1,0:T(8,128)(2,1)S(1)} %concatenate.139), channel_id=1, source_target_pairs={{0,8},{2,10},{4,12},{6,14},{8,0},{10,2},{12,4},{14,6},{16,24},{18,... | collective-permute-start | bytes 344072 | tf_op jit(solution)/shard_map/ppermute | solution.py:821
  150.6 6.0 %collective-permute-start.22 = (bf16[112,512]{1,0:T(8,128)(2,1)S(1)}, bf16[112,512]{1,0:T(8,128)(2,1)S(1)}, u32[]{:S(2)}, u32[]{:S(2)}) collective-permute-start(bf16[112,512]{1,0:T(8,128)(2,1)S(1)} %concatenate.139), channel_id=1, source_target_pairs={{0,12},{2,14},{4,8},{6,10},{8,4},{10,6},{12,0},{14,2},{16,28},{18,... | collective-permute-start | bytes 344072 | tf_op jit(solution)/shard_map/ppermute | solution.py:847
  157.8 3.5 %collective-permute-start.26 = (bf16[2,576,512]{2,1,0:T(8,128)(2,1)S(1)}, bf16[2,576,512]{2,1,0:T(8,128)(2,1)S(1)}, u32[]{:S(2)}, u32[]{:S(2)}) collective-permute-start(bf16[2,576,512]{2,1,0:T(8,128)(2,1)S(1)} %maximum_select_fusion.ffn_mine), channel_id=1, source_target_pairs={{0,2},{2,0},{4,6},{6,4},{8,10},{10,8},{12,14},{14,12},{16,18},{18,... | collective-permute-start | bytes 3538952 | tf_op jit(solution)/shard_map/ppermute | solution.py:821
  157.8 3.4 %collective-permute-start.27 = (bf16[400,512]{1,0:T(8,128)(2,1)S(1)}, bf16[400,512]{1,0:T(8,128)(2,1)S(1)}, u32[]{:S(2)}, u32[]{:S(2)}) collective-permute-start(bf16[400,512]{1,0:T(8,128)(2,1)S(1)} %concatenate.159), channel_id=1, source_target_pairs={{0,2},{2,0},{4,6},{6,4},{8,10},{10,8},{12,14},{14,12},{16,18},{18,... | collective-permute-start | bytes 1228808 | tf_op jit(solution)/shard_map/ppermute | solution.py:821

commit v6 on v5

--- a/solution.py
+++ b/solution.py
@@ -21,6 +21,7 @@
 VMEM_LIMIT = 56 * 1024 * 1024
 FORWARD_VMEM = 52 * 1024 * 1024
 BACKWARD_VMEM = 48 * 1024 * 1024
+INPUT_VMEM = 40 * 1024 * 1024
 FINISH_VMEM = 24 * 1024 * 1024
 
 
@@ -718,7 +719,7 @@
         ],
         out_specs=row,
         out_shape=jax.ShapeDtypeStruct(tokens.shape, BF16),
-        compiler_params=pltpu.CompilerParams(vmem_limit_bytes=VMEM_LIMIT),
+        compiler_params=pltpu.CompilerParams(vmem_limit_bytes=INPUT_VMEM),
         cost_estimate=pl.CostEstimate(flops=2 * 10**9, bytes_accessed=8 * 2**20, transcendentals=0),
     )(tokens, grad_hidden, gain, *grads, *packs)
 

time: 166 us -> 166 us (level)
  waiting for transfers between devices: 22.2 us -> 26.7 us
  Pallas kernels: 97.6 us -> 95.6 us
    ppermute x25, starting transfers between devices: 28 us -> 24.4 us  [swap(): return lax.ppermute(array, axis, [(i, i ^ bit) for i in range(size)])]
    ppermute x3, starting transfers between devices: 1.77 us -> 4.67 us  [swap_diagonal(): lax.ppermute(array, 'dp', [(i, i ^ first ^ last) for i in range(size)])]
    ppermute x3, waiting for transfers between devices: 1.69 us -> 4.47 us  [swap_diagonal(): lax.ppermute(array, 'dp', [(i, i ^ first ^ last) for i in range(size)])]
    pallas_call x1, Pallas kernels: 6.36 us -> 4.17 us  [input_grad(): pl.pallas_call(input_body, grid=(rows,), in_specs=[row, row, whole(gain),...]
    ppermute x25, waiting for transfers between devices: 20.5 us -> 22.2 us  [swap(): return lax.ppermute(array, axis, [(i, i ^ bit) for i in range(size)])]
    unnamed x45 -> x43, local copies, waits for them, and re-layouts: 5.08 us -> 3.57 us
  transfers between devices with their start and end apart: 28 -> 28, of which waited for: 9 -> 10; matrix products, arithmetic and copies ran while one was open for 3% -> 3% of each run, Pallas kernels for 39% -> 38%
where the time goes in v6:
time: 166 us; the launch traced here: 165 us
  Pallas kernels  95.6 us (58%)
  starting transfers between devices  29.1 us (18%)
  waiting for transfers between devices  26.7 us (16%)
  local copies, waits for them, and re-layouts  8.02 us (5%)
  other arithmetic  4.63 us (3%)
    pallas_call x1, Pallas kernels, middle_layer(): pl.pallas_call(middle_body, grid=(tiles,), in_specs=[tiled(width), tiled(...  29.7 us
    pallas_call x2, Pallas kernels, attention_forward(): pl.pallas_call(body, grid=(rows, pairs), in_specs=in_specs, out_specs=out...  29.3 us
    pallas_call x3, Pallas kernels, attention_backward(): pl.pallas_call(backward_body, grid=(many, rows, 2), in_specs=[pl.BlockSpe...  28.7 us
    ppermute x25, starting transfers between devices, swap(): return lax.ppermute(array, axis, [(i, i ^ bit) for i in range(size)])  24.4 us
    ppermute x25, waiting for transfers between devices, swap(): return lax.ppermute(array, axis, [(i, i ^ bit) for i in range(size)])  22.2 us
    ppermute x3, starting transfers between devices, swap_diagonal(): lax.ppermute(array, 'dp', [(i, i ^ first ^ last) for i in range(size)])  4.67 us
    ppermute x3, waiting for transfers between devices, swap_diagonal(): lax.ppermute(array, 'dp', [(i, i ^ first ^ last) for i in range(size)])  4.47 us
    pallas_call x1, Pallas kernels, input_grad(): pl.pallas_call(input_body, grid=(rows,), in_specs=[row, row, whole(gain),...  4.17 us
  transfers between devices with their start and end apart: 28, of which 10 were waited for; matrix products, arithmetic and copies ran while one was open for 3% of the time, Pallas kernels for 38%

profile of v6, /device:TPU:0, one launch (start us, length us, event | category | flops | bytes accessed | tf_op | source)
XLA Modules:
  0.0 165.3 jit_solution(14189038920095294862)
XLA Ops:
  0.7 1.0 constant_dynamic-slice_fusion.5
  1.7 1.1 constant_dynamic-slice_fusion.3
  2.8 3.0 %collective-permute-start = (bf16[256,768]{1,0:T(8,128)(2,1)S(1)}, bf16[256,768]{1,0:T(8,128)(2,1)S(1)}, u32[]{:S(2)}, u32[]{:S(2)}) collective-permute-start(bf16[256,768]{1,0:T(8,128)(2,1)S(1)} %pad_maximum_fusion.1), channel_id=1, source_target_pairs={{0,1},{1,0},{2,3},{3,2},{4,5},{5,4},{6,7},{7,6},{8,9},{9,8},{10,11... | collective-permute-start | bytes 1179656 | tf_op jit(solution)/shard_map/ppermute | solution.py:822
  6.0 0.9 constant_dynamic-slice_fusion.1
  7.0 0.2 collective-permute-start.2
  7.2 0.6 copy-done.8
  8.0 15.6 %shard_map.255 = (bf16[2,1024,512]{2,1,0:T(8,128)(2,1)}, bf16[512,768]{1,0:T(8,128)(2,1)}, bf16[2,2,2560,128]{3,2,1,0:T(8,128)(2,1)}, bf16[2,2,2,512,1024]{4,3,2,1,0:T(8,128)(2,1)}, bf16[2,512,256]{2,1,0:T(8,128)(2,1)S(1)}) custom-call(s32[4]{0:T(128)S(1)} %copy-done.12, bf16[2,512,512]{2,1,0:T(8,128)(2,1)} %tok_ref.4, bf16[4,512,512]{2,1,0:T(8,128)(2,1)} %mem_ref.1, ...), custom_call_target="tpu_custom_call" | custom-call | flops 6000000000 | bytes 16777216 | tf_op jit(solution)/shard_map/pallas_call | solution.py:180
  23.6 0.8 copy-done.3
  24.4 1.7 %collective-permute-done.1.sibling_ref = bf16[256,768]{1,0:T(8,128)(2,1)S(1)} collective-permute-done((bf16[256,768]{1,0:T(8,128)(2,1)S(1)}, bf16[256,768]{1,0:T(8,128)(2,1)S(1)}, u32[]{:S(2)}, u32[]{:S(2)}) %collective-permute-start.1) | collective-permute-done | bytes 393248 | tf_op jit(solution)/shard_map/ppermute | solution.py:822
  26.1 13.7 %shard_map.256 = (bf16[512,768]{1,0:T(8,128)(2,1)}, bf16[2,2,2560,128]{3,2,1,0:T(8,128)(2,1)}, bf16[2,2,2,512,1024]{4,3,2,1,0:T(8,128)(2,1)}, bf16[2,512,256]{2,1,0:T(8,128)(2,1)S(1)}) custom-call(s32[4]{0:T(128)S(1)} %copy-done.12, bf16[2,1024,512]{2,1,0:T(8,128)(2,1)} %get-tuple-element.89.kv_ref.kv_far, ...), custom_call_target="tpu_custom_call" | custom-call | flops 6000000000 | bytes 16777216 | tf_op jit(solution)/shard_map/pallas_call | solution.py:180
  39.8 0.8 copy-done.13
  40.6 2.8 %collective-permute-done.3.sibling_far = bf16[1152,512]{1,0:T(8,128)(2,1)S(1)} collective-permute-done((bf16[1152,512]{1,0:T(8,128)(2,1)S(1)}, bf16[1152,512]{1,0:T(8,128)(2,1)S(1)}, u32[]{:S(2)}, u32[]{:S(2)}) %collective-permute-start.3) | collective-permute-done | bytes 1179680 | tf_op jit(solution)/shard_map/ppermute | solution.py:822
  43.5 1.1 copy-done.20
  44.5 29.7 %shard_map.257 = (bf16[2,512,512]{2,1,0:T(8,128)(2,1)}, f32[2,512,512]{2,1,0:T(8,128)}, bf16[2,512,256]{2,1,0:T(8,128)(2,1)}, bf16[2,512,256]{2,1,0:T(8,128)(2,1...) custom-call(bf16[2,512,512]{2,1,0:T(8,128)(2,1)} %tok_ref.4, ...), custom_call_target="tpu_custom_call" | custom-call | flops 15000000512 | bytes 31457280 | tf_op jit(solution)/shard_map/pallas_call | solution.py:460
  74.3 0.2 collective-permute-start.5
  74.5 0.4 collective-permute-start.4
  74.8 0.7 slice.110
  75.6 1.8 %collective-permute-done.5 = bf16[2,576,512]{2,1,0:T(8,128)(2,1)S(1)} collective-permute-done((bf16[2,576,512]{2,1,0:T(8,128)(2,1)}, bf16[2,576,512]{2,1,0:T(8,128)(2,1)S(1)}, u32[]{:S(2)}, u32[]{:S(2)}) %collective-permute-start.5) | collective-permute-done | bytes 1179680 | tf_op jit(solution)/shard_map/ppermute | solution.py:822
  77.4 1.7 %add_convert_fusion = (bf16[1,576,512]{2,1,0:T(8,128)(2,1)S(1)}, bf16[576,512]{1,0:T(8,128)(2,1)S(1)}) fusion(bf16[2,576,512]{2,1,0:T(8,128)(2,1)S(1)} %collective-permute-done.5, bf16[2,576,512]{2,1,0:T(8,128)(2,1)} %get-tuple-element.102), kind=kLoop, calls=%fused_computation.2 | loop fusion | flops 2359296 | bytes 3538944 | tf_op jit(solution)/shard_map/convert_element_type | solution.py:870
  79.1 1.4 collective-permute-start.7
  80.5 0.3 add_convert_fusion.1
  80.9 1.5 collective-permute-start.6
  82.4 13.8 %shard_map.258 = (bf16[2,2,384,512]{3,2,1,0:T(8,128)(2,1)S(1)}, bf16[2,3,128,512]{3,2,1,0:T(8,128)(2,1)S(1)}, f32[2,8,512]{2,1,0:T(8,128)S(1)}) custom-call(s32[4]{0:T(128)S(1)} %copy-done.12, bf16[2,2,2560,128]{3,2,1,0:T(8,128)(2,1)} %get-tuple-element.97.qkv_ref, bf16[2,2,2,512,1024]{4,3,2,1,0:T(8,128)(2,1)} %get-tuple-element.98.p_ref, ...), custom_call_target="tpu_custom_call" | custom-call | flops 8000000000 | bytes 16777216 | tf_op jit(solution)/shard_map/pallas_call | solution.py:629
  96.3 0.2 fusion.2
  96.5 1.0 collective-permute-start.8
  97.5 0.2 fusion.5
  97.7 0.6 collective-permute-start.9
  98.3 7.4 %shard_map.259 = (bf16[1,2,384,512]{3,2,1,0:T(8,128)(2,1)S(1)}, bf16[1,3,128,512]{3,2,1,0:T(8,128)(2,1)S(1)}, f32[1,8,512]{2,1,0:T(8,128)S(1)}) custom-call(s32[4]{0:T(128)S(1)} %copy-done.12, bf16[2,2,2560,128]{3,2,1,0:T(8,128)(2,1)} %get-tuple-element.108.qkv_ref, bf16[2,2,2,512,1024]{4,3,2,1,0:T(8,128)(2,1)} %get-tuple-element.109.p_ref, ...), custom_call_target="tpu_custom_call" | custom-call | flops 4000000000 | bytes 8388608 | tf_op jit(solution)/shard_map/pallas_call | solution.py:629
  105.8 0.4 add_convert_fusion.7
  106.3 0.1 fusion
  106.4 1.3 collective-permute-start.13
  107.7 2.0 %collective-permute-start.11 = (bf16[3,128,512]{2,1,0:T(8,128)(2,1)S(1)}, bf16[3,128,512]{2,1,0:T(8,128)(2,1)S(1)}, u32[]{:S(2)}, u32[]{:S(2)}) collective-permute-start(bf16[3,128,512]{2,1,0:T(8,128)(2,1)S(1)} %fusion), channel_id=1, source_target_pairs={{0,1},{1,0},{2,3},{3,2},{4,5},{5,4},{6,7},{7,6},{8,9},{9,8},{10,11... | collective-permute-start | bytes 1179656 | tf_op jit(solution)/shard_map/ppermute | solution.py:822
  109.8 7.5 %shard_map.260 = (bf16[1,2,384,512]{3,2,1,0:T(8,128)(2,1)S(1)}, bf16[1,3,128,512]{3,2,1,0:T(8,128)(2,1)S(1)}, f32[1,8,512]{2,1,0:T(8,128)S(1)}) custom-call(s32[4]{0:T(128)S(1)} %copy-done.12, bf16[2,2,2560,128]{3,2,1,0:T(8,128)(2,1)} %get-tuple-element.108.qkv_ref, bf16[2,2,2,512,1024]{4,3,2,1,0:T(8,128)(2,1)} %get-tuple-element.109.p_ref, ...), custom_call_target="tpu_custom_call" | custom-call | flops 4000000000 | bytes 8388608 | tf_op jit(solution)/shard_map/pallas_call | solution.py:629
  117.3 0.5 add_convert_fusion.5
  117.8 2.7 %collective-permute-start.14 = (bf16[288,512]{1,0:T(8,128)(2,1)S(1)}, bf16[288,512]{1,0:T(8,128)(2,1)S(1)}, u32[]{:S(2)}, u32[]{:S(2)}) collective-permute-start(bf16[288,512]{1,0:T(8,128)(2,1)S(1)} %add_convert_fusion.5), channel_id=1, source_target_pairs={{0,16},{2,18},{4,20},{6,22},{8,24},{10,26},{12,28},{14,30},{16,0},... | collective-permute-start | bytes 884744 | tf_op jit(solution)/shard_map/ppermute | solution.py:822
  120.5 0.1 fusion.12
  120.6 0.8 collective-permute-start.15
  121.4 0.8 collective-permute-start.16
  122.2 2.0 %collective-permute-start.17 = (bf16[3,32,512]{2,1,0:T(8,128)(2,1)S(1)}, bf16[3,32,512]{2,1,0:T(8,128)(2,1)S(1)}, u32[]{:S(2)}, u32[]{:S(2)}) collective-permute-start(bf16[3,32,512]{2,1,0:T(8,128)(2,1)S(1)} %get-tuple-element.171), channel_id=1, source_target_pairs={{0,12},{2,14},{4,8},{6,10},{8,4},{10,6},{12,0},{14,2},{16,28},{18,... | collective-permute-start | bytes 294920 | tf_op jit(solution)/shard_map/ppermute | solution.py:848
  124.2 0.8 collective-permute-start.18
  124.9 4.2 %shard_map.261 = bf16[2,512,512]{2,1,0:T(8,128)(2,1)} custom-call(bf16[2,512,512]{2,1,0:T(8,128)(2,1)S(1)} %copy-done.6, f32[2,512,512]{2,1,0:T(8,128)S(1)} %copy-done.2, f32[1,512]{1,0:T(1,128)S(1)} %bitcast.78, bf16[2,2,384,512]{3,2,1,0:T(8,128)(2,1)S(1)} %get-tuple-element.134.oth_ref, bf16[1,2,384,512]{3,2,1,0:T(8,128)(2,1)S(1)} %get-tuple-element.135.own_first_ref, ...), custom_call_target="tpu_custom_call" | custom-call | flops 2000000000 | bytes 8388608 | tf_op jit(solution)/shard_map/pallas_call | solution.py:710
  129.1 0.8 collective-permute-done.17
  129.9 0.1 add_convert_fusion.10
  130.0 0.1 concatenate.137
  130.2 3.0 %collective-permute-start.19 = (bf16[112,512]{1,0:T(8,128)(2,1)S(1)}, bf16[112,512]{1,0:T(8,128)(2,1)S(1)}, u32[]{:S(2)}, u32[]{:S(2)}) collective-permute-start(bf16[112,512]{1,0:T(8,128)(2,1)S(1)} %concatenate.137), channel_id=1, source_target_pairs={{0,16},{2,18},{4,20},{6,22},{8,24},{10,26},{12,28},{14,30},{16,0},... | collective-permute-start | bytes 344072 | tf_op jit(solution)/shard_map/ppermute | solution.py:822
  133.2 0.5 collective-permute-done.14
  133.8 0.5 collective-permute-start.23
  134.3 0.7 collective-permute-start.24
  135.1 2.3 %collective-permute-start.25 = (bf16[288,512]{1,0:T(8,128)(2,1)S(1)}, bf16[288,512]{1,0:T(8,128)(2,1)S(1)}, u32[]{:S(2)}, u32[]{:S(2)}) collective-permute-start(bf16[288,512]{1,0:T(8,128)(2,1)S(1)} %add_convert_fusion.4), channel_id=1, source_target_pairs={{0,12},{2,14},{4,8},{6,10},{8,4},{10,6},{12,0},{14,2},{16,28},{18,... | collective-permute-start | bytes 884744 | tf_op jit(solution)/shard_map/ppermute | solution.py:848
  137.4 0.1 collective-permute-done.19
  137.6 0.1 concatenate.139
  137.7 1.8 %collective-permute-start.20 = (bf16[112,512]{1,0:T(8,128)(2,1)S(1)}, bf16[112,512]{1,0:T(8,128)(2,1)S(1)}, u32[]{:S(2)}, u32[]{:S(2)}) collective-permute-start(bf16[112,512]{1,0:T(8,128)(2,1)S(1)} %concatenate.139), channel_id=1, source_target_pairs={{0,4},{2,6},{4,0},{6,2},{8,12},{10,14},{12,8},{14,10},{16,20},{18,... | collective-permute-start | bytes 344072 | tf_op jit(solution)/shard_map/ppermute | solution.py:822
  139.5 1.0 collective-permute-start.21
  140.5 10.6 %collective-permute-done.20 = bf16[112,512]{1,0:T(8,128)(2,1)S(1)} collective-permute-done((bf16[112,512]{1,0:T(8,128)(2,1)S(1)}, bf16[112,512]{1,0:T(8,128)(2,1)S(1)}, u32[]{:S(2)}, u32[]{:S(2)}) %collective-permute-start.20) | collective-permute-done | bytes 114720 | tf_op jit(solution)/shard_map/ppermute | solution.py:822
  151.1 0.4 collective-permute-start.22
  151.5 1.6 collective-permute-done.21
  153.1 3.7 %collective-permute-done.22 = bf16[112,512]{1,0:T(8,128)(2,1)S(1)} collective-permute-done((bf16[112,512]{1,0:T(8,128)(2,1)S(1)}, bf16[112,512]{1,0:T(8,128)(2,1)S(1)}, u32[]{:S(2)}, u32[]{:S(2)}) %collective-permute-start.22) | collective-permute-done | bytes 114720 | tf_op jit(solution)/shard_map/ppermute | solution.py:848
  157.0 0.2 maximum_select_fusion.1
  157.3 0.2 maximum_select_fusion.2
  157.5 0.2 maximum_select_fusion.ffn_mine
  157.7 0.3 concatenate.159
  158.0 0.5 collective-permute-start.27
  158.5 2.9 %collective-permute-done.27.attn_sibling = bf16[400,512]{1,0:T(8,128)(2,1)S(1)} collective-permute-done((bf16[400,512]{1,0:T(8,128)(2,1)S(1)}, bf16[400,512]{1,0:T(8,128)(2,1)S(1)}, u32[]{:S(2)}, u32[]{:S(2)}) %collective-permute-start.27) | collective-permute-done | bytes 409632 | tf_op jit(solution)/shard_map/ppermute | solution.py:822
  161.5 3.7 %shard_map.262 = (f32[512,256]{1,0:T(8,128)}, f32[512,256]{1,0:T(8,128)}, f32[512,256]{1,0:T(8,128)}, f32[256,512]{1,0:T(8,128)}, f32[512,1024]{1,0:T(8,128)}, /...) custom-call(bf16[2,576,512]{2,1,0:T(8,128)(2,1)S(1)} %maximum_select, ...), custom_call_target="tpu_custom_call" | custom-call | tf_op jit(solution)/shard_map/pallas_call | solution.py:808
  (90 shorter events, 1.2 us)
Async XLA Ops:
  0.6 5.2 %copy-start.18 = (bf16[1024,512]{1,0:T(8,128)(2,1)S(1)}, bf16[1024,512]{1,0:T(8,128)(2,1)}, u32[]{:S(2)}) copy-start(bf16[1024,512]{1,0:T(8,128)(2,1)} %down_far.1) | copy-start | bytes 3145732
  1.7 4.2 %copy-start.17 = (bf16[512,1024]{1,0:T(8,128)(2,1)S(1)}, bf16[512,1024]{1,0:T(8,128)(2,1)}, u32[]{:S(2)}) copy-start(bf16[512,1024]{1,0:T(8,128)(2,1)} %up_far.1) | copy-start | bytes 3145732
  2.8 21.6 %collective-permute-start = (bf16[256,768]{1,0:T(8,128)(2,1)S(1)}, bf16[256,768]{1,0:T(8,128)(2,1)S(1)}, u32[]{:S(2)}, u32[]{:S(2)}) collective-permute-start(bf16[256,768]{1,0:T(8,128)(2,1)S(1)} %pad_maximum_fusion.1), channel_id=1, source_target_pairs={{0,1},{1,0},{2,3},{3,2},{4,5},{5,4},{6,7},{7,6},{8,9},{9,8},{10,11... | collective-permute-start | bytes 1179656 | tf_op jit(solution)/shard_map/ppermute | solution.py:822
  6.9 1.0 copy-start.8
  6.9 1.0 copy-start.9
  6.9 1.1 copy-start.10
  6.9 1.1 copy-start.11
  6.9 1.1 copy-start.12
  7.0 33.6 %collective-permute-start.2 = (bf16[1152,512]{1,0:T(8,128)(2,1)S(1)}, bf16[1152,512]{1,0:T(8,128)(2,1)S(1)}, u32[]{:S(2)}, u32[]{:S(2)}) collective-permute-start(bf16[1152,512]{1,0:T(8,128)(2,1)S(1)} %pad_maximum_fusion), channel_id=1, source_target_pairs={{0,1},{1,0},{2,3},{3,2},{4,5},{5,4},{6,7},{7,6},{8,9},{9,8},{10,11... | collective-permute-start | bytes 3538952 | tf_op jit(solution)/shard_map/ppermute | solution.py:822
  23.6 0.8 copy-start.3
  24.4 1.7 %collective-permute-start.1 = (bf16[256,768]{1,0:T(8,128)(2,1)S(1)}, bf16[256,768]{1,0:T(8,128)(2,1)S(1)}, u32[]{:S(2)}, u32[]{:S(2)}) collective-permute-start(bf16[256,768]{1,0:T(8,128)(2,1)S(1)} %collective-permute-done.mine_ref), channel_id=1, source_target_pairs={{0,2},{2,0},{4,6},{6,4},{8,10},{10,8},{12,14},{14,12},{16,18},{18,... | collective-permute-start | bytes 1179656 | tf_op jit(solution)/shard_map/ppermute | solution.py:822
  39.8 0.8 copy-start.13
  40.6 2.9 %copy-start.19 = (bf16[1152,512]{1,0:T(8,128)(2,1)}, bf16[1152,512]{1,0:T(8,128)(2,1)S(1)}, u32[]{:S(2)}) copy-start(bf16[1152,512]{1,0:T(8,128)(2,1)S(1)} %collective-permute-done.2.mine_far) | copy-start | bytes 3538948
  40.6 2.8 %collective-permute-start.3 = (bf16[1152,512]{1,0:T(8,128)(2,1)S(1)}, bf16[1152,512]{1,0:T(8,128)(2,1)S(1)}, u32[]{:S(2)}, u32[]{:S(2)}) collective-permute-start(bf16[1152,512]{1,0:T(8,128)(2,1)S(1)} %collective-permute-done.2.mine_far), channel_id=1, source_target_pairs={{0,2},{2,0},{4,6},{6,4},{8,10},{10,8},{12,14},{14,12},{16,18},{18,... | collective-permute-start | bytes 3538952 | tf_op jit(solution)/shard_map/ppermute | solution.py:822
  43.4 1.1 copy-start.20
  74.3 3.1 %collective-permute-start.5 = (bf16[2,576,512]{2,1,0:T(8,128)(2,1)}, bf16[2,576,512]{2,1,0:T(8,128)(2,1)S(1)}, u32[]{:S(2)}, u32[]{:S(2)}) collective-permute-start(bf16[2,576,512]{2,1,0:T(8,128)(2,1)} %get-tuple-element.103), channel_id=1, source_target_pairs={{0,2},{2,0},{4,6},{6,4},{8,10},{10,8},{12,14},{14,12},{16,18},{18,... | collective-permute-start | bytes 3538952 | tf_op jit(solution)/shard_map/ppermute | solution.py:822
  74.5 6.0 %collective-permute-start.4 = (bf16[2,576,512]{2,1,0:T(8,128)(2,1)}, bf16[2,576,512]{2,1,0:T(8,128)(2,1)S(1)}, u32[]{:S(2)}, u32[]{:S(2)}) collective-permute-start(bf16[2,576,512]{2,1,0:T(8,128)(2,1)} %get-tuple-element.101), channel_id=1, source_target_pairs={{0,2},{2,0},{4,6},{6,4},{8,10},{10,8},{12,14},{14,12},{16,18},{18,... | collective-permute-start | bytes 3538952 | tf_op jit(solution)/shard_map/ppermute | solution.py:822
  77.4 3.1 %copy-start.16 = (bf16[2,576,512]{2,1,0:T(8,128)(2,1)S(1)}, bf16[2,576,512]{2,1,0:T(8,128)(2,1)}, u32[]{:S(2)}) copy-start(bf16[2,576,512]{2,1,0:T(8,128)(2,1)} %get-tuple-element.100) | copy-start | bytes 3538948
  79.1 17.2 %collective-permute-start.7 = (bf16[576,512]{1,0:T(8,128)(2,1)S(1)}, bf16[576,512]{1,0:T(8,128)(2,1)S(1)}, u32[]{:S(2)}, u32[]{:S(2)}) collective-permute-start(bf16[576,512]{1,0:T(8,128)(2,1)S(1)} %get-tuple-element.168), channel_id=1, source_target_pairs={{0,1},{1,0},{2,3},{3,2},{4,5},{5,4},{6,7},{7,6},{8,9},{9,8},{10,11... | collective-permute-start | bytes 1769480 | tf_op jit(solution)/shard_map/ppermute | solution.py:822
  80.5 1.9 %copy-start.7 = (bf16[512,768]{1,0:T(8,128)(2,1)S(1)}, bf16[512,768]{1,0:T(8,128)(2,1)}, u32[]{:S(2)}) copy-start(bf16[512,768]{1,0:T(8,128)(2,1)} %get-tuple-element.106.pack_ref.oth_pack_ref) | copy-start | bytes 2359300
  80.5 1.9 %copy-start.14 = (bf16[2,512,256]{2,1,0:T(8,128)(2,1)S(1)}, bf16[2,512,256]{2,1,0:T(8,128)(2,1)}, u32[]{:S(2)}) copy-start(bf16[2,512,256]{2,1,0:T(8,128)(2,1)} %copy-done.13) | copy-start | bytes 1572868
  80.5 1.9 %copy-start.15 = (bf16[2,512,256]{2,1,0:T(8,128)(2,1)S(1)}, bf16[2,512,256]{2,1,0:T(8,128)(2,1)}, u32[]{:S(2)}) copy-start(bf16[2,512,256]{2,1,0:T(8,128)(2,1)} %get-tuple-element.105.gctx_ref) | copy-start | bytes 1572868
  80.9 15.6 %collective-permute-start.6 = (bf16[2,288,512]{2,1,0:T(8,128)(2,1)S(1)}, bf16[2,288,512]{2,1,0:T(8,128)(2,1)S(1)}, u32[]{:S(2)}, u32[]{:S(2)}) collective-permute-start(bf16[2,288,512]{2,1,0:T(8,128)(2,1)S(1)} %get-tuple-element.104), channel_id=1, source_target_pairs={{0,4},{2,6},{4,0},{6,2},{8,12},{10,14},{12,8},{14,10},{16,20},{18,... | collective-permute-start | bytes 1769480 | tf_op jit(solution)/shard_map/ppermute | solution.py:822
  96.2 2.0 %copy-start.5 = (bf16[2,512,256]{2,1,0:T(8,128)(2,1)S(1)}, bf16[2,512,256]{2,1,0:T(8,128)(2,1)}, u32[]{:S(2)}) copy-start(bf16[2,512,256]{2,1,0:T(8,128)(2,1)} %get-tuple-element.125.gctx_ref) | copy-start | bytes 1572868
  96.3 2.0 %copy-start = (bf16[2,1024,512]{2,1,0:T(8,128)(2,1)S(1)}, bf16[2,1024,512]{2,1,0:T(8,128)(2,1)}, u32[]{:S(2)}) copy-start(bf16[2,1024,512]{2,1,0:T(8,128)(2,1)} %get-tuple-element.89.kv_ref.kv_far) | copy-start | bytes 6291460
  96.5 1.8 %copy-start.1 = (bf16[512,768]{1,0:T(8,128)(2,1)S(1)}, bf16[512,768]{1,0:T(8,128)(2,1)}, u32[]{:S(2)}) copy-start(bf16[512,768]{1,0:T(8,128)(2,1)} %get-tuple-element.117.pack_ref.own_pack_ref) | copy-start | bytes 2359300
  96.5 1.9 %copy-start.4 = (bf16[2,512,256]{2,1,0:T(8,128)(2,1)S(1)}, bf16[2,512,256]{2,1,0:T(8,128)(2,1)}, u32[]{:S(2)}) copy-start(bf16[2,512,256]{2,1,0:T(8,128)(2,1)} %copy-done.3) | copy-start | bytes 1572868
  96.5 9.3 %collective-permute-start.8 = (bf16[288,512]{1,0:T(8,128)(2,1)S(1)}, bf16[288,512]{1,0:T(8,128)(2,1)S(1)}, u32[]{:S(2)}, u32[]{:S(2)}) collective-permute-start(bf16[288,512]{1,0:T(8,128)(2,1)S(1)} %get-tuple-element.177), channel_id=1, source_target_pairs={{0,4},{2,6},{4,0},{6,2},{8,12},{10,14},{12,8},{14,10},{16,20},{18,... | collective-permute-start | bytes 884744 | tf_op jit(solution)/shard_map/ppermute | solution.py:822
  97.7 8.1 %collective-permute-start.9 = (bf16[288,512]{1,0:T(8,128)(2,1)S(1)}, bf16[288,512]{1,0:T(8,128)(2,1)S(1)}, u32[]{:S(2)}, u32[]{:S(2)}) collective-permute-start(bf16[288,512]{1,0:T(8,128)(2,1)S(1)} %get-tuple-element.114), channel_id=1, source_target_pairs={{0,1},{1,0},{2,3},{3,2},{4,5},{5,4},{6,7},{7,6},{8,9},{9,8},{10,11... | collective-permute-start | bytes 884744 | tf_op jit(solution)/shard_map/ppermute | solution.py:822
  98.2 8.0 %collective-permute-start.10 = (bf16[3,128,512]{2,1,0:T(8,128)(2,1)S(1)}, bf16[3,128,512]{2,1,0:T(8,128)(2,1)S(1)}, u32[]{:S(2)}, u32[]{:S(2)}) collective-permute-start(bf16[3,128,512]{2,1,0:T(8,128)(2,1)S(1)} %slice_bitcast_fusion), channel_id=1, source_target_pairs={{0,2},{2,0},{4,6},{6,4},{8,10},{10,8},{12,14},{14,12},{16,18},{18,... | collective-permute-start | bytes 1179656 | tf_op jit(solution)/shard_map/ppermute | solution.py:822
  106.4 10.9 %collective-permute-start.13 = (bf16[288,512]{1,0:T(8,128)(2,1)S(1)}, bf16[288,512]{1,0:T(8,128)(2,1)S(1)}, u32[]{:S(2)}, u32[]{:S(2)}) collective-permute-start(bf16[288,512]{1,0:T(8,128)(2,1)S(1)} %add_convert_fusion.7), channel_id=1, source_target_pairs={{0,8},{2,10},{4,12},{6,14},{8,0},{10,2},{12,4},{14,6},{16,24},{18,... | collective-permute-start | bytes 884744 | tf_op jit(solution)/shard_map/ppermute | solution.py:822
  107.6 12.8 %collective-permute-start.12 = (bf16[3,128,512]{2,1,0:T(8,128)(2,1)S(1)}, bf16[3,128,512]{2,1,0:T(8,128)(2,1)S(1)}, u32[]{:S(2)}, u32[]{:S(2)}) collective-permute-start(bf16[3,128,512]{2,1,0:T(8,128)(2,1)S(1)} %bitcast.79), channel_id=1, source_target_pairs={{0,2},{2,0},{4,6},{6,4},{8,10},{10,8},{12,14},{14,12},{16,18},{18,... | collective-permute-start | bytes 1179656 | tf_op jit(solution)/shard_map/ppermute | solution.py:822
  107.7 12.7 %collective-permute-start.11 = (bf16[3,128,512]{2,1,0:T(8,128)(2,1)S(1)}, bf16[3,128,512]{2,1,0:T(8,128)(2,1)S(1)}, u32[]{:S(2)}, u32[]{:S(2)}) collective-permute-start(bf16[3,128,512]{2,1,0:T(8,128)(2,1)S(1)} %fusion), channel_id=1, source_target_pairs={{0,1},{1,0},{2,3},{3,2},{4,5},{5,4},{6,7},{7,6},{8,9},{9,8},{10,11... | collective-permute-start | bytes 1179656 | tf_op jit(solution)/shard_map/ppermute | solution.py:822
  109.8 15.2 %copy-start.6 = (bf16[2,512,512]{2,1,0:T(8,128)(2,1)S(1)}, bf16[2,512,512]{2,1,0:T(8,128)(2,1)}, u32[]{:S(2)}) copy-start(bf16[2,512,512]{2,1,0:T(8,128)(2,1)} %tok_ref.4) | copy-start | bytes 3145732
  117.3 7.6 %copy-start.2 = (f32[2,512,512]{2,1,0:T(8,128)S(1)}, f32[2,512,512]{2,1,0:T(8,128)}, u32[]{:S(2)}) copy-start(f32[2,512,512]{2,1,0:T(8,128)} %get-tuple-element.133.grad_hidden_ref) | copy-start | bytes 6291460
  117.8 15.9 %collective-permute-start.14 = (bf16[288,512]{1,0:T(8,128)(2,1)S(1)}, bf16[288,512]{1,0:T(8,128)(2,1)S(1)}, u32[]{:S(2)}, u32[]{:S(2)}) collective-permute-start(bf16[288,512]{1,0:T(8,128)(2,1)S(1)} %add_convert_fusion.5), channel_id=1, source_target_pairs={{0,16},{2,18},{4,20},{6,22},{8,24},{10,26},{12,28},{14,30},{16,0},... | collective-permute-start | bytes 884744 | tf_op jit(solution)/shard_map/ppermute | solution.py:822
  120.6 8.5 %collective-permute-start.15 = (bf16[3,32,512]{2,1,0:T(8,128)(2,1)S(1)}, bf16[3,32,512]{2,1,0:T(8,128)(2,1)S(1)}, u32[]{:S(2)}, u32[]{:S(2)}) collective-permute-start(bf16[3,32,512]{2,1,0:T(8,128)(2,1)S(1)} %get-tuple-element.131), channel_id=1, source_target_pairs={{0,4},{2,6},{4,0},{6,2},{8,12},{10,14},{12,8},{14,10},{16,20},{18,... | collective-permute-start | bytes 294920 | tf_op jit(solution)/shard_map/ppermute | solution.py:822
  121.4 7.7 %collective-permute-start.16 = (bf16[3,32,512]{2,1,0:T(8,128)(2,1)S(1)}, bf16[3,32,512]{2,1,0:T(8,128)(2,1)S(1)}, u32[]{:S(2)}, u32[]{:S(2)}) collective-permute-start(bf16[3,32,512]{2,1,0:T(8,128)(2,1)S(1)} %get-tuple-element.172), channel_id=1, source_target_pairs={{0,8},{2,10},{4,12},{6,14},{8,0},{10,2},{12,4},{14,6},{16,24},{18,... | collective-permute-start | bytes 294920 | tf_op jit(solution)/shard_map/ppermute | solution.py:822
  122.2 7.7 %collective-permute-start.17 = (bf16[3,32,512]{2,1,0:T(8,128)(2,1)S(1)}, bf16[3,32,512]{2,1,0:T(8,128)(2,1)S(1)}, u32[]{:S(2)}, u32[]{:S(2)}) collective-permute-start(bf16[3,32,512]{2,1,0:T(8,128)(2,1)S(1)} %get-tuple-element.171), channel_id=1, source_target_pairs={{0,12},{2,14},{4,8},{6,10},{8,4},{10,6},{12,0},{14,2},{16,28},{18,... | collective-permute-start | bytes 294920 | tf_op jit(solution)/shard_map/ppermute | solution.py:848
  124.2 4.9 %collective-permute-start.18 = (f32[5,512]{1,0:T(8,128)S(1)}, f32[5,512]{1,0:T(8,128)S(1)}, u32[]{:S(2)}, u32[]{:S(2)}) collective-permute-start(f32[5,512]{1,0:T(8,128)S(1)} %pad_maximum_fusion.2), channel_id=1, source_target_pairs={{0,1},{1,0},{2,3},{3,2},{4,5},{5,4},{6,7},{7,6},{8,9},{9,8},{10,11... | collective-permute-start | bytes 30728 | tf_op jit(solution)/shard_map/ppermute | solution.py:822
  130.2 7.3 %collective-permute-start.19 = (bf16[112,512]{1,0:T(8,128)(2,1)S(1)}, bf16[112,512]{1,0:T(8,128)(2,1)S(1)}, u32[]{:S(2)}, u32[]{:S(2)}) collective-permute-start(bf16[112,512]{1,0:T(8,128)(2,1)S(1)} %concatenate.137), channel_id=1, source_target_pairs={{0,16},{2,18},{4,20},{6,22},{8,24},{10,26},{12,28},{14,30},{16,0},... | collective-permute-start | bytes 344072 | tf_op jit(solution)/shard_map/ppermute | solution.py:822
  133.8 22.9 %collective-permute-start.23 = (bf16[288,512]{1,0:T(8,128)(2,1)S(1)}, bf16[288,512]{1,0:T(8,128)(2,1)S(1)}, u32[]{:S(2)}, u32[]{:S(2)}) collective-permute-start(bf16[288,512]{1,0:T(8,128)(2,1)S(1)} %add_convert_fusion.4), channel_id=1, source_target_pairs={{0,4},{2,6},{4,0},{6,2},{8,12},{10,14},{12,8},{14,10},{16,20},{18,... | collective-permute-start | bytes 884744 | tf_op jit(solution)/shard_map/ppermute | solution.py:822
  134.3 22.4 %collective-permute-start.24 = (bf16[288,512]{1,0:T(8,128)(2,1)S(1)}, bf16[288,512]{1,0:T(8,128)(2,1)S(1)}, u32[]{:S(2)}, u32[]{:S(2)}) collective-permute-start(bf16[288,512]{1,0:T(8,128)(2,1)S(1)} %add_convert_fusion.4), channel_id=1, source_target_pairs={{0,8},{2,10},{4,12},{6,14},{8,0},{10,2},{12,4},{14,6},{16,24},{18,... | collective-permute-start | bytes 884744 | tf_op jit(solution)/shard_map/ppermute | solution.py:822
  135.1 21.7 %collective-permute-start.25 = (bf16[288,512]{1,0:T(8,128)(2,1)S(1)}, bf16[288,512]{1,0:T(8,128)(2,1)S(1)}, u32[]{:S(2)}, u32[]{:S(2)}) collective-permute-start(bf16[288,512]{1,0:T(8,128)(2,1)S(1)} %add_convert_fusion.4), channel_id=1, source_target_pairs={{0,12},{2,14},{4,8},{6,10},{8,4},{10,6},{12,0},{14,2},{16,28},{18,... | collective-permute-start | bytes 884744 | tf_op jit(solution)/shard_map/ppermute | solution.py:848
  137.7 13.4 %collective-permute-start.20 = (bf16[112,512]{1,0:T(8,128)(2,1)S(1)}, bf16[112,512]{1,0:T(8,128)(2,1)S(1)}, u32[]{:S(2)}, u32[]{:S(2)}) collective-permute-start(bf16[112,512]{1,0:T(8,128)(2,1)S(1)} %concatenate.139), channel_id=1, source_target_pairs={{0,4},{2,6},{4,0},{6,2},{8,12},{10,14},{12,8},{14,10},{16,20},{18,... | collective-permute-start | bytes 344072 | tf_op jit(solution)/shard_map/ppermute | solution.py:822
  139.5 13.6 %collective-permute-start.21 = (bf16[112,512]{1,0:T(8,128)(2,1)S(1)}, bf16[112,512]{1,0:T(8,128)(2,1)S(1)}, u32[]{:S(2)}, u32[]{:S(2)}) collective-permute-start(bf16[112,512]{1,0:T(8,128)(2,1)S(1)} %concatenate.139), channel_id=1, source_target_pairs={{0,8},{2,10},{4,12},{6,14},{8,0},{10,2},{12,4},{14,6},{16,24},{18,... | collective-permute-start | bytes 344072 | tf_op jit(solution)/shard_map/ppermute | solution.py:822
  151.1 5.7 %collective-permute-start.22 = (bf16[112,512]{1,0:T(8,128)(2,1)S(1)}, bf16[112,512]{1,0:T(8,128)(2,1)S(1)}, u32[]{:S(2)}, u32[]{:S(2)}) collective-permute-start(bf16[112,512]{1,0:T(8,128)(2,1)S(1)} %concatenate.139), channel_id=1, source_target_pairs={{0,12},{2,14},{4,8},{6,10},{8,4},{10,6},{12,0},{14,2},{16,28},{18,... | collective-permute-start | bytes 344072 | tf_op jit(solution)/shard_map/ppermute | solution.py:848
  158.0 3.5 %collective-permute-start.26 = (bf16[2,576,512]{2,1,0:T(8,128)(2,1)S(1)}, bf16[2,576,512]{2,1,0:T(8,128)(2,1)S(1)}, u32[]{:S(2)}, u32[]{:S(2)}) collective-permute-start(bf16[2,576,512]{2,1,0:T(8,128)(2,1)S(1)} %maximum_select_fusion.ffn_mine), channel_id=1, source_target_pairs={{0,2},{2,0},{4,6},{6,4},{8,10},{10,8},{12,14},{14,12},{16,18},{18,... | collective-permute-start | bytes 3538952 | tf_op jit(solution)/shard_map/ppermute | solution.py:822
  158.0 3.4 %collective-permute-start.27 = (bf16[400,512]{1,0:T(8,128)(2,1)S(1)}, bf16[400,512]{1,0:T(8,128)(2,1)S(1)}, u32[]{:S(2)}, u32[]{:S(2)}) collective-permute-start(bf16[400,512]{1,0:T(8,128)(2,1)S(1)} %concatenate.159), channel_id=1, source_target_pairs={{0,2},{2,0},{4,6},{6,4},{8,10},{10,8},{12,14},{14,12},{16,18},{18,... | collective-permute-start | bytes 1228808 | tf_op jit(solution)/shard_map/ppermute | solution.py:822

commit v7 on v6

--- a/solution.py
+++ b/solution.py
@@ -1059,14 +1059,14 @@
     sent_z = attn.total(lambda p: quarter(p, 0, 1))
     sent_d = attn.total(lambda p: quarter(p, 1, 1))
     kept = attn.total(lambda p: quarter(p, 0, 0))
+    come_d = swap_diagonal(sent_d, first_bit, last_bit)
+    come_z = swap(sent_z, "dp", last_bit)
     come_x = swap(sent_x, "dp", first_bit)
-    come_z = swap(sent_z, "dp", last_bit)
-    come_d = swap_diagonal(sent_d, first_bit, last_bit)
     small_sent = after(small, sent_x, sent_z, sent_d)
     small_come = swap(small_sent, "mp", 1)
     grad_input = input_grad(
         tokens,
-        after(grad_hidden, small_sent),
+        after(grad_hidden, sent_x, sent_z, sent_d),
         attn_gain,
         (g_oth, g_own_first, g_own_last),
         (oth[0], own[0]),

time: 166 us -> 165 us (level)
  transfers between devices with their start and end apart: 28 -> 28, of which waited for: 10 -> 12; matrix products, arithmetic and copies ran while one was open for 3% -> 4% of each run, Pallas kernels for 38% -> 38%
where the time goes in v7:
time: 165 us; the launch traced here: 164 us
  Pallas kernels  95.5 us (58%)
  starting transfers between devices  28.9 us (18%)
  waiting for transfers between devices  25.7 us (16%)
  local copies, waits for them, and re-layouts  8.01 us (5%)
  other arithmetic  4.63 us (3%)
    pallas_call x1, Pallas kernels, middle_layer(): pl.pallas_call(middle_body, grid=(tiles,), in_specs=[tiled(width), tiled(...  29.7 us
    pallas_call x2, Pallas kernels, attention_forward(): pl.pallas_call(body, grid=(rows, pairs), in_specs=in_specs, out_specs=out...  29.3 us
    pallas_call x3, Pallas kernels, attention_backward(): pl.pallas_call(backward_body, grid=(many, rows, 2), in_specs=[pl.BlockSpe...  28.7 us
    ppermute x25, starting transfers between devices, swap(): return lax.ppermute(array, axis, [(i, i ^ bit) for i in range(size)])  24.5 us
    ppermute x25, waiting for transfers between devices, swap(): return lax.ppermute(array, axis, [(i, i ^ bit) for i in range(size)])  21.7 us
    ppermute x3, starting transfers between devices, swap_diagonal(): lax.ppermute(array, 'dp', [(i, i ^ first ^ last) for i in range(size)])  4.41 us
    pallas_call x1, Pallas kernels, input_grad(): pl.pallas_call(input_body, grid=(rows,), in_specs=[row, row, whole(gain),...  4.17 us
    ppermute x3, waiting for transfers between devices, swap_diagonal(): lax.ppermute(array, 'dp', [(i, i ^ first ^ last) for i in range(size)])  4 us
  transfers between devices with their start and end apart: 28, of which 12 were waited for; matrix products, arithmetic and copies ran while one was open for 4% of the time, Pallas kernels for 38%

profile of v7, /device:TPU:0, one launch (start us, length us, event | category | flops | bytes accessed | tf_op | source)
XLA Modules:
  0.0 164.1 jit_solution(14189038920095294862)
XLA Ops:
  0.7 1.0 constant_dynamic-slice_fusion.5
  1.7 1.1 constant_dynamic-slice_fusion.3
  2.8 3.0 %collective-permute-start = (bf16[256,768]{1,0:T(8,128)(2,1)S(1)}, bf16[256,768]{1,0:T(8,128)(2,1)S(1)}, u32[]{:S(2)}, u32[]{:S(2)}) collective-permute-start(bf16[256,768]{1,0:T(8,128)(2,1)S(1)} %pad_maximum_fusion.1), channel_id=1, source_target_pairs={{0,1},{1,0},{2,3},{3,2},{4,5},{5,4},{6,7},{7,6},{8,9},{9,8},{10,11... | collective-permute-start | bytes 1179656 | tf_op jit(solution)/shard_map/ppermute | solution.py:822
  6.0 0.9 constant_dynamic-slice_fusion.1
  7.0 0.2 collective-permute-start.2
  7.2 0.6 copy-done.8
  8.0 15.6 %shard_map.255 = (bf16[2,1024,512]{2,1,0:T(8,128)(2,1)}, bf16[512,768]{1,0:T(8,128)(2,1)}, bf16[2,2,2560,128]{3,2,1,0:T(8,128)(2,1)}, bf16[2,2,2,512,1024]{4,3,2,1,0:T(8,128)(2,1)}, bf16[2,512,256]{2,1,0:T(8,128)(2,1)S(1)}) custom-call(s32[4]{0:T(128)S(1)} %copy-done.12, bf16[2,512,512]{2,1,0:T(8,128)(2,1)} %tok_ref.4, bf16[4,512,512]{2,1,0:T(8,128)(2,1)} %mem_ref.1, ...), custom_call_target="tpu_custom_call" | custom-call | flops 6000000000 | bytes 16777216 | tf_op jit(solution)/shard_map/pallas_call | solution.py:180
  23.6 0.8 copy-done.3
  24.4 1.7 %collective-permute-done.1.sibling_ref = bf16[256,768]{1,0:T(8,128)(2,1)S(1)} collective-permute-done((bf16[256,768]{1,0:T(8,128)(2,1)S(1)}, bf16[256,768]{1,0:T(8,128)(2,1)S(1)}, u32[]{:S(2)}, u32[]{:S(2)}) %collective-permute-start.1) | collective-permute-done | bytes 393248 | tf_op jit(solution)/shard_map/ppermute | solution.py:822
  26.1 13.7 %shard_map.256 = (bf16[512,768]{1,0:T(8,128)(2,1)}, bf16[2,2,2560,128]{3,2,1,0:T(8,128)(2,1)}, bf16[2,2,2,512,1024]{4,3,2,1,0:T(8,128)(2,1)}, bf16[2,512,256]{2,1,0:T(8,128)(2,1)S(1)}) custom-call(s32[4]{0:T(128)S(1)} %copy-done.12, bf16[2,1024,512]{2,1,0:T(8,128)(2,1)} %get-tuple-element.89.kv_ref.kv_far, ...), custom_call_target="tpu_custom_call" | custom-call | flops 6000000000 | bytes 16777216 | tf_op jit(solution)/shard_map/pallas_call | solution.py:180
  39.8 0.8 copy-done.13
  40.6 2.8 %collective-permute-done.3.sibling_far = bf16[1152,512]{1,0:T(8,128)(2,1)S(1)} collective-permute-done((bf16[1152,512]{1,0:T(8,128)(2,1)S(1)}, bf16[1152,512]{1,0:T(8,128)(2,1)S(1)}, u32[]{:S(2)}, u32[]{:S(2)}) %collective-permute-start.3) | collective-permute-done | bytes 1179680 | tf_op jit(solution)/shard_map/ppermute | solution.py:822
  43.5 1.1 copy-done.20
  44.5 29.7 %shard_map.257 = (bf16[2,512,512]{2,1,0:T(8,128)(2,1)}, f32[2,512,512]{2,1,0:T(8,128)}, bf16[2,512,256]{2,1,0:T(8,128)(2,1)}, bf16[2,512,256]{2,1,0:T(8,128)(2,1...) custom-call(bf16[2,512,512]{2,1,0:T(8,128)(2,1)} %tok_ref.4, ...), custom_call_target="tpu_custom_call" | custom-call | flops 15000000512 | bytes 31457280 | tf_op jit(solution)/shard_map/pallas_call | solution.py:460
  74.3 0.2 collective-permute-start.5
  74.5 0.4 collective-permute-start.4
  74.8 0.7 slice.124
  75.6 1.8 %collective-permute-done.5 = bf16[2,576,512]{2,1,0:T(8,128)(2,1)S(1)} collective-permute-done((bf16[2,576,512]{2,1,0:T(8,128)(2,1)}, bf16[2,576,512]{2,1,0:T(8,128)(2,1)S(1)}, u32[]{:S(2)}, u32[]{:S(2)}) %collective-permute-start.5) | collective-permute-done | bytes 1179680 | tf_op jit(solution)/shard_map/ppermute | solution.py:822
  77.4 1.7 %add_convert_fusion = (bf16[1,576,512]{2,1,0:T(8,128)(2,1)S(1)}, bf16[576,512]{1,0:T(8,128)(2,1)S(1)}) fusion(bf16[2,576,512]{2,1,0:T(8,128)(2,1)S(1)} %collective-permute-done.5, bf16[2,576,512]{2,1,0:T(8,128)(2,1)} %get-tuple-element.104), kind=kLoop, calls=%fused_computation.2 | loop fusion | flops 2359296 | bytes 3538944 | tf_op jit(solution)/shard_map/convert_element_type | solution.py:870
  79.1 1.4 collective-permute-start.7
  80.5 0.3 add_convert_fusion.1
  80.9 1.5 collective-permute-start.6
  82.4 13.8 %shard_map.258 = (bf16[2,2,384,512]{3,2,1,0:T(8,128)(2,1)S(1)}, bf16[2,3,128,512]{3,2,1,0:T(8,128)(2,1)S(1)}, f32[2,8,512]{2,1,0:T(8,128)S(1)}) custom-call(s32[4]{0:T(128)S(1)} %copy-done.12, bf16[2,2,2560,128]{3,2,1,0:T(8,128)(2,1)} %get-tuple-element.99.qkv_ref, bf16[2,2,2,512,1024]{4,3,2,1,0:T(8,128)(2,1)} %get-tuple-element.100.p_ref, ...), custom_call_target="tpu_custom_call" | custom-call | flops 8000000000 | bytes 16777216 | tf_op jit(solution)/shard_map/pallas_call | solution.py:629
  96.3 0.2 fusion.2
  96.5 1.0 collective-permute-start.8
  97.5 0.2 fusion.5
  97.7 0.6 collective-permute-start.9
  98.3 7.4 %shard_map.259 = (bf16[1,2,384,512]{3,2,1,0:T(8,128)(2,1)S(1)}, bf16[1,3,128,512]{3,2,1,0:T(8,128)(2,1)S(1)}, f32[1,8,512]{2,1,0:T(8,128)S(1)}) custom-call(s32[4]{0:T(128)S(1)} %copy-done.12, bf16[2,2,2560,128]{3,2,1,0:T(8,128)(2,1)} %get-tuple-element.96.qkv_ref, bf16[2,2,2,512,1024]{4,3,2,1,0:T(8,128)(2,1)} %get-tuple-element.97.p_ref, ...), custom_call_target="tpu_custom_call" | custom-call | flops 4000000000 | bytes 8388608 | tf_op jit(solution)/shard_map/pallas_call | solution.py:629
  105.8 0.4 add_convert_fusion.7
  106.3 0.1 fusion
  106.4 2.1 %collective-permute-start.13 = (bf16[288,512]{1,0:T(8,128)(2,1)S(1)}, bf16[288,512]{1,0:T(8,128)(2,1)S(1)}, u32[]{:S(2)}, u32[]{:S(2)}) collective-permute-start(bf16[288,512]{1,0:T(8,128)(2,1)S(1)} %add_convert_fusion.7), channel_id=1, source_target_pairs={{0,8},{2,10},{4,12},{6,14},{8,0},{10,2},{12,4},{14,6},{16,24},{18,... | collective-permute-start | bytes 884744 | tf_op jit(solution)/shard_map/ppermute | solution.py:822
  108.5 1.3 collective-permute-start.11
  109.8 7.5 %shard_map.260 = (bf16[1,2,384,512]{3,2,1,0:T(8,128)(2,1)S(1)}, bf16[1,3,128,512]{3,2,1,0:T(8,128)(2,1)S(1)}, f32[1,8,512]{2,1,0:T(8,128)S(1)}) custom-call(s32[4]{0:T(128)S(1)} %copy-done.12, bf16[2,2,2560,128]{3,2,1,0:T(8,128)(2,1)} %get-tuple-element.96.qkv_ref, bf16[2,2,2,512,1024]{4,3,2,1,0:T(8,128)(2,1)} %get-tuple-element.97.p_ref, ...), custom_call_target="tpu_custom_call" | custom-call | flops 4000000000 | bytes 8388608 | tf_op jit(solution)/shard_map/pallas_call | solution.py:629
  117.3 0.5 add_convert_fusion.5
  117.8 2.0 %collective-permute-start.14 = (bf16[288,512]{1,0:T(8,128)(2,1)S(1)}, bf16[288,512]{1,0:T(8,128)(2,1)S(1)}, u32[]{:S(2)}, u32[]{:S(2)}) collective-permute-start(bf16[288,512]{1,0:T(8,128)(2,1)S(1)} %add_convert_fusion.5), channel_id=1, source_target_pairs={{0,16},{2,18},{4,20},{6,22},{8,24},{10,26},{12,28},{14,30},{16,0},... | collective-permute-start | bytes 884744 | tf_op jit(solution)/shard_map/ppermute | solution.py:822
  119.8 0.2 collective-permute-done.11
  120.0 0.1 fusion.12
  120.1 0.9 collective-permute-start.15
  121.0 0.6 collective-permute-start.16
  121.7 2.0 %collective-permute-start.17 = (bf16[3,32,512]{2,1,0:T(8,128)(2,1)S(1)}, bf16[3,32,512]{2,1,0:T(8,128)(2,1)S(1)}, u32[]{:S(2)}, u32[]{:S(2)}) collective-permute-start(bf16[3,32,512]{2,1,0:T(8,128)(2,1)S(1)} %get-tuple-element.171), channel_id=1, source_target_pairs={{0,12},{2,14},{4,8},{6,10},{8,4},{10,6},{12,0},{14,2},{16,28},{18,... | collective-permute-start | bytes 294920 | tf_op jit(solution)/shard_map/ppermute | solution.py:848
  123.7 1.1 collective-permute-start.18
  124.8 4.2 %shard_map.261 = bf16[2,512,512]{2,1,0:T(8,128)(2,1)} custom-call(bf16[2,512,512]{2,1,0:T(8,128)(2,1)S(1)} %copy-done.6, f32[2,512,512]{2,1,0:T(8,128)S(1)} %copy-done.2, f32[1,512]{1,0:T(1,128)S(1)} %bitcast.78, bf16[2,2,384,512]{3,2,1,0:T(8,128)(2,1)S(1)} %get-tuple-element.129.oth_ref, bf16[1,2,384,512]{3,2,1,0:T(8,128)(2,1)S(1)} %get-tuple-element.130.own_first_ref, ...), custom_call_target="tpu_custom_call" | custom-call | flops 2000000000 | bytes 8388608 | tf_op jit(solution)/shard_map/pallas_call | solution.py:710
  128.9 0.2 collective-permute-done.16
  129.1 1.1 collective-permute-done.17
  130.3 0.1 concatenate.137
  130.5 2.8 %collective-permute-start.19 = (bf16[112,512]{1,0:T(8,128)(2,1)S(1)}, bf16[112,512]{1,0:T(8,128)(2,1)S(1)}, u32[]{:S(2)}, u32[]{:S(2)}) collective-permute-start(bf16[112,512]{1,0:T(8,128)(2,1)S(1)} %concatenate.137), channel_id=1, source_target_pairs={{0,16},{2,18},{4,20},{6,22},{8,24},{10,26},{12,28},{14,30},{16,0},... | collective-permute-start | bytes 344072 | tf_op jit(solution)/shard_map/ppermute | solution.py:822
  133.3 0.1 collective-permute-done.14
  133.5 0.9 collective-permute-start.23
  134.4 0.3 collective-permute-start.24
  134.7 2.4 %collective-permute-start.25 = (bf16[288,512]{1,0:T(8,128)(2,1)S(1)}, bf16[288,512]{1,0:T(8,128)(2,1)S(1)}, u32[]{:S(2)}, u32[]{:S(2)}) collective-permute-start(bf16[288,512]{1,0:T(8,128)(2,1)S(1)} %add_convert_fusion.4), channel_id=1, source_target_pairs={{0,12},{2,14},{4,8},{6,10},{8,4},{10,6},{12,0},{14,2},{16,28},{18,... | collective-permute-start | bytes 884744 | tf_op jit(solution)/shard_map/ppermute | solution.py:848
  137.0 0.8 collective-permute-done.19
  137.9 0.1 concatenate.139
  138.1 0.6 collective-permute-start.20
  138.6 3.0 %collective-permute-start.21 = (bf16[112,512]{1,0:T(8,128)(2,1)S(1)}, bf16[112,512]{1,0:T(8,128)(2,1)S(1)}, u32[]{:S(2)}, u32[]{:S(2)}) collective-permute-start(bf16[112,512]{1,0:T(8,128)(2,1)S(1)} %concatenate.139), channel_id=1, source_target_pairs={{0,8},{2,10},{4,12},{6,14},{8,0},{10,2},{12,4},{14,6},{16,24},{18,... | collective-permute-start | bytes 344072 | tf_op jit(solution)/shard_map/ppermute | solution.py:822
  141.6 8.2 %collective-permute-done.20 = bf16[112,512]{1,0:T(8,128)(2,1)S(1)} collective-permute-done((bf16[112,512]{1,0:T(8,128)(2,1)S(1)}, bf16[112,512]{1,0:T(8,128)(2,1)S(1)}, u32[]{:S(2)}, u32[]{:S(2)}) %collective-permute-start.20) | collective-permute-done | bytes 114720 | tf_op jit(solution)/shard_map/ppermute | solution.py:822
  149.9 2.7 %collective-permute-done.21 = bf16[112,512]{1,0:T(8,128)(2,1)S(1)} collective-permute-done((bf16[112,512]{1,0:T(8,128)(2,1)S(1)}, bf16[112,512]{1,0:T(8,128)(2,1)S(1)}, u32[]{:S(2)}, u32[]{:S(2)}) %collective-permute-start.21) | collective-permute-done | bytes 114720 | tf_op jit(solution)/shard_map/ppermute | solution.py:822
  152.6 2.9 %collective-permute-done.22 = bf16[112,512]{1,0:T(8,128)(2,1)S(1)} collective-permute-done((bf16[112,512]{1,0:T(8,128)(2,1)S(1)}, bf16[112,512]{1,0:T(8,128)(2,1)S(1)}, u32[]{:S(2)}, u32[]{:S(2)}) %collective-permute-start.22) | collective-permute-done | bytes 114720 | tf_op jit(solution)/shard_map/ppermute | solution.py:848
  155.9 0.2 maximum_select_fusion.1
  156.1 0.2 maximum_select_fusion.2
  156.3 0.2 maximum_select_fusion.ffn_mine
  156.5 0.3 concatenate.159
  156.9 0.5 collective-permute-start.27
  157.4 2.9 %collective-permute-done.27.attn_sibling = bf16[400,512]{1,0:T(8,128)(2,1)S(1)} collective-permute-done((bf16[400,512]{1,0:T(8,128)(2,1)S(1)}, bf16[400,512]{1,0:T(8,128)(2,1)S(1)}, u32[]{:S(2)}, u32[]{:S(2)}) %collective-permute-start.27) | collective-permute-done | bytes 409632 | tf_op jit(solution)/shard_map/ppermute | solution.py:822
  160.3 3.7 %shard_map.262 = (f32[512,256]{1,0:T(8,128)}, f32[512,256]{1,0:T(8,128)}, f32[512,256]{1,0:T(8,128)}, f32[256,512]{1,0:T(8,128)}, f32[512,1024]{1,0:T(8,128)}, /...) custom-call(bf16[2,576,512]{2,1,0:T(8,128)(2,1)S(1)} %maximum_select, ...), custom_call_target="tpu_custom_call" | custom-call | tf_op jit(solution)/shard_map/pallas_call | solution.py:808
  (90 shorter events, 1.2 us)
Async XLA Ops:
  0.6 5.2 %copy-start.18 = (bf16[1024,512]{1,0:T(8,128)(2,1)S(1)}, bf16[1024,512]{1,0:T(8,128)(2,1)}, u32[]{:S(2)}) copy-start(bf16[1024,512]{1,0:T(8,128)(2,1)} %down_far.1) | copy-start | bytes 3145732
  1.7 4.2 %copy-start.17 = (bf16[512,1024]{1,0:T(8,128)(2,1)S(1)}, bf16[512,1024]{1,0:T(8,128)(2,1)}, u32[]{:S(2)}) copy-start(bf16[512,1024]{1,0:T(8,128)(2,1)} %up_far.1) | copy-start | bytes 3145732
  2.8 21.6 %collective-permute-start = (bf16[256,768]{1,0:T(8,128)(2,1)S(1)}, bf16[256,768]{1,0:T(8,128)(2,1)S(1)}, u32[]{:S(2)}, u32[]{:S(2)}) collective-permute-start(bf16[256,768]{1,0:T(8,128)(2,1)S(1)} %pad_maximum_fusion.1), channel_id=1, source_target_pairs={{0,1},{1,0},{2,3},{3,2},{4,5},{5,4},{6,7},{7,6},{8,9},{9,8},{10,11... | collective-permute-start | bytes 1179656 | tf_op jit(solution)/shard_map/ppermute | solution.py:822
  6.9 1.0 copy-start.8
  6.9 1.0 copy-start.9
  6.9 1.1 copy-start.10
  6.9 1.1 copy-start.11
  6.9 1.1 copy-start.12
  7.0 33.6 %collective-permute-start.2 = (bf16[1152,512]{1,0:T(8,128)(2,1)S(1)}, bf16[1152,512]{1,0:T(8,128)(2,1)S(1)}, u32[]{:S(2)}, u32[]{:S(2)}) collective-permute-start(bf16[1152,512]{1,0:T(8,128)(2,1)S(1)} %pad_maximum_fusion), channel_id=1, source_target_pairs={{0,1},{1,0},{2,3},{3,2},{4,5},{5,4},{6,7},{7,6},{8,9},{9,8},{10,11... | collective-permute-start | bytes 3538952 | tf_op jit(solution)/shard_map/ppermute | solution.py:822
  23.6 0.8 copy-start.3
  24.4 1.7 %collective-permute-start.1 = (bf16[256,768]{1,0:T(8,128)(2,1)S(1)}, bf16[256,768]{1,0:T(8,128)(2,1)S(1)}, u32[]{:S(2)}, u32[]{:S(2)}) collective-permute-start(bf16[256,768]{1,0:T(8,128)(2,1)S(1)} %collective-permute-done.mine_ref), channel_id=1, source_target_pairs={{0,2},{2,0},{4,6},{6,4},{8,10},{10,8},{12,14},{14,12},{16,18},{18,... | collective-permute-start | bytes 1179656 | tf_op jit(solution)/shard_map/ppermute | solution.py:822
  39.8 0.8 copy-start.13
  40.6 2.9 %copy-start.19 = (bf16[1152,512]{1,0:T(8,128)(2,1)}, bf16[1152,512]{1,0:T(8,128)(2,1)S(1)}, u32[]{:S(2)}) copy-start(bf16[1152,512]{1,0:T(8,128)(2,1)S(1)} %collective-permute-done.2.mine_far) | copy-start | bytes 3538948
  40.6 2.8 %collective-permute-start.3 = (bf16[1152,512]{1,0:T(8,128)(2,1)S(1)}, bf16[1152,512]{1,0:T(8,128)(2,1)S(1)}, u32[]{:S(2)}, u32[]{:S(2)}) collective-permute-start(bf16[1152,512]{1,0:T(8,128)(2,1)S(1)} %collective-permute-done.2.mine_far), channel_id=1, source_target_pairs={{0,2},{2,0},{4,6},{6,4},{8,10},{10,8},{12,14},{14,12},{16,18},{18,... | collective-permute-start | bytes 3538952 | tf_op jit(solution)/shard_map/ppermute | solution.py:822
  43.4 1.1 copy-start.20
  74.3 3.1 %collective-permute-start.5 = (bf16[2,576,512]{2,1,0:T(8,128)(2,1)}, bf16[2,576,512]{2,1,0:T(8,128)(2,1)S(1)}, u32[]{:S(2)}, u32[]{:S(2)}) collective-permute-start(bf16[2,576,512]{2,1,0:T(8,128)(2,1)} %get-tuple-element.105), channel_id=1, source_target_pairs={{0,2},{2,0},{4,6},{6,4},{8,10},{10,8},{12,14},{14,12},{16,18},{18,... | collective-permute-start | bytes 3538952 | tf_op jit(solution)/shard_map/ppermute | solution.py:822
  74.5 6.0 %collective-permute-start.4 = (bf16[2,576,512]{2,1,0:T(8,128)(2,1)}, bf16[2,576,512]{2,1,0:T(8,128)(2,1)S(1)}, u32[]{:S(2)}, u32[]{:S(2)}) collective-permute-start(bf16[2,576,512]{2,1,0:T(8,128)(2,1)} %get-tuple-element.103), channel_id=1, source_target_pairs={{0,2},{2,0},{4,6},{6,4},{8,10},{10,8},{12,14},{14,12},{16,18},{18,... | collective-permute-start | bytes 3538952 | tf_op jit(solution)/shard_map/ppermute | solution.py:822
  77.4 3.1 %copy-start.16 = (bf16[2,576,512]{2,1,0:T(8,128)(2,1)S(1)}, bf16[2,576,512]{2,1,0:T(8,128)(2,1)}, u32[]{:S(2)}) copy-start(bf16[2,576,512]{2,1,0:T(8,128)(2,1)} %get-tuple-element.102) | copy-start | bytes 3538948
  79.1 17.2 %collective-permute-start.7 = (bf16[576,512]{1,0:T(8,128)(2,1)S(1)}, bf16[576,512]{1,0:T(8,128)(2,1)S(1)}, u32[]{:S(2)}, u32[]{:S(2)}) collective-permute-start(bf16[576,512]{1,0:T(8,128)(2,1)S(1)} %get-tuple-element.168), channel_id=1, source_target_pairs={{0,1},{1,0},{2,3},{3,2},{4,5},{5,4},{6,7},{7,6},{8,9},{9,8},{10,11... | collective-permute-start | bytes 1769480 | tf_op jit(solution)/shard_map/ppermute | solution.py:822
  80.5 1.9 %copy-start.7 = (bf16[512,768]{1,0:T(8,128)(2,1)S(1)}, bf16[512,768]{1,0:T(8,128)(2,1)}, u32[]{:S(2)}) copy-start(bf16[512,768]{1,0:T(8,128)(2,1)} %get-tuple-element.108.pack_ref.oth_pack_ref) | copy-start | bytes 2359300
  80.5 1.9 %copy-start.14 = (bf16[2,512,256]{2,1,0:T(8,128)(2,1)S(1)}, bf16[2,512,256]{2,1,0:T(8,128)(2,1)}, u32[]{:S(2)}) copy-start(bf16[2,512,256]{2,1,0:T(8,128)(2,1)} %copy-done.13) | copy-start | bytes 1572868
  80.5 1.9 %copy-start.15 = (bf16[2,512,256]{2,1,0:T(8,128)(2,1)S(1)}, bf16[2,512,256]{2,1,0:T(8,128)(2,1)}, u32[]{:S(2)}) copy-start(bf16[2,512,256]{2,1,0:T(8,128)(2,1)} %get-tuple-element.107.gctx_ref) | copy-start | bytes 1572868
  80.9 15.6 %collective-permute-start.6 = (bf16[2,288,512]{2,1,0:T(8,128)(2,1)S(1)}, bf16[2,288,512]{2,1,0:T(8,128)(2,1)S(1)}, u32[]{:S(2)}, u32[]{:S(2)}) collective-permute-start(bf16[2,288,512]{2,1,0:T(8,128)(2,1)S(1)} %get-tuple-element.106), channel_id=1, source_target_pairs={{0,4},{2,6},{4,0},{6,2},{8,12},{10,14},{12,8},{14,10},{16,20},{18,... | collective-permute-start | bytes 1769480 | tf_op jit(solution)/shard_map/ppermute | solution.py:822
  96.2 2.0 %copy-start.5 = (bf16[2,512,256]{2,1,0:T(8,128)(2,1)S(1)}, bf16[2,512,256]{2,1,0:T(8,128)(2,1)}, u32[]{:S(2)}) copy-start(bf16[2,512,256]{2,1,0:T(8,128)(2,1)} %get-tuple-element.122.gctx_ref) | copy-start | bytes 1572868
  96.3 2.0 %copy-start = (bf16[2,1024,512]{2,1,0:T(8,128)(2,1)S(1)}, bf16[2,1024,512]{2,1,0:T(8,128)(2,1)}, u32[]{:S(2)}) copy-start(bf16[2,1024,512]{2,1,0:T(8,128)(2,1)} %get-tuple-element.89.kv_ref.kv_far) | copy-start | bytes 6291460
  96.5 1.8 %copy-start.1 = (bf16[512,768]{1,0:T(8,128)(2,1)S(1)}, bf16[512,768]{1,0:T(8,128)(2,1)}, u32[]{:S(2)}) copy-start(bf16[512,768]{1,0:T(8,128)(2,1)} %get-tuple-element.115.pack_ref.own_pack_ref) | copy-start | bytes 2359300
  96.5 1.9 %copy-start.4 = (bf16[2,512,256]{2,1,0:T(8,128)(2,1)S(1)}, bf16[2,512,256]{2,1,0:T(8,128)(2,1)}, u32[]{:S(2)}) copy-start(bf16[2,512,256]{2,1,0:T(8,128)(2,1)} %copy-done.3) | copy-start | bytes 1572868
  96.5 9.3 %collective-permute-start.8 = (bf16[288,512]{1,0:T(8,128)(2,1)S(1)}, bf16[288,512]{1,0:T(8,128)(2,1)S(1)}, u32[]{:S(2)}, u32[]{:S(2)}) collective-permute-start(bf16[288,512]{1,0:T(8,128)(2,1)S(1)} %get-tuple-element.177), channel_id=1, source_target_pairs={{0,4},{2,6},{4,0},{6,2},{8,12},{10,14},{12,8},{14,10},{16,20},{18,... | collective-permute-start | bytes 884744 | tf_op jit(solution)/shard_map/ppermute | solution.py:822
  97.7 8.1 %collective-permute-start.9 = (bf16[288,512]{1,0:T(8,128)(2,1)S(1)}, bf16[288,512]{1,0:T(8,128)(2,1)S(1)}, u32[]{:S(2)}, u32[]{:S(2)}) collective-permute-start(bf16[288,512]{1,0:T(8,128)(2,1)S(1)} %get-tuple-element.112), channel_id=1, source_target_pairs={{0,1},{1,0},{2,3},{3,2},{4,5},{5,4},{6,7},{7,6},{8,9},{9,8},{10,11... | collective-permute-start | bytes 884744 | tf_op jit(solution)/shard_map/ppermute | solution.py:822
  98.2 8.0 %collective-permute-start.10 = (bf16[3,128,512]{2,1,0:T(8,128)(2,1)S(1)}, bf16[3,128,512]{2,1,0:T(8,128)(2,1)S(1)}, u32[]{:S(2)}, u32[]{:S(2)}) collective-permute-start(bf16[3,128,512]{2,1,0:T(8,128)(2,1)S(1)} %slice_bitcast_fusion), channel_id=1, source_target_pairs={{0,2},{2,0},{4,6},{6,4},{8,10},{10,8},{12,14},{14,12},{16,18},{18,... | collective-permute-start | bytes 1179656 | tf_op jit(solution)/shard_map/ppermute | solution.py:822
  106.4 10.9 %collective-permute-start.13 = (bf16[288,512]{1,0:T(8,128)(2,1)S(1)}, bf16[288,512]{1,0:T(8,128)(2,1)S(1)}, u32[]{:S(2)}, u32[]{:S(2)}) collective-permute-start(bf16[288,512]{1,0:T(8,128)(2,1)S(1)} %add_convert_fusion.7), channel_id=1, source_target_pairs={{0,8},{2,10},{4,12},{6,14},{8,0},{10,2},{12,4},{14,6},{16,24},{18,... | collective-permute-start | bytes 884744 | tf_op jit(solution)/shard_map/ppermute | solution.py:822
  108.5 11.3 %collective-permute-start.12 = (bf16[3,128,512]{2,1,0:T(8,128)(2,1)S(1)}, bf16[3,128,512]{2,1,0:T(8,128)(2,1)S(1)}, u32[]{:S(2)}, u32[]{:S(2)}) collective-permute-start(bf16[3,128,512]{2,1,0:T(8,128)(2,1)S(1)} %bitcast.79), channel_id=1, source_target_pairs={{0,2},{2,0},{4,6},{6,4},{8,10},{10,8},{12,14},{14,12},{16,18},{18,... | collective-permute-start | bytes 1179656 | tf_op jit(solution)/shard_map/ppermute | solution.py:822
  108.5 11.5 %collective-permute-start.11 = (bf16[3,128,512]{2,1,0:T(8,128)(2,1)S(1)}, bf16[3,128,512]{2,1,0:T(8,128)(2,1)S(1)}, u32[]{:S(2)}, u32[]{:S(2)}) collective-permute-start(bf16[3,128,512]{2,1,0:T(8,128)(2,1)S(1)} %fusion), channel_id=1, source_target_pairs={{0,1},{1,0},{2,3},{3,2},{4,5},{5,4},{6,7},{7,6},{8,9},{9,8},{10,11... | collective-permute-start | bytes 1179656 | tf_op jit(solution)/shard_map/ppermute | solution.py:822
  109.8 15.0 %copy-start.6 = (bf16[2,512,512]{2,1,0:T(8,128)(2,1)S(1)}, bf16[2,512,512]{2,1,0:T(8,128)(2,1)}, u32[]{:S(2)}) copy-start(bf16[2,512,512]{2,1,0:T(8,128)(2,1)} %tok_ref.4) | copy-start | bytes 3145732
  117.3 7.4 %copy-start.2 = (f32[2,512,512]{2,1,0:T(8,128)S(1)}, f32[2,512,512]{2,1,0:T(8,128)}, u32[]{:S(2)}) copy-start(f32[2,512,512]{2,1,0:T(8,128)} %get-tuple-element.128.grad_hidden_ref) | copy-start | bytes 6291460
  117.8 15.6 %collective-permute-start.14 = (bf16[288,512]{1,0:T(8,128)(2,1)S(1)}, bf16[288,512]{1,0:T(8,128)(2,1)S(1)}, u32[]{:S(2)}, u32[]{:S(2)}) collective-permute-start(bf16[288,512]{1,0:T(8,128)(2,1)S(1)} %add_convert_fusion.5), channel_id=1, source_target_pairs={{0,16},{2,18},{4,20},{6,22},{8,24},{10,26},{12,28},{14,30},{16,0},... | collective-permute-start | bytes 884744 | tf_op jit(solution)/shard_map/ppermute | solution.py:822
  120.1 8.8 %collective-permute-start.15 = (bf16[3,32,512]{2,1,0:T(8,128)(2,1)S(1)}, bf16[3,32,512]{2,1,0:T(8,128)(2,1)S(1)}, u32[]{:S(2)}, u32[]{:S(2)}) collective-permute-start(bf16[3,32,512]{2,1,0:T(8,128)(2,1)S(1)} %get-tuple-element.127), channel_id=1, source_target_pairs={{0,4},{2,6},{4,0},{6,2},{8,12},{10,14},{12,8},{14,10},{16,20},{18,... | collective-permute-start | bytes 294920 | tf_op jit(solution)/shard_map/ppermute | solution.py:822
  121.0 8.1 %collective-permute-start.16 = (bf16[3,32,512]{2,1,0:T(8,128)(2,1)S(1)}, bf16[3,32,512]{2,1,0:T(8,128)(2,1)S(1)}, u32[]{:S(2)}, u32[]{:S(2)}) collective-permute-start(bf16[3,32,512]{2,1,0:T(8,128)(2,1)S(1)} %get-tuple-element.172), channel_id=1, source_target_pairs={{0,8},{2,10},{4,12},{6,14},{8,0},{10,2},{12,4},{14,6},{16,24},{18,... | collective-permute-start | bytes 294920 | tf_op jit(solution)/shard_map/ppermute | solution.py:822
  121.7 8.5 %collective-permute-start.17 = (bf16[3,32,512]{2,1,0:T(8,128)(2,1)S(1)}, bf16[3,32,512]{2,1,0:T(8,128)(2,1)S(1)}, u32[]{:S(2)}, u32[]{:S(2)}) collective-permute-start(bf16[3,32,512]{2,1,0:T(8,128)(2,1)S(1)} %get-tuple-element.171), channel_id=1, source_target_pairs={{0,12},{2,14},{4,8},{6,10},{8,4},{10,6},{12,0},{14,2},{16,28},{18,... | collective-permute-start | bytes 294920 | tf_op jit(solution)/shard_map/ppermute | solution.py:848
  123.7 5.2 %collective-permute-start.18 = (f32[5,512]{1,0:T(8,128)S(1)}, f32[5,512]{1,0:T(8,128)S(1)}, u32[]{:S(2)}, u32[]{:S(2)}) collective-permute-start(f32[5,512]{1,0:T(8,128)S(1)} %pad_maximum_fusion.2), channel_id=1, source_target_pairs={{0,1},{1,0},{2,3},{3,2},{4,5},{5,4},{6,7},{7,6},{8,9},{9,8},{10,11... | collective-permute-start | bytes 30728 | tf_op jit(solution)/shard_map/ppermute | solution.py:822
  130.5 7.4 %collective-permute-start.19 = (bf16[112,512]{1,0:T(8,128)(2,1)S(1)}, bf16[112,512]{1,0:T(8,128)(2,1)S(1)}, u32[]{:S(2)}, u32[]{:S(2)}) collective-permute-start(bf16[112,512]{1,0:T(8,128)(2,1)S(1)} %concatenate.137), channel_id=1, source_target_pairs={{0,16},{2,18},{4,20},{6,22},{8,24},{10,26},{12,28},{14,30},{16,0},... | collective-permute-start | bytes 344072 | tf_op jit(solution)/shard_map/ppermute | solution.py:822
  133.5 22.1 %collective-permute-start.23 = (bf16[288,512]{1,0:T(8,128)(2,1)S(1)}, bf16[288,512]{1,0:T(8,128)(2,1)S(1)}, u32[]{:S(2)}, u32[]{:S(2)}) collective-permute-start(bf16[288,512]{1,0:T(8,128)(2,1)S(1)} %add_convert_fusion.4), channel_id=1, source_target_pairs={{0,4},{2,6},{4,0},{6,2},{8,12},{10,14},{12,8},{14,10},{16,20},{18,... | collective-permute-start | bytes 884744 | tf_op jit(solution)/shard_map/ppermute | solution.py:822
  134.4 21.2 %collective-permute-start.24 = (bf16[288,512]{1,0:T(8,128)(2,1)S(1)}, bf16[288,512]{1,0:T(8,128)(2,1)S(1)}, u32[]{:S(2)}, u32[]{:S(2)}) collective-permute-start(bf16[288,512]{1,0:T(8,128)(2,1)S(1)} %add_convert_fusion.4), channel_id=1, source_target_pairs={{0,8},{2,10},{4,12},{6,14},{8,0},{10,2},{12,4},{14,6},{16,24},{18,... | collective-permute-start | bytes 884744 | tf_op jit(solution)/shard_map/ppermute | solution.py:822
  134.7 20.9 %collective-permute-start.25 = (bf16[288,512]{1,0:T(8,128)(2,1)S(1)}, bf16[288,512]{1,0:T(8,128)(2,1)S(1)}, u32[]{:S(2)}, u32[]{:S(2)}) collective-permute-start(bf16[288,512]{1,0:T(8,128)(2,1)S(1)} %add_convert_fusion.4), channel_id=1, source_target_pairs={{0,12},{2,14},{4,8},{6,10},{8,4},{10,6},{12,0},{14,2},{16,28},{18,... | collective-permute-start | bytes 884744 | tf_op jit(solution)/shard_map/ppermute | solution.py:848
  138.1 11.8 %collective-permute-start.20 = (bf16[112,512]{1,0:T(8,128)(2,1)S(1)}, bf16[112,512]{1,0:T(8,128)(2,1)S(1)}, u32[]{:S(2)}, u32[]{:S(2)}) collective-permute-start(bf16[112,512]{1,0:T(8,128)(2,1)S(1)} %concatenate.139), channel_id=1, source_target_pairs={{0,4},{2,6},{4,0},{6,2},{8,12},{10,14},{12,8},{14,10},{16,20},{18,... | collective-permute-start | bytes 344072 | tf_op jit(solution)/shard_map/ppermute | solution.py:822
  138.6 14.0 %collective-permute-start.21 = (bf16[112,512]{1,0:T(8,128)(2,1)S(1)}, bf16[112,512]{1,0:T(8,128)(2,1)S(1)}, u32[]{:S(2)}, u32[]{:S(2)}) collective-permute-start(bf16[112,512]{1,0:T(8,128)(2,1)S(1)} %concatenate.139), channel_id=1, source_target_pairs={{0,8},{2,10},{4,12},{6,14},{8,0},{10,2},{12,4},{14,6},{16,24},{18,... | collective-permute-start | bytes 344072 | tf_op jit(solution)/shard_map/ppermute | solution.py:822
  149.9 5.7 %collective-permute-start.22 = (bf16[112,512]{1,0:T(8,128)(2,1)S(1)}, bf16[112,512]{1,0:T(8,128)(2,1)S(1)}, u32[]{:S(2)}, u32[]{:S(2)}) collective-permute-start(bf16[112,512]{1,0:T(8,128)(2,1)S(1)} %concatenate.139), channel_id=1, source_target_pairs={{0,12},{2,14},{4,8},{6,10},{8,4},{10,6},{12,0},{14,2},{16,28},{18,... | collective-permute-start | bytes 344072 | tf_op jit(solution)/shard_map/ppermute | solution.py:848
  156.8 3.5 %collective-permute-start.26 = (bf16[2,576,512]{2,1,0:T(8,128)(2,1)S(1)}, bf16[2,576,512]{2,1,0:T(8,128)(2,1)S(1)}, u32[]{:S(2)}, u32[]{:S(2)}) collective-permute-start(bf16[2,576,512]{2,1,0:T(8,128)(2,1)S(1)} %maximum_select_fusion.ffn_mine), channel_id=1, source_target_pairs={{0,2},{2,0},{4,6},{6,4},{8,10},{10,8},{12,14},{14,12},{16,18},{18,... | collective-permute-start | bytes 3538952 | tf_op jit(solution)/shard_map/ppermute | solution.py:822
  156.9 3.4 %collective-permute-start.27 = (bf16[400,512]{1,0:T(8,128)(2,1)S(1)}, bf16[400,512]{1,0:T(8,128)(2,1)S(1)}, u32[]{:S(2)}, u32[]{:S(2)}) collective-permute-start(bf16[400,512]{1,0:T(8,128)(2,1)S(1)} %concatenate.159), channel_id=1, source_target_pairs={{0,2},{2,0},{4,6},{6,4},{8,10},{10,8},{12,14},{14,12},{16,18},{18,... | collective-permute-start | bytes 1228808 | tf_op jit(solution)/shard_map/ppermute | solution.py:822
